TPU v7x, 128 devices: a whole 4x4x4 slice. The times are simulated.
128 devices in a mesh: row: 16 (over x_hi, y, core), vec: 8 (over z, x_lo).
Axes of the slice: x: 4 (x_hi: 2, x_lo: 2; x = x_hi * 2 + x_lo), y: 4, z: 4, core: 2. Of those that a mesh axis runs over, the one named last changes fastest.
Arguments:
- eigvecs: float32 [32768, 8192], P('row', 'vec'), may hold values from -6 to 6
- wy_v: float32 [2, 256, 256, 128], P(None, ('row', 'vec')), as said below
- wy_t: float32 [2, 256, 128, 128], P(None, ('row', 'vec')), as said below
Outputs:
- back_vectors: float32 [32768, 8192], P('row', 'vec')
Inputs may be any that keep to these rules, and one draw needn't show every extreme that they name: Each block wy_v[g, k] is unit lower trapezoidal: ones on its diagonal, zeros above it. wy_t[g, k] is upper triangular and makes I - wy_v[g, k] wy_t[g, k] wy_v[g, k]^T the product, in order, of the 128 reflectors I - tau_i v_i v_i^T of its columns v_i, with tau_i = 2 / (v_i^T v_i).
All inputs are finite; a program needn't handle non-finite values.
Results may differ from a plain program's by a relative error of at most 0.0003.
Values sent between devices are 32-bit elements; how exact they have to be, the bound alone decides.
No kernel may reach another device: no remote copies, remote signals or barrier semaphores. Data moves between devices by JAX's collectives and lax.ppermute only.
A program may use at most 128 MiB of HBM per device.

v0:
```python
import jax
import jax.numpy as jnp
from jax import lax
from jax.sharding import PartitionSpec as P


def passed_along(shard, axis, by):
    size = lax.axis_size(axis)
    pairs = [(i, i + by) for i in range(size) if 0 <= i + by < size]
    return lax.ppermute(shard, axis, pairs)


def apply_blocks(extended, reflectors, factors):
    band_width = reflectors.shape[2]

    def apply_one(block_index, working):
        start = (block_index * band_width).astype(jnp.int32)
        window_rows = lax.dynamic_slice_in_dim(working, start, 2 * band_width, 0)
        projected = lax.dot_general(
            reflectors[block_index],
            window_rows,
            (((0,), (0,)), ((), ())),
            precision=lax.Precision.HIGHEST,
            preferred_element_type=jnp.float32,
        )
        weights = jnp.dot(
            factors[block_index],
            projected,
            precision=lax.Precision.HIGHEST,
            preferred_element_type=jnp.float32,
        )
        correction = jnp.dot(
            reflectors[block_index],
            weights,
            precision=lax.Precision.HIGHEST,
            preferred_element_type=jnp.float32,
        )
        return lax.dynamic_update_slice_in_dim(working, window_rows - correction, start, 0)

    return lax.fori_loop(0, reflectors.shape[0], apply_one, extended)


def run_piece(current, incoming, col_start, piece_cols, reflectors, factors):
    band_width = incoming.shape[0]
    slab_cols = lax.dynamic_slice_in_dim(current, col_start, piece_cols, 1)
    extended = jnp.concatenate([incoming, slab_cols], axis=0)
    extended = apply_blocks(extended, reflectors, factors)
    current = lax.dynamic_update_slice_in_dim(current, extended[band_width:], col_start, 1)
    return (current, extended[:band_width], extended[extended.shape[0] - band_width :])


def keep_state(carried):
    return carried


def local(eigvecs, wy_v, wy_t):
    band_width = wy_t.shape[-1]
    rows_dev, cols_dev = eigvecs.shape
    row_count = lax.axis_size("row")
    row_index = lax.axis_index("row")
    piece_count = 4
    piece_cols = cols_dev // piece_count
    all_reflectors, all_factors = (
        lax.all_gather(wy_v, "vec", axis=1, tiled=True),
        lax.all_gather(wy_t, "vec", axis=1, tiled=True),
    )
    matrix = eigvecs
    step_count = row_count + piece_count - 1
    for group_index in range(all_reflectors.shape[0]):
        reflectors = all_reflectors[group_index]
        factors = all_factors[group_index]

        def advance(turn_index, carried_state):
            incoming = passed_along(carried_state[2], "row", 1)
            piece_index = turn_index - row_index
            active = (piece_index >= 0) & (piece_index < piece_count)
            col_start = jnp.clip(piece_index, 0, piece_count - 1) * piece_cols

            def process(carried):
                current, upper_rows, outgoing = carried
                current, top_rows, bottom_rows = run_piece(
                    current, incoming, col_start, piece_cols, reflectors, factors
                )
                upper_rows = lax.dynamic_update_slice_in_dim(upper_rows, top_rows, col_start, 1)
                return (current, upper_rows, bottom_rows)

            return lax.cond(active, process, keep_state, carried_state)

        start_upper = jnp.zeros((band_width, cols_dev), jnp.float32)
        start_edge = jnp.zeros((band_width, piece_cols), jnp.float32)
        matrix, upper_rows, last_edge = lax.fori_loop(
            0, step_count, advance, (matrix, start_upper, start_edge)
        )
        returned = passed_along(upper_rows, "row", -1)
        bottom = jnp.where(row_index < row_count - 1, returned, matrix[rows_dev - band_width :])
        matrix = jnp.concatenate([matrix[: rows_dev - band_width], bottom], axis=0)
    return matrix


def solution(mesh):
    placed = (
        P("row", "vec"),
        P(None, ("row", "vec"), None, None),
        P(None, ("row", "vec"), None, None),
    )
    return jax.shard_map(
        local, mesh=mesh, in_specs=placed, out_specs=P("row", "vec"), check_vma=False
    )
```

profile of v0, /device:TPU:29, one launch (start us, length us, event | category | flops | bytes accessed | tf_op | source)
XLA Modules:
  0.0 2212.6 jit_solution(11955178469399164258)
XLA Ops:
  6.5 8.4 copy.59
  15.8 53.3 %all-gather.5.cloned.1.call-done = f32[2,16,128,128]{3,2,1,0:T(8,128)} async-done(((f32[2,2,128,128]{3,2,1,0:T(8,128)}), f32[2,16,128,128]{3,2,1,0:T(8,128)}) %all-gather.5.cloned.1.call-update) | async-done | bytes 2097168 | tf_op jit(solution)/shard_map/all_gather | solution.py:65
  69.0 2.7 slice_bitcast_fusion.2
  71.7 89.0 %all-gather.3.cloned.1.call-done = f32[2,16,256,128]{3,2,1,0:T(8,128)} async-done(((f32[2,2,256,128]{3,2,1,0:T(8,128)}), f32[2,16,256,128]{3,2,1,0:T(8,128)}) %all-gather.3.cloned.1.call-update) | async-done | bytes 4194320 | tf_op jit(solution)/shard_map/all_gather | solution.py:64
  160.8 4.8 slice_bitcast_fusion
  166.5 1301.0 %while.64 = (s32[]{:T(128)}, f32[2048,1024]{1,0:T(8,128)}, f32[128,1024]{1,0:T(8,128)}, f32[128,256]{1,0:T(8,128)S(1)}, s32[]{:T(128)}, /*index=5*/f32[16,256,12...) while((s32[]{:T(128)}, f32[2048,1024]{1,0:T(8,128)}, f32[128,1024]{1,0:T(8,128)}, ...), condition=%wide.region_5.6_spmd, body=%wide.region_0.5_spmd.sunk | while | flops 252280832 | bytes 15534144 | solution.py:91
  167.8 2.3 collective-permute-done.1
  171.4 5.0 collective-permute-done.1
  177.7 5.0 collective-permute-done.1
  184.0 5.0 collective-permute-done.1
  190.2 5.0 collective-permute-done.1
  196.5 5.0 collective-permute-done.1
  202.8 5.0 collective-permute-done.1
  209.1 5.0 collective-permute-done.1
  215.3 5.0 collective-permute-done.1
  221.6 5.0 collective-permute-done.1
  227.9 5.9 collective-permute-done.1
  235.1 8.6 collective-permute-done.1
  244.9 8.6 collective-permute-done.1
  254.8 8.6 collective-permute-done.1
  264.7 8.6 collective-permute-done.1
  274.6 909.0 %collective-permute-done.1 = f32[128,256]{1,0:T(8,128)S(1)} collective-permute-done((f32[128,256]{1,0:T(8,128)S(1)}, f32[128,256]{1,0:T(8,128)S(1)}, u32[]{:S(2)}, u32[]{:S(2)}) %collective-permute-start.1) | collective-permute-done | bytes 131104 | tf_op jit(solution)/shard_map/while/body/eval_jaxpr/ppermute | solution.py:10
  1183.6 63.6 %conditional.4 = ((f32[2048,1024]{1,0:T(8,128)}, f32[128,1024]{1,0:T(8,128)}, f32[128,256]{1,0:T(8,128)S(1)})) conditional(s32[]{:T(128)} %convert_element_type.16, (f32[2048,1024]{1,0:T(8,128)}, f32[128,1024]{1,0:T(8,128)}, f32[128,256]{1,0:T(8,128)S(1)}) %tuple.130, (s32[]{:T(128)}, f32[2048,1024]{1,0:T(8,128)}, f32[128,256]{1,0:T(8,128)S(1)}, ...), branch_computations={%region_1.1_spmd, %region_2.4_spmd} | conditional | flops 252280832 | bytes 15009605 | solution.py:87
  1185.5 59.6 %while.62 = (s32[]{:T(128)}, f32[2176,256]{1,0:T(8,128)S(1)}, f32[16,256,128]{2,1,0:T(8,128)}, f32[16,128,128]{2,1,0:T(8,128)}, s32[]{:T(128)}, /*index=5*/s32[]{:T(128)}, s32[]{:T(128)}, s32[]{:T(128)}) while((s32[]{:T(128)}, f32[2176,256]{1,0:T(8,128)S(1)}, f32[16,256,128]{2,1,0:T(8,128)}, f32[16,128,128]{2,1,0:T(8,128)}, s32[]{:T(128)}, ...), condition=%wide.region_4.3_spmd, body=%wide.region_3.2_spmd.sunk | while | flops 251723776 | bytes 1640075 | solution.py:40
  1248.5 8.6 collective-permute-done.1
  1257.1 63.6 %conditional.4 = ((f32[2048,1024]{1,0:T(8,128)}, f32[128,1024]{1,0:T(8,128)}, f32[128,256]{1,0:T(8,128)S(1)})) conditional(s32[]{:T(128)} %convert_element_type.16, (f32[2048,1024]{1,0:T(8,128)}, f32[128,1024]{1,0:T(8,128)}, f32[128,256]{1,0:T(8,128)S(1)}) %tuple.130, (s32[]{:T(128)}, f32[2048,1024]{1,0:T(8,128)}, f32[128,256]{1,0:T(8,128)S(1)}, ...), branch_computations={%region_1.1_spmd, %region_2.4_spmd} | conditional | flops 252280832 | bytes 15009605 | solution.py:87
  1259.0 59.6 %while.62 = (s32[]{:T(128)}, f32[2176,256]{1,0:T(8,128)S(1)}, f32[16,256,128]{2,1,0:T(8,128)}, f32[16,128,128]{2,1,0:T(8,128)}, s32[]{:T(128)}, /*index=5*/s32[]{:T(128)}, s32[]{:T(128)}, s32[]{:T(128)}) while((s32[]{:T(128)}, f32[2176,256]{1,0:T(8,128)S(1)}, f32[16,256,128]{2,1,0:T(8,128)}, f32[16,128,128]{2,1,0:T(8,128)}, s32[]{:T(128)}, ...), condition=%wide.region_4.3_spmd, body=%wide.region_3.2_spmd.sunk | while | flops 251723776 | bytes 1640075 | solution.py:40
  1322.0 8.4 collective-permute-done.1
  1330.4 63.6 %conditional.4 = ((f32[2048,1024]{1,0:T(8,128)}, f32[128,1024]{1,0:T(8,128)}, f32[128,256]{1,0:T(8,128)S(1)})) conditional(s32[]{:T(128)} %convert_element_type.16, (f32[2048,1024]{1,0:T(8,128)}, f32[128,1024]{1,0:T(8,128)}, f32[128,256]{1,0:T(8,128)S(1)}) %tuple.130, (s32[]{:T(128)}, f32[2048,1024]{1,0:T(8,128)}, f32[128,256]{1,0:T(8,128)S(1)}, ...), branch_computations={%region_1.1_spmd, %region_2.4_spmd} | conditional | flops 252280832 | bytes 15009605 | solution.py:87
  1332.2 59.5 %while.62 = (s32[]{:T(128)}, f32[2176,256]{1,0:T(8,128)S(1)}, f32[16,256,128]{2,1,0:T(8,128)}, f32[16,128,128]{2,1,0:T(8,128)}, s32[]{:T(128)}, /*index=5*/s32[]{:T(128)}, s32[]{:T(128)}, s32[]{:T(128)}) while((s32[]{:T(128)}, f32[2176,256]{1,0:T(8,128)S(1)}, f32[16,256,128]{2,1,0:T(8,128)}, f32[16,128,128]{2,1,0:T(8,128)}, s32[]{:T(128)}, ...), condition=%wide.region_4.3_spmd, body=%wide.region_3.2_spmd.sunk | while | flops 251723776 | bytes 1640075 | solution.py:40
  1395.2 8.6 collective-permute-done.1
  1403.9 63.6 %conditional.4 = ((f32[2048,1024]{1,0:T(8,128)}, f32[128,1024]{1,0:T(8,128)}, f32[128,256]{1,0:T(8,128)S(1)})) conditional(s32[]{:T(128)} %convert_element_type.16, (f32[2048,1024]{1,0:T(8,128)}, f32[128,1024]{1,0:T(8,128)}, f32[128,256]{1,0:T(8,128)S(1)}) %tuple.130, (s32[]{:T(128)}, f32[2048,1024]{1,0:T(8,128)}, f32[128,256]{1,0:T(8,128)S(1)}, ...), branch_computations={%region_1.1_spmd, %region_2.4_spmd} | conditional | flops 252280832 | bytes 15009605 | solution.py:87
  1405.8 59.6 %while.62 = (s32[]{:T(128)}, f32[2176,256]{1,0:T(8,128)S(1)}, f32[16,256,128]{2,1,0:T(8,128)}, f32[16,128,128]{2,1,0:T(8,128)}, s32[]{:T(128)}, /*index=5*/s32[]{:T(128)}, s32[]{:T(128)}, s32[]{:T(128)}) while((s32[]{:T(128)}, f32[2176,256]{1,0:T(8,128)S(1)}, f32[16,256,128]{2,1,0:T(8,128)}, f32[16,128,128]{2,1,0:T(8,128)}, s32[]{:T(128)}, ...), condition=%wide.region_4.3_spmd, body=%wide.region_3.2_spmd.sunk | while | flops 251723776 | bytes 1640075 | solution.py:40
  1468.8 7.8 slice.50
  1477.7 8.3 pad_maximum_fusion.2
  1486.9 700.3 %while.65 = (s32[]{:T(128)}, f32[2048,1024]{1,0:T(8,128)}, f32[128,1024]{1,0:T(8,128)}, f32[128,256]{1,0:T(8,128)S(1)}, s32[]{:T(128)}, /*index=5*/f32[16,256,12...) while((s32[]{:T(128)}, f32[2048,1024]{1,0:T(8,128)}, ...), condition=%wide.region_11.12_spmd, body=%wide.region_6.11_spmd.sunk | while | flops 252280832 | bytes 15533636 | solution.py:91
  1488.2 1.9 collective-permute-done
  1494.7 4.6 collective-permute-done
  1500.6 5.0 collective-permute-done
  1506.9 5.0 collective-permute-done
  1513.2 5.0 collective-permute-done
  1519.4 5.0 collective-permute-done
  1525.7 5.0 collective-permute-done
  1532.0 5.0 collective-permute-done
  1538.3 5.0 collective-permute-done
  1544.5 5.0 collective-permute-done
  1550.8 5.0 collective-permute-done
  1557.1 5.0 collective-permute-done
  1563.4 5.0 collective-permute-done
  1569.7 5.0 collective-permute-done
  1575.9 381.1 %collective-permute-done = f32[128,256]{1,0:T(8,128)S(1)} collective-permute-done((f32[128,256]{1,0:T(8,128)S(1)}, f32[128,256]{1,0:T(8,128)S(1)}, u32[]{:S(2)}, u32[]{:S(2)}) %collective-permute-start) | collective-permute-done | bytes 131104 | tf_op jit(solution)/shard_map/while/body/eval_jaxpr/ppermute | solution.py:10
  1957.1 50.1 %conditional.5 = ((f32[2048,1024]{1,0:T(8,128)}, f32[128,1024]{1,0:T(8,128)}, f32[128,256]{1,0:T(8,128)S(1)})) conditional(s32[]{:T(128)} %convert_element_type.17, (f32[2048,1024]{1,0:T(8,128)}, f32[128,1024]{1,0:T(8,128)}, f32[128,256]{1,0:T(8,128)S(1)}) %tuple.133, (s32[]{:T(128)}, f32[2048,1024]{1,0:T(8,128)}, f32[128,256]{1,0:T(8,128)S(1)}, ...), branch_computations={%region_7.7_spmd, %region_8.10_spmd} | conditional | flops 252280832 | bytes 15009097 | solution.py:87
  1958.9 46.1 %while.63 = (s32[]{:T(128)}, f32[2176,256]{1,0:T(8,128)S(1)}, f32[16,256,128]{2,1,0:T(8,128)}, f32[16,128,128]{2,1,0:T(8,128)S(1)}, s32[]{:T(128)}, /*index=5*/s32[]{:T(128)}, s32[]{:T(128)}, s32[]{:T(128)}) while((s32[]{:T(128)}, f32[2176,256]{1,0:T(8,128)S(1)}, f32[16,256,128]{2,1,0:T(8,128)}, f32[16,128,128]{2,1,0:T(8,128)S(1)}, ...), condition=%wide.region_10.9_spmd, body=%wide.region_9.8_spmd.sunk | while | flops 251723776 | bytes 1639567 | solution.py:40
  2008.5 8.6 collective-permute-done
  2017.1 50.1 %conditional.5 = ((f32[2048,1024]{1,0:T(8,128)}, f32[128,1024]{1,0:T(8,128)}, f32[128,256]{1,0:T(8,128)S(1)})) conditional(s32[]{:T(128)} %convert_element_type.17, (f32[2048,1024]{1,0:T(8,128)}, f32[128,1024]{1,0:T(8,128)}, f32[128,256]{1,0:T(8,128)S(1)}) %tuple.133, (s32[]{:T(128)}, f32[2048,1024]{1,0:T(8,128)}, f32[128,256]{1,0:T(8,128)S(1)}, ...), branch_computations={%region_7.7_spmd, %region_8.10_spmd} | conditional | flops 252280832 | bytes 15009097 | solution.py:87
  2018.9 46.1 %while.63 = (s32[]{:T(128)}, f32[2176,256]{1,0:T(8,128)S(1)}, f32[16,256,128]{2,1,0:T(8,128)}, f32[16,128,128]{2,1,0:T(8,128)S(1)}, s32[]{:T(128)}, /*index=5*/s32[]{:T(128)}, s32[]{:T(128)}, s32[]{:T(128)}) while((s32[]{:T(128)}, f32[2176,256]{1,0:T(8,128)S(1)}, f32[16,256,128]{2,1,0:T(8,128)}, f32[16,128,128]{2,1,0:T(8,128)S(1)}, ...), condition=%wide.region_10.9_spmd, body=%wide.region_9.8_spmd.sunk | while | flops 251723776 | bytes 1639567 | solution.py:40
  2068.5 8.7 collective-permute-done
  2077.1 50.1 %conditional.5 = ((f32[2048,1024]{1,0:T(8,128)}, f32[128,1024]{1,0:T(8,128)}, f32[128,256]{1,0:T(8,128)S(1)})) conditional(s32[]{:T(128)} %convert_element_type.17, (f32[2048,1024]{1,0:T(8,128)}, f32[128,1024]{1,0:T(8,128)}, f32[128,256]{1,0:T(8,128)S(1)}) %tuple.133, (s32[]{:T(128)}, f32[2048,1024]{1,0:T(8,128)}, f32[128,256]{1,0:T(8,128)S(1)}, ...), branch_computations={%region_7.7_spmd, %region_8.10_spmd} | conditional | flops 252280832 | bytes 15009097 | solution.py:87
  2079.0 46.1 %while.63 = (s32[]{:T(128)}, f32[2176,256]{1,0:T(8,128)S(1)}, f32[16,256,128]{2,1,0:T(8,128)}, f32[16,128,128]{2,1,0:T(8,128)S(1)}, s32[]{:T(128)}, /*index=5*/s32[]{:T(128)}, s32[]{:T(128)}, s32[]{:T(128)}) while((s32[]{:T(128)}, f32[2176,256]{1,0:T(8,128)S(1)}, f32[16,256,128]{2,1,0:T(8,128)}, f32[16,128,128]{2,1,0:T(8,128)S(1)}, ...), condition=%wide.region_10.9_spmd, body=%wide.region_9.8_spmd.sunk | while | flops 251723776 | bytes 1639567 | solution.py:40
  2128.6 8.6 collective-permute-done
  2137.1 50.1 %conditional.5 = ((f32[2048,1024]{1,0:T(8,128)}, f32[128,1024]{1,0:T(8,128)}, f32[128,256]{1,0:T(8,128)S(1)})) conditional(s32[]{:T(128)} %convert_element_type.17, (f32[2048,1024]{1,0:T(8,128)}, f32[128,1024]{1,0:T(8,128)}, f32[128,256]{1,0:T(8,128)S(1)}) %tuple.133, (s32[]{:T(128)}, f32[2048,1024]{1,0:T(8,128)}, f32[128,256]{1,0:T(8,128)S(1)}, ...), branch_computations={%region_7.7_spmd, %region_8.10_spmd} | conditional | flops 252280832 | bytes 15009097 | solution.py:87
  2139.0 46.1 %while.63 = (s32[]{:T(128)}, f32[2176,256]{1,0:T(8,128)S(1)}, f32[16,256,128]{2,1,0:T(8,128)}, f32[16,128,128]{2,1,0:T(8,128)S(1)}, s32[]{:T(128)}, /*index=5*/s32[]{:T(128)}, s32[]{:T(128)}, s32[]{:T(128)}) while((s32[]{:T(128)}, f32[2176,256]{1,0:T(8,128)S(1)}, f32[16,256,128]{2,1,0:T(8,128)}, f32[16,128,128]{2,1,0:T(8,128)S(1)}, ...), condition=%wide.region_10.9_spmd, body=%wide.region_9.8_spmd.sunk | while | flops 251723776 | bytes 1639567 | solution.py:40
  2188.5 7.8 slice.54
  2197.5 8.3 pad_maximum_fusion.3
  (499 shorter events, 507.1 us)
Async XLA Ops:
  6.5 62.5 %all-gather.5.cloned.1.call-start = ((), (), s32[]{:S(2)}) async-start(), calls=%async_computation.1 | async-start | bytes 2359296 | tf_op jit(solution)/shard_map/all_gather | solution.py:65
  15.0 145.8 %all-gather.3.cloned.1.call-start = ((), (), s32[]{:S(2)}) async-start(), calls=%async_computation | async-start | bytes 4718592 | tf_op jit(solution)/shard_map/all_gather | solution.py:64
  166.5 3.6 collective-permute-start.1
  170.1 6.3 collective-permute-start.1
  176.4 6.3 collective-permute-start.1
  182.7 6.3 collective-permute-start.1
  188.9 6.3 collective-permute-start.1
  195.2 6.3 collective-permute-start.1
  201.5 6.3 collective-permute-start.1
  207.8 6.3 collective-permute-start.1
  214.0 6.3 collective-permute-start.1
  220.3 6.3 collective-permute-start.1
  226.6 7.2 collective-permute-start.1
  233.8 9.9 collective-permute-start.1
  243.6 9.9 collective-permute-start.1
  253.5 9.9 collective-permute-start.1
  263.4 9.9 collective-permute-start.1
  273.3 910.3 %collective-permute-start.1 = (f32[128,256]{1,0:T(8,128)S(1)}, f32[128,256]{1,0:T(8,128)S(1)}, u32[]{:S(2)}, u32[]{:S(2)}) collective-permute-start(f32[128,256]{1,0:T(8,128)S(1)} %get-tuple-element.796), channel_id=1, source_target_pairs={{0,8},{8,16},{16,24},{24,32},{32,40},{40,48},{48,56},{56,64},{64,7... | collective-permute-start | bytes 393224 | tf_op jit(solution)/shard_map/while/body/eval_jaxpr/ppermute | solution.py:10
  1247.2 9.9 collective-permute-start.1
  1320.7 9.7 collective-permute-start.1
  1393.9 9.9 collective-permute-start.1
  1467.5 9.1 collective-permute-start.2
  1486.9 3.2 collective-permute-start
  1490.2 3.2 collective-permute-start
  1493.4 5.9 collective-permute-start
  1499.3 6.3 collective-permute-start
  1505.6 6.3 collective-permute-start
  1511.9 6.3 collective-permute-start
  1518.1 6.3 collective-permute-start
  1524.4 6.3 collective-permute-start
  1530.7 6.3 collective-permute-start
  1537.0 6.3 collective-permute-start
  1543.2 6.3 collective-permute-start
  1549.5 6.3 collective-permute-start
  1555.8 6.3 collective-permute-start
  1562.1 6.3 collective-permute-start
  1568.4 6.3 collective-permute-start
  1574.6 382.4 %collective-permute-start = (f32[128,256]{1,0:T(8,128)S(1)}, f32[128,256]{1,0:T(8,128)S(1)}, u32[]{:S(2)}, u32[]{:S(2)}) collective-permute-start(f32[128,256]{1,0:T(8,128)S(1)} %get-tuple-element.826), channel_id=1, source_target_pairs={{0,8},{8,16},{16,24},{24,32},{32,40},{40,48},{48,56},{56,64},{64,7... | collective-permute-start | bytes 393224 | tf_op jit(solution)/shard_map/while/body/eval_jaxpr/ppermute | solution.py:10
  2007.2 9.9 collective-permute-start
  2067.2 10.0 collective-permute-start
  2127.3 9.9 collective-permute-start
  2187.2 9.1 collective-permute-start.3
Sparse Core Ops, SparseCore 0:
  15.1 53.8 all-gather.4
  70.7 90.0 all-gather.2
where the time goes:
time: 2220 us; the launch traced here: 2210 us
  waiting for transfers between devices  1640 us (74%)
  matrix products  417 us (19%)
  local copies, waits for them, and re-layouts  64.3 us (3%)
  starting transfers between devices  51.3 us (2%)
    ppermute x40, waiting for transfers between devices, passed_along(): return lax.ppermute(shard, axis, pairs)  1500 us
    dot_general x128, matrix products, apply_one(): lax.dot_general(reflectors[block_index], window_rows, (((0,), (0,)), ((),...  166 us
    dot_general x128, matrix products, apply_one(): jnp.dot(reflectors[block_index], weights, precision=lax.Precision.HIGHEST...  163 us
    all_gather x1, waiting for transfers between devices, local(): lax.all_gather(wy_v, 'vec', axis=1, tiled=True)  89 us
    dot_general x128, matrix products, apply_one(): jnp.dot(factors[block_index], projected, precision=lax.Precision.HIGHEST,...  87.7 us
    all_gather x1, waiting for transfers between devices, local(): lax.all_gather(wy_t, 'vec', axis=1, tiled=True)  53.3 us
    ppermute x40, starting transfers between devices, passed_along(): return lax.ppermute(shard, axis, pairs)  51.3 us
  transfers between devices with their start and end apart: 42, of which 40 were waited for; matrix products, arithmetic and copies ran while one was open for 1% of the time, Pallas kernels for 0%

commit v1 on v0

v1 whole, which is shorter than its diff:
```python
import jax
import jax.numpy as jnp
from jax import lax
from jax.experimental import pallas as pl
from jax.experimental.pallas import tpu as pltpu
from jax.sharding import PartitionSpec as P

F32 = jnp.float32
BF16 = jnp.bfloat16
Z_SIZE = 4
Y_SIZE = 4
HIGHEST = lax.Precision.HIGHEST


def dot(a, b, precision=None):
    return jnp.dot(a, b, precision=precision, preferred_element_type=F32)


def split(value):
    high = value.astype(BF16)
    return high, (value - high.astype(F32)).astype(BF16)


def dot3(a, b):
    a_high, a_low = split(a)
    b_high, b_low = split(b)
    return dot(a_high, b_high) + (dot(a_low, b_high) + dot(a_high, b_low))


def along_z(value, by):
    pairs = [(v, ((v // 2 + by) % Z_SIZE) * 2 + v % 2) for v in range(2 * Z_SIZE)]
    return lax.ppermute(value, "vec", pairs)


def across_x(value):
    return lax.ppermute(value, "vec", [(v, v ^ 1) for v in range(2 * Z_SIZE)])


def across_core(value):
    return lax.ppermute(value, "row", [(i, i ^ 1) for i in range(lax.axis_size("row"))])


def along_y(value, by):
    def target(i):
        high, y, core = i // (2 * Y_SIZE), (i // 2) % Y_SIZE, i % 2
        return (high * Y_SIZE + (y + by) % Y_SIZE) * 2 + core

    return lax.ppermute(value, "row", [(i, target(i)) for i in range(lax.axis_size("row"))])


def from_next_row(value):
    return lax.ppermute(value, "row", [(i + 1, i) for i in range(lax.axis_size("row") - 1)])


def gather_groups(packed):
    first, second = {(0, 0): packed[0]}, {(0, 0): packed[1]}
    first[0, 1] = across_x(first[0, 0])
    first[3, 0] = along_z(first[0, 0], 1)
    first[1, 0] = along_z(first[0, 0], -1)
    first[3, 1] = across_x(first[3, 0])
    first[2, 0] = along_z(first[3, 0], 1)
    first[1, 1] = along_z(first[0, 1], -1)
    own, _ = lax.optimization_barrier((second[0, 0], first[3, 1]))
    first[2, 1] = across_x(first[2, 0])
    second[3, 0] = along_z(own, 1)
    second[1, 0] = along_z(own, -1)
    own, _ = lax.optimization_barrier((own, first[2, 1]))
    second[0, 1] = across_x(own)
    second[2, 0] = along_z(second[3, 0], 1)
    second[3, 1] = along_z(second[0, 1], 1)
    second[1, 1] = along_z(second[0, 1], -1)
    second[2, 1] = across_x(second[2, 0])
    keys = [(dz, dx) for dz in range(Z_SIZE) for dx in range(2)]
    return [first[key] for key in keys], [second[key] for key in keys]


def place_of(index):
    vec = lax.axis_index("vec")
    z, x = vec // 2, vec % 2
    dz, dx = index // 2, index % 2
    return lax.rem(z + dz, Z_SIZE) * 2 + lax.rem(x + dx, 2)


def pick_kernel(*refs):
    pieces, out, sem = refs[:-2], refs[-2], refs[-1]
    for index, piece in enumerate(pieces):

        @pl.when(place_of(index) == 0)
        def _():
            copy = pltpu.make_async_copy(piece, out, sem)
            copy.start()
            copy.wait()


def pick_first(pieces):
    return pl.pallas_call(
        pick_kernel,
        out_shape=jax.ShapeDtypeStruct(pieces[0].shape, F32),
        in_specs=[pl.BlockSpec(memory_space=pl.ANY)] * len(pieces),
        out_specs=pl.BlockSpec(memory_space=pl.ANY),
        scratch_shapes=[pltpu.SemaphoreType.DMA],
    )(*pieces)


def build_reflection(packed):
    width = packed.shape[1]
    rows = lax.broadcasted_iota(jnp.int32, (width, width), 0)
    cols = lax.broadcasted_iota(jnp.int32, (width, width), 1)
    top = packed[:width]
    unit = jnp.where(rows == cols, 1.0, jnp.where(rows > cols, top, 0.0))
    factor = jnp.where(rows <= cols, top, 0.0)
    vectors = jnp.concatenate([unit, packed[width:]], axis=0)
    weighted = dot(vectors, factor, HIGHEST)
    update = lax.dot_general(
        weighted, vectors, (((1,), (1,)), ((), ())), precision=HIGHEST, preferred_element_type=F32
    )
    rows = lax.broadcasted_iota(jnp.int32, update.shape, 0)
    cols = lax.broadcasted_iota(jnp.int32, update.shape, 1)
    high, low = split(jnp.where(rows == cols, 1.0, 0.0) - update)
    return jnp.concatenate([high, low], axis=0)


def sweep(pieces, extra, block_count, prologue, data, tail, unit_in, width, unit_cols):
    piece_count = len(pieces)
    data_cols = data.shape[1]
    total_cols = data_cols + unit_cols
    out_blocks = block_count - 1
    last_data = data.shape[0] // width - 1
    has_tail = tail is not None

    def kernel(*refs):
        ins = list(refs[: piece_count + 1])
        at = piece_count + 1
        data_ref = refs[at]
        other_ref = refs[at + 1]
        out, unit_out, state_out, blocks, reflections, sems = refs[at + 2 :]
        body(
            piece_count, block_count, prologue, width, has_tail,
            ins[:piece_count], ins[piece_count], data_ref, other_ref,
            out, unit_out, state_out, blocks, reflections, sems,
        )

    if has_tail:
        other = tail
        other_spec = pl.BlockSpec((width, data_cols), lambda k: (jnp.clip(k - last_data - 1, 0, 1), 0))
    else:
        other = unit_in
        other_spec = pl.BlockSpec((width, unit_in.shape[1]), lambda k: (k, 0))
    any_spec = pl.BlockSpec(memory_space=pl.ANY)
    flops = 2 * block_count * (2 * width) ** 2 * (total_cols * 3 + 2 * width * 6)
    return pl.pallas_call(
        kernel,
        grid=(block_count,),
        out_shape=(
            jax.ShapeDtypeStruct((out_blocks * width, data_cols), F32),
            jax.ShapeDtypeStruct((out_blocks * width, unit_cols), F32),
            jax.ShapeDtypeStruct((width, total_cols), F32),
        ),
        in_specs=[any_spec] * (piece_count + 1)
        + [pl.BlockSpec((width, data_cols), lambda k: (jnp.minimum(k, last_data), 0)), other_spec],
        out_specs=(
            pl.BlockSpec((width, data_cols), lambda k: (jnp.maximum(k - 1, 0), 0)),
            pl.BlockSpec((width, unit_cols), lambda k: (jnp.maximum(k - 1, 0), 0)),
            pl.BlockSpec((width, total_cols), lambda k: (0, 0)),
        ),
        scratch_shapes=[
            pltpu.VMEM((block_count, 2 * width, width), F32),
            pltpu.VMEM((2, 4 * width, 2 * width), BF16),
            pltpu.SemaphoreType.DMA((piece_count + 1,)),
        ],
        compiler_params=pltpu.CompilerParams(vmem_limit_bytes=40 * 2**20),
        cost_estimate=pl.CostEstimate(flops=flops, bytes_accessed=2 * 4 * data.size, transcendentals=0),
    )(*pieces, extra, data, other)


def body(
    piece_count, block_count, prologue, width, has_tail,
    pieces, extra, data, other, out, unit_out, state, blocks, reflections, sems,
):
    step = pl.program_id(0)
    is_first = lax.axis_index("row") == 0
    data_cols = data.shape[1]
    total_cols = state.shape[1]
    main_blocks = 2 * piece_count

    @pl.when(step == 0)
    def _():
        copies = []
        for index, piece in enumerate(pieces):
            place = place_of(index)
            copies.append(pltpu.make_async_copy(piece, blocks.at[pl.ds(2 * place, 2)], sems.at[index]))
        left = block_count - main_blocks
        copies.append(
            pltpu.make_async_copy(
                extra.at[pl.ds(0, left)], blocks.at[pl.ds(main_blocks, left)], sems.at[piece_count]
            )
        )
        for copy in copies:
            copy.start()
        for copy in copies:
            copy.wait()
        state[...] = jnp.zeros_like(state)
        reflections[0] = build_reflection(blocks[0])

    @pl.when(step == prologue)
    def _():
        @pl.when(jnp.logical_not(is_first))
        def _():
            state[:, :data_cols] = jnp.zeros((width, data_cols), F32)

        rows = lax.broadcasted_iota(jnp.int32, (width, width), 0)
        cols = lax.broadcasted_iota(jnp.int32, (width, width), 1)
        if total_cols - width > data_cols:
            state[:, data_cols : total_cols - width] = jnp.zeros((width, total_cols - width - data_cols), F32)
        state[:, total_cols - width :] = jnp.where(rows == cols, 1.0, 0.0)

    current = lax.rem(step, 2)
    reflection = reflections[current]
    upcoming = build_reflection(blocks[jnp.minimum(step + 1, block_count - 1)])
    for start in range(0, total_cols, 2 * width):
        size = min(2 * width, total_cols - start)
        if start < data_cols:
            lower = data[:, start : start + size]
            if has_tail:
                lower = jnp.where(step >= main_blocks, other[:, start : start + size], lower)
        elif has_tail:
            lower = jnp.zeros((width, size), F32)
        else:
            lower = jnp.concatenate([other[...], jnp.zeros((width, size - other.shape[1]), F32)], axis=1)
            lower = jnp.where(step >= prologue, lower, 0.0)
        high, low = split(jnp.concatenate([state[:, start : start + size], lower], axis=0))
        both = dot(reflection, high)
        cross = dot(reflection[: 2 * width], low)
        result = both[: 2 * width] + (both[2 * width :] + cross)
        if start < data_cols:
            out[:, start : start + size] = result[:width]
        else:
            unit_out[:, start - data_cols : start - data_cols + size] = result[:width]
        state[:, start : start + size] = result[width:]
    reflections[1 - current] = upcoming


def correct_kernel(rows_ref, response_ref, incoming_ref, out_ref, high_ref, low_ref):
    @pl.when(pl.program_id(0) == 0)
    def _():
        high, low = split(incoming_ref[...])
        high_ref[...] = high
        low_ref[...] = low

    high, low = split(response_ref[...])
    out_ref[...] = rows_ref[...] + (
        dot(high, high_ref[...]) + (dot(low, high_ref[...]) + dot(high, low_ref[...]))
    )


def correct(rows, response, incoming, tile=256):
    count, cols = rows.shape
    depth = response.shape[1]
    return pl.pallas_call(
        correct_kernel,
        grid=(count // tile,),
        out_shape=jax.ShapeDtypeStruct(rows.shape, F32),
        in_specs=[
            pl.BlockSpec((tile, cols), lambda k: (k, 0)),
            pl.BlockSpec((tile, depth), lambda k: (k, 0)),
            pl.BlockSpec((depth, cols), lambda k: (0, 0)),
        ],
        out_specs=pl.BlockSpec((tile, cols), lambda k: (k, 0)),
        scratch_shapes=[pltpu.VMEM((depth, cols), BF16), pltpu.VMEM((depth, cols), BF16)],
        compiler_params=pltpu.CompilerParams(vmem_limit_bytes=40 * 2**20),
    )(rows, response, incoming)


def incoming_state(transition, offset):
    row = lax.axis_index("row")
    core, y = row % 2, (row // 2) % Y_SIZE
    half = offset.shape[1] // 2
    quarter = half // Y_SIZE
    own_half = lax.dynamic_slice_in_dim(offset, core * half, half, 1)
    sent_half = lax.dynamic_slice_in_dim(offset, (1 - core) * half, half, 1)
    received = across_core(jnp.concatenate([transition, sent_half], axis=1))
    depth = transition.shape[1]
    own = jnp.concatenate([transition, own_half], axis=1)
    lower = jnp.where(core == 0, own, received)
    upper = jnp.where(core == 0, received, own)
    chip = dot(upper[:, :depth], lower, HIGHEST)
    chip_transition = chip[:, :depth]
    chip_offset = chip[:, depth:] + upper[:, depth:]

    def with_quarter(index):
        return jnp.concatenate(
            [chip_transition, lax.dynamic_slice_in_dim(chip_offset, index * quarter, quarter, 1)], axis=1
        )

    relative = [with_quarter(y)] + [along_y(with_quarter((y + d) % Y_SIZE), d) for d in range(1, Y_SIZE)]
    stacked = jnp.stack(relative)
    chips = [lax.dynamic_index_in_dim(stacked, (y - at) % Y_SIZE, 0, False) for at in range(Y_SIZE)]
    states = [chips[0][:, depth:]]
    for at in range(1, Y_SIZE):
        states.append(dot(chips[at][:, :depth], states[-1], HIGHEST) + chips[at][:, depth:])
    size = lax.axis_size("row")
    entering = lax.ppermute(states[-1], "row", [(i, i + size // 2) for i in range(size // 2)])
    result = [entering]
    for at in range(Y_SIZE - 1):
        result.append(dot(chips[at][:, :depth], result[-1], HIGHEST) + chips[at][:, depth:])
    result = jnp.stack(result)
    back = [lax.dynamic_index_in_dim(result, (y + d) % Y_SIZE, 0, False) for d in range(Y_SIZE)]
    arrived = jnp.stack([back[0]] + [along_y(back[d], d) for d in range(1, Y_SIZE)])
    into_chip = jnp.concatenate(
        [lax.dynamic_index_in_dim(arrived, (y - at) % Y_SIZE, 0, False) for at in range(Y_SIZE)], axis=1
    )
    into_second = dot(lower[:, :depth], into_chip, HIGHEST) + lower[:, depth:]
    kept = jnp.where(core == 0, into_chip, into_second)
    given = jnp.where(core == 0, into_second, into_chip)
    other = across_core(given)
    return jnp.where(
        core == 0, jnp.concatenate([kept, other], axis=1), jnp.concatenate([other, kept], axis=1)
    )


def local(eigvecs, wy_v, wy_t):
    width = wy_t.shape[-1]
    rows_dev, cols_dev = eigvecs.shape
    own_blocks = rows_dev // width
    below = lax.broadcasted_iota(jnp.int32, (width, width), 0) > lax.broadcasted_iota(
        jnp.int32, (width, width), 1
    )
    packed = jnp.concatenate(
        [jnp.where(below, wy_v[:, :, :width], wy_t), wy_v[:, :, width:]], axis=2
    )
    tail = from_next_row(eigvecs[: 2 * width])
    first, second = gather_groups(packed)
    first_extra = from_next_row(pick_first(first))
    second_extra = from_next_row(pick_first(second))
    middle, middle_unit, first_state = sweep(
        first, first_extra, own_blocks + 2, 2, eigvecs, tail, None, width, width
    )
    rows, response, second_state = sweep(
        second, second_extra, own_blocks + 1, 1, middle, None, middle_unit, width, 2 * width
    )
    unit = first_state[:, cols_dev:]
    transition = jnp.concatenate(
        [jnp.concatenate([unit, jnp.zeros_like(unit)], axis=1), second_state[:, cols_dev:]], axis=0
    )
    offset = jnp.concatenate([first_state[:, :cols_dev], second_state[:, :cols_dev]], axis=0)
    incoming = incoming_state(transition, offset)
    return correct(rows, response, incoming)


def solution(mesh):
    placed = (
        P("row", "vec"),
        P(None, ("row", "vec"), None, None),
        P(None, ("row", "vec"), None, None),
    )
    return jax.shard_map(
        local, mesh=mesh, in_specs=placed, out_specs=P("row", "vec"), check_vma=False
    )
```

time: 2220 us -> 208 us (0.09)
  the two profiles are of different devices: /device:TPU:29 before, /device:TPU:5 now
where the time goes in v1:
time: 208 us; the launch traced here: 207 us
  Pallas kernels  78 us (38%)
  waiting for transfers between devices  56.2 us (27%)
  starting transfers between devices  45.8 us (22%)
  local copies, waits for them, and re-layouts  15.1 us (7%)
  matrix products  5.71 us (3%)
  other arithmetic  5.43 us (3%)
    pallas_call x2, Pallas kernels, sweep(): pl.pallas_call(kernel, grid=(block_count,), out_shape=(jax.ShapeDtypeStru...  53 us
    ppermute x6, waiting for transfers between devices, along_y(): lax.ppermute(value, 'row', [(i, target(i)) for i in range(lax.axis_size('...  24.5 us
    ppermute x3, starting transfers between devices, from_next_row(): lax.ppermute(value, 'row', [(i + 1, i) for i in range(lax.axis_size('row'...  24.1 us
    pallas_call x2, Pallas kernels, pick_first(): pl.pallas_call(pick_kernel, out_shape=jax.ShapeDtypeStruct(pieces[0].shap...  18.1 us
    unnamed x68, local copies, waits for them, and re-layouts  12.4 us
    ppermute x5, waiting for transfers between devices, across_x(): return lax.ppermute(value, 'vec', [(v, v ^ 1) for v in range(2 * Z_SIZE)])  11.9 us
    ppermute x9, waiting for transfers between devices, along_z(): return lax.ppermute(value, 'vec', pairs)  9.31 us
    ppermute x9, starting transfers between devices, along_z(): return lax.ppermute(value, 'vec', pairs)  7.97 us
  transfers between devices with their start and end apart: 26, of which 14 were waited for; matrix products, arithmetic and copies ran while one was open for 1% of the time, Pallas kernels for 22%

profile of v1, /device:TPU:5, one launch (start us, length us, event | category | flops | bytes accessed | tf_op | source)
XLA Modules:
  0.0 207.1 jit_solution(2677281232225436088)
XLA Ops:
  0.0 1.2 fusion.23
  1.3 1.7 collective-permute-start
  3.0 8.2 %collective-permute-done.refs_6_ = f32[2,256,128]{2,1,0:T(8,128)S(1)} collective-permute-done((f32[2,256,128]{2,1,0:T(8,128)S(1)}, f32[2,256,128]{2,1,0:T(8,128)S(1)}, u32[]{:S(2)}, u32[]{:S(2)}) %collective-permute-start) | collective-permute-done | bytes 262176 | tf_op jit(solution)/shard_map/ppermute | solution.py:32
  11.1 0.9 collective-permute-start.1
  12.0 2.3 %slice.78 = f32[256,1024]{1,0:T(8,128)} slice(f32[2048,1024]{1,0:T(8,128)} %refs_9_.1), slice={[0:256], [0:1024]} | slice | bytes 2097152 | tf_op jit(solution)/shard_map/slice | solution.py:331
  14.3 3.4 %collective-permute-start.16 = (f32[256,1024]{1,0:T(8,128)}, f32[256,1024]{1,0:T(8,128)}, u32[]{:S(2)}, u32[]{:S(2)}) collective-permute-start(f32[256,1024]{1,0:T(8,128)} %slice.78), channel_id=1, source_target_pairs={{8,0},{16,8},{24,16},{32,24},{40,32},{48,40},{56,48},{64,56},{72,6... | collective-permute-start | bytes 3145736 | tf_op jit(solution)/shard_map/ppermute | solution.py:52
  17.8 1.1 collective-permute-done.2.refs_4_
  18.9 0.9 collective-permute-start.3
  19.8 0.8 collective-permute-start.12
  20.6 2.5 %collective-permute-start.13 = (f32[2,256,128]{2,1,0:T(8,128)S(1)}, f32[2,256,128]{2,1,0:T(8,128)S(1)}, u32[]{:S(2)}, u32[]{:S(2)}) collective-permute-start(f32[2,256,128]{2,1,0:T(8,128)S(1)} %get-tuple-element.43.refs_0_), channel_id=1, source_target_pairs={{0,6},{1,7},{2,0},{3,1},{4,2},{5,3},{6,4},{7,5},{8,14},{9,15},{10,... | collective-permute-start | bytes 786440 | tf_op jit(solution)/shard_map/ppermute | solution.py:32
  23.0 3.8 %collective-permute-done.3.refs_5_ = f32[2,256,128]{2,1,0:T(8,128)S(1)} collective-permute-done((f32[2,256,128]{2,1,0:T(8,128)S(1)}, f32[2,256,128]{2,1,0:T(8,128)S(1)}, u32[]{:S(2)}, u32[]{:S(2)}) %collective-permute-start.3) | collective-permute-done | bytes 262176 | tf_op jit(solution)/shard_map/ppermute | solution.py:36
  26.8 1.2 collective-permute-start.4
  28.0 4.2 %collective-permute-done.12.refs_1_ = f32[2,256,128]{2,1,0:T(8,128)S(1)} collective-permute-done((f32[2,256,128]{2,1,0:T(8,128)S(1)}, f32[2,256,128]{2,1,0:T(8,128)S(1)}, u32[]{:S(2)}, u32[]{:S(2)}) %collective-permute-start.12) | collective-permute-done | bytes 262176 | tf_op jit(solution)/shard_map/ppermute | solution.py:36
  32.1 1.1 collective-permute-start.14
  33.2 0.6 collective-permute-start.5
  33.8 4.0 %collective-permute-done.4.refs_1_ = f32[2,256,128]{2,1,0:T(8,128)S(1)} collective-permute-done((f32[2,256,128]{2,1,0:T(8,128)S(1)}, f32[2,256,128]{2,1,0:T(8,128)S(1)}, u32[]{:S(2)}, u32[]{:S(2)}) %collective-permute-start.4) | collective-permute-done | bytes 262176 | tf_op jit(solution)/shard_map/ppermute | solution.py:36
  37.8 1.0 collective-permute-start.6
  38.8 0.5 collective-permute-start.9
  39.3 0.7 copy-done.28
  40.0 1.1 collective-permute-start.10
  41.1 9.1 %shard_map.38 = f32[2,256,128]{2,1,0:T(8,128)} custom-call(f32[2,256,128]{2,1,0:T(8,128)} %copy-done.4, f32[2,256,128]{2,1,0:T(8,128)} %copy-done.20, f32[2,256,128]{2,1,0:T(8,128)} %copy-done.22, f32[2,256,128]{2,1,0:T(8,128)} %copy-done.28, f32[2,256,128]{2,1,0:T(8,128)} %copy-done.8, f32[2,256,128]{2,1,0:T(8,128)} %copy-done.14, ...), custom_call_target="tpu_custom_call" | custom-call | tf_op jit(solution)/shard_map/pallas_call | solution.py:96
  50.3 18.6 %collective-permute-start.15 = (f32[2,256,128]{2,1,0:T(8,128)}, f32[2,256,128]{2,1,0:T(8,128)}, u32[]{:S(2)}, u32[]{:S(2)}) collective-permute-start(f32[2,256,128]{2,1,0:T(8,128)} %shard_map.38), channel_id=1, source_target_pairs={{8,0},{16,8},{24,16},{32,24},{40,32},{48,40},{56,48},{64,56},{72,6... | collective-permute-start | bytes 786440 | tf_op jit(solution)/shard_map/ppermute | solution.py:52
  69.1 0.7 copy-done.26
  69.7 9.0 %shard_map.37 = f32[2,256,128]{2,1,0:T(8,128)} custom-call(f32[2,256,128]{2,1,0:T(8,128)} %copy-done.2, f32[2,256,128]{2,1,0:T(8,128)} %copy-done.16, f32[2,256,128]{2,1,0:T(8,128)} %copy-done.24, f32[2,256,128]{2,1,0:T(8,128)} %copy-done.26, f32[2,256,128]{2,1,0:T(8,128)} %copy-done.18, f32[2,256,128]{2,1,0:T(8,128)} %collective-permute-done.9.refs_5_, ...), custom_call_target="tpu_custom_call" | custom-call | tf_op jit(solution)/shard_map/pallas_call | solution.py:96
  78.8 2.1 collective-permute-start.11
  81.0 3.4 %copy-done.30 = f32[2048,1024]{1,0:T(8,128)S(1)} copy-done((f32[2048,1024]{1,0:T(8,128)S(1)}, f32[2048,1024]{1,0:T(8,128)}, u32[]{:S(2)}) %copy-start.30) | copy-done | bytes 8388632
  84.4 27.8 %shard_map.39 = (f32[2176,1024]{1,0:T(8,128)}, f32[2176,128]{1,0:T(8,128)S(1)}, f32[128,1152]{1,0:T(8,128)S(1)}) custom-call(f32[2,256,128]{2,1,0:T(8,128)S(1)} %copy-done.5, f32[2,256,128]{2,1,0:T(8,128)S(1)} %copy-done.21, f32[2,256,128]{2,1,0:T(8,128)S(1)} %copy-done.23, f32[2,256,128]{2,1,0:T(8,128)S(1)} %copy-done.29, f32[2,256,128]{2,1,0:T(8,128)S(1)} %copy-done.9, ...), custom_call_target="tpu_custom_call" | custom-call | flops 11777605632 | bytes 16777216 | tf_op jit(solution)/shard_map/pallas_call | solution.py:151
  112.3 25.2 %shard_map.40 = (f32[2048,1024]{1,0:T(8,128)S(1)}, f32[2048,256]{1,0:T(8,128)S(1)}, f32[128,1280]{1,0:T(8,128)S(1)}) custom-call(f32[2,256,128]{2,1,0:T(8,128)S(1)} %copy-done.3, f32[2,256,128]{2,1,0:T(8,128)S(1)} %copy-done.17, f32[2,256,128]{2,1,0:T(8,128)S(1)} %copy-done.25, f32[2,256,128]{2,1,0:T(8,128)S(1)} %copy-done.27, ...), custom_call_target="tpu_custom_call" | custom-call | flops 11978932224 | bytes 17825792 | tf_op jit(solution)/shard_map/pallas_call | solution.py:151
  137.5 3.4 %copy-done = f32[2048,1024]{1,0:T(8,128)} copy-done((f32[2048,1024]{1,0:T(8,128)}, f32[2048,1024]{1,0:T(8,128)S(1)}, u32[]{:S(2)}) %copy-start) | copy-done | bytes 8388632
  141.0 0.1 fusion.2
  141.1 0.1 pad_maximum_fusion.1
  141.1 0.1 collective-permute-start.17
  141.3 2.3 %collective-permute-done.17 = f32[256,768]{1,0:T(8,128)} collective-permute-done((f32[256,768]{1,0:T(8,128)S(1)}, f32[256,768]{1,0:T(8,128)}, u32[]{:S(2)}, u32[]{:S(2)}) %collective-permute-start.17) | collective-permute-done | bytes 786464 | tf_op jit(solution)/shard_map/ppermute | solution.py:40
  143.6 1.2 broadcast_select_fusion.1
  144.9 0.8 fusion.14
  145.7 0.1 slice_add_fusion
  145.8 0.1 constant_dynamic-slice_fusion.4
  145.9 1.1 fusion.4
  147.1 3.3 %collective-permute-start.19 = (f32[256,384]{1,0:T(8,128)}, f32[256,384]{1,0:T(8,128)}, u32[]{:S(2)}, u32[]{:S(2)}) collective-permute-start(f32[256,384]{1,0:T(8,128)} %get-tuple-element.49), channel_id=1, source_target_pairs={{0,32},{8,40},{16,48},{24,56},{32,0},{40,8},{48,16},{56,24},{64,96... | collective-permute-start | bytes 1179656 | tf_op jit(solution)/shard_map/ppermute | solution.py:48
  150.3 7.7 %collective-permute-done.20 = f32[256,384]{1,0:T(8,128)} collective-permute-done((f32[256,384]{1,0:T(8,128)}, f32[256,384]{1,0:T(8,128)}, u32[]{:S(2)}, u32[]{:S(2)}) %collective-permute-start.20) | collective-permute-done | bytes 393248 | tf_op jit(solution)/shard_map/ppermute | solution.py:48
  158.0 1.6 collective-permute-done.19
  159.5 9.1 %collective-permute-done.18 = f32[256,384]{1,0:T(8,128)} collective-permute-done((f32[256,384]{1,0:T(8,128)}, f32[256,384]{1,0:T(8,128)}, u32[]{:S(2)}, u32[]{:S(2)}) %collective-permute-start.18) | collective-permute-done | bytes 393248 | tf_op jit(solution)/shard_map/ppermute | solution.py:48
  168.6 1.3 pad_maximum_fusion
  170.0 0.1 dynamic-slice_bitcast_fusion.3
  170.1 0.8 copy-done.31
  170.9 0.4 convolution_add_fusion.5
  171.3 0.4 convolution_add_fusion.4
  171.7 0.4 fusion.11
  172.0 1.3 collective-permute-start.21
  173.4 6.6 %collective-permute-done.21 = f32[256,128]{1,0:T(8,128)S(1)} collective-permute-done((f32[256,128]{1,0:T(8,128)S(1)}, f32[256,128]{1,0:T(8,128)S(1)}, u32[]{:S(2)}, u32[]{:S(2)}) %collective-permute-start.21) | collective-permute-done | bytes 131104 | tf_op jit(solution)/shard_map/ppermute | solution.py:302
  180.0 1.4 convolution_add_fusion.3
  181.4 1.4 convolution_add_fusion.2
  182.7 0.4 fusion
  183.2 0.1 collective-permute-start.24
  183.3 1.5 collective-permute-start.23
  184.9 2.3 %collective-permute-done.24 = f32[256,128]{1,0:T(8,128)S(1)} collective-permute-done((f32[256,128]{1,0:T(8,128)S(1)}, f32[256,128]{1,0:T(8,128)S(1)}, u32[]{:S(2)}, u32[]{:S(2)}) %collective-permute-start.24) | collective-permute-done | bytes 131104 | tf_op jit(solution)/shard_map/ppermute | solution.py:48
  187.1 1.6 collective-permute-done.23
  188.7 2.3 %collective-permute-done.22 = f32[256,128]{1,0:T(8,128)S(1)} collective-permute-done((f32[256,128]{1,0:T(8,128)S(1)}, f32[256,128]{1,0:T(8,128)S(1)}, u32[]{:S(2)}, u32[]{:S(2)}) %collective-permute-start.22) | collective-permute-done | bytes 131104 | tf_op jit(solution)/shard_map/ppermute | solution.py:48
  191.2 0.6 broadcast_select_fusion.3
  191.8 3.2 %collective-permute-start.25 = (f32[256,512]{1,0:T(8,128)S(1)}, f32[256,512]{1,0:T(8,128)S(1)}, u32[]{:S(2)}, u32[]{:S(2)}) collective-permute-start(f32[256,512]{1,0:T(8,128)S(1)} %get-tuple-element.28), channel_id=1, source_target_pairs={{0,8},{8,0},{16,24},{24,16},{32,40},{40,32},{48,56},{56,48},{64,72... | collective-permute-start | bytes 1572872 | tf_op jit(solution)/shard_map/ppermute | solution.py:40
  195.0 1.5 collective-permute-done.25
  196.6 0.2 maximum_select_fusion.incoming_ref
  196.8 3.4 %copy-done.1 = f32[2048,1024]{1,0:T(8,128)S(1)} copy-done((f32[2048,1024]{1,0:T(8,128)S(1)}, f32[2048,1024]{1,0:T(8,128)}, u32[]{:S(2)}) %copy-start.1) | copy-done | bytes 8388632
  200.2 6.9 %shard_map.41 = f32[2048,1024]{1,0:T(8,128)} custom-call(f32[2048,1024]{1,0:T(8,128)S(1)} %copy-done.1, f32[2048,256]{1,0:T(8,128)S(1)} %get-tuple-element.18.response_ref, f32[256,1024]{1,0:T(8,128)S(1)} %maximum_select_fusion.incoming_ref), custom_call_target="tpu_custom_call" | custom-call | tf_op jit(solution)/shard_map/pallas_call | solution.py:259
  (91 shorter events, 0.5 us)
Async XLA Ops:
  1.2 39.9 %copy-start.4 = (f32[2,256,128]{2,1,0:T(8,128)}, f32[2,256,128]{2,1,0:T(8,128)S(1)}, u32[]{:S(2)}) copy-start(f32[2,256,128]{2,1,0:T(8,128)S(1)} %get-tuple-element.43.refs_0_) | copy-start | bytes 786436
  1.2 49.0 %copy-start.2 = (f32[2,256,128]{2,1,0:T(8,128)}, f32[2,256,128]{2,1,0:T(8,128)S(1)}, u32[]{:S(2)}) copy-start(f32[2,256,128]{2,1,0:T(8,128)S(1)} %get-tuple-element.14.refs_0_) | copy-start | bytes 786436
  1.3 9.9 %collective-permute-start = (f32[2,256,128]{2,1,0:T(8,128)S(1)}, f32[2,256,128]{2,1,0:T(8,128)S(1)}, u32[]{:S(2)}, u32[]{:S(2)}) collective-permute-start(f32[2,256,128]{2,1,0:T(8,128)S(1)} %get-tuple-element.43.refs_0_), channel_id=1, source_target_pairs={{0,2},{1,3},{2,4},{3,5},{4,6},{5,7},{6,0},{7,1},{8,10},{9,11},{10,... | collective-permute-start | bytes 786440 | tf_op jit(solution)/shard_map/ppermute | solution.py:32
  11.1 30.0 %copy-start.6 = (f32[2,256,128]{2,1,0:T(8,128)}, f32[2,256,128]{2,1,0:T(8,128)S(1)}, u32[]{:S(2)}) copy-start(f32[2,256,128]{2,1,0:T(8,128)S(1)} %collective-permute-done.refs_6_) | copy-start | bytes 786436
  11.1 7.8 %collective-permute-start.2 = (f32[2,256,128]{2,1,0:T(8,128)S(1)}, f32[2,256,128]{2,1,0:T(8,128)S(1)}, u32[]{:S(2)}, u32[]{:S(2)}) collective-permute-start(f32[2,256,128]{2,1,0:T(8,128)S(1)} %collective-permute-done.refs_6_), channel_id=1, source_target_pairs={{0,2},{1,3},{2,4},{3,5},{4,6},{5,7},{6,0},{7,1},{8,10},{9,11},{10,... | collective-permute-start | bytes 786440 | tf_op jit(solution)/shard_map/ppermute | solution.py:32
  11.1 8.7 %collective-permute-start.1 = (f32[2,256,128]{2,1,0:T(8,128)S(1)}, f32[2,256,128]{2,1,0:T(8,128)S(1)}, u32[]{:S(2)}, u32[]{:S(2)}) collective-permute-start(f32[2,256,128]{2,1,0:T(8,128)S(1)} %collective-permute-done.refs_6_), channel_id=1, source_target_pairs={{0,1},{1,0},{2,3},{3,2},{4,5},{5,4},{6,7},{7,6},{8,9},{9,8},{10,11... | collective-permute-start | bytes 786440 | tf_op jit(solution)/shard_map/ppermute | solution.py:36
  14.3 66.6 %collective-permute-start.16 = (f32[256,1024]{1,0:T(8,128)}, f32[256,1024]{1,0:T(8,128)}, u32[]{:S(2)}, u32[]{:S(2)}) collective-permute-start(f32[256,1024]{1,0:T(8,128)} %slice.78), channel_id=1, source_target_pairs={{8,0},{16,8},{24,16},{32,24},{40,32},{48,40},{56,48},{64,56},{72,6... | collective-permute-start | bytes 3145736 | tf_op jit(solution)/shard_map/ppermute | solution.py:52
  18.9 22.2 %copy-start.8 = (f32[2,256,128]{2,1,0:T(8,128)}, f32[2,256,128]{2,1,0:T(8,128)S(1)}, u32[]{:S(2)}) copy-start(f32[2,256,128]{2,1,0:T(8,128)S(1)} %collective-permute-done.2.refs_4_) | copy-start | bytes 786436
  18.9 7.9 %collective-permute-start.3 = (f32[2,256,128]{2,1,0:T(8,128)S(1)}, f32[2,256,128]{2,1,0:T(8,128)S(1)}, u32[]{:S(2)}, u32[]{:S(2)}) collective-permute-start(f32[2,256,128]{2,1,0:T(8,128)S(1)} %collective-permute-done.2.refs_4_), channel_id=1, source_target_pairs={{0,1},{1,0},{2,3},{3,2},{4,5},{5,4},{6,7},{7,6},{8,9},{9,8},{10,11... | collective-permute-start | bytes 786440 | tf_op jit(solution)/shard_map/ppermute | solution.py:36
  19.8 21.3 %copy-start.10 = (f32[2,256,128]{2,1,0:T(8,128)}, f32[2,256,128]{2,1,0:T(8,128)S(1)}, u32[]{:S(2)}) copy-start(f32[2,256,128]{2,1,0:T(8,128)S(1)} %collective-permute-done.1.refs_7_) | copy-start | bytes 786436
  19.8 8.2 %collective-permute-start.7 = (f32[2,256,128]{2,1,0:T(8,128)S(1)}, f32[2,256,128]{2,1,0:T(8,128)S(1)}, u32[]{:S(2)}, u32[]{:S(2)}) collective-permute-start(f32[2,256,128]{2,1,0:T(8,128)S(1)} %get-tuple-element.14.refs_0_), channel_id=1, source_target_pairs={{0,2},{1,3},{2,4},{3,5},{4,6},{5,7},{6,0},{7,1},{8,10},{9,11},{10,... | collective-permute-start | bytes 786440 | tf_op jit(solution)/shard_map/ppermute | solution.py:32
  19.8 12.3 %collective-permute-start.12 = (f32[2,256,128]{2,1,0:T(8,128)S(1)}, f32[2,256,128]{2,1,0:T(8,128)S(1)}, u32[]{:S(2)}, u32[]{:S(2)}) collective-permute-start(f32[2,256,128]{2,1,0:T(8,128)S(1)} %get-tuple-element.43.refs_0_), channel_id=1, source_target_pairs={{0,1},{1,0},{2,3},{3,2},{4,5},{5,4},{6,7},{7,6},{8,9},{9,8},{10,11... | collective-permute-start | bytes 786440 | tf_op jit(solution)/shard_map/ppermute | solution.py:36
  20.6 12.6 %collective-permute-start.13 = (f32[2,256,128]{2,1,0:T(8,128)S(1)}, f32[2,256,128]{2,1,0:T(8,128)S(1)}, u32[]{:S(2)}, u32[]{:S(2)}) collective-permute-start(f32[2,256,128]{2,1,0:T(8,128)S(1)} %get-tuple-element.43.refs_0_), channel_id=1, source_target_pairs={{0,6},{1,7},{2,0},{3,1},{4,2},{5,3},{6,4},{7,5},{8,14},{9,15},{10,... | collective-permute-start | bytes 786440 | tf_op jit(solution)/shard_map/ppermute | solution.py:32
  26.8 14.3 %copy-start.14 = (f32[2,256,128]{2,1,0:T(8,128)}, f32[2,256,128]{2,1,0:T(8,128)S(1)}, u32[]{:S(2)}) copy-start(f32[2,256,128]{2,1,0:T(8,128)S(1)} %collective-permute-done.3.refs_5_) | copy-start | bytes 786436
  26.8 10.9 %collective-permute-start.4 = (f32[2,256,128]{2,1,0:T(8,128)S(1)}, f32[2,256,128]{2,1,0:T(8,128)S(1)}, u32[]{:S(2)}, u32[]{:S(2)}) collective-permute-start(f32[2,256,128]{2,1,0:T(8,128)S(1)} %get-tuple-element.14.refs_0_), channel_id=1, source_target_pairs={{0,1},{1,0},{2,3},{3,2},{4,5},{5,4},{6,7},{7,6},{8,9},{9,8},{10,11... | collective-permute-start | bytes 786440 | tf_op jit(solution)/shard_map/ppermute | solution.py:36
  28.0 41.0 %copy-start.12 = (f32[2,256,128]{2,1,0:T(8,128)}, f32[2,256,128]{2,1,0:T(8,128)S(1)}, u32[]{:S(2)}) copy-start(f32[2,256,128]{2,1,0:T(8,128)S(1)} %collective-permute-done.7.refs_6_) | copy-start | bytes 786436
  28.0 10.8 %collective-permute-start.8 = (f32[2,256,128]{2,1,0:T(8,128)S(1)}, f32[2,256,128]{2,1,0:T(8,128)S(1)}, u32[]{:S(2)}, u32[]{:S(2)}) collective-permute-start(f32[2,256,128]{2,1,0:T(8,128)S(1)} %collective-permute-done.7.refs_6_), channel_id=1, source_target_pairs={{0,2},{1,3},{2,4},{3,5},{4,6},{5,7},{6,0},{7,1},{8,10},{9,11},{10,... | collective-permute-start | bytes 786440 | tf_op jit(solution)/shard_map/ppermute | solution.py:32
  32.1 9.0 %copy-start.20 = (f32[2,256,128]{2,1,0:T(8,128)}, f32[2,256,128]{2,1,0:T(8,128)S(1)}, u32[]{:S(2)}) copy-start(f32[2,256,128]{2,1,0:T(8,128)S(1)} %collective-permute-done.12.refs_1_) | copy-start | bytes 786436
  32.1 7.2 %collective-permute-start.14 = (f32[2,256,128]{2,1,0:T(8,128)S(1)}, f32[2,256,128]{2,1,0:T(8,128)S(1)}, u32[]{:S(2)}, u32[]{:S(2)}) collective-permute-start(f32[2,256,128]{2,1,0:T(8,128)S(1)} %collective-permute-done.12.refs_1_), channel_id=1, source_target_pairs={{0,6},{1,7},{2,0},{3,1},{4,2},{5,3},{6,4},{7,5},{8,14},{9,15},{10,... | collective-permute-start | bytes 786440 | tf_op jit(solution)/shard_map/ppermute | solution.py:32
  33.2 7.9 %copy-start.22 = (f32[2,256,128]{2,1,0:T(8,128)}, f32[2,256,128]{2,1,0:T(8,128)S(1)}, u32[]{:S(2)}) copy-start(f32[2,256,128]{2,1,0:T(8,128)S(1)} %collective-permute-done.13.refs_2_) | copy-start | bytes 786436
  33.2 17.1 %collective-permute-start.5 = (f32[2,256,128]{2,1,0:T(8,128)S(1)}, f32[2,256,128]{2,1,0:T(8,128)S(1)}, u32[]{:S(2)}, u32[]{:S(2)}) collective-permute-start(f32[2,256,128]{2,1,0:T(8,128)S(1)} %get-tuple-element.14.refs_0_), channel_id=1, source_target_pairs={{0,6},{1,7},{2,0},{3,1},{4,2},{5,3},{6,4},{7,5},{8,14},{9,15},{10,... | collective-permute-start | bytes 786440 | tf_op jit(solution)/shard_map/ppermute | solution.py:32
  37.8 31.3 %copy-start.16 = (f32[2,256,128]{2,1,0:T(8,128)}, f32[2,256,128]{2,1,0:T(8,128)S(1)}, u32[]{:S(2)}) copy-start(f32[2,256,128]{2,1,0:T(8,128)S(1)} %collective-permute-done.4.refs_1_) | copy-start | bytes 786436
  37.8 31.2 %collective-permute-start.6 = (f32[2,256,128]{2,1,0:T(8,128)S(1)}, f32[2,256,128]{2,1,0:T(8,128)S(1)}, u32[]{:S(2)}, u32[]{:S(2)}) collective-permute-start(f32[2,256,128]{2,1,0:T(8,128)S(1)} %collective-permute-done.4.refs_1_), channel_id=1, source_target_pairs={{0,6},{1,7},{2,0},{3,1},{4,2},{5,3},{6,4},{7,5},{8,14},{9,15},{10,... | collective-permute-start | bytes 786440 | tf_op jit(solution)/shard_map/ppermute | solution.py:32
  38.8 30.2 %copy-start.18 = (f32[2,256,128]{2,1,0:T(8,128)}, f32[2,256,128]{2,1,0:T(8,128)S(1)}, u32[]{:S(2)}) copy-start(f32[2,256,128]{2,1,0:T(8,128)S(1)} %collective-permute-done.8.refs_4_) | copy-start | bytes 786436
  38.8 30.2 %collective-permute-start.9 = (f32[2,256,128]{2,1,0:T(8,128)S(1)}, f32[2,256,128]{2,1,0:T(8,128)}, u32[]{:S(2)}, u32[]{:S(2)}) collective-permute-start(f32[2,256,128]{2,1,0:T(8,128)S(1)} %collective-permute-done.8.refs_4_), channel_id=1, source_target_pairs={{0,1},{1,0},{2,3},{3,2},{4,5},{5,4},{6,7},{7,6},{8,9},{9,8},{10,11... | collective-permute-start | bytes 786440 | tf_op jit(solution)/shard_map/ppermute | solution.py:36
  39.3 0.7 copy-start.28
  40.0 29.0 %collective-permute-start.10 = (f32[2,256,128]{2,1,0:T(8,128)S(1)}, f32[2,256,128]{2,1,0:T(8,128)}, u32[]{:S(2)}, u32[]{:S(2)}) collective-permute-start(f32[2,256,128]{2,1,0:T(8,128)S(1)} %collective-permute-done.4.refs_1_), channel_id=1, source_target_pairs={{0,2},{1,3},{2,4},{3,5},{4,6},{5,7},{6,0},{7,1},{8,10},{9,11},{10,... | collective-permute-start | bytes 786440 | tf_op jit(solution)/shard_map/ppermute | solution.py:32
  50.2 30.7 %copy-start.5 = (f32[2,256,128]{2,1,0:T(8,128)S(1)}, f32[2,256,128]{2,1,0:T(8,128)}, u32[]{:S(2)}) copy-start(f32[2,256,128]{2,1,0:T(8,128)} %copy-done.4) | copy-start | bytes 786436
  50.2 30.7 %copy-start.7 = (f32[2,256,128]{2,1,0:T(8,128)S(1)}, f32[2,256,128]{2,1,0:T(8,128)}, u32[]{:S(2)}) copy-start(f32[2,256,128]{2,1,0:T(8,128)} %copy-done.6) | copy-start | bytes 786436
  50.3 30.7 %copy-start.9 = (f32[2,256,128]{2,1,0:T(8,128)S(1)}, f32[2,256,128]{2,1,0:T(8,128)}, u32[]{:S(2)}) copy-start(f32[2,256,128]{2,1,0:T(8,128)} %copy-done.8) | copy-start | bytes 786436
  50.3 30.7 %copy-start.11 = (f32[2,256,128]{2,1,0:T(8,128)S(1)}, f32[2,256,128]{2,1,0:T(8,128)}, u32[]{:S(2)}) copy-start(f32[2,256,128]{2,1,0:T(8,128)} %copy-done.10) | copy-start | bytes 786436
  50.3 30.7 %copy-start.15 = (f32[2,256,128]{2,1,0:T(8,128)S(1)}, f32[2,256,128]{2,1,0:T(8,128)}, u32[]{:S(2)}) copy-start(f32[2,256,128]{2,1,0:T(8,128)} %copy-done.14) | copy-start | bytes 786436
  50.3 30.7 %copy-start.21 = (f32[2,256,128]{2,1,0:T(8,128)S(1)}, f32[2,256,128]{2,1,0:T(8,128)}, u32[]{:S(2)}) copy-start(f32[2,256,128]{2,1,0:T(8,128)} %copy-done.20) | copy-start | bytes 786436
  50.3 30.7 %copy-start.23 = (f32[2,256,128]{2,1,0:T(8,128)S(1)}, f32[2,256,128]{2,1,0:T(8,128)}, u32[]{:S(2)}) copy-start(f32[2,256,128]{2,1,0:T(8,128)} %copy-done.22) | copy-start | bytes 786436
  50.3 18.7 %copy-start.24 = (f32[2,256,128]{2,1,0:T(8,128)}, f32[2,256,128]{2,1,0:T(8,128)S(1)}, u32[]{:S(2)}) copy-start(f32[2,256,128]{2,1,0:T(8,128)S(1)} %collective-permute-done.5.refs_2_) | copy-start | bytes 786436
  50.3 30.7 %copy-start.29 = (f32[2,256,128]{2,1,0:T(8,128)S(1)}, f32[2,256,128]{2,1,0:T(8,128)}, u32[]{:S(2)}) copy-start(f32[2,256,128]{2,1,0:T(8,128)} %copy-done.28) | copy-start | bytes 786436
  50.3 30.6 %collective-permute-start.15 = (f32[2,256,128]{2,1,0:T(8,128)}, f32[2,256,128]{2,1,0:T(8,128)}, u32[]{:S(2)}, u32[]{:S(2)}) collective-permute-start(f32[2,256,128]{2,1,0:T(8,128)} %shard_map.38), channel_id=1, source_target_pairs={{8,0},{16,8},{24,16},{32,24},{40,32},{48,40},{56,48},{64,56},{72,6... | collective-permute-start | bytes 786440 | tf_op jit(solution)/shard_map/ppermute | solution.py:52
  69.0 0.7 copy-start.26
  78.8 33.5 %copy-start.3 = (f32[2,256,128]{2,1,0:T(8,128)S(1)}, f32[2,256,128]{2,1,0:T(8,128)}, u32[]{:S(2)}) copy-start(f32[2,256,128]{2,1,0:T(8,128)} %copy-done.2) | copy-start | bytes 786436
  78.8 33.5 %copy-start.13 = (f32[2,256,128]{2,1,0:T(8,128)S(1)}, f32[2,256,128]{2,1,0:T(8,128)}, u32[]{:S(2)}) copy-start(f32[2,256,128]{2,1,0:T(8,128)} %copy-done.12) | copy-start | bytes 786436
  78.8 33.5 %copy-start.17 = (f32[2,256,128]{2,1,0:T(8,128)S(1)}, f32[2,256,128]{2,1,0:T(8,128)}, u32[]{:S(2)}) copy-start(f32[2,256,128]{2,1,0:T(8,128)} %copy-done.16) | copy-start | bytes 786436
  78.8 33.5 %copy-start.19 = (f32[2,256,128]{2,1,0:T(8,128)S(1)}, f32[2,256,128]{2,1,0:T(8,128)}, u32[]{:S(2)}) copy-start(f32[2,256,128]{2,1,0:T(8,128)} %copy-done.18) | copy-start | bytes 786436
  78.8 33.5 %copy-start.25 = (f32[2,256,128]{2,1,0:T(8,128)S(1)}, f32[2,256,128]{2,1,0:T(8,128)}, u32[]{:S(2)}) copy-start(f32[2,256,128]{2,1,0:T(8,128)} %copy-done.24) | copy-start | bytes 786436
  78.8 33.5 %copy-start.27 = (f32[2,256,128]{2,1,0:T(8,128)S(1)}, f32[2,256,128]{2,1,0:T(8,128)}, u32[]{:S(2)}) copy-start(f32[2,256,128]{2,1,0:T(8,128)} %copy-done.26) | copy-start | bytes 786436
  78.8 33.4 %collective-permute-start.11 = (f32[2,256,128]{2,1,0:T(8,128)}, f32[2,256,128]{2,1,0:T(8,128)S(1)}, u32[]{:S(2)}, u32[]{:S(2)}) collective-permute-start(f32[2,256,128]{2,1,0:T(8,128)} %shard_map.37), channel_id=1, source_target_pairs={{8,0},{16,8},{24,16},{32,24},{40,32},{48,40},{56,48},{64,56},{72,6... | collective-permute-start | bytes 786440 | tf_op jit(solution)/shard_map/ppermute | solution.py:52
  81.0 3.4 %copy-start.30 = (f32[2048,1024]{1,0:T(8,128)S(1)}, f32[2048,1024]{1,0:T(8,128)}, u32[]{:S(2)}) copy-start(f32[2048,1024]{1,0:T(8,128)} %refs_9_.1) | copy-start | bytes 25165828
  112.2 28.8 %copy-start.33 = (f32[128,128]{1,0:T(8,128)}, f32[128,128]{1,0:T(8,128)S(1)}, u32[]{:S(2)}) copy-start(f32[128,128]{1,0:T(8,128)S(1)} %slice.79) | copy-start | bytes 196612
  137.5 3.4 %copy-start = (f32[2048,1024]{1,0:T(8,128)}, f32[2048,1024]{1,0:T(8,128)S(1)}, u32[]{:S(2)}) copy-start(f32[2048,1024]{1,0:T(8,128)S(1)} %get-tuple-element.17.rows_ref) | copy-start | bytes 25165828
  141.1 2.5 %collective-permute-start.17 = (f32[256,768]{1,0:T(8,128)S(1)}, f32[256,768]{1,0:T(8,128)}, u32[]{:S(2)}, u32[]{:S(2)}) collective-permute-start(f32[256,768]{1,0:T(8,128)S(1)} %pad_maximum_fusion.1), channel_id=1, source_target_pairs={{0,8},{8,0},{16,24},{24,16},{32,40},{40,32},{48,56},{56,48},{64,72... | collective-permute-start | bytes 2359304 | tf_op jit(solution)/shard_map/ppermute | solution.py:40
  147.1 10.9 %collective-permute-start.20 = (f32[256,384]{1,0:T(8,128)}, f32[256,384]{1,0:T(8,128)}, u32[]{:S(2)}, u32[]{:S(2)}) collective-permute-start(f32[256,384]{1,0:T(8,128)} %get-tuple-element.50), channel_id=1, source_target_pairs={{0,48},{8,56},{16,0},{24,8},{32,16},{40,24},{48,32},{56,40},{64,11... | collective-permute-start | bytes 1179656 | tf_op jit(solution)/shard_map/ppermute | solution.py:48
  147.1 12.5 %collective-permute-start.19 = (f32[256,384]{1,0:T(8,128)}, f32[256,384]{1,0:T(8,128)}, u32[]{:S(2)}, u32[]{:S(2)}) collective-permute-start(f32[256,384]{1,0:T(8,128)} %get-tuple-element.49), channel_id=1, source_target_pairs={{0,32},{8,40},{16,48},{24,56},{32,0},{40,8},{48,16},{56,24},{64,96... | collective-permute-start | bytes 1179656 | tf_op jit(solution)/shard_map/ppermute | solution.py:48
  150.3 18.3 %collective-permute-start.18 = (f32[256,384]{1,0:T(8,128)}, f32[256,384]{1,0:T(8,128)}, u32[]{:S(2)}, u32[]{:S(2)}) collective-permute-start(f32[256,384]{1,0:T(8,128)} %get-tuple-element.48), channel_id=1, source_target_pairs={{0,16},{8,24},{16,32},{24,40},{32,48},{40,56},{48,0},{56,8},{64,80... | collective-permute-start | bytes 1179656 | tf_op jit(solution)/shard_map/ppermute | solution.py:48
  170.1 0.8 copy-start.31
  170.1 1.2 copy-start.32
  172.0 8.0 %collective-permute-start.21 = (f32[256,128]{1,0:T(8,128)S(1)}, f32[256,128]{1,0:T(8,128)S(1)}, u32[]{:S(2)}, u32[]{:S(2)}) collective-permute-start(f32[256,128]{1,0:T(8,128)S(1)} %fusion.11), channel_id=1, source_target_pairs={{0,64},{8,72},{16,80},{24,88},{32,96},{40,104},{48,112},{56,120},{... | collective-permute-start | bytes 393224 | tf_op jit(solution)/shard_map/ppermute | solution.py:302
  183.2 3.9 %collective-permute-start.24 = (f32[256,128]{1,0:T(8,128)S(1)}, f32[256,128]{1,0:T(8,128)S(1)}, u32[]{:S(2)}, u32[]{:S(2)}) collective-permute-start(f32[256,128]{1,0:T(8,128)S(1)} %get-tuple-element.36), channel_id=1, source_target_pairs={{0,48},{8,56},{16,0},{24,8},{32,16},{40,24},{48,32},{56,40},{64,11... | collective-permute-start | bytes 393224 | tf_op jit(solution)/shard_map/ppermute | solution.py:48
  183.3 5.4 %collective-permute-start.23 = (f32[256,128]{1,0:T(8,128)S(1)}, f32[256,128]{1,0:T(8,128)S(1)}, u32[]{:S(2)}, u32[]{:S(2)}) collective-permute-start(f32[256,128]{1,0:T(8,128)S(1)} %get-tuple-element.37), channel_id=1, source_target_pairs={{0,32},{8,40},{16,48},{24,56},{32,0},{40,8},{48,16},{56,24},{64,96... | collective-permute-start | bytes 393224 | tf_op jit(solution)/shard_map/ppermute | solution.py:48
  184.9 6.2 %collective-permute-start.22 = (f32[256,128]{1,0:T(8,128)S(1)}, f32[256,128]{1,0:T(8,128)S(1)}, u32[]{:S(2)}, u32[]{:S(2)}) collective-permute-start(f32[256,128]{1,0:T(8,128)S(1)} %get-tuple-element.38), channel_id=1, source_target_pairs={{0,16},{8,24},{16,32},{24,40},{32,48},{40,56},{48,0},{56,8},{64,80... | collective-permute-start | bytes 393224 | tf_op jit(solution)/shard_map/ppermute | solution.py:48
  191.8 4.8 %collective-permute-start.25 = (f32[256,512]{1,0:T(8,128)S(1)}, f32[256,512]{1,0:T(8,128)S(1)}, u32[]{:S(2)}, u32[]{:S(2)}) collective-permute-start(f32[256,512]{1,0:T(8,128)S(1)} %get-tuple-element.28), channel_id=1, source_target_pairs={{0,8},{8,0},{16,24},{24,16},{32,40},{40,32},{48,56},{56,48},{64,72... | collective-permute-start | bytes 1572872 | tf_op jit(solution)/shard_map/ppermute | solution.py:40
  196.8 3.4 %copy-start.1 = (f32[2048,1024]{1,0:T(8,128)S(1)}, f32[2048,1024]{1,0:T(8,128)}, u32[]{:S(2)}) copy-start(f32[2048,1024]{1,0:T(8,128)} %copy-done) | copy-start | bytes 25165828

commit v2 on v0

v2 whole, which is shorter than its diff:
```python
import functools

import jax
import jax.numpy as jnp
from jax import lax
from jax.experimental import pallas as pl
from jax.experimental.pallas import tpu as pltpu
from jax.sharding import PartitionSpec as P

F32 = jnp.float32
BF16 = jnp.bfloat16
Z_SIZE = 4
Y_SIZE = 4
HIGHEST = lax.Precision.HIGHEST
VMEM_BYTES = 56 * 2**20


def dot(a, b, precision=None):
    return jnp.dot(a, b, precision=precision, preferred_element_type=F32)


def dot_transposed(a, b):
    return lax.dot_general(a, b, (((1,), (1,)), ((), ())), preferred_element_type=F32)


def split(value):
    high = value.astype(BF16)
    return high, (value - high.astype(F32)).astype(BF16)


def along_z(value, by):
    pairs = [(v, ((v // 2 + by) % Z_SIZE) * 2 + v % 2) for v in range(2 * Z_SIZE)]
    return lax.ppermute(value, "vec", pairs)


def across_x(value):
    return lax.ppermute(value, "vec", [(v, v ^ 1) for v in range(2 * Z_SIZE)])


def across_core(value):
    return lax.ppermute(value, "row", [(i, i ^ 1) for i in range(lax.axis_size("row"))])


def along_y(value, by):
    def target(i):
        high, y, core = i // (2 * Y_SIZE), (i // 2) % Y_SIZE, i % 2
        return (high * Y_SIZE + (y + by) % Y_SIZE) * 2 + core

    return lax.ppermute(value, "row", [(i, target(i)) for i in range(lax.axis_size("row"))])


def from_next_row(value):
    return lax.ppermute(value, "row", [(i + 1, i) for i in range(lax.axis_size("row") - 1)])


def together(*values):
    return lax.optimization_barrier(values)


def place_of(index):
    vec = lax.axis_index("vec")
    z, x = vec // 2, vec % 2
    dz, dx = index // 2, index % 2
    return lax.rem(z + dz, Z_SIZE) * 2 + lax.rem(x + dx, 2)


def pick_kernel(keys, *refs):
    pieces, out, sems = refs[:-2], refs[-2], refs[-1]
    for (dz, dx), piece in zip(keys, pieces):

        @pl.when(place_of(2 * dz + dx) == 0)
        def _():
            copies = [
                pltpu.make_async_copy(piece.at[0], out.at[pl.ds(0, 2)], sems.at[0]),
                pltpu.make_async_copy(piece.at[1, pl.ds(0, 1)], out.at[pl.ds(2, 1)], sems.at[1]),
            ]
            for copy in copies:
                copy.start()
            for copy in copies:
                copy.wait()


def pick_first(pieces):
    keys = list(pieces)
    return pl.pallas_call(
        functools.partial(pick_kernel, keys),
        out_shape=jax.ShapeDtypeStruct((3,) + pieces[keys[0]].shape[2:], F32),
        in_specs=[pl.BlockSpec(memory_space=pl.ANY)] * len(keys),
        out_specs=pl.BlockSpec(memory_space=pltpu.VMEM),
        scratch_shapes=[pltpu.SemaphoreType.DMA((2,))],
        compiler_params=pltpu.CompilerParams(vmem_limit_bytes=VMEM_BYTES),
    )(*[pieces[key] for key in keys])


def build_reflection(packed):
    width = packed.shape[1]
    rows = lax.broadcasted_iota(jnp.int32, (width, width), 0)
    cols = lax.broadcasted_iota(jnp.int32, (width, width), 1)
    top = packed[:width]
    unit = jnp.where(rows == cols, 1.0, jnp.where(rows > cols, top, 0.0))
    factor = jnp.where(rows <= cols, top, 0.0)
    vectors = jnp.concatenate([unit, packed[width:]], axis=0)
    high, low = split(vectors)
    factor_high, factor_low = split(factor)
    both = dot(jnp.concatenate([high, low], axis=0), factor_high)
    weighted_high, weighted_low = split(
        both[: 2 * width] + (both[2 * width :] + dot(high, factor_low))
    )
    both = dot_transposed(jnp.concatenate([weighted_high, weighted_low], axis=0), high)
    update = both[: 2 * width] + (both[2 * width :] + dot_transposed(weighted_high, low))
    rows = lax.broadcasted_iota(jnp.int32, update.shape, 0)
    cols = lax.broadcasted_iota(jnp.int32, update.shape, 1)
    return split(jnp.where(rows == cols, 1.0, 0.0) - update)


def build_kernel(parts, has_input, *refs):
    count = max(part[0] for part in parts) + 1
    pieces = refs[:count]
    outs = refs[count + (2 if has_input else 0) :][:2]
    staged, sems = refs[-2], refs[-1]
    depth = staged.shape[2]
    copies = []
    at = 0
    for index, (source, blocks, group, place) in enumerate(parts):
        size = len(blocks)
        for block in blocks:
            high, low = build_reflection(pieces[source][block])
            staged[at, :depth] = high
            staged[at, depth:] = low
            at += 1
        first = place(lax.axis_index("vec"))
        copy = pltpu.make_async_copy(
            staged.at[pl.ds(at - size, size)], outs[group].at[pl.ds(first, size)], sems.at[index]
        )
        copy.start()
        copies.append(copy)
    for copy in copies:
        copy.wait()


def build(buffers, shapes, pieces, parts):
    depth = pieces[0].shape[-2]
    blocks = sum(len(part[1]) for part in parts)
    has_input = buffers is not None
    any_spec = pl.BlockSpec(memory_space=pl.ANY)
    return pl.pallas_call(
        functools.partial(build_kernel, parts, has_input),
        out_shape=tuple(jax.ShapeDtypeStruct(shape, BF16) for shape in shapes),
        in_specs=[pl.BlockSpec(memory_space=pltpu.VMEM)] * len(pieces) + ([any_spec] * 2 if has_input else []),
        out_specs=(any_spec, any_spec),
        scratch_shapes=[pltpu.VMEM((blocks, 2 * depth, depth), BF16), pltpu.SemaphoreType.DMA((len(parts),))],
        input_output_aliases={len(pieces): 0, len(pieces) + 1: 1} if has_input else {},
        compiler_params=pltpu.CompilerParams(vmem_limit_bytes=VMEM_BYTES),
        cost_estimate=pl.CostEstimate(
            flops=blocks * 300_000_000, bytes_accessed=blocks * depth * depth * 6, transcendentals=0
        ),
    )(*pieces, *(buffers if has_input else ()))


def parts_of(keys):
    return [
        (source, [(group, block) for block in range(2)], group, lambda vec, key=key: 2 * place_of(2 * key[0] + key[1]))
        for source, key in enumerate(keys)
        for group in range(2)
    ]


def apply(reflection, upper, lower):
    depth = reflection.shape[1]
    high, low = split(jnp.concatenate([upper, lower], axis=0))
    both = dot(reflection, high)
    result = both[:depth] + (both[depth:] + dot(reflection[:depth], low))
    return result[: depth // 2], result[depth // 2 :]


def chunks(total, size=256):
    return [(start, min(size, total - start)) for start in range(0, total, size)]


def sweep_kernel(width, unit, other_half, *refs):
    if unit:
        first_hbm, second_hbm, out, state_out, first, second, first_state, second_state, between, result, sems = refs
        data = None
    else:
        (first_hbm, second_hbm, data_hbm, tail_hbm, out, state_out) = refs[:6]
        first, second, data, first_state, second_state, between, result, sems = refs[6:]
    first_cols, second_cols = first_state.shape[1], second_state.shape[1]
    first_count, second_count = first.shape[0], second.shape[0]
    granules = first_count // 2

    def copies_of(m):
        result = [pltpu.make_async_copy(first_hbm.at[pl.ds(2 * m, 2)], first.at[pl.ds(2 * m, 2)], sems.at[0, m])]
        if not unit:
            core = lax.rem(lax.axis_index("row"), 2)
            half = (1 - core) if other_half else core
            cols = pl.ds(pl.multiple_of(half * first_cols, first_cols), first_cols)
            if isinstance(m, int) and m == granules - 1:
                source = tail_hbm.at[:, cols]
            else:
                source = data_hbm.at[pl.ds(m * 2 * width, 2 * width), cols]
            result.append(pltpu.make_async_copy(source, data.at[m], sems.at[1, m]))
        return result

    def second_copy(m):
        size = 1 if isinstance(m, int) and 2 * m + 1 >= second_count else 2
        return pltpu.make_async_copy(second_hbm.at[pl.ds(2 * m, size)], second.at[pl.ds(2 * m, size)], sems.at[2, m])

    def out_copy(block):
        return pltpu.make_async_copy(
            result.at[pl.ds(block * width, width)], out.at[pl.ds(block * width, width)], sems.at[3, block]
        )

    for m in range(granules):
        for copy in copies_of(m):
            copy.start()
        second_copy(m).start()
    for m in range(2):
        for copy in copies_of(m):
            copy.wait()
    second_copy(0).wait()

    def first_step(m, odd):
        reflection = first[2 * m + odd]
        for start, size in chunks(first_cols):
            if unit:
                lower = jnp.zeros((width, size), F32)
            else:
                lower = data[m, odd * width : (odd + 1) * width, start : start + size]
            top, bottom = apply(reflection, first_state[:, start : start + size], lower)
            between[:, start : start + size] = top
            first_state[:, start : start + size] = bottom

    def second_step(index, keep):
        reflection = second[index]
        for start, size in chunks(second_cols):
            top, bottom = apply(
                reflection, second_state[:, start : start + size], between[:, start : start + size]
            )
            if keep:
                row = (index - 1) * width
                if not isinstance(row, int):
                    row = pl.multiple_of(row, width)
                result[pl.ds(row, width), start : start + size] = top
            second_state[:, start : start + size] = bottom

    def both_steps(m, odd):
        index = 2 * m + odd - 2
        second_step(index, True)
        first_step(m, odd)
        out_copy(index - 1).start()

    if unit:
        rows = lax.broadcasted_iota(jnp.int32, (width, width), 0)
        cols = lax.broadcasted_iota(jnp.int32, (width, width), 1)
        eye = jnp.where(rows == cols, 1.0, 0.0)
        first_state[...] = eye
        second_state[...] = jnp.concatenate([jnp.zeros((width, width), F32), eye], axis=1)
        between[...] = jnp.zeros_like(between)
    else:
        first_state[...] = jnp.zeros_like(first_state)
        second_state[...] = jnp.zeros_like(second_state)

        @pl.when(lax.axis_index("row") == 0)
        def _():
            first_step(0, 0)
            first_step(0, 1)
            second_step(0, False)

    first_step(1, 0)
    both_steps(1, 1)

    @pl.loop(2, granules - 1)
    def _(m):
        for copy in copies_of(m):
            copy.wait()
        second_copy(m - 1).wait()
        both_steps(m, 0)
        both_steps(m, 1)

    last = granules - 1
    for copy in copies_of(last):
        copy.wait()
    second_copy(last - 1).wait()
    both_steps(last, 0)
    both_steps(last, 1)
    second_copy(last).wait()
    second_step(second_count - 1, True)
    out_copy(second_count - 2).start()
    if unit:
        zeros = jnp.zeros((width, width), F32)
        state_out[:width] = jnp.concatenate([first_state[...], zeros], axis=1)
    else:
        state_out[:width] = first_state[...]
    state_out[width:] = second_state[...]
    for block in range(second_count - 1):
        out_copy(block).wait()


def sweep(buffers, data=None, tail=None, other_half=False, unit=False):
    first, second = buffers
    depth = first.shape[2]
    width = depth // 2
    blocks = second.shape[0] - 1
    granules = first.shape[0] // 2
    first_cols = width if unit else data.shape[1] // 2
    second_cols = 2 * width if unit else first_cols
    any_spec = pl.BlockSpec(memory_space=pl.ANY)
    rows = blocks * width
    scratch = [pltpu.VMEM(first.shape, BF16), pltpu.VMEM(second.shape, BF16)]
    if not unit:
        scratch.append(pltpu.VMEM((granules, 2 * width, first_cols), F32))
    scratch += [
        pltpu.VMEM((width, first_cols), F32),
        pltpu.VMEM((width, second_cols), F32),
        pltpu.VMEM((width, second_cols), F32),
        pltpu.VMEM((rows, second_cols), F32),
        pltpu.SemaphoreType.DMA((4, blocks)),
    ]
    ins = (first, second) if unit else (first, second, data, tail)
    return pl.pallas_call(
        functools.partial(sweep_kernel, width, unit, other_half),
        out_shape=(
            jax.ShapeDtypeStruct((rows, second_cols), F32),
            jax.ShapeDtypeStruct((depth, second_cols), F32),
        ),
        in_specs=[any_spec] * len(ins),
        out_specs=(any_spec, pl.BlockSpec(memory_space=pltpu.VMEM)),
        scratch_shapes=scratch,
        compiler_params=pltpu.CompilerParams(vmem_limit_bytes=VMEM_BYTES),
        cost_estimate=pl.CostEstimate(
            flops=6 * blocks * depth * depth * (first_cols + second_cols),
            bytes_accessed=30 * 2**20,
            transcendentals=0,
        ),
    )(*ins)


def correct_kernel(other_ref, own_ref, response_ref, incoming_ref, out_ref, high_ref, low_ref):
    @pl.when(pl.program_id(0) == 0)
    def _():
        high, low = split(incoming_ref[...])
        high_ref[...] = high
        low_ref[...] = low

    core = lax.rem(lax.axis_index("row"), 2)
    half = own_ref.shape[1]
    high, low = split(response_ref[...])
    both = jnp.concatenate([high, low], axis=0)
    tile = high.shape[0]
    for at in range(2):
        cols = slice(at * half, (at + 1) * half)
        sums = dot(both, high_ref[:, cols])
        update = sums[:tile] + (sums[tile:] + dot(high, low_ref[:, cols]))
        out_ref[:, cols] = jnp.where(core == at, own_ref[...], other_ref[...]) + update


def correct(other, own, response, incoming, tile=256):
    count, half = own.shape
    depth = response.shape[1]
    cols = 2 * half
    tiled = pl.BlockSpec((tile, half), lambda k: (k, 0))
    return pl.pallas_call(
        correct_kernel,
        grid=(count // tile,),
        out_shape=jax.ShapeDtypeStruct((count, cols), F32),
        in_specs=[
            tiled,
            tiled,
            pl.BlockSpec((tile, depth), lambda k: (k, 0)),
            pl.BlockSpec((depth, cols), lambda k: (0, 0)),
        ],
        out_specs=pl.BlockSpec((tile, cols), lambda k: (k, 0)),
        scratch_shapes=[pltpu.VMEM((depth, cols), BF16), pltpu.VMEM((depth, cols), BF16)],
        compiler_params=pltpu.CompilerParams(vmem_limit_bytes=VMEM_BYTES),
    )(other, own, response, incoming)


def local(eigvecs, wy_v, wy_t):
    width = wy_t.shape[-1]
    rows_dev, cols_dev = eigvecs.shape
    own_blocks = rows_dev // width
    row = lax.axis_index("row")
    core, y = row % 2, (row // 2) % Y_SIZE
    below = lax.broadcasted_iota(jnp.int32, (width, width), 0) > lax.broadcasted_iota(
        jnp.int32, (width, width), 1
    )
    packed = jnp.concatenate(
        [jnp.where(below, wy_v[:, :, :width], wy_t), wy_v[:, :, width:]], axis=2
    )
    tail = from_next_row(eigvecs[: 2 * width])
    depth = 2 * width
    shapes = ((own_blocks + 2, 2 * depth, depth), (own_blocks + 1, 2 * depth, depth))

    own = packed
    p01, p30, p10 = across_x(own), along_z(own, 1), along_z(own, -1)
    buffers = build(None, shapes, [own], parts_of([(0, 0)]))
    p01, p30, p10, *buffers = together(p01, p30, p10, *buffers)
    p31, p20, p11 = across_x(p30), along_z(p30, 1), along_z(p01, -1)
    buffers = build(buffers, shapes, [p01, p30, p10], parts_of([(0, 1), (3, 0), (1, 0)]))
    p31, p20, p11, tail, *buffers = together(p31, p20, p11, tail, *buffers)
    last = [across_x(p20[0]), along_z(p31[1, :1], 1), along_z(p11[1, 1:], -1)]
    known = {(0, 0): own, (0, 1): p01, (3, 0): p30, (1, 0): p10, (3, 1): p31, (2, 0): p20, (1, 1): p11}
    picked = pick_first(known)
    vecs, rows = lax.axis_size("vec"), lax.axis_size("row")
    late = 5
    extras = [
        lax.ppermute(
            picked,
            ("row", "vec"),
            [((i + 1) * vecs + v, i * vecs + v) for i in range(rows - 1) for v in range(vecs) if v != late],
        ),
        lax.ppermute(
            picked, ("row", "vec"), [((i + 1) * vecs + late - 1, i * vecs + late) for i in range(rows - 1)]
        ),
    ]
    buffers = build(buffers, shapes, [p31, p20, p11], parts_of([(3, 1), (2, 0), (1, 1)]))
    *arrived, _, _ = together(*last, *extras, *buffers)
    extra = jnp.where(lax.axis_index("vec") == late, arrived[4], arrived[3])
    opposite = 2 * 2 + 1
    buffers = build(
        buffers,
        shapes,
        [arrived[0], arrived[1], arrived[2], extra],
        [
            (0, [0, 1], 0, lambda vec: 2 * place_of(opposite)),
            (1, [0], 1, lambda vec: 2 * place_of(opposite)),
            (2, [0], 1, lambda vec: 2 * place_of(opposite) + 1),
            (3, [0, 1], 0, lambda vec: own_blocks),
            (3, [2], 1, lambda vec: own_blocks),
        ],
    )

    response, transition = sweep(buffers, unit=True)
    received_transition = across_core(transition)
    other_rows, other_offset = sweep(buffers, eigvecs, tail, other_half=True)
    received_offset = across_core(other_offset)
    lower_transition = jnp.where(core == 0, transition, received_transition)
    upper_transition = jnp.where(core == 0, received_transition, transition)
    chip_transition = dot(upper_transition, lower_transition, HIGHEST)
    part = lax.dynamic_slice_in_dim(chip_transition, core * width, width, 0)
    parts = jnp.stack([part] + [along_y(part, d) for d in range(1, Y_SIZE)])
    own_rows, own_offset = sweep(buffers, eigvecs, tail, other_half=False)
    other_parts = across_core(parts)
    lower_offset = jnp.where(core == 0, own_offset, received_offset)
    upper_offset = jnp.where(core == 0, received_offset, own_offset)
    chip_offset = dot(upper_transition, lower_offset, HIGHEST) + upper_offset
    quarter = chip_offset.shape[1] // Y_SIZE

    def quarter_of(index):
        return lax.dynamic_slice_in_dim(chip_offset, index * quarter, quarter, 1)

    offsets = jnp.stack(
        [quarter_of(y)] + [along_y(quarter_of((y + d) % Y_SIZE), d) for d in range(1, Y_SIZE)]
    )

    def at_chip(stacked, index):
        return lax.dynamic_index_in_dim(stacked, (y - index) % Y_SIZE, 0, False)

    transitions = jnp.where(
        core == 0,
        jnp.concatenate([parts, other_parts], axis=1),
        jnp.concatenate([other_parts, parts], axis=1),
    )
    steps = [(at_chip(transitions, at), at_chip(offsets, at)) for at in range(Y_SIZE)]
    state = steps[0][1]
    for at in range(1, Y_SIZE):
        state = dot(steps[at][0], state, HIGHEST) + steps[at][1]
    size = lax.axis_size("row")
    entering = lax.ppermute(state, "row", [(i, i + size // 2) for i in range(size // 2)])
    result = [entering]
    for at in range(Y_SIZE - 1):
        result.append(dot(steps[at][0], result[-1], HIGHEST) + steps[at][1])
    result = jnp.stack(result)
    back = [lax.dynamic_index_in_dim(result, (y + d) % Y_SIZE, 0, False) for d in range(Y_SIZE)]
    arrived = jnp.stack([back[0]] + [along_y(back[d], d) for d in range(1, Y_SIZE)])
    into_chip = jnp.concatenate([at_chip(arrived, at) for at in range(Y_SIZE)], axis=1)
    into_second = dot(lower_transition, into_chip, HIGHEST) + lower_offset
    kept = jnp.where(core == 0, into_chip, into_second)
    given = jnp.where(core == 0, into_second, into_chip)
    taken = across_core(given)
    incoming = jnp.where(
        core == 0, jnp.concatenate([kept, taken], axis=1), jnp.concatenate([taken, kept], axis=1)
    )
    return correct(other_rows, own_rows, response, incoming)


def solution(mesh):
    placed = (
        P("row", "vec"),
        P(None, ("row", "vec"), None, None),
        P(None, ("row", "vec"), None, None),
    )
    return jax.shard_map(
        local, mesh=mesh, in_specs=placed, out_specs=P("row", "vec"), check_vma=False
    )
```

time: 2220 us -> 154 us (0.07)
  the two profiles are of different devices: /device:TPU:29 before, /device:TPU:71 now
where the time goes in v2:
time: 154 us; the launch traced here: 153 us
  Pallas kernels  63.6 us (41%)
  waiting for transfers between devices  39.5 us (26%)
  starting transfers between devices  35.7 us (23%)
  matrix products  5.06 us (3%)
  other arithmetic  4.48 us (3%)
  local copies, waits for them, and re-layouts  4.45 us (3%)
    pallas_call x3, Pallas kernels, sweep(): pl.pallas_call(functools.partial(sweep_kernel, width, unit, other_half),...  34.6 us
    ppermute x3, waiting for transfers between devices, across_x(): return lax.ppermute(value, 'vec', [(v, v ^ 1) for v in range(2 * Z_SIZE)])  17 us
    pallas_call x4, Pallas kernels, build(): pl.pallas_call(functools.partial(build_kernel, parts, has_input), out_sha...  16.2 us
    ppermute x9, waiting for transfers between devices, along_y(): lax.ppermute(value, 'row', [(i, target(i)) for i in range(lax.axis_size('...  13.3 us
    ppermute x3, starting transfers between devices, across_x(): return lax.ppermute(value, 'vec', [(v, v ^ 1) for v in range(2 * Z_SIZE)])  12 us
    pallas_call x1, Pallas kernels, correct(): pl.pallas_call(correct_kernel, grid=(count // tile,), out_shape=jax.Shape...  11.9 us
    ppermute x9, starting transfers between devices, along_y(): lax.ppermute(value, 'row', [(i, target(i)) for i in range(lax.axis_size('...  8.61 us
    ppermute x1, waiting for transfers between devices, local(): lax.ppermute(state, 'row', [(i, i + size // 2) for i in range(size // 2)])  6.37 us
  transfers between devices with their start and end apart: 26, of which 13 were waited for; matrix products, arithmetic and copies ran while one was open for 3% of the time, Pallas kernels for 25%

profile of v2, /device:TPU:71, one launch (start us, length us, event | category | flops | bytes accessed | tf_op | source)
XLA Modules:
  0.0 153.2 jit_solution(16236329916990720969)
XLA Ops:
  0.0 1.2 slice_select_fusion
  1.2 0.6 collective-permute-start
  1.9 1.3 collective-permute-start.1
  3.2 0.1 collective-permute-start.2
  3.3 1.3 slice.20
  4.6 3.4 %collective-permute-start.6 = (f32[256,1024]{1,0:T(8,128)S(1)}, f32[256,1024]{1,0:T(8,128)}, u32[]{:S(2)}, u32[]{:S(2)}) collective-permute-start(f32[256,1024]{1,0:T(8,128)S(1)} %slice.20), channel_id=1, source_target_pairs={{8,0},{16,8},{24,16},{32,24},{40,32},{48,40},{56,48},{64,56},{72,6... | collective-permute-start | bytes 3145736 | tf_op jit(solution)/shard_map/ppermute | solution.py:53
  8.1 2.9 %shard_map.37 = (bf16[18,512,256]{2,1,0:T(8,128)(2,1)}, bf16[17,512,256]{2,1,0:T(8,128)(2,1)}) custom-call(f32[2,2,256,128]{3,2,1,0:T(8,128)} %copy-done.2), custom_call_target="tpu_custom_call" | custom-call | flops 1200000000 | bytes 1572864 | tf_op jit(solution)/shard_map/pallas_call | solution.py:146
  11.0 3.2 %collective-permute-done.refs_0_.refs_1_ = f32[2,2,256,128]{3,2,1,0:T(8,128)S(1)} collective-permute-done((f32[2,2,256,128]{3,2,1,0:T(8,128)S(1)}, f32[2,2,256,128]{3,2,1,0:T(8,128)S(1)}, u32[]{:S(2)}, u32[]{:S(2)}) %collective-permute-start) | collective-permute-done | bytes 524320 | tf_op jit(solution)/shard_map/ppermute | solution.py:37
  14.2 0.2 collective-permute-done.1.refs_1_.refs_2_
  14.4 1.0 collective-permute-done.2.refs_2_.refs_3_
  15.5 0.8 copy-done.8
  16.3 0.9 collective-permute-start.3
  17.2 1.4 collective-permute-start.4
  18.7 4.8 %shard_map.38 = (bf16[18,512,256]{2,1,0:T(8,128)(2,1)}, bf16[17,512,256]{2,1,0:T(8,128)(2,1)}) custom-call(f32[2,2,256,128]{3,2,1,0:T(8,128)} %copy-done.7, f32[2,2,256,128]{3,2,1,0:T(8,128)} %collective-permute-done.1.refs_1_.refs_2_, f32[2,2,256,128]{3,2,1,0:T(8,128)} %copy-done.8, ...), custom_call_target="tpu_custom_call", output_to_operand_aliasing={{0}: (3, {}), {1}: (4, {})} | custom-call | flops 3600000000 | bytes 4718592 | tf_op jit(solution)/shard_map/pallas_call | solution.py:146
  23.5 7.0 %collective-permute-done.3.refs_4_.refs_0_ = f32[2,2,256,128]{3,2,1,0:T(8,128)S(1)} collective-permute-done((f32[2,2,256,128]{3,2,1,0:T(8,128)}, f32[2,2,256,128]{3,2,1,0:T(8,128)S(1)}, u32[]{:S(2)}, u32[]{:S(2)}) %collective-permute-start.3) | collective-permute-done | bytes 524320 | tf_op jit(solution)/shard_map/ppermute | solution.py:37
  30.6 0.7 copy-done.4
  31.3 0.3 copy-done.3
  31.6 0.2 copy-done.5
  31.8 0.8 shard_map.39
  32.6 0.7 collective-permute-start.10
  33.3 1.3 collective-permute-start.11
  34.6 0.9 slice_bitcast_fusion.1
  35.5 10.5 %collective-permute-start.7 = (f32[2,256,128]{2,1,0:T(8,128)S(1)}, f32[2,256,128]{2,1,0:T(8,128)S(1)}, u32[]{:S(2)}, u32[]{:S(2)}) collective-permute-start(f32[2,256,128]{2,1,0:T(8,128)S(1)} %slice_bitcast_fusion), channel_id=1, source_target_pairs={{0,1},{1,0},{2,3},{3,2},{4,5},{5,4},{6,7},{7,6},{8,9},{9,8},{10,11... | collective-permute-start | bytes 786440 | tf_op jit(solution)/shard_map/ppermute | solution.py:37
  46.0 0.7 collective-permute-start.8
  46.7 0.8 collective-permute-start.9
  47.4 4.8 %shard_map.40 = (bf16[18,512,256]{2,1,0:T(8,128)(2,1)}, bf16[17,512,256]{2,1,0:T(8,128)(2,1)}) custom-call(f32[2,2,256,128]{3,2,1,0:T(8,128)} %copy-done.4, f32[2,2,256,128]{3,2,1,0:T(8,128)} %copy-done.3, f32[2,2,256,128]{3,2,1,0:T(8,128)} %copy-done.5, ...), custom_call_target="tpu_custom_call", output_to_operand_aliasing={{0}: (3, {}), {1}: (4, {})} | custom-call | flops 3600000000 | bytes 4718592 | tf_op jit(solution)/shard_map/pallas_call | solution.py:146
  52.3 6.7 %collective-permute-done.7.refs_0_ = f32[2,256,128]{2,1,0:T(8,128)S(1)} collective-permute-done((f32[2,256,128]{2,1,0:T(8,128)S(1)}, f32[2,256,128]{2,1,0:T(8,128)S(1)}, u32[]{:S(2)}, u32[]{:S(2)}) %collective-permute-start.7) | collective-permute-done | bytes 262176 | tf_op jit(solution)/shard_map/ppermute | solution.py:37
  59.0 0.8 broadcast_select_fusion.4.refs_3_
  59.9 3.7 %shard_map.41 = (bf16[18,512,256]{2,1,0:T(8,128)(2,1)}, bf16[17,512,256]{2,1,0:T(8,128)(2,1)}) custom-call(f32[2,256,128]{2,1,0:T(8,128)} %copy-done.9, f32[1,256,128]{2,1,0:T(8,128)} %copy-done.10, f32[1,256,128]{2,1,0:T(8,128)} %copy-done.11, f32[3,256,128]{2,1,0:T(8,128)} %broadcast_select_fusion.4.refs_3_, ...), custom_call_target="tpu_custom_call", output_to_operand_aliasing={{0}: (4, {}), {1}: (5, {})} | custom-call | flops 2100000000 | bytes 2752512 | tf_op jit(solution)/shard_map/pallas_call | solution.py:146
  63.6 9.3 %shard_map.44 = (f32[2048,256]{1,0:T(8,128)}, f32[256,256]{1,0:T(8,128)}) custom-call(bf16[18,512,256]{2,1,0:T(8,128)(2,1)} %get-tuple-element.56.refs_0_, bf16[17,512,256]{2,1,0:T(8,128)(2,1)} %get-tuple-element.57.refs_1_), custom_call_target="tpu_custom_call" | custom-call | flops 2415919104 | bytes 31457280 | tf_op jit(solution)/shard_map/pallas_call | solution.py:320
  73.0 0.3 collective-permute-start.12
  73.2 12.6 %shard_map.42 = (f32[2048,512]{1,0:T(8,128)}, f32[256,512]{1,0:T(8,128)}) custom-call(bf16[18,512,256]{2,1,0:T(8,128)(2,1)} %get-tuple-element.56.refs_0_, bf16[17,512,256]{2,1,0:T(8,128)(2,1)} %get-tuple-element.57.refs_1_, f32[2048,1024]{1,0:T(8,128)} %refs_2_.3, f32[256,1024]{1,0:T(8,128)} %collective-permute-done.6.refs_3_), custom_call_target="tpu_custom_call" | custom-call | flops 6442450944 | bytes 31457280 | tf_op jit(solution)/shard_map/pallas_call | solution.py:320
  85.9 0.6 collective-permute-start.17
  86.5 0.4 fusion.19
  87.0 0.1 collective-permute-start.14
  87.1 1.4 collective-permute-start.13
  88.4 12.6 %shard_map.43 = (f32[2048,512]{1,0:T(8,128)}, f32[256,512]{1,0:T(8,128)}) custom-call(bf16[18,512,256]{2,1,0:T(8,128)(2,1)} %get-tuple-element.56.refs_0_, bf16[17,512,256]{2,1,0:T(8,128)(2,1)} %get-tuple-element.57.refs_1_, f32[2048,1024]{1,0:T(8,128)} %refs_2_.3, f32[256,1024]{1,0:T(8,128)} %collective-permute-done.6.refs_3_), custom_call_target="tpu_custom_call" | custom-call | flops 6442450944 | bytes 31457280 | tf_op jit(solution)/shard_map/pallas_call | solution.py:320
  101.2 0.7 collective-permute-start.16
  101.9 1.7 %convolution_add_fusion.1 = f32[256,512]{1,0:T(8,128)S(1)} fusion(f32[256,512]{1,0:T(8,128)S(1)} %collective-permute-done.17, f32[256,512]{1,0:T(8,128)} %get-tuple-element.63, pred[]{:T(512)S(6)} %eq.36, f32[256,256]{1,0:T(8,128)S(1)} %collective-permute-done.12, f32[256,256]{1,0:T(8,128)S(1)} %copy-done), kind=kOutput, calls=%fused_computation.1 | convolution fusion | flops 403111936 | bytes 2097153 | tf_op jit(solution)/shard_map/dot_general | solution.py:19
  103.7 2.5 %collective-permute-start.20 = (f32[256,128]{1,0:T(8,128)S(1)}, f32[256,128]{1,0:T(8,128)S(1)}, u32[]{:S(2)}, u32[]{:S(2)}) collective-permute-start(f32[256,128]{1,0:T(8,128)S(1)} %get-tuple-element.76), channel_id=1, source_target_pairs={{0,48},{8,56},{16,0},{24,8},{32,16},{40,24},{48,32},{56,40},{64,11... | collective-permute-start | bytes 393224 | tf_op jit(solution)/shard_map/ppermute | solution.py:49
  106.1 1.6 %collective-permute-start.19 = (f32[256,128]{1,0:T(8,128)S(1)}, f32[256,128]{1,0:T(8,128)S(1)}, u32[]{:S(2)}, u32[]{:S(2)}) collective-permute-start(f32[256,128]{1,0:T(8,128)S(1)} %get-tuple-element.77), channel_id=1, source_target_pairs={{0,32},{8,40},{16,48},{24,56},{32,0},{40,8},{48,16},{56,24},{64,96... | collective-permute-start | bytes 393224 | tf_op jit(solution)/shard_map/ppermute | solution.py:49
  107.7 0.8 collective-permute-start.18
  108.4 0.4 collective-permute-done.20
  108.8 3.4 %collective-permute-done.19 = f32[256,128]{1,0:T(8,128)S(1)} collective-permute-done((f32[256,128]{1,0:T(8,128)S(1)}, f32[256,128]{1,0:T(8,128)S(1)}, u32[]{:S(2)}, u32[]{:S(2)}) %collective-permute-start.19) | collective-permute-done | bytes 131104 | tf_op jit(solution)/shard_map/ppermute | solution.py:49
  112.2 3.6 %collective-permute-done.18 = f32[256,128]{1,0:T(8,128)S(1)} collective-permute-done((f32[256,128]{1,0:T(8,128)S(1)}, f32[256,128]{1,0:T(8,128)S(1)}, u32[]{:S(2)}, u32[]{:S(2)}) %collective-permute-start.18) | collective-permute-done | bytes 131104 | tf_op jit(solution)/shard_map/ppermute | solution.py:49
  115.8 1.1 maximum_select_fusion
  117.0 0.4 convolution_add_fusion.6
  117.3 0.4 convolution_add_fusion.5
  117.7 0.4 fusion.8
  118.1 1.5 collective-permute-start.21
  119.7 6.4 %collective-permute-done.21 = f32[256,128]{1,0:T(8,128)S(1)} collective-permute-done((f32[256,128]{1,0:T(8,128)S(1)}, f32[256,128]{1,0:T(8,128)S(1)}, u32[]{:S(2)}, u32[]{:S(2)}) %collective-permute-start.21) | collective-permute-done | bytes 131104 | tf_op jit(solution)/shard_map/ppermute | solution.py:469
  126.0 0.4 convolution_add_fusion.4
  126.4 0.4 convolution_add_fusion.3
  126.8 0.4 fusion
  127.4 1.5 collective-permute-start.23
  128.8 0.8 collective-permute-start.22
  129.6 1.6 %collective-permute-done.24 = f32[256,128]{1,0:T(8,128)S(1)} collective-permute-done((f32[256,128]{1,0:T(8,128)S(1)}, f32[256,128]{1,0:T(8,128)S(1)}, u32[]{:S(2)}, u32[]{:S(2)}) %collective-permute-start.24) | collective-permute-done | bytes 131104 | tf_op jit(solution)/shard_map/ppermute | solution.py:49
  131.2 1.6 %collective-permute-done.23 = f32[256,128]{1,0:T(8,128)S(1)} collective-permute-done((f32[256,128]{1,0:T(8,128)S(1)}, f32[256,128]{1,0:T(8,128)S(1)}, u32[]{:S(2)}, u32[]{:S(2)}) %collective-permute-start.23) | collective-permute-done | bytes 131104 | tf_op jit(solution)/shard_map/ppermute | solution.py:49
  132.8 2.7 %collective-permute-done.22 = f32[256,128]{1,0:T(8,128)S(1)} collective-permute-done((f32[256,128]{1,0:T(8,128)S(1)}, f32[256,128]{1,0:T(8,128)S(1)}, u32[]{:S(2)}, u32[]{:S(2)}) %collective-permute-start.22) | collective-permute-done | bytes 131104 | tf_op jit(solution)/shard_map/ppermute | solution.py:49
  135.6 0.7 broadcast_select_fusion.1
  136.3 2.3 %collective-permute-start.25 = (f32[256,512]{1,0:T(8,128)S(1)}, f32[256,512]{1,0:T(8,128)S(1)}, u32[]{:S(2)}, u32[]{:S(2)}) collective-permute-start(f32[256,512]{1,0:T(8,128)S(1)} %get-tuple-element.66), channel_id=1, source_target_pairs={{0,8},{8,0},{16,24},{24,16},{32,40},{40,32},{48,56},{56,48},{64,72... | collective-permute-start | bytes 1572872 | tf_op jit(solution)/shard_map/ppermute | solution.py:41
  138.6 1.5 %collective-permute-done.25 = f32[256,512]{1,0:T(8,128)S(1)} collective-permute-done((f32[256,512]{1,0:T(8,128)S(1)}, f32[256,512]{1,0:T(8,128)S(1)}, u32[]{:S(2)}, u32[]{:S(2)}) %collective-permute-start.25) | collective-permute-done | bytes 524320 | tf_op jit(solution)/shard_map/ppermute | solution.py:41
  140.1 1.2 maximum_select_fusion.1.incoming_ref
  141.3 11.9 %shard_map.45 = f32[2048,1024]{1,0:T(8,128)} custom-call(f32[2048,512]{1,0:T(8,128)} %get-tuple-element.59.other_ref, f32[2048,512]{1,0:T(8,128)} %get-tuple-element.60.own_ref, f32[2048,256]{1,0:T(8,128)} %get-tuple-element.61.response_ref, f32[256,1024]{1,0:T(8,128)} %maximum_select_fusion.1.incoming_ref), custom_call_target="tpu_custom_call" | custom-call | tf_op jit(solution)/shard_map/pallas_call | solution.py:362
  (49 shorter events, 0.7 us)
Async XLA Ops:
  1.2 6.8 %copy-start.2 = (f32[2,2,256,128]{3,2,1,0:T(8,128)}, f32[2,2,256,128]{3,2,1,0:T(8,128)S(1)}, u32[]{:S(2)}) copy-start(f32[2,2,256,128]{3,2,1,0:T(8,128)S(1)} %pad_maximum_fusion.refs_0_) | copy-start | bytes 1572868
  1.2 13.0 %collective-permute-start = (f32[2,2,256,128]{3,2,1,0:T(8,128)S(1)}, f32[2,2,256,128]{3,2,1,0:T(8,128)S(1)}, u32[]{:S(2)}, u32[]{:S(2)}) collective-permute-start(f32[2,2,256,128]{3,2,1,0:T(8,128)S(1)} %pad_maximum_fusion.refs_0_), channel_id=1, source_target_pairs={{0,1},{1,0},{2,3},{3,2},{4,5},{5,4},{6,7},{7,6},{8,9},{9,8},{10,11... | collective-permute-start | bytes 1572872 | tf_op jit(solution)/shard_map/ppermute | solution.py:37
  1.9 12.6 %collective-permute-start.1 = (f32[2,2,256,128]{3,2,1,0:T(8,128)S(1)}, f32[2,2,256,128]{3,2,1,0:T(8,128)}, u32[]{:S(2)}, u32[]{:S(2)}) collective-permute-start(f32[2,2,256,128]{3,2,1,0:T(8,128)S(1)} %pad_maximum_fusion.refs_0_), channel_id=1, source_target_pairs={{0,2},{1,3},{2,4},{3,5},{4,6},{5,7},{6,0},{7,1},{8,10},{9,11},{10,... | collective-permute-start | bytes 1572872 | tf_op jit(solution)/shard_map/ppermute | solution.py:33
  3.2 12.3 %collective-permute-start.2 = (f32[2,2,256,128]{3,2,1,0:T(8,128)S(1)}, f32[2,2,256,128]{3,2,1,0:T(8,128)S(1)}, u32[]{:S(2)}, u32[]{:S(2)}) collective-permute-start(f32[2,2,256,128]{3,2,1,0:T(8,128)S(1)} %pad_maximum_fusion.refs_0_), channel_id=1, source_target_pairs={{0,6},{1,7},{2,0},{3,1},{4,2},{5,3},{6,4},{7,5},{8,14},{9,15},{10,... | collective-permute-start | bytes 1572872 | tf_op jit(solution)/shard_map/ppermute | solution.py:33
  4.6 25.9 %collective-permute-start.6 = (f32[256,1024]{1,0:T(8,128)S(1)}, f32[256,1024]{1,0:T(8,128)}, u32[]{:S(2)}, u32[]{:S(2)}) collective-permute-start(f32[256,1024]{1,0:T(8,128)S(1)} %slice.20), channel_id=1, source_target_pairs={{8,0},{16,8},{24,16},{32,24},{40,32},{48,40},{56,48},{64,56},{72,6... | collective-permute-start | bytes 3145736 | tf_op jit(solution)/shard_map/ppermute | solution.py:53
  14.2 4.4 %copy-start.7 = (f32[2,2,256,128]{3,2,1,0:T(8,128)}, f32[2,2,256,128]{3,2,1,0:T(8,128)S(1)}, u32[]{:S(2)}) copy-start(f32[2,2,256,128]{3,2,1,0:T(8,128)S(1)} %collective-permute-done.refs_0_.refs_1_) | copy-start | bytes 1572868
  15.5 0.8 copy-start.8
  16.3 14.2 %collective-permute-start.3 = (f32[2,2,256,128]{3,2,1,0:T(8,128)}, f32[2,2,256,128]{3,2,1,0:T(8,128)S(1)}, u32[]{:S(2)}, u32[]{:S(2)}) collective-permute-start(f32[2,2,256,128]{3,2,1,0:T(8,128)} %collective-permute-done.1.refs_1_.refs_2_), channel_id=1, source_target_pairs={{0,1},{1,0},{2,3},{3,2},{4,5},{5,4},{6,7},{7,6},{8,9},{9,8},{10,11... | collective-permute-start | bytes 1572872 | tf_op jit(solution)/shard_map/ppermute | solution.py:37
  17.2 13.3 %collective-permute-start.4 = (f32[2,2,256,128]{3,2,1,0:T(8,128)}, f32[2,2,256,128]{3,2,1,0:T(8,128)S(1)}, u32[]{:S(2)}, u32[]{:S(2)}) collective-permute-start(f32[2,2,256,128]{3,2,1,0:T(8,128)} %collective-permute-done.1.refs_1_.refs_2_), channel_id=1, source_target_pairs={{0,2},{1,3},{2,4},{3,5},{4,6},{5,7},{6,0},{7,1},{8,10},{9,11},{10,... | collective-permute-start | bytes 1572872 | tf_op jit(solution)/shard_map/ppermute | solution.py:33
  18.6 11.9 %collective-permute-start.5 = (f32[2,2,256,128]{3,2,1,0:T(8,128)S(1)}, f32[2,2,256,128]{3,2,1,0:T(8,128)S(1)}, u32[]{:S(2)}, u32[]{:S(2)}) collective-permute-start(f32[2,2,256,128]{3,2,1,0:T(8,128)S(1)} %collective-permute-done.refs_0_.refs_1_), channel_id=1, source_target_pairs={{0,6},{1,7},{2,0},{3,1},{4,2},{5,3},{6,4},{7,5},{8,14},{9,15},{10,... | collective-permute-start | bytes 1572872 | tf_op jit(solution)/shard_map/ppermute | solution.py:33
  30.5 0.8 copy-start.4
  30.5 1.1 copy-start.3
  30.5 1.2 copy-start.5
  32.6 26.5 %collective-permute-start.10 = (f32[3,256,128]{2,1,0:T(8,128)}, f32[3,256,128]{2,1,0:T(8,128)S(1)}, u32[]{:S(2)}, u32[]{:S(2)}) collective-permute-start(f32[3,256,128]{2,1,0:T(8,128)} %shard_map.39), channel_id=1, source_target_pairs={{8,0},{9,1},{10,2},{11,3},{12,4},{14,6},{15,7},{16,8},{17,9},{18,1... | collective-permute-start | bytes 1179656 | tf_op jit(solution)/shard_map/ppermute | solution.py:407
  33.3 25.8 %collective-permute-start.11 = (f32[3,256,128]{2,1,0:T(8,128)}, f32[3,256,128]{2,1,0:T(8,128)S(1)}, u32[]{:S(2)}, u32[]{:S(2)}) collective-permute-start(f32[3,256,128]{2,1,0:T(8,128)} %shard_map.39), channel_id=1, source_target_pairs={{12,5},{20,13},{28,21},{36,29},{44,37},{52,45},{60,53},{68,61},{76... | collective-permute-start | bytes 1179656 | tf_op jit(solution)/shard_map/ppermute | solution.py:412
  35.5 23.5 %collective-permute-start.7 = (f32[2,256,128]{2,1,0:T(8,128)S(1)}, f32[2,256,128]{2,1,0:T(8,128)S(1)}, u32[]{:S(2)}, u32[]{:S(2)}) collective-permute-start(f32[2,256,128]{2,1,0:T(8,128)S(1)} %slice_bitcast_fusion), channel_id=1, source_target_pairs={{0,1},{1,0},{2,3},{3,2},{4,5},{5,4},{6,7},{7,6},{8,9},{9,8},{10,11... | collective-permute-start | bytes 786440 | tf_op jit(solution)/shard_map/ppermute | solution.py:37
  46.0 6.3 %collective-permute-start.8 = (f32[1,256,128]{2,1,0:T(8,128)S(1)}, f32[1,256,128]{2,1,0:T(8,128)S(1)}, u32[]{:S(2)}, u32[]{:S(2)}) collective-permute-start(f32[1,256,128]{2,1,0:T(8,128)S(1)} %slice_bitcast_fusion.2), channel_id=1, source_target_pairs={{0,2},{1,3},{2,4},{3,5},{4,6},{5,7},{6,0},{7,1},{8,10},{9,11},{10,... | collective-permute-start | bytes 393224 | tf_op jit(solution)/shard_map/ppermute | solution.py:33
  46.7 5.6 %collective-permute-start.9 = (f32[1,256,128]{2,1,0:T(8,128)S(1)}, f32[1,256,128]{2,1,0:T(8,128)S(1)}, u32[]{:S(2)}, u32[]{:S(2)}) collective-permute-start(f32[1,256,128]{2,1,0:T(8,128)S(1)} %slice_bitcast_fusion.1), channel_id=1, source_target_pairs={{0,6},{1,7},{2,0},{3,1},{4,2},{5,3},{6,4},{7,5},{8,14},{9,15},{10,... | collective-permute-start | bytes 393224 | tf_op jit(solution)/shard_map/ppermute | solution.py:33
  52.3 7.6 %copy-start.10 = (f32[1,256,128]{2,1,0:T(8,128)}, f32[1,256,128]{2,1,0:T(8,128)S(1)}, u32[]{:S(2)}) copy-start(f32[1,256,128]{2,1,0:T(8,128)S(1)} %collective-permute-done.8.refs_1_) | copy-start | bytes 393220
  52.3 7.6 %copy-start.11 = (f32[1,256,128]{2,1,0:T(8,128)}, f32[1,256,128]{2,1,0:T(8,128)S(1)}, u32[]{:S(2)}) copy-start(f32[1,256,128]{2,1,0:T(8,128)S(1)} %collective-permute-done.9.refs_2_) | copy-start | bytes 393220
  59.0 0.8 copy-start.9
  73.0 13.5 %copy-start = (f32[256,256]{1,0:T(8,128)S(1)}, f32[256,256]{1,0:T(8,128)}, u32[]{:S(2)}) copy-start(f32[256,256]{1,0:T(8,128)} %get-tuple-element.62) | copy-start | bytes 786436
  73.0 13.5 %collective-permute-start.12 = (f32[256,256]{1,0:T(8,128)}, f32[256,256]{1,0:T(8,128)S(1)}, u32[]{:S(2)}, u32[]{:S(2)}) collective-permute-start(f32[256,256]{1,0:T(8,128)} %get-tuple-element.62), channel_id=1, source_target_pairs={{0,8},{8,0},{16,24},{24,16},{32,40},{40,32},{48,56},{56,48},{64,72... | collective-permute-start | bytes 786440 | tf_op jit(solution)/shard_map/ppermute | solution.py:41
  85.9 16.0 %collective-permute-start.17 = (f32[256,512]{1,0:T(8,128)}, f32[256,512]{1,0:T(8,128)S(1)}, u32[]{:S(2)}, u32[]{:S(2)}) collective-permute-start(f32[256,512]{1,0:T(8,128)} %get-tuple-element.64), channel_id=1, source_target_pairs={{0,8},{8,0},{16,24},{24,16},{32,40},{40,32},{48,56},{56,48},{64,72... | collective-permute-start | bytes 1572872 | tf_op jit(solution)/shard_map/ppermute | solution.py:41
  86.9 14.2 %collective-permute-start.15 = (f32[128,256]{1,0:T(8,128)S(1)}, f32[128,256]{1,0:T(8,128)S(1)}, u32[]{:S(2)}, u32[]{:S(2)}) collective-permute-start(f32[128,256]{1,0:T(8,128)S(1)} %constant_dynamic-slice_fusion.4), channel_id=1, source_target_pairs={{0,48},{8,56},{16,0},{24,8},{32,16},{40,24},{48,32},{56,40},{64,11... | collective-permute-start | bytes 393224 | tf_op jit(solution)/shard_map/ppermute | solution.py:49
  87.0 14.1 %collective-permute-start.14 = (f32[128,256]{1,0:T(8,128)S(1)}, f32[128,256]{1,0:T(8,128)S(1)}, u32[]{:S(2)}, u32[]{:S(2)}) collective-permute-start(f32[128,256]{1,0:T(8,128)S(1)} %constant_dynamic-slice_fusion.4), channel_id=1, source_target_pairs={{0,32},{8,40},{16,48},{24,56},{32,0},{40,8},{48,16},{56,24},{64,96... | collective-permute-start | bytes 393224 | tf_op jit(solution)/shard_map/ppermute | solution.py:49
  87.1 14.1 %collective-permute-start.13 = (f32[128,256]{1,0:T(8,128)S(1)}, f32[128,256]{1,0:T(8,128)S(1)}, u32[]{:S(2)}, u32[]{:S(2)}) collective-permute-start(f32[128,256]{1,0:T(8,128)S(1)} %constant_dynamic-slice_fusion.4), channel_id=1, source_target_pairs={{0,16},{8,24},{16,32},{24,40},{32,48},{40,56},{48,0},{56,8},{64,80... | collective-permute-start | bytes 393224 | tf_op jit(solution)/shard_map/ppermute | solution.py:49
  101.1 14.7 %copy-start.6 = (f32[128,256]{1,0:T(8,128)}, f32[128,256]{1,0:T(8,128)S(1)}, u32[]{:S(2)}) copy-start(f32[128,256]{1,0:T(8,128)S(1)} %collective-permute-done.13) | copy-start | bytes 393220
  101.2 14.6 %collective-permute-start.16 = (f32[4,128,256]{2,1,0:T(8,128)S(1)}, f32[4,128,256]{2,1,0:T(8,128)S(1)}, u32[]{:S(2)}, u32[]{:S(2)}) collective-permute-start(f32[4,128,256]{2,1,0:T(8,128)S(1)} %pad_maximum_fusion.1), channel_id=1, source_target_pairs={{0,8},{8,0},{16,24},{24,16},{32,40},{40,32},{48,56},{56,48},{64,72... | collective-permute-start | bytes 1572872 | tf_op jit(solution)/shard_map/ppermute | solution.py:41
  103.7 5.2 %collective-permute-start.20 = (f32[256,128]{1,0:T(8,128)S(1)}, f32[256,128]{1,0:T(8,128)S(1)}, u32[]{:S(2)}, u32[]{:S(2)}) collective-permute-start(f32[256,128]{1,0:T(8,128)S(1)} %get-tuple-element.76), channel_id=1, source_target_pairs={{0,48},{8,56},{16,0},{24,8},{32,16},{40,24},{48,32},{56,40},{64,11... | collective-permute-start | bytes 393224 | tf_op jit(solution)/shard_map/ppermute | solution.py:49
  106.1 6.1 %collective-permute-start.19 = (f32[256,128]{1,0:T(8,128)S(1)}, f32[256,128]{1,0:T(8,128)S(1)}, u32[]{:S(2)}, u32[]{:S(2)}) collective-permute-start(f32[256,128]{1,0:T(8,128)S(1)} %get-tuple-element.77), channel_id=1, source_target_pairs={{0,32},{8,40},{16,48},{24,56},{32,0},{40,8},{48,16},{56,24},{64,96... | collective-permute-start | bytes 393224 | tf_op jit(solution)/shard_map/ppermute | solution.py:49
  107.7 8.1 %collective-permute-start.18 = (f32[256,128]{1,0:T(8,128)S(1)}, f32[256,128]{1,0:T(8,128)S(1)}, u32[]{:S(2)}, u32[]{:S(2)}) collective-permute-start(f32[256,128]{1,0:T(8,128)S(1)} %get-tuple-element.78), channel_id=1, source_target_pairs={{0,16},{8,24},{16,32},{24,40},{32,48},{40,56},{48,0},{56,8},{64,80... | collective-permute-start | bytes 393224 | tf_op jit(solution)/shard_map/ppermute | solution.py:49
  116.9 18.7 %copy-start.1 = (f32[256,512]{1,0:T(8,128)S(1)}, f32[256,512]{1,0:T(8,128)}, u32[]{:S(2)}) copy-start(f32[256,512]{1,0:T(8,128)} %get-tuple-element.63) | copy-start | bytes 1572868
  118.1 7.9 %collective-permute-start.21 = (f32[256,128]{1,0:T(8,128)S(1)}, f32[256,128]{1,0:T(8,128)S(1)}, u32[]{:S(2)}, u32[]{:S(2)}) collective-permute-start(f32[256,128]{1,0:T(8,128)S(1)} %fusion.8), channel_id=1, source_target_pairs={{0,64},{8,72},{16,80},{24,88},{32,96},{40,104},{48,112},{56,120},{... | collective-permute-start | bytes 393224 | tf_op jit(solution)/shard_map/ppermute | solution.py:469
  127.3 3.9 %collective-permute-start.24 = (f32[256,128]{1,0:T(8,128)S(1)}, f32[256,128]{1,0:T(8,128)S(1)}, u32[]{:S(2)}, u32[]{:S(2)}) collective-permute-start(f32[256,128]{1,0:T(8,128)S(1)} %get-tuple-element.72), channel_id=1, source_target_pairs={{0,48},{8,56},{16,0},{24,8},{32,16},{40,24},{48,32},{56,40},{64,11... | collective-permute-start | bytes 393224 | tf_op jit(solution)/shard_map/ppermute | solution.py:49
  127.4 5.4 %collective-permute-start.23 = (f32[256,128]{1,0:T(8,128)S(1)}, f32[256,128]{1,0:T(8,128)S(1)}, u32[]{:S(2)}, u32[]{:S(2)}) collective-permute-start(f32[256,128]{1,0:T(8,128)S(1)} %get-tuple-element.73), channel_id=1, source_target_pairs={{0,32},{8,40},{16,48},{24,56},{32,0},{40,8},{48,16},{56,24},{64,96... | collective-permute-start | bytes 393224 | tf_op jit(solution)/shard_map/ppermute | solution.py:49
  128.8 6.7 %collective-permute-start.22 = (f32[256,128]{1,0:T(8,128)S(1)}, f32[256,128]{1,0:T(8,128)S(1)}, u32[]{:S(2)}, u32[]{:S(2)}) collective-permute-start(f32[256,128]{1,0:T(8,128)S(1)} %get-tuple-element.74), channel_id=1, source_target_pairs={{0,16},{8,24},{16,32},{24,40},{32,48},{40,56},{48,0},{56,8},{64,80... | collective-permute-start | bytes 393224 | tf_op jit(solution)/shard_map/ppermute | solution.py:49
  136.3 3.8 %collective-permute-start.25 = (f32[256,512]{1,0:T(8,128)S(1)}, f32[256,512]{1,0:T(8,128)S(1)}, u32[]{:S(2)}, u32[]{:S(2)}) collective-permute-start(f32[256,512]{1,0:T(8,128)S(1)} %get-tuple-element.66), channel_id=1, source_target_pairs={{0,8},{8,0},{16,24},{24,16},{32,40},{40,32},{48,56},{56,48},{64,72... | collective-permute-start | bytes 1572872 | tf_op jit(solution)/shard_map/ppermute | solution.py:41

commit v3 on v2

--- a/solution.py
+++ b/solution.py
@@ -114,9 +114,8 @@
 
 
 def build_kernel(parts, has_input, *refs):
-    count = max(part[0] for part in parts) + 1
-    pieces = refs[:count]
-    outs = refs[count + (2 if has_input else 0) :][:2]
+    pieces = refs[: len(refs) - (6 if has_input else 4)]
+    outs = refs[-4:-2]
     staged, sems = refs[-2], refs[-1]
     depth = staged.shape[2]
     copies = []
@@ -124,7 +123,12 @@
     for index, (source, blocks, group, place) in enumerate(parts):
         size = len(blocks)
         for block in blocks:
-            high, low = build_reflection(pieces[source][block])
+            if isinstance(source, tuple):
+                usual, late, late_vec = source
+                packed = jnp.where(lax.axis_index("vec") == late_vec, pieces[late][block], pieces[usual][block])
+            else:
+                packed = pieces[source][block]
+            high, low = build_reflection(packed)
             staged[at, :depth] = high
             staged[at, depth:] = low
             at += 1
@@ -177,7 +181,7 @@
     return [(start, min(size, total - start)) for start in range(0, total, size)]
 
 
-def sweep_kernel(width, unit, other_half, *refs):
+def sweep_kernel(width, unit, *refs):
     if unit:
         first_hbm, second_hbm, out, state_out, first, second, first_state, second_state, between, result, sems = refs
         data = None
@@ -191,13 +195,10 @@
     def copies_of(m):
         result = [pltpu.make_async_copy(first_hbm.at[pl.ds(2 * m, 2)], first.at[pl.ds(2 * m, 2)], sems.at[0, m])]
         if not unit:
-            core = lax.rem(lax.axis_index("row"), 2)
-            half = (1 - core) if other_half else core
-            cols = pl.ds(pl.multiple_of(half * first_cols, first_cols), first_cols)
             if isinstance(m, int) and m == granules - 1:
-                source = tail_hbm.at[:, cols]
+                source = tail_hbm
             else:
-                source = data_hbm.at[pl.ds(m * 2 * width, 2 * width), cols]
+                source = data_hbm.at[pl.ds(m * 2 * width, 2 * width)]
             result.append(pltpu.make_async_copy(source, data.at[m], sems.at[1, m]))
         return result
 
@@ -296,13 +297,13 @@
         out_copy(block).wait()
 
 
-def sweep(buffers, data=None, tail=None, other_half=False, unit=False):
+def sweep(buffers, data=None, tail=None, unit=False):
     first, second = buffers
     depth = first.shape[2]
     width = depth // 2
     blocks = second.shape[0] - 1
     granules = first.shape[0] // 2
-    first_cols = width if unit else data.shape[1] // 2
+    first_cols = width if unit else data.shape[1]
     second_cols = 2 * width if unit else first_cols
     any_spec = pl.BlockSpec(memory_space=pl.ANY)
     rows = blocks * width
@@ -318,7 +319,7 @@
     ]
     ins = (first, second) if unit else (first, second, data, tail)
     return pl.pallas_call(
-        functools.partial(sweep_kernel, width, unit, other_half),
+        functools.partial(sweep_kernel, width, unit),
         out_shape=(
             jax.ShapeDtypeStruct((rows, second_cols), F32),
             jax.ShapeDtypeStruct((depth, second_cols), F32),
@@ -335,44 +336,54 @@
     )(*ins)
 
 
-def correct_kernel(other_ref, own_ref, response_ref, incoming_ref, out_ref, high_ref, low_ref):
-    @pl.when(pl.program_id(0) == 0)
-    def _():
-        high, low = split(incoming_ref[...])
-        high_ref[...] = high
-        low_ref[...] = low
-
-    core = lax.rem(lax.axis_index("row"), 2)
-    half = own_ref.shape[1]
-    high, low = split(response_ref[...])
-    both = jnp.concatenate([high, low], axis=0)
-    tile = high.shape[0]
-    for at in range(2):
-        cols = slice(at * half, (at + 1) * half)
-        sums = dot(both, high_ref[:, cols])
-        update = sums[:tile] + (sums[tile:] + dot(high, low_ref[:, cols]))
-        out_ref[:, cols] = jnp.where(core == at, own_ref[...], other_ref[...]) + update
-
-
-def correct(other, own, response, incoming, tile=256):
-    count, half = own.shape
-    depth = response.shape[1]
-    cols = 2 * half
-    tiled = pl.BlockSpec((tile, half), lambda k: (k, 0))
+def correct_kernel(tile, rows_hbm, response_hbm, incoming, out_hbm, rows, response, sems):
+    count = rows.shape[0] // tile
+
+    def span(index):
+        return pl.ds(index * tile, tile)
+
+    arrivals = [
+        (
+            pltpu.make_async_copy(response_hbm.at[span(k)], response.at[span(k)], sems.at[0, k]),
+            pltpu.make_async_copy(rows_hbm.at[span(k)], rows.at[span(k)], sems.at[1, k]),
+        )
+        for k in range(count)
+    ]
+    for pair in arrivals:
+        for copy in pair:
+            copy.start()
+    incoming_high, incoming_low = split(incoming[...])
+    departures = []
+    for k in range(count):
+        for copy in arrivals[k]:
+            copy.wait()
+        high, low = split(response[k * tile : (k + 1) * tile])
+        both = jnp.concatenate([high, low], axis=0)
+        for start, size in chunks(rows.shape[1], 512):
+            at = (slice(k * tile, (k + 1) * tile), slice(start, start + size))
+            sums = dot(both, incoming_high[:, at[1]])
+            rows[at] = rows[at] + (sums[:tile] + (sums[tile:] + dot(high, incoming_low[:, at[1]])))
+        copy = pltpu.make_async_copy(rows.at[span(k)], out_hbm.at[span(k)], sems.at[2, k])
+        copy.start()
+        departures.append(copy)
+    for copy in departures:
+        copy.wait()
+
+
+def correct(rows, response, incoming, tile=256):
+    any_spec = pl.BlockSpec(memory_space=pl.ANY)
     return pl.pallas_call(
-        correct_kernel,
-        grid=(count // tile,),
-        out_shape=jax.ShapeDtypeStruct((count, cols), F32),
-        in_specs=[
-            tiled,
-            tiled,
-            pl.BlockSpec((tile, depth), lambda k: (k, 0)),
-            pl.BlockSpec((depth, cols), lambda k: (0, 0)),
+        functools.partial(correct_kernel, tile),
+        out_shape=jax.ShapeDtypeStruct(rows.shape, F32),
+        in_specs=[any_spec, any_spec, pl.BlockSpec(memory_space=pltpu.VMEM)],
+        out_specs=any_spec,
+        scratch_shapes=[
+            pltpu.VMEM(rows.shape, F32),
+            pltpu.VMEM(response.shape, F32),
+            pltpu.SemaphoreType.DMA((3, rows.shape[0] // tile)),
         ],
-        out_specs=pl.BlockSpec((tile, cols), lambda k: (k, 0)),
-        scratch_shapes=[pltpu.VMEM((depth, cols), BF16), pltpu.VMEM((depth, cols), BF16)],
         compiler_params=pltpu.CompilerParams(vmem_limit_bytes=VMEM_BYTES),
-    )(other, own, response, incoming)
+    )(rows, response, incoming)
 
 
 def local(eigvecs, wy_v, wy_t):
@@ -397,7 +408,7 @@
     p01, p30, p10, *buffers = together(p01, p30, p10, *buffers)
     p31, p20, p11 = across_x(p30), along_z(p30, 1), along_z(p01, -1)
     buffers = build(buffers, shapes, [p01, p30, p10], parts_of([(0, 1), (3, 0), (1, 0)]))
-    p31, p20, p11, tail, *buffers = together(p31, p20, p11, tail, *buffers)
+    p31, p20, p11, *buffers = together(p31, p20, p11, *buffers)
     last = [across_x(p20[0]), along_z(p31[1, :1], 1), along_z(p11[1, 1:], -1)]
     known = {(0, 0): own, (0, 1): p01, (3, 0): p30, (1, 0): p10, (3, 1): p31, (2, 0): p20, (1, 1): p11}
     picked = pick_first(known)
@@ -415,36 +426,36 @@
     ]
     buffers = build(buffers, shapes, [p31, p20, p11], parts_of([(3, 1), (2, 0), (1, 1)]))
     *arrived, _, _ = together(*last, *extras, *buffers)
-    extra = jnp.where(lax.axis_index("vec") == late, arrived[4], arrived[3])
     opposite = 2 * 2 + 1
     buffers = build(
         buffers,
         shapes,
-        [arrived[0], arrived[1], arrived[2], extra],
+        arrived,
         [
             (0, [0, 1], 0, lambda vec: 2 * place_of(opposite)),
             (1, [0], 1, lambda vec: 2 * place_of(opposite)),
             (2, [0], 1, lambda vec: 2 * place_of(opposite) + 1),
-            (3, [0, 1], 0, lambda vec: own_blocks),
-            (3, [2], 1, lambda vec: own_blocks),
+            ((3, 4, late), [0, 1], 0, lambda vec: own_blocks),
+            ((3, 4, late), [2], 1, lambda vec: own_blocks),
         ],
     )
 
     response, transition = sweep(buffers, unit=True)
     received_transition = across_core(transition)
-    other_rows, other_offset = sweep(buffers, eigvecs, tail, other_half=True)
-    received_offset = across_core(other_offset)
     lower_transition = jnp.where(core == 0, transition, received_transition)
     upper_transition = jnp.where(core == 0, received_transition, transition)
     chip_transition = dot(upper_transition, lower_transition, HIGHEST)
-    part = lax.dynamic_slice_in_dim(chip_transition, core * width, width, 0)
-    parts = jnp.stack([part] + [along_y(part, d) for d in range(1, Y_SIZE)])
-    own_rows, own_offset = sweep(buffers, eigvecs, tail, other_half=False)
-    other_parts = across_core(parts)
+    chip_transition, *buffers = together(chip_transition, *buffers)
+    transitions = [chip_transition] + [along_y(chip_transition, d) for d in range(1, Y_SIZE)]
+    swept, offset = sweep(buffers, eigvecs, tail)
+    offset, *transitions = together(offset, *transitions)
+    half = cols_dev // 2
+    own_offset = lax.dynamic_slice_in_dim(offset, core * half, half, 1)
+    received_offset = across_core(lax.dynamic_slice_in_dim(offset, (1 - core) * half, half, 1))
     lower_offset = jnp.where(core == 0, own_offset, received_offset)
     upper_offset = jnp.where(core == 0, received_offset, own_offset)
     chip_offset = dot(upper_transition, lower_offset, HIGHEST) + upper_offset
-    quarter = chip_offset.shape[1] // Y_SIZE
+    quarter = half // Y_SIZE
 
     def quarter_of(index):
         return lax.dynamic_slice_in_dim(chip_offset, index * quarter, quarter, 1)
@@ -452,15 +463,11 @@
     offsets = jnp.stack(
         [quarter_of(y)] + [along_y(quarter_of((y + d) % Y_SIZE), d) for d in range(1, Y_SIZE)]
     )
+    transitions = jnp.stack(transitions)
 
     def at_chip(stacked, index):
         return lax.dynamic_index_in_dim(stacked, (y - index) % Y_SIZE, 0, False)
 
-    transitions = jnp.where(
-        core == 0,
-        jnp.concatenate([parts, other_parts], axis=1),
-        jnp.concatenate([other_parts, parts], axis=1),
-    )
     steps = [(at_chip(transitions, at), at_chip(offsets, at)) for at in range(Y_SIZE)]
     state = steps[0][1]
     for at in range(1, Y_SIZE):
@@ -481,7 +488,7 @@
     incoming = jnp.where(
         core == 0, jnp.concatenate([kept, taken], axis=1), jnp.concatenate([taken, kept], axis=1)
     )
-    return correct(other_rows, own_rows, response, incoming)
+    return correct(swept, response, incoming)
 
 
 def solution(mesh):

time: 154 us -> 146 us (0.948)
  the two profiles are of different devices: /device:TPU:71 before, /device:TPU:5 now
where the time goes in v3:
time: 146 us; the launch traced here: 144 us
  Pallas kernels  55.8 us (38%)
  starting transfers between devices  38.7 us (27%)
  waiting for transfers between devices  32.9 us (23%)
  matrix products  6.36 us (4%)
  local copies, waits for them, and re-layouts  5.68 us (4%)
  other arithmetic  3.5 us (2%)
    pallas_call x2, Pallas kernels, sweep(): pl.pallas_call(functools.partial(sweep_kernel, width, unit), out_shape=(j...  28.5 us
    pallas_call x4, Pallas kernels, build(): pl.pallas_call(functools.partial(build_kernel, parts, has_input), out_sha...  16.4 us
    ppermute x9, waiting for transfers between devices, along_y(): lax.ppermute(value, 'row', [(i, target(i)) for i in range(lax.axis_size('...  11.1 us
    ppermute x9, starting transfers between devices, along_y(): lax.ppermute(value, 'row', [(i, target(i)) for i in range(lax.axis_size('...  9.54 us
    pallas_call x1, Pallas kernels, correct(): pl.pallas_call(functools.partial(correct_kernel, tile), out_shape=jax.Sha...  9.18 us
    ppermute x6, starting transfers between devices, along_z(): return lax.ppermute(value, 'vec', pairs)  9.03 us
    ppermute x3, starting transfers between devices, across_core(): lax.ppermute(value, 'row', [(i, i ^ 1) for i in range(lax.axis_size('row'...  7.15 us
    dot_general x9, matrix products, dot(): return jnp.dot(a, b, precision=precision, preferred_element_type=F32)  6.36 us
  transfers between devices with their start and end apart: 25, of which 13 were waited for; matrix products, arithmetic and copies ran while one was open for 3% of the time, Pallas kernels for 32%

profile of v3, /device:TPU:5, one launch (start us, length us, event | category | flops | bytes accessed | tf_op | source)
XLA Modules:
  0.0 143.7 jit_solution(3300481043762780695)
XLA Ops:
  0.0 1.2 slice_select_fusion
  1.2 1.0 collective-permute-start
  2.2 1.6 %collective-permute-start.1 = (f32[2,2,256,128]{3,2,1,0:T(8,128)S(1)}, f32[2,2,256,128]{3,2,1,0:T(8,128)S(1)}, u32[]{:S(2)}, u32[]{:S(2)}) collective-permute-start(f32[2,2,256,128]{3,2,1,0:T(8,128)S(1)} %pad_maximum_fusion.1.refs_0_), channel_id=1, source_target_pairs={{0,2},{1,3},{2,4},{3,5},{4,6},{5,7},{6,0},{7,1},{8,10},{9,11},{10,... | collective-permute-start | bytes 1572872 | tf_op jit(solution)/shard_map/ppermute | solution.py:33
  3.9 2.1 %collective-permute-start.2 = (f32[2,2,256,128]{3,2,1,0:T(8,128)S(1)}, f32[2,2,256,128]{3,2,1,0:T(8,128)S(1)}, u32[]{:S(2)}, u32[]{:S(2)}) collective-permute-start(f32[2,2,256,128]{3,2,1,0:T(8,128)S(1)} %pad_maximum_fusion.1.refs_0_), channel_id=1, source_target_pairs={{0,6},{1,7},{2,0},{3,1},{4,2},{5,3},{6,4},{7,5},{8,14},{9,15},{10,... | collective-permute-start | bytes 1572872 | tf_op jit(solution)/shard_map/ppermute | solution.py:33
  6.0 2.9 %shard_map.37 = (bf16[18,512,256]{2,1,0:T(8,128)(2,1)}, bf16[17,512,256]{2,1,0:T(8,128)(2,1)}) custom-call(f32[2,2,256,128]{3,2,1,0:T(8,128)} %copy-done.4), custom_call_target="tpu_custom_call" | custom-call | flops 1200000000 | bytes 1572864 | tf_op jit(solution)/shard_map/pallas_call | solution.py:150
  8.9 5.2 %collective-permute-done.refs_0_.refs_1_ = f32[2,2,256,128]{3,2,1,0:T(8,128)S(1)} collective-permute-done((f32[2,2,256,128]{3,2,1,0:T(8,128)S(1)}, f32[2,2,256,128]{3,2,1,0:T(8,128)S(1)}, u32[]{:S(2)}, u32[]{:S(2)}) %collective-permute-start) | collective-permute-done | bytes 524320 | tf_op jit(solution)/shard_map/ppermute | solution.py:37
  14.1 3.2 %collective-permute-done.1.refs_1_.refs_2_ = f32[2,2,256,128]{3,2,1,0:T(8,128)S(1)} collective-permute-done((f32[2,2,256,128]{3,2,1,0:T(8,128)S(1)}, f32[2,2,256,128]{3,2,1,0:T(8,128)S(1)}, u32[]{:S(2)}, u32[]{:S(2)}) %collective-permute-start.1) | collective-permute-done | bytes 524320 | tf_op jit(solution)/shard_map/ppermute | solution.py:33
  17.3 0.6 collective-permute-start.3
  18.0 0.3 collective-permute-start.4
  18.2 2.4 %collective-permute-start.5 = (f32[2,2,256,128]{3,2,1,0:T(8,128)S(1)}, f32[2,2,256,128]{3,2,1,0:T(8,128)S(1)}, u32[]{:S(2)}, u32[]{:S(2)}) collective-permute-start(f32[2,2,256,128]{3,2,1,0:T(8,128)S(1)} %collective-permute-done.refs_0_.refs_1_), channel_id=1, source_target_pairs={{0,6},{1,7},{2,0},{3,1},{4,2},{5,3},{6,4},{7,5},{8,14},{9,15},{10,... | collective-permute-start | bytes 1572872 | tf_op jit(solution)/shard_map/ppermute | solution.py:33
  20.6 1.3 slice.23
  21.9 4.3 %collective-permute-start.12 = (f32[256,1024]{1,0:T(8,128)S(1)}, f32[256,1024]{1,0:T(8,128)}, u32[]{:S(2)}, u32[]{:S(2)}) collective-permute-start(f32[256,1024]{1,0:T(8,128)S(1)} %slice.23), channel_id=1, source_target_pairs={{8,0},{16,8},{24,16},{32,24},{40,32},{48,40},{56,48},{64,56},{72,6... | collective-permute-start | bytes 3145736 | tf_op jit(solution)/shard_map/ppermute | solution.py:53
  26.3 4.8 %shard_map.38 = (bf16[18,512,256]{2,1,0:T(8,128)(2,1)}, bf16[17,512,256]{2,1,0:T(8,128)(2,1)}) custom-call(f32[2,2,256,128]{3,2,1,0:T(8,128)} %copy-done.8, f32[2,2,256,128]{3,2,1,0:T(8,128)} %copy-done.9, f32[2,2,256,128]{3,2,1,0:T(8,128)} %copy-done.10, ...), custom_call_target="tpu_custom_call", output_to_operand_aliasing={{0}: (3, {}), {1}: (4, {})} | custom-call | flops 3600000000 | bytes 4718592 | tf_op jit(solution)/shard_map/pallas_call | solution.py:150
  31.2 0.7 copy-done.6
  31.9 0.2 copy-done.5
  32.1 0.2 copy-done.7
  32.3 1.8 %shard_map.39 = f32[3,256,128]{2,1,0:T(8,128)} custom-call(f32[2,2,256,128]{3,2,1,0:T(8,128)} %copy-done.4, f32[2,2,256,128]{3,2,1,0:T(8,128)} %copy-done.8, f32[2,2,256,128]{3,2,1,0:T(8,128)} %copy-done.9, f32[2,2,256,128]{3,2,1,0:T(8,128)} %copy-done.10, f32[2,2,256,128]{3,2,1,0:T(8,128)} %copy-done.6, f32[2,2,256,128]{3,2,1,0:T(8,128)} %copy-done.5, ...), custom_call_target="tpu_custom_call" | custom-call | tf_op jit(solution)/shard_map/pallas_call | solution.py:85
  34.0 4.1 %collective-permute-start.9 = (f32[3,256,128]{2,1,0:T(8,128)}, f32[3,256,128]{2,1,0:T(8,128)S(1)}, u32[]{:S(2)}, u32[]{:S(2)}) collective-permute-start(f32[3,256,128]{2,1,0:T(8,128)} %shard_map.39), channel_id=1, source_target_pairs={{8,0},{9,1},{10,2},{11,3},{12,4},{14,6},{15,7},{16,8},{17,9},{18,1... | collective-permute-start | bytes 1179656 | tf_op jit(solution)/shard_map/ppermute | solution.py:418
  38.2 0.7 collective-permute-start.10
  38.8 0.4 collective-permute-start.7
  39.2 0.9 slice_bitcast_fusion.1
  40.1 1.0 collective-permute-start.6
  41.1 3.1 %collective-permute-done.7.refs_1_ = f32[1,256,128]{2,1,0:T(8,128)S(1)} collective-permute-done((f32[1,256,128]{2,1,0:T(8,128)S(1)}, f32[1,256,128]{2,1,0:T(8,128)S(1)}, u32[]{:S(2)}, u32[]{:S(2)}) %collective-permute-start.7) | collective-permute-done | bytes 131104 | tf_op jit(solution)/shard_map/ppermute | solution.py:33
  44.3 2.2 %collective-permute-start.8 = (f32[1,256,128]{2,1,0:T(8,128)S(1)}, f32[1,256,128]{2,1,0:T(8,128)S(1)}, u32[]{:S(2)}, u32[]{:S(2)}) collective-permute-start(f32[1,256,128]{2,1,0:T(8,128)S(1)} %slice_bitcast_fusion.1), channel_id=1, source_target_pairs={{0,6},{1,7},{2,0},{3,1},{4,2},{5,3},{6,4},{7,5},{8,14},{9,15},{10,... | collective-permute-start | bytes 393224 | tf_op jit(solution)/shard_map/ppermute | solution.py:33
  46.5 4.8 %shard_map.40 = (bf16[18,512,256]{2,1,0:T(8,128)(2,1)}, bf16[17,512,256]{2,1,0:T(8,128)(2,1)}) custom-call(f32[2,2,256,128]{3,2,1,0:T(8,128)} %copy-done.6, f32[2,2,256,128]{3,2,1,0:T(8,128)} %copy-done.5, f32[2,2,256,128]{3,2,1,0:T(8,128)} %copy-done.7, ...), custom_call_target="tpu_custom_call", output_to_operand_aliasing={{0}: (3, {}), {1}: (4, {})} | custom-call | flops 3600000000 | bytes 4718592 | tf_op jit(solution)/shard_map/pallas_call | solution.py:150
  51.4 0.6 copy-done.16
  52.2 0.2 copy-done.12
  52.4 3.8 %shard_map.41 = (bf16[18,512,256]{2,1,0:T(8,128)(2,1)}, bf16[17,512,256]{2,1,0:T(8,128)(2,1)}) custom-call(f32[2,256,128]{2,1,0:T(8,128)} %copy-done.13, f32[1,256,128]{2,1,0:T(8,128)} %copy-done.15, f32[1,256,128]{2,1,0:T(8,128)} %copy-done.16, f32[3,256,128]{2,1,0:T(8,128)} %copy-done.11, ...), custom_call_target="tpu_custom_call", output_to_operand_aliasing={{0}: (5, {}), {1}: (6, {})} | custom-call | flops 2100000000 | bytes 2752512 | tf_op jit(solution)/shard_map/pallas_call | solution.py:150
  56.2 9.3 %shard_map.42 = (f32[2048,256]{1,0:T(8,128)}, f32[256,256]{1,0:T(8,128)}) custom-call(bf16[18,512,256]{2,1,0:T(8,128)(2,1)} %get-tuple-element.64.refs_0_, bf16[17,512,256]{2,1,0:T(8,128)(2,1)} %get-tuple-element.65.refs_1_), custom_call_target="tpu_custom_call" | custom-call | flops 2415919104 | bytes 31457280 | tf_op jit(solution)/shard_map/pallas_call | solution.py:321
  65.6 1.7 %collective-permute-start.11 = (f32[256,256]{1,0:T(8,128)}, f32[256,256]{1,0:T(8,128)S(1)}, u32[]{:S(2)}, u32[]{:S(2)}) collective-permute-start(f32[256,256]{1,0:T(8,128)} %get-tuple-element.63), channel_id=1, source_target_pairs={{0,8},{8,0},{16,24},{24,16},{32,40},{40,32},{48,56},{56,48},{64,72... | collective-permute-start | bytes 786440 | tf_op jit(solution)/shard_map/ppermute | solution.py:41
  67.3 1.4 collective-permute-done.11
  68.6 1.3 fusion.17
  70.0 1.0 collective-permute-start.13
  71.0 2.6 %collective-permute-start.14 = (f32[256,256]{1,0:T(8,128)S(1)}, f32[256,256]{1,0:T(8,128)S(1)}, u32[]{:S(2)}, u32[]{:S(2)}) collective-permute-start(f32[256,256]{1,0:T(8,128)S(1)} %fusion.17), channel_id=1, source_target_pairs={{0,32},{8,40},{16,48},{24,56},{32,0},{40,8},{48,16},{56,24},{64,96... | collective-permute-start | bytes 786440 | tf_op jit(solution)/shard_map/ppermute | solution.py:49
  73.7 1.0 collective-permute-start.15
  74.7 19.1 %shard_map.43 = (f32[2048,1024]{1,0:T(8,128)}, f32[256,1024]{1,0:T(8,128)}) custom-call(bf16[18,512,256]{2,1,0:T(8,128)(2,1)} %get-tuple-element.64.refs_0_, bf16[17,512,256]{2,1,0:T(8,128)(2,1)} %get-tuple-element.65.refs_1_, f32[2048,1024]{1,0:T(8,128)} %refs_2_.1, f32[256,1024]{1,0:T(8,128)} %collective-permute-done.12.refs_3_), custom_call_target="tpu_custom_call" | custom-call | flops 12884901888 | bytes 31457280 | tf_op jit(solution)/shard_map/pallas_call | solution.py:321
  93.9 1.2 constant_dynamic-slice_fusion.4
  95.1 1.3 collective-permute-start.16
  96.4 1.5 %collective-permute-done.16 = f32[256,512]{1,0:T(8,128)S(1)} collective-permute-done((f32[256,512]{1,0:T(8,128)S(1)}, f32[256,512]{1,0:T(8,128)S(1)}, u32[]{:S(2)}, u32[]{:S(2)}) %collective-permute-start.16) | collective-permute-done | bytes 524320 | tf_op jit(solution)/shard_map/ppermute | solution.py:41
  97.9 2.0 %convolution_add_fusion.1 = f32[256,512]{1,0:T(8,128)S(1)} fusion(f32[256,512]{1,0:T(8,128)S(1)} %collective-permute-done.16, f32[256,1024]{1,0:T(8,128)} %get-tuple-element.74, s32[]{:T(128)S(6)} %select_n.176, pred[]{:T(512)S(6)} %eq.31, f32[256,256]{1,0:T(8,128)S(1)} %collective-permute-done.11, f32[256,256]{1,0:T(8,128)S(1)} %copy-done), kind=kOutput, calls=%fused_computation.1 | convolution fusion | flops 403111936 | bytes 3148288 | tf_op jit(solution)/shard_map/dot_general | solution.py:19
  100.1 2.2 %collective-permute-start.18 = (f32[256,128]{1,0:T(8,128)S(1)}, f32[256,128]{1,0:T(8,128)S(1)}, u32[]{:S(2)}, u32[]{:S(2)}) collective-permute-start(f32[256,128]{1,0:T(8,128)S(1)} %get-tuple-element.87), channel_id=1, source_target_pairs={{0,32},{8,40},{16,48},{24,56},{32,0},{40,8},{48,16},{56,24},{64,96... | collective-permute-start | bytes 393224 | tf_op jit(solution)/shard_map/ppermute | solution.py:49
  102.3 1.0 pad_maximum_fusion
  103.4 1.4 collective-permute-done.19
  104.8 1.6 %collective-permute-done.18 = f32[256,128]{1,0:T(8,128)S(1)} collective-permute-done((f32[256,128]{1,0:T(8,128)S(1)}, f32[256,128]{1,0:T(8,128)S(1)}, u32[]{:S(2)}, u32[]{:S(2)}) %collective-permute-start.18) | collective-permute-done | bytes 131104 | tf_op jit(solution)/shard_map/ppermute | solution.py:49
  106.4 3.0 %collective-permute-done.17 = f32[256,128]{1,0:T(8,128)S(1)} collective-permute-done((f32[256,128]{1,0:T(8,128)S(1)}, f32[256,128]{1,0:T(8,128)S(1)}, u32[]{:S(2)}, u32[]{:S(2)}) %collective-permute-start.17) | collective-permute-done | bytes 131104 | tf_op jit(solution)/shard_map/ppermute | solution.py:49
  109.4 0.4 convolution_add_fusion.6
  109.8 0.4 convolution_add_fusion.5
  110.2 0.4 bitcast_add_fusion
  110.5 1.3 collective-permute-start.20
  111.9 5.9 %collective-permute-done.20 = f32[256,128]{1,0:T(8,128)S(1)} collective-permute-done((f32[256,128]{1,0:T(8,128)S(1)}, f32[256,128]{1,0:T(8,128)S(1)}, u32[]{:S(2)}, u32[]{:S(2)}) %collective-permute-start.20) | collective-permute-done | bytes 131104 | tf_op jit(solution)/shard_map/ppermute | solution.py:476
  117.8 0.4 convolution_add_fusion.4
  118.1 0.4 convolution_add_fusion.3
  118.5 0.4 fusion
  119.0 0.9 collective-permute-start.23
  119.9 1.4 collective-permute-start.22
  121.3 0.3 collective-permute-start.21
  121.6 1.6 %collective-permute-done.23 = f32[256,128]{1,0:T(8,128)S(1)} collective-permute-done((f32[256,128]{1,0:T(8,128)S(1)}, f32[256,128]{1,0:T(8,128)S(1)}, u32[]{:S(2)}, u32[]{:S(2)}) %collective-permute-start.23) | collective-permute-done | bytes 131104 | tf_op jit(solution)/shard_map/ppermute | solution.py:49
  123.1 2.2 %collective-permute-done.22 = f32[256,128]{1,0:T(8,128)S(1)} collective-permute-done((f32[256,128]{1,0:T(8,128)S(1)}, f32[256,128]{1,0:T(8,128)S(1)}, u32[]{:S(2)}, u32[]{:S(2)}) %collective-permute-start.22) | collective-permute-done | bytes 131104 | tf_op jit(solution)/shard_map/ppermute | solution.py:49
  125.3 1.4 collective-permute-done.21
  126.8 0.7 broadcast_select_fusion.1
  127.5 4.2 %collective-permute-start.24 = (f32[256,512]{1,0:T(8,128)S(1)}, f32[256,512]{1,0:T(8,128)S(1)}, u32[]{:S(2)}, u32[]{:S(2)}) collective-permute-start(f32[256,512]{1,0:T(8,128)S(1)} %get-tuple-element.76), channel_id=1, source_target_pairs={{0,8},{8,0},{16,24},{24,16},{32,40},{40,32},{48,56},{56,48},{64,72... | collective-permute-start | bytes 1572872 | tf_op jit(solution)/shard_map/ppermute | solution.py:41
  131.7 1.5 %collective-permute-done.24 = f32[256,512]{1,0:T(8,128)S(1)} collective-permute-done((f32[256,512]{1,0:T(8,128)S(1)}, f32[256,512]{1,0:T(8,128)S(1)}, u32[]{:S(2)}, u32[]{:S(2)}) %collective-permute-start.24) | collective-permute-done | bytes 524320 | tf_op jit(solution)/shard_map/ppermute | solution.py:41
  133.2 1.1 maximum_select_fusion.incoming
  134.3 9.2 %shard_map.44 = f32[2048,1024]{1,0:T(8,128)} custom-call(f32[2048,1024]{1,0:T(8,128)} %get-tuple-element.66.rows_hbm, f32[2048,256]{1,0:T(8,128)} %get-tuple-element.67.response_hbm, f32[256,1024]{1,0:T(8,128)} %maximum_select_fusion.incoming), custom_call_target="tpu_custom_call" | custom-call | tf_op jit(solution)/shard_map/pallas_call | solution.py:375
  (53 shorter events, 0.8 us)
Async XLA Ops:
  1.2 4.8 %copy-start.4 = (f32[2,2,256,128]{3,2,1,0:T(8,128)}, f32[2,2,256,128]{3,2,1,0:T(8,128)S(1)}, u32[]{:S(2)}) copy-start(f32[2,2,256,128]{3,2,1,0:T(8,128)S(1)} %pad_maximum_fusion.1.refs_0_) | copy-start | bytes 1572868
  1.2 12.9 %collective-permute-start = (f32[2,2,256,128]{3,2,1,0:T(8,128)S(1)}, f32[2,2,256,128]{3,2,1,0:T(8,128)S(1)}, u32[]{:S(2)}, u32[]{:S(2)}) collective-permute-start(f32[2,2,256,128]{3,2,1,0:T(8,128)S(1)} %pad_maximum_fusion.1.refs_0_), channel_id=1, source_target_pairs={{0,1},{1,0},{2,3},{3,2},{4,5},{5,4},{6,7},{7,6},{8,9},{9,8},{10,11... | collective-permute-start | bytes 1572872 | tf_op jit(solution)/shard_map/ppermute | solution.py:37
  2.2 15.1 %collective-permute-start.1 = (f32[2,2,256,128]{3,2,1,0:T(8,128)S(1)}, f32[2,2,256,128]{3,2,1,0:T(8,128)S(1)}, u32[]{:S(2)}, u32[]{:S(2)}) collective-permute-start(f32[2,2,256,128]{3,2,1,0:T(8,128)S(1)} %pad_maximum_fusion.1.refs_0_), channel_id=1, source_target_pairs={{0,2},{1,3},{2,4},{3,5},{4,6},{5,7},{6,0},{7,1},{8,10},{9,11},{10,... | collective-permute-start | bytes 1572872 | tf_op jit(solution)/shard_map/ppermute | solution.py:33
  3.9 13.5 %collective-permute-start.2 = (f32[2,2,256,128]{3,2,1,0:T(8,128)S(1)}, f32[2,2,256,128]{3,2,1,0:T(8,128)S(1)}, u32[]{:S(2)}, u32[]{:S(2)}) collective-permute-start(f32[2,2,256,128]{3,2,1,0:T(8,128)S(1)} %pad_maximum_fusion.1.refs_0_), channel_id=1, source_target_pairs={{0,6},{1,7},{2,0},{3,1},{4,2},{5,3},{6,4},{7,5},{8,14},{9,15},{10,... | collective-permute-start | bytes 1572872 | tf_op jit(solution)/shard_map/ppermute | solution.py:33
  14.1 12.1 %copy-start.8 = (f32[2,2,256,128]{3,2,1,0:T(8,128)}, f32[2,2,256,128]{3,2,1,0:T(8,128)S(1)}, u32[]{:S(2)}) copy-start(f32[2,2,256,128]{3,2,1,0:T(8,128)S(1)} %collective-permute-done.refs_0_.refs_1_) | copy-start | bytes 1572868
  17.3 8.9 %copy-start.9 = (f32[2,2,256,128]{3,2,1,0:T(8,128)}, f32[2,2,256,128]{3,2,1,0:T(8,128)S(1)}, u32[]{:S(2)}) copy-start(f32[2,2,256,128]{3,2,1,0:T(8,128)S(1)} %collective-permute-done.1.refs_1_.refs_2_) | copy-start | bytes 1572868
  17.3 8.9 %copy-start.10 = (f32[2,2,256,128]{3,2,1,0:T(8,128)}, f32[2,2,256,128]{3,2,1,0:T(8,128)S(1)}, u32[]{:S(2)}) copy-start(f32[2,2,256,128]{3,2,1,0:T(8,128)S(1)} %collective-permute-done.2.refs_2_.refs_3_) | copy-start | bytes 1572868
  17.3 13.8 %collective-permute-start.3 = (f32[2,2,256,128]{3,2,1,0:T(8,128)S(1)}, f32[2,2,256,128]{3,2,1,0:T(8,128)S(1)}, u32[]{:S(2)}, u32[]{:S(2)}) collective-permute-start(f32[2,2,256,128]{3,2,1,0:T(8,128)S(1)} %collective-permute-done.1.refs_1_.refs_2_), channel_id=1, source_target_pairs={{0,1},{1,0},{2,3},{3,2},{4,5},{5,4},{6,7},{7,6},{8,9},{9,8},{10,11... | collective-permute-start | bytes 1572872 | tf_op jit(solution)/shard_map/ppermute | solution.py:37
  18.0 13.2 %collective-permute-start.4 = (f32[2,2,256,128]{3,2,1,0:T(8,128)S(1)}, f32[2,2,256,128]{3,2,1,0:T(8,128)S(1)}, u32[]{:S(2)}, u32[]{:S(2)}) collective-permute-start(f32[2,2,256,128]{3,2,1,0:T(8,128)S(1)} %collective-permute-done.1.refs_1_.refs_2_), channel_id=1, source_target_pairs={{0,2},{1,3},{2,4},{3,5},{4,6},{5,7},{6,0},{7,1},{8,10},{9,11},{10,... | collective-permute-start | bytes 1572872 | tf_op jit(solution)/shard_map/ppermute | solution.py:33
  18.2 12.9 %collective-permute-start.5 = (f32[2,2,256,128]{3,2,1,0:T(8,128)S(1)}, f32[2,2,256,128]{3,2,1,0:T(8,128)S(1)}, u32[]{:S(2)}, u32[]{:S(2)}) collective-permute-start(f32[2,2,256,128]{3,2,1,0:T(8,128)S(1)} %collective-permute-done.refs_0_.refs_1_), channel_id=1, source_target_pairs={{0,6},{1,7},{2,0},{3,1},{4,2},{5,3},{6,4},{7,5},{8,14},{9,15},{10,... | collective-permute-start | bytes 1572872 | tf_op jit(solution)/shard_map/ppermute | solution.py:33
  21.9 52.8 %collective-permute-start.12 = (f32[256,1024]{1,0:T(8,128)S(1)}, f32[256,1024]{1,0:T(8,128)}, u32[]{:S(2)}, u32[]{:S(2)}) collective-permute-start(f32[256,1024]{1,0:T(8,128)S(1)} %slice.23), channel_id=1, source_target_pairs={{8,0},{16,8},{24,16},{32,24},{40,32},{48,40},{56,48},{64,56},{72,6... | collective-permute-start | bytes 3145736 | tf_op jit(solution)/shard_map/ppermute | solution.py:53
  31.1 0.8 copy-start.6
  31.1 1.0 copy-start.5
  31.2 1.1 copy-start.7
  34.0 17.3 %collective-permute-start.9 = (f32[3,256,128]{2,1,0:T(8,128)}, f32[3,256,128]{2,1,0:T(8,128)S(1)}, u32[]{:S(2)}, u32[]{:S(2)}) collective-permute-start(f32[3,256,128]{2,1,0:T(8,128)} %shard_map.39), channel_id=1, source_target_pairs={{8,0},{9,1},{10,2},{11,3},{12,4},{14,6},{15,7},{16,8},{17,9},{18,1... | collective-permute-start | bytes 1179656 | tf_op jit(solution)/shard_map/ppermute | solution.py:418
  38.2 13.2 %collective-permute-start.10 = (f32[3,256,128]{2,1,0:T(8,128)}, f32[3,256,128]{2,1,0:T(8,128)S(1)}, u32[]{:S(2)}, u32[]{:S(2)}) collective-permute-start(f32[3,256,128]{2,1,0:T(8,128)} %shard_map.39), channel_id=1, source_target_pairs={{12,5},{20,13},{28,21},{36,29},{44,37},{52,45},{60,53},{68,61},{76... | collective-permute-start | bytes 1179656 | tf_op jit(solution)/shard_map/ppermute | solution.py:423
  38.8 5.4 %collective-permute-start.7 = (f32[1,256,128]{2,1,0:T(8,128)S(1)}, f32[1,256,128]{2,1,0:T(8,128)S(1)}, u32[]{:S(2)}, u32[]{:S(2)}) collective-permute-start(f32[1,256,128]{2,1,0:T(8,128)S(1)} %slice_bitcast_fusion.2), channel_id=1, source_target_pairs={{0,2},{1,3},{2,4},{3,5},{4,6},{5,7},{6,0},{7,1},{8,10},{9,11},{10,... | collective-permute-start | bytes 393224 | tf_op jit(solution)/shard_map/ppermute | solution.py:33
  40.1 11.2 %collective-permute-start.6 = (f32[2,256,128]{2,1,0:T(8,128)S(1)}, f32[2,256,128]{2,1,0:T(8,128)S(1)}, u32[]{:S(2)}, u32[]{:S(2)}) collective-permute-start(f32[2,256,128]{2,1,0:T(8,128)S(1)} %slice_bitcast_fusion), channel_id=1, source_target_pairs={{0,1},{1,0},{2,3},{3,2},{4,5},{5,4},{6,7},{7,6},{8,9},{9,8},{10,11... | collective-permute-start | bytes 786440 | tf_op jit(solution)/shard_map/ppermute | solution.py:37
  44.3 7.1 %copy-start.15 = (f32[1,256,128]{2,1,0:T(8,128)}, f32[1,256,128]{2,1,0:T(8,128)S(1)}, u32[]{:S(2)}) copy-start(f32[1,256,128]{2,1,0:T(8,128)S(1)} %collective-permute-done.7.refs_1_) | copy-start | bytes 393220
  44.3 7.1 %collective-permute-start.8 = (f32[1,256,128]{2,1,0:T(8,128)S(1)}, f32[1,256,128]{2,1,0:T(8,128)S(1)}, u32[]{:S(2)}, u32[]{:S(2)}) collective-permute-start(f32[1,256,128]{2,1,0:T(8,128)S(1)} %slice_bitcast_fusion.1), channel_id=1, source_target_pairs={{0,6},{1,7},{2,0},{3,1},{4,2},{5,3},{6,4},{7,5},{8,14},{9,15},{10,... | collective-permute-start | bytes 393224 | tf_op jit(solution)/shard_map/ppermute | solution.py:33
  51.3 0.6 copy-start.16
  51.4 0.7 copy-start.13
  51.4 0.8 copy-start.11
  51.4 1.0 copy-start.12
  65.6 3.1 %collective-permute-start.11 = (f32[256,256]{1,0:T(8,128)}, f32[256,256]{1,0:T(8,128)S(1)}, u32[]{:S(2)}, u32[]{:S(2)}) collective-permute-start(f32[256,256]{1,0:T(8,128)} %get-tuple-element.63), channel_id=1, source_target_pairs={{0,8},{8,0},{16,24},{24,16},{32,40},{40,32},{48,56},{56,48},{64,72... | collective-permute-start | bytes 786440 | tf_op jit(solution)/shard_map/ppermute | solution.py:41
  70.0 27.9 %copy-start = (f32[256,256]{1,0:T(8,128)S(1)}, f32[256,256]{1,0:T(8,128)}, u32[]{:S(2)}) copy-start(f32[256,256]{1,0:T(8,128)} %get-tuple-element.63) | copy-start | bytes 786436
  70.0 23.9 %collective-permute-start.13 = (f32[256,256]{1,0:T(8,128)S(1)}, f32[256,256]{1,0:T(8,128)S(1)}, u32[]{:S(2)}, u32[]{:S(2)}) collective-permute-start(f32[256,256]{1,0:T(8,128)S(1)} %fusion.17), channel_id=1, source_target_pairs={{0,16},{8,24},{16,32},{24,40},{32,48},{40,56},{48,0},{56,8},{64,80... | collective-permute-start | bytes 786440 | tf_op jit(solution)/shard_map/ppermute | solution.py:49
  71.0 22.8 %collective-permute-start.14 = (f32[256,256]{1,0:T(8,128)S(1)}, f32[256,256]{1,0:T(8,128)S(1)}, u32[]{:S(2)}, u32[]{:S(2)}) collective-permute-start(f32[256,256]{1,0:T(8,128)S(1)} %fusion.17), channel_id=1, source_target_pairs={{0,32},{8,40},{16,48},{24,56},{32,0},{40,8},{48,16},{56,24},{64,96... | collective-permute-start | bytes 786440 | tf_op jit(solution)/shard_map/ppermute | solution.py:49
  73.7 20.2 %collective-permute-start.15 = (f32[256,256]{1,0:T(8,128)S(1)}, f32[256,256]{1,0:T(8,128)S(1)}, u32[]{:S(2)}, u32[]{:S(2)}) collective-permute-start(f32[256,256]{1,0:T(8,128)S(1)} %fusion.17), channel_id=1, source_target_pairs={{0,48},{8,56},{16,0},{24,8},{32,16},{40,24},{48,32},{56,40},{64,11... | collective-permute-start | bytes 786440 | tf_op jit(solution)/shard_map/ppermute | solution.py:49
  93.9 8.4 %copy-start.14 = (f32[256,256]{1,0:T(8,128)}, f32[256,256]{1,0:T(8,128)S(1)}, u32[]{:S(2)}) copy-start(f32[256,256]{1,0:T(8,128)S(1)} %collective-permute-done.15) | copy-start | bytes 786436
  95.1 2.8 %collective-permute-start.16 = (f32[256,512]{1,0:T(8,128)S(1)}, f32[256,512]{1,0:T(8,128)S(1)}, u32[]{:S(2)}, u32[]{:S(2)}) collective-permute-start(f32[256,512]{1,0:T(8,128)S(1)} %constant_dynamic-slice_fusion.4), channel_id=1, source_target_pairs={{0,8},{8,0},{16,24},{24,16},{32,40},{40,32},{48,56},{56,48},{64,72... | collective-permute-start | bytes 1572872 | tf_op jit(solution)/shard_map/ppermute | solution.py:41
  97.9 4.4 %copy-start.2 = (f32[256,512]{1,0:T(8,128)}, f32[256,512]{1,0:T(8,128)S(1)}, u32[]{:S(2)}) copy-start(f32[256,512]{1,0:T(8,128)S(1)} %collective-permute-done.16) | copy-start | bytes 1572868
  100.1 4.7 %collective-permute-start.19 = (f32[256,128]{1,0:T(8,128)S(1)}, f32[256,128]{1,0:T(8,128)S(1)}, u32[]{:S(2)}, u32[]{:S(2)}) collective-permute-start(f32[256,128]{1,0:T(8,128)S(1)} %get-tuple-element.86), channel_id=1, source_target_pairs={{0,48},{8,56},{16,0},{24,8},{32,16},{40,24},{48,32},{56,40},{64,11... | collective-permute-start | bytes 393224 | tf_op jit(solution)/shard_map/ppermute | solution.py:49
  100.1 6.2 %collective-permute-start.18 = (f32[256,128]{1,0:T(8,128)S(1)}, f32[256,128]{1,0:T(8,128)S(1)}, u32[]{:S(2)}, u32[]{:S(2)}) collective-permute-start(f32[256,128]{1,0:T(8,128)S(1)} %get-tuple-element.87), channel_id=1, source_target_pairs={{0,32},{8,40},{16,48},{24,56},{32,0},{40,8},{48,16},{56,24},{64,96... | collective-permute-start | bytes 393224 | tf_op jit(solution)/shard_map/ppermute | solution.py:49
  102.3 7.0 %collective-permute-start.17 = (f32[256,128]{1,0:T(8,128)S(1)}, f32[256,128]{1,0:T(8,128)S(1)}, u32[]{:S(2)}, u32[]{:S(2)}) collective-permute-start(f32[256,128]{1,0:T(8,128)S(1)} %get-tuple-element.88), channel_id=1, source_target_pairs={{0,16},{8,24},{16,32},{24,40},{32,48},{40,56},{48,0},{56,8},{64,80... | collective-permute-start | bytes 393224 | tf_op jit(solution)/shard_map/ppermute | solution.py:49
  103.4 23.4 %copy-start.1 = (f32[256,1024]{1,0:T(8,128)S(1)}, f32[256,1024]{1,0:T(8,128)}, u32[]{:S(2)}) copy-start(f32[256,1024]{1,0:T(8,128)} %get-tuple-element.74) | copy-start | bytes 3145732
  110.5 7.2 %collective-permute-start.20 = (f32[256,128]{1,0:T(8,128)S(1)}, f32[256,128]{1,0:T(8,128)S(1)}, u32[]{:S(2)}, u32[]{:S(2)}) collective-permute-start(f32[256,128]{1,0:T(8,128)S(1)} %bitcast_add_fusion), channel_id=1, source_target_pairs={{0,64},{8,72},{16,80},{24,88},{32,96},{40,104},{48,112},{56,120},{... | collective-permute-start | bytes 393224 | tf_op jit(solution)/shard_map/ppermute | solution.py:476
  111.9 14.9 %copy-start.3 = (f32[256,512]{1,0:T(8,128)S(1)}, f32[256,512]{1,0:T(8,128)}, u32[]{:S(2)}) copy-start(f32[256,512]{1,0:T(8,128)} %copy-done.2) | copy-start | bytes 1572868
  119.0 4.1 %collective-permute-start.23 = (f32[256,128]{1,0:T(8,128)S(1)}, f32[256,128]{1,0:T(8,128)S(1)}, u32[]{:S(2)}, u32[]{:S(2)}) collective-permute-start(f32[256,128]{1,0:T(8,128)S(1)} %get-tuple-element.82), channel_id=1, source_target_pairs={{0,48},{8,56},{16,0},{24,8},{32,16},{40,24},{48,32},{56,40},{64,11... | collective-permute-start | bytes 393224 | tf_op jit(solution)/shard_map/ppermute | solution.py:49
  119.9 5.4 %collective-permute-start.22 = (f32[256,128]{1,0:T(8,128)S(1)}, f32[256,128]{1,0:T(8,128)S(1)}, u32[]{:S(2)}, u32[]{:S(2)}) collective-permute-start(f32[256,128]{1,0:T(8,128)S(1)} %get-tuple-element.83), channel_id=1, source_target_pairs={{0,32},{8,40},{16,48},{24,56},{32,0},{40,8},{48,16},{56,24},{64,96... | collective-permute-start | bytes 393224 | tf_op jit(solution)/shard_map/ppermute | solution.py:49
  121.3 5.4 %collective-permute-start.21 = (f32[256,128]{1,0:T(8,128)S(1)}, f32[256,128]{1,0:T(8,128)S(1)}, u32[]{:S(2)}, u32[]{:S(2)}) collective-permute-start(f32[256,128]{1,0:T(8,128)S(1)} %get-tuple-element.84), channel_id=1, source_target_pairs={{0,16},{8,24},{16,32},{24,40},{32,48},{40,56},{48,0},{56,8},{64,80... | collective-permute-start | bytes 393224 | tf_op jit(solution)/shard_map/ppermute | solution.py:49
  127.5 5.7 %collective-permute-start.24 = (f32[256,512]{1,0:T(8,128)S(1)}, f32[256,512]{1,0:T(8,128)S(1)}, u32[]{:S(2)}, u32[]{:S(2)}) collective-permute-start(f32[256,512]{1,0:T(8,128)S(1)} %get-tuple-element.76), channel_id=1, source_target_pairs={{0,8},{8,0},{16,24},{24,16},{32,40},{40,32},{48,56},{56,48},{64,72... | collective-permute-start | bytes 1572872 | tf_op jit(solution)/shard_map/ppermute | solution.py:41

commit v4 on v3

v4 whole, which is shorter than its diff:
```python
import functools

import jax
import jax.numpy as jnp
from jax import lax
from jax.experimental import pallas as pl
from jax.experimental.pallas import tpu as pltpu
from jax.sharding import PartitionSpec as P

F32 = jnp.float32
BF16 = jnp.bfloat16
Z_SIZE = 4
Y_SIZE = 4
VMEM_BYTES = 56 * 2**20


def dot(a, b, precision=None):
    return jnp.dot(a, b, precision=precision, preferred_element_type=F32)


def dot_transposed(a, b):
    return lax.dot_general(a, b, (((1,), (1,)), ((), ())), preferred_element_type=F32)


def split(value):
    high = value.astype(BF16)
    return high, (value - high.astype(F32)).astype(BF16)


def dot3(a, b):
    high, low = split(a)
    b_high, b_low = split(b)
    count = a.shape[0]
    both = dot(jnp.concatenate([high, low], axis=0), b_high)
    return both[:count] + (both[count:] + dot(high, b_low))


def along_z(value, by):
    pairs = [(v, ((v // 2 + by) % Z_SIZE) * 2 + v % 2) for v in range(2 * Z_SIZE)]
    return lax.ppermute(value, "vec", pairs)


def across_x(value):
    return lax.ppermute(value, "vec", [(v, v ^ 1) for v in range(2 * Z_SIZE)])


def across_core(value):
    return lax.ppermute(value, "row", [(i, i ^ 1) for i in range(lax.axis_size("row"))])


def along_y(value, by):
    def target(i):
        high, y, core = i // (2 * Y_SIZE), (i // 2) % Y_SIZE, i % 2
        return (high * Y_SIZE + (y + by) % Y_SIZE) * 2 + core

    return lax.ppermute(value, "row", [(i, target(i)) for i in range(lax.axis_size("row"))])


def from_next_row(value):
    return lax.ppermute(value, "row", [(i + 1, i) for i in range(lax.axis_size("row") - 1)])


def together(*values):
    return lax.optimization_barrier(values)


def place_of(index):
    vec = lax.axis_index("vec")
    z, x = vec // 2, vec % 2
    dz, dx = index // 2, index % 2
    return lax.rem(z + dz, Z_SIZE) * 2 + lax.rem(x + dx, 2)


def pick_kernel(sources, *refs):
    pieces, out, sems = refs[:-2], refs[-2], refs[-1]
    for (dz, dx), where in sources:

        @pl.when(place_of(2 * dz + dx) == 0)
        def _():
            if len(where) == 1:
                first, second = pieces[where[0]].at[0], pieces[where[0]].at[1, pl.ds(0, 1)]
            else:
                first, second = pieces[where[0]], pieces[where[1]].at[pl.ds(0, 1)]
            copies = [
                pltpu.make_async_copy(first, out.at[pl.ds(0, 2)], sems.at[0]),
                pltpu.make_async_copy(second, out.at[pl.ds(2, 1)], sems.at[1]),
            ]
            for copy in copies:
                copy.start()
            for copy in copies:
                copy.wait()


def pick_first(known):
    arrays, sources = [], []
    for key, held in known.items():
        sources.append((key, tuple(range(len(arrays), len(arrays) + len(held)))))
        arrays += held
    return pl.pallas_call(
        functools.partial(pick_kernel, sources),
        out_shape=jax.ShapeDtypeStruct((3,) + arrays[0].shape[-2:], F32),
        in_specs=[pl.BlockSpec(memory_space=pl.ANY)] * len(arrays),
        out_specs=pl.BlockSpec(memory_space=pltpu.VMEM),
        scratch_shapes=[pltpu.SemaphoreType.DMA((2,))],
        compiler_params=pltpu.CompilerParams(vmem_limit_bytes=VMEM_BYTES),
    )(*arrays)


def build_reflection(packed):
    width = packed.shape[1]
    rows = lax.broadcasted_iota(jnp.int32, (width, width), 0)
    cols = lax.broadcasted_iota(jnp.int32, (width, width), 1)
    top = packed[:width]
    unit = jnp.where(rows == cols, 1.0, jnp.where(rows > cols, top, 0.0))
    factor = jnp.where(rows <= cols, top, 0.0)
    vectors = jnp.concatenate([unit, packed[width:]], axis=0)
    high, low = split(vectors)
    factor_high, factor_low = split(factor)
    both = dot(jnp.concatenate([high, low], axis=0), factor_high)
    weighted_high, weighted_low = split(
        both[: 2 * width] + (both[2 * width :] + dot(high, factor_low))
    )
    both = dot_transposed(jnp.concatenate([weighted_high, weighted_low], axis=0), high)
    update = both[: 2 * width] + (both[2 * width :] + dot_transposed(weighted_high, low))
    rows = lax.broadcasted_iota(jnp.int32, update.shape, 0)
    cols = lax.broadcasted_iota(jnp.int32, update.shape, 1)
    return split(jnp.where(rows == cols, 1.0, 0.0) - update)


def build_kernel(parts, has_input, *refs):
    pieces = refs[: len(refs) - (6 if has_input else 4)]
    outs = refs[-4:-2]
    staged, sems = refs[-2], refs[-1]
    depth = staged.shape[2]
    copies = []
    at = 0
    for index, (source, blocks, group, place) in enumerate(parts):
        size = len(blocks)
        for block in blocks:
            if isinstance(source, tuple):
                usual, late, late_vec = source
                packed = jnp.where(lax.axis_index("vec") == late_vec, pieces[late][block], pieces[usual][block])
            else:
                packed = pieces[source][block]
            high, low = build_reflection(packed)
            staged[at, :depth] = high
            staged[at, depth:] = low
            at += 1
        first = place(lax.axis_index("vec"))
        copy = pltpu.make_async_copy(
            staged.at[pl.ds(at - size, size)], outs[group].at[pl.ds(first, size)], sems.at[index]
        )
        copy.start()
        copies.append(copy)
    for copy in copies:
        copy.wait()


def build(buffers, shapes, pieces, parts):
    depth = pieces[0].shape[-2]
    blocks = sum(len(part[1]) for part in parts)
    has_input = buffers is not None
    any_spec = pl.BlockSpec(memory_space=pl.ANY)
    return pl.pallas_call(
        functools.partial(build_kernel, parts, has_input),
        out_shape=tuple(jax.ShapeDtypeStruct(shape, BF16) for shape in shapes),
        in_specs=[pl.BlockSpec(memory_space=pltpu.VMEM)] * len(pieces) + ([any_spec] * 2 if has_input else []),
        out_specs=(any_spec, any_spec),
        scratch_shapes=[pltpu.VMEM((blocks, 2 * depth, depth), BF16), pltpu.SemaphoreType.DMA((len(parts),))],
        input_output_aliases={len(pieces): 0, len(pieces) + 1: 1} if has_input else {},
        compiler_params=pltpu.CompilerParams(vmem_limit_bytes=VMEM_BYTES),
        cost_estimate=pl.CostEstimate(
            flops=blocks * 300_000_000, bytes_accessed=blocks * depth * depth * 6, transcendentals=0
        ),
    )(*pieces, *(buffers if has_input else ()))


def placed(source, key, groups=(0, 1), whole=True):
    place = lambda vec: 2 * place_of(2 * key[0] + key[1])
    return [(source, [(group, 0), (group, 1)] if whole else [0, 1], group, place) for group in groups]


def apply(reflection, upper, lower):
    depth = reflection.shape[1]
    high, low = split(jnp.concatenate([upper, lower], axis=0))
    both = dot(reflection, high)
    result = both[:depth] + (both[depth:] + dot(reflection[:depth], low))
    return result[: depth // 2], result[depth // 2 :]


def chunks(total, size=256):
    return [(start, min(size, total - start)) for start in range(0, total, size)]


def first_step(reflection, state, lower, between):
    width, total = state.shape
    for start, size in chunks(total):
        cols = slice(start, start + size)
        below = jnp.zeros((width, size), F32) if lower is None else lower[:, cols]
        top, bottom = apply(reflection, state[:, cols], below)
        between[:, cols] = top
        state[:, cols] = bottom


def second_step(reflection, state, between, out):
    for start, size in chunks(state.shape[1]):
        cols = slice(start, start + size)
        top, bottom = apply(reflection, state[:, cols], between[:, cols])
        if out is not None:
            out[:, cols] = top
        state[:, cols] = bottom


def sweep_copies(first_hbm, second_hbm, data_hbm, tail_hbm, first, second, data, sems):
    granules = first.shape[0] // 2
    rows = 0 if data is None else data.shape[1]

    def first_copies(m):
        copies = [pltpu.make_async_copy(first_hbm.at[pl.ds(2 * m, 2)], first.at[pl.ds(2 * m, 2)], sems.at[0, m])]
        if data is not None:
            is_last = isinstance(m, int) and m == granules - 1
            source = tail_hbm if is_last else data_hbm.at[pl.ds(m * rows, rows)]
            copies.append(pltpu.make_async_copy(source, data.at[m], sems.at[1, m]))
        return copies

    def second_copies(m):
        size = 1 if isinstance(m, int) and 2 * m + 1 >= second.shape[0] else 2
        return [pltpu.make_async_copy(second_hbm.at[pl.ds(2 * m, size)], second.at[pl.ds(2 * m, size)], sems.at[2, m])]

    return first_copies, second_copies


def start_all(copies):
    for copy in copies:
        copy.start()


def wait_all(copies):
    for copy in copies:
        copy.wait()


def run_sweep(first, second, data, first_state, second_state, between, result, out, first_copies, second_copies, sems):
    width = first_state.shape[0]
    granules = first.shape[0] // 2
    blocks = second.shape[0] - 1

    def out_copy(block):
        return pltpu.make_async_copy(
            result.at[pl.ds(block * width, width)], out.at[pl.ds(block * width, width)], sems.at[3, block]
        )

    def rows_of(m, odd):
        return None if data is None else data.at[m, pl.ds(odd * width, width)]

    def finished(block):
        start = block * width
        return result.at[pl.ds(start if isinstance(start, int) else pl.multiple_of(start, width), width)]

    def both_steps(m, odd):
        index = 2 * m + odd - 2
        second_step(second[index], second_state, between, finished(index - 1))
        first_step(first[2 * m + odd], first_state, rows_of(m, odd), between)
        out_copy(index - 1).start()

    wait_all(first_copies(1))
    first_step(first[2], first_state, rows_of(1, 0), between)
    both_steps(1, 1)

    @pl.loop(2, granules - 1)
    def _(m):
        wait_all(first_copies(m))
        wait_all(second_copies(m - 1))
        both_steps(m, 0)
        both_steps(m, 1)

    last = granules - 1
    wait_all(first_copies(last))
    wait_all(second_copies(last - 1))
    both_steps(last, 0)
    both_steps(last, 1)
    wait_all(second_copies(last))
    second_step(second[blocks], second_state, between, finished(blocks - 1))
    out_copy(blocks - 1).start()
    for block in range(blocks):
        out_copy(block).wait()


def unit_kernel(
    first_hbm, second_hbm, data_hbm, out, transition, initial,
    first, second, data, first_state, second_state, between, data_between, result, sems,
):
    width = first_state.shape[0]
    first_copies, second_copies = sweep_copies(first_hbm, second_hbm, None, None, first, second, None, sems)
    granules = first.shape[0] // 2
    is_first = lax.axis_index("row") == 0

    @pl.when(is_first)
    def _():
        rows = pltpu.make_async_copy(data_hbm.at[pl.ds(0, 2 * width)], data, sems.at[1, 0])
        copies = first_copies(0) + second_copies(0) + [rows]
        start_all(copies)
        result[...] = jnp.zeros_like(result)
        transition[...] = jnp.zeros_like(transition)
        initial[...] = jnp.zeros_like(initial)
        cleared = pltpu.make_async_copy(result, out, sems.at[3, 0])
        cleared.start()
        wait_all(copies)
        upper, lower = initial.at[pl.ds(0, width)], initial.at[pl.ds(width, width)]
        first_step(first[0], upper, data.at[pl.ds(0, width)], data_between)
        first_step(first[1], upper, data.at[pl.ds(width, width)], data_between)
        second_step(second[0], lower, data_between, None)
        cleared.wait()

    @pl.when(jnp.logical_not(is_first))
    def _():
        for m in range(granules):
            start_all(first_copies(m) + second_copies(m))
        rows = lax.broadcasted_iota(jnp.int32, (width, width), 0)
        cols = lax.broadcasted_iota(jnp.int32, (width, width), 1)
        eye = jnp.where(rows == cols, 1.0, 0.0)
        zeros = jnp.zeros((width, width), F32)
        first_state[...] = eye
        second_state[...] = jnp.concatenate([zeros, eye], axis=1)
        between[...] = jnp.zeros_like(between)
        initial[...] = jnp.zeros_like(initial)
        wait_all(first_copies(0) + second_copies(0))
        run_sweep(
            first, second, None, first_state, second_state, between, result, out, first_copies, second_copies, sems
        )
        transition[:width] = jnp.concatenate([first_state[...], zeros], axis=1)
        transition[width:] = second_state[...]


def data_kernel(
    first_hbm, second_hbm, data_hbm, tail_hbm, initial, out, own_state, sent_state,
    first, second, data, first_state, second_state, between, result, sems,
):
    width = first_state.shape[0]
    first_copies, second_copies = sweep_copies(
        first_hbm, second_hbm, data_hbm, tail_hbm, first, second, data, sems
    )
    for m in range(first.shape[0] // 2):
        start_all(first_copies(m) + second_copies(m))
    first_state[...] = initial[:width]
    second_state[...] = initial[width:]
    wait_all(first_copies(0) + second_copies(0))
    run_sweep(first, second, data, first_state, second_state, between, result, out, first_copies, second_copies, sems)
    half = own_state.shape[1]
    core = lax.rem(lax.axis_index("row"), 2)
    for target, side in ((own_state, core), (sent_state, 1 - core)):
        cols = pl.ds(pl.multiple_of(side * half, half), half)
        target[:width] = first_state[:, cols]
        target[width:] = second_state[:, cols]


ANY = pl.BlockSpec(memory_space=pl.ANY)
VMEM = pl.BlockSpec(memory_space=pltpu.VMEM)
PARAMS = pltpu.CompilerParams(vmem_limit_bytes=VMEM_BYTES)
CORRECT_PARAMS = pltpu.CompilerParams(vmem_limit_bytes=50 * 2**20)
SMALL_PARAMS = pltpu.CompilerParams(vmem_limit_bytes=16 * 2**20)


def estimate(blocks, depth, cols):
    return pl.CostEstimate(
        flops=6 * blocks * depth * depth * cols, bytes_accessed=30 * 2**20, transcendentals=0
    )


def sweep_units(buffers, data):
    first, second = buffers
    depth = first.shape[2]
    width, blocks, cols = depth // 2, second.shape[0] - 1, data.shape[1]
    return pl.pallas_call(
        unit_kernel,
        out_shape=(
            jax.ShapeDtypeStruct((blocks * width, depth), F32),
            jax.ShapeDtypeStruct((depth, depth), F32),
            jax.ShapeDtypeStruct((depth, cols), F32),
        ),
        in_specs=[ANY] * 3,
        out_specs=(ANY, VMEM, VMEM),
        scratch_shapes=[
            pltpu.VMEM(first.shape, BF16),
            pltpu.VMEM(second.shape, BF16),
            pltpu.VMEM((depth, cols), F32),
            pltpu.VMEM((width, width), F32),
            pltpu.VMEM((width, depth), F32),
            pltpu.VMEM((width, depth), F32),
            pltpu.VMEM((width, cols), F32),
            pltpu.VMEM((blocks * width, depth), F32),
            pltpu.SemaphoreType.DMA((4, blocks)),
        ],
        compiler_params=PARAMS,
        cost_estimate=estimate(blocks, depth, 3 * depth),
    )(first, second, data)


def sweep_data(buffers, data, tail, initial):
    first, second = buffers
    depth = first.shape[2]
    width, blocks, cols = depth // 2, second.shape[0] - 1, data.shape[1]
    return pl.pallas_call(
        data_kernel,
        out_shape=(
            jax.ShapeDtypeStruct((blocks * width, cols), F32),
            jax.ShapeDtypeStruct((depth, cols // 2), F32),
            jax.ShapeDtypeStruct((depth, cols // 2), F32),
        ),
        in_specs=[ANY] * 4 + [VMEM],
        out_specs=(ANY, VMEM, VMEM),
        scratch_shapes=[
            pltpu.VMEM(first.shape, BF16),
            pltpu.VMEM(second.shape, BF16),
            pltpu.VMEM((first.shape[0] // 2, depth, cols), F32),
            pltpu.VMEM((width, cols), F32),
            pltpu.VMEM((width, cols), F32),
            pltpu.VMEM((width, cols), F32),
            pltpu.VMEM((blocks * width, cols), F32),
            pltpu.SemaphoreType.DMA((4, blocks)),
        ],
        compiler_params=PARAMS,
        cost_estimate=estimate(blocks, depth, 2 * cols),
    )(first, second, data, tail, initial)


def small(kernel, outs, *args, scratch=()):
    return pl.pallas_call(
        kernel,
        out_shape=tuple(jax.ShapeDtypeStruct(shape, F32) for shape in outs),
        in_specs=[VMEM] * len(args),
        out_specs=tuple(VMEM for _ in outs),
        scratch_shapes=[pltpu.VMEM(shape, F32) for shape in scratch],
        compiler_params=SMALL_PARAMS,
    )(*args)


def position():
    row = lax.axis_index("row")
    return lax.rem(row, 2), lax.rem(row // 2, Y_SIZE)


def chip_at(d):
    return lax.rem(position()[1] + Y_SIZE - d, Y_SIZE)


def lanes(index, size):
    return pl.ds(pl.multiple_of(index * size, size), size)


def by_core(at_first, otherwise):
    return jnp.where(position()[0] == 0, at_first, otherwise)


def chip_transition_kernel(own, received, out):
    out[...] = dot3(by_core(received[...], own[...]), by_core(own[...], received[...]))


def chip_offset_kernel(own_transition, received_transition, own, received, *refs):
    outs, chip = refs[:-1], refs[-1]
    upper = by_core(received_transition[...], own_transition[...])
    chip[...] = dot3(upper, by_core(own[...], received[...])) + by_core(received[...], own[...])
    size = outs[0].shape[1]
    for d, out in enumerate(outs):
        out[...] = chip[:, lanes(chip_at(Y_SIZE - d), size)]


def products_kernel(*refs):
    transitions, ordered, products = refs[:Y_SIZE], refs[Y_SIZE], refs[Y_SIZE + 1]
    for d, transition in enumerate(transitions):
        ordered[chip_at(d)] = transition[...]
    product = ordered[0]
    products[0] = product
    for at in range(1, Y_SIZE - 1):
        product = dot3(ordered[at], product)
        products[at] = product


def chain_kernel(ordered, *refs):
    offsets, partial, total, placed_offsets = refs[:Y_SIZE], refs[-3], refs[-2], refs[-1]
    for d, offset in enumerate(offsets):
        placed_offsets[chip_at(d)] = offset[...]
    state = placed_offsets[0]
    for at in range(1, Y_SIZE):
        partial[at - 1] = state
        state = dot3(ordered[at], state) + placed_offsets[at]
    total[...] = state


def entering_kernel(entering, products, partial, *refs):
    outs, states = refs[:-1], refs[-1]
    states[0] = entering[...]
    for at in range(1, Y_SIZE):
        states[at] = dot3(products[at - 1], entering[...]) + partial[at - 1]
    for d, out in enumerate(outs):
        out[...] = states[chip_at(Y_SIZE - d)]


def core_kernel(own_transition, received_transition, own, received, *refs):
    arrived, kept, given, chip = refs[:Y_SIZE], refs[-3], refs[-2], refs[-1]
    size = arrived[0].shape[1]
    for d, part in enumerate(arrived):
        chip[:, lanes(chip_at(d), size)] = part[...]
    lower = by_core(own_transition[...], received_transition[...])
    into_second = dot3(lower, chip[...]) + by_core(own[...], received[...])
    kept[...] = by_core(chip[...], into_second)
    given[...] = by_core(into_second, chip[...])


def correct_kernel(tile, rows_hbm, response_hbm, kept, taken, out_hbm, rows, response, incoming_high, incoming_low, sems):
    count = rows.shape[0] // tile

    def span(index):
        return pl.ds(index * tile, tile)

    arrivals = [
        (
            pltpu.make_async_copy(response_hbm.at[span(k)], response.at[span(k)], sems.at[0, k]),
            pltpu.make_async_copy(rows_hbm.at[span(k)], rows.at[span(k)], sems.at[1, k]),
        )
        for k in range(count)
    ]
    for pair in arrivals:
        for copy in pair:
            copy.start()
    core = position()[0]
    for part, side in ((kept, core), (taken, 1 - core)):
        high, low = split(part[...])
        incoming_high[:, lanes(side, part.shape[1])] = high
        incoming_low[:, lanes(side, part.shape[1])] = low
    departures = []
    for k in range(count):
        for copy in arrivals[k]:
            copy.wait()
        high, low = split(response[k * tile : (k + 1) * tile])
        both = jnp.concatenate([high, low], axis=0)
        for start, size in chunks(rows.shape[1], 512):
            at = (slice(k * tile, (k + 1) * tile), slice(start, start + size))
            sums = dot(both, incoming_high[:, at[1]])
            rows[at] = rows[at] + (sums[:tile] + (sums[tile:] + dot(high, incoming_low[:, at[1]])))
        copy = pltpu.make_async_copy(rows.at[span(k)], out_hbm.at[span(k)], sems.at[2, k])
        copy.start()
        departures.append(copy)
    for copy in departures:
        copy.wait()


def correct(rows, response, kept, taken, tile=256):
    incoming = (response.shape[1], rows.shape[1])
    return pl.pallas_call(
        functools.partial(correct_kernel, tile),
        out_shape=jax.ShapeDtypeStruct(rows.shape, F32),
        in_specs=[ANY, ANY, VMEM, VMEM],
        out_specs=ANY,
        scratch_shapes=[
            pltpu.VMEM(rows.shape, F32),
            pltpu.VMEM(response.shape, F32),
            pltpu.VMEM(incoming, BF16),
            pltpu.VMEM(incoming, BF16),
            pltpu.SemaphoreType.DMA((3, rows.shape[0] // tile)),
        ],
        compiler_params=CORRECT_PARAMS,
    )(rows, response, kept, taken)


def local(eigvecs, wy_v, wy_t):
    width = wy_t.shape[-1]
    rows_dev, cols_dev = eigvecs.shape
    own_blocks = rows_dev // width
    below = lax.broadcasted_iota(jnp.int32, (width, width), 0) > lax.broadcasted_iota(
        jnp.int32, (width, width), 1
    )
    own = jnp.concatenate([jnp.where(below, wy_v[:, :, :width], wy_t), wy_v[:, :, width:]], axis=2)
    tail = from_next_row(eigvecs[: 2 * width])
    depth = 2 * width
    shapes = ((own_blocks + 2, 2 * depth, depth), (own_blocks + 1, 2 * depth, depth))

    f30, s30 = along_z(own[0], 1), along_z(own[1], 1)
    p01, p10 = across_x(own), along_z(own, -1)
    buffers = build(None, shapes, [own], placed(0, (0, 0)))
    f30, *buffers = together(f30, *buffers)
    f31, f20, p11 = across_x(f30), along_z(f30, 1), along_z(p01, -1)
    s31, s20 = across_x(s30), along_z(s30, 1)
    buffers = build(
        buffers,
        shapes,
        [p01, p10, f30, s30],
        placed(0, (0, 1)) + placed(1, (1, 0)) + placed(2, (3, 0), (0,), False) + placed(3, (3, 0), (1,), False),
    )
    f20, s31, *buffers = together(f20, s31, *buffers)
    f21, s21 = across_x(f20), along_z(s31, 1)
    picked = pick_first(
        {
            (0, 0): [own],
            (0, 1): [p01],
            (1, 0): [p10],
            (1, 1): [p11],
            (3, 0): [f30, s30],
            (3, 1): [f31, s31],
            (2, 0): [f20, s20],
        }
    )
    vecs, rows = lax.axis_size("vec"), lax.axis_size("row")
    late = 5
    extras = [
        lax.ppermute(
            picked,
            ("row", "vec"),
            [((i + 1) * vecs + v, i * vecs + v) for i in range(rows - 1) for v in range(vecs) if v != late],
        ),
        lax.ppermute(
            picked, ("row", "vec"), [((i + 1) * vecs + late - 1, i * vecs + late) for i in range(rows - 1)]
        ),
    ]
    buffers = build(
        buffers,
        shapes,
        [p11, f31, s31, f20, s20],
        placed(0, (1, 1))
        + placed(1, (3, 1), (0,), False)
        + placed(2, (3, 1), (1,), False)
        + placed(3, (2, 0), (0,), False)
        + placed(4, (2, 0), (1,), False),
    )
    buffers = build(
        buffers,
        shapes,
        [f21, s21, *extras],
        placed(0, (2, 1), (0,), False)
        + placed(1, (2, 1), (1,), False)
        + [((2, 3, late), [0, 1], 0, lambda vec: own_blocks), ((2, 3, late), [2], 1, lambda vec: own_blocks)],
    )

    half, quarter = cols_dev // 2, cols_dev // (2 * Y_SIZE)
    response, transition, initial = sweep_units(buffers, eigvecs)
    received_transition = across_core(transition)
    (chip_transition,) = small(chip_transition_kernel, [(depth, depth)], transition, received_transition)
    chip_transition, *buffers = together(chip_transition, *buffers)
    transitions = [chip_transition] + [along_y(chip_transition, d) for d in range(1, Y_SIZE)]
    swept, own_offset, sent_offset = sweep_data(buffers, eigvecs, tail, initial)
    sent_offset, *transitions = together(sent_offset, *transitions)
    received_offset = across_core(sent_offset)
    cores = (transition, received_transition, own_offset, received_offset)
    offsets = small(chip_offset_kernel, [(depth, quarter)] * Y_SIZE, *cores, scratch=[(depth, half)])
    offsets = [offsets[0]] + [along_y(offsets[d], d) for d in range(1, Y_SIZE)]
    ordered, products = small(
        products_kernel, [(Y_SIZE, depth, depth), (Y_SIZE - 1, depth, depth)], *transitions
    )
    partial, total = small(
        chain_kernel,
        [(Y_SIZE - 1, depth, quarter), (depth, quarter)],
        ordered,
        *offsets,
        scratch=[(Y_SIZE, depth, quarter)],
    )
    entering = lax.ppermute(total, "row", [(i, i + rows // 2) for i in range(rows // 2)])
    back = small(
        entering_kernel,
        [(depth, quarter)] * Y_SIZE,
        entering,
        products,
        partial,
        scratch=[(Y_SIZE, depth, quarter)],
    )
    arrived = [back[0]] + [along_y(back[d], d) for d in range(1, Y_SIZE)]
    kept, given = small(core_kernel, [(depth, half)] * 2, *cores, *arrived, scratch=[(depth, half)])
    return correct(swept, response, kept, across_core(given))


def solution(mesh):
    placed_in = (
        P("row", "vec"),
        P(None, ("row", "vec"), None, None),
        P(None, ("row", "vec"), None, None),
    )
    return jax.shard_map(
        local, mesh=mesh, in_specs=placed_in, out_specs=P("row", "vec"), check_vma=False
    )
```

time: 146 us -> 153 us (1.048)
  starting transfers between devices: 38.7 us -> 50.2 us
  matrix products: 6.36 us -> 0 us
  Pallas kernels: 55.8 us -> 58.9 us
  other arithmetic: 3.5 us -> 1.25 us
    ppermute x3, starting transfers between devices: 7.15 us -> 17.7 us  [across_core(): lax.ppermute(value, 'row', [(i, i ^ 1) for i in range(lax.axis_size('row'...]
    ppermute x3 -> x4, waiting for transfers between devices: 5.2 us -> 14 us  [across_x(): return lax.ppermute(value, 'vec', [(v, v ^ 1) for v in range(2 * Z_SIZE)])]
    dot_general x9 -> x0, matrix products: 6.36 us -> none  [dot(): return jnp.dot(a, b, precision=precision, preferred_element_type=F32)]
    pallas_call x3 -> x9, Pallas kernels: 30.2 us -> 35.6 us  [the longest x1 20.4 us: sweep_data(): pl.pallas_call(data_kernel, out_shape=(jax.ShapeDtypeStruct((blocks * wid...]
    ppermute x9, waiting for transfers between devices: 11.1 us -> 6.58 us  [along_y(): lax.ppermute(value, 'row', [(i, target(i)) for i in range(lax.axis_size('...]
    ppermute x6 -> x7, waiting for transfers between devices: 6.36 us -> 2.6 us  [along_z(): return lax.ppermute(value, 'vec', pairs)]
    unnamed x34 -> x40, local copies, waits for them, and re-layouts: 2.09 us -> 5.68 us
    ppermute x9, starting transfers between devices: 9.54 us -> 12 us  [along_y(): lax.ppermute(value, 'row', [(i, target(i)) for i in range(lax.axis_size('...]
  transfers between devices with their start and end apart: 25 -> 27, of which waited for: 13 -> 13; matrix products, arithmetic and copies ran while one was open for 3% -> 1% of each run, Pallas kernels for 32% -> 31%
where the time goes in v4:
time: 153 us; the launch traced here: 152 us
  Pallas kernels  58.9 us (38%)
  starting transfers between devices  50.2 us (33%)
  waiting for transfers between devices  34 us (22%)
  local copies, waits for them, and re-layouts  7.01 us (5%)
    pallas_call x1, Pallas kernels, sweep_data(): pl.pallas_call(data_kernel, out_shape=(jax.ShapeDtypeStruct((blocks * wid...  20.4 us
    ppermute x3, starting transfers between devices, across_core(): lax.ppermute(value, 'row', [(i, i ^ 1) for i in range(lax.axis_size('row'...  17.7 us
    pallas_call x4, Pallas kernels, build(): pl.pallas_call(functools.partial(build_kernel, parts, has_input), out_sha...  16.3 us
    ppermute x4, waiting for transfers between devices, across_x(): return lax.ppermute(value, 'vec', [(v, v ^ 1) for v in range(2 * Z_SIZE)])  14 us
    ppermute x9, starting transfers between devices, along_y(): lax.ppermute(value, 'row', [(i, target(i)) for i in range(lax.axis_size('...  12 us
    pallas_call x1, Pallas kernels, sweep_units(): pl.pallas_call(unit_kernel, out_shape=(jax.ShapeDtypeStruct((blocks * wid...  9.89 us
    ppermute x7, starting transfers between devices, along_z(): return lax.ppermute(value, 'vec', pairs)  7.75 us
    pallas_call x1, Pallas kernels, correct(): pl.pallas_call(functools.partial(correct_kernel, tile), out_shape=jax.Sha...  7.05 us
  transfers between devices with their start and end apart: 27, of which 13 were waited for; matrix products, arithmetic and copies ran while one was open for 1% of the time, Pallas kernels for 31%

profile of v4, /device:TPU:5, one launch (start us, length us, event | category | flops | bytes accessed | tf_op | source)
XLA Modules:
  0.0 151.9 jit_solution(5174691101305551202)
XLA Ops:
  0.0 1.2 fusion.4
  1.2 1.0 collective-permute-start.4
  2.2 3.8 %collective-permute-start.5 = (f32[2,2,256,128]{3,2,1,0:T(8,128)S(1)}, f32[2,2,256,128]{3,2,1,0:T(8,128)S(1)}, u32[]{:S(2)}, u32[]{:S(2)}) collective-permute-start(f32[2,2,256,128]{3,2,1,0:T(8,128)S(1)} %pad_maximum_fusion.refs_0_), channel_id=1, source_target_pairs={{0,6},{1,7},{2,0},{3,1},{4,2},{5,3},{6,4},{7,5},{8,14},{9,15},{10,... | collective-permute-start | bytes 1572872 | tf_op jit(solution)/shard_map/ppermute | solution.py:40
  6.0 0.1 collective-permute-start
  6.1 0.1 collective-permute-start.2
  6.2 7.9 %collective-permute-done.4.refs_0_.refs_1_ = f32[2,2,256,128]{3,2,1,0:T(8,128)S(1)} collective-permute-done((f32[2,2,256,128]{3,2,1,0:T(8,128)S(1)}, f32[2,2,256,128]{3,2,1,0:T(8,128)S(1)}, u32[]{:S(2)}, u32[]{:S(2)}) %collective-permute-start.4) | collective-permute-done | bytes 524320 | tf_op jit(solution)/shard_map/ppermute | solution.py:44
  14.1 3.8 %collective-permute-start.8 = (f32[2,2,256,128]{3,2,1,0:T(8,128)S(1)}, f32[2,2,256,128]{3,2,1,0:T(8,128)S(1)}, u32[]{:S(2)}, u32[]{:S(2)}) collective-permute-start(f32[2,2,256,128]{3,2,1,0:T(8,128)S(1)} %collective-permute-done.4.refs_0_.refs_1_), channel_id=1, source_target_pairs={{0,6},{1,7},{2,0},{3,1},{4,2},{5,3},{6,4},{7,5},{8,14},{9,15},{10,... | collective-permute-start | bytes 1572872 | tf_op jit(solution)/shard_map/ppermute | solution.py:40
  17.9 2.9 %shard_map.37 = (bf16[18,512,256]{2,1,0:T(8,128)(2,1)}, bf16[17,512,256]{2,1,0:T(8,128)(2,1)}) custom-call(f32[2,2,256,128]{3,2,1,0:T(8,128)} %copy-done.5), custom_call_target="tpu_custom_call" | custom-call | flops 1200000000 | bytes 1572864 | tf_op jit(solution)/shard_map/pallas_call | solution.py:164
  20.8 1.0 collective-permute-start.9
  21.8 0.1 collective-permute-start.10
  21.9 0.6 collective-permute-start.3
  22.5 0.1 copy-done.8
  22.7 4.8 %shard_map.38 = (bf16[18,512,256]{2,1,0:T(8,128)(2,1)}, bf16[17,512,256]{2,1,0:T(8,128)(2,1)}) custom-call(f32[2,2,256,128]{3,2,1,0:T(8,128)} %copy-done.7, f32[2,2,256,128]{3,2,1,0:T(8,128)} %copy-done.8, f32[2,256,128]{2,1,0:T(8,128)} %copy-done.13, f32[2,256,128]{2,1,0:T(8,128)} %copy-done.14, ...), custom_call_target="tpu_custom_call", output_to_operand_aliasing={{0}: (4, {}), {1}: (5, {})} | custom-call | flops 3600000000 | bytes 4718592 | tf_op jit(solution)/shard_map/pallas_call | solution.py:164
  27.5 5.0 %collective-permute-done.3.refs_7_.refs_2_ = f32[2,256,128]{2,1,0:T(8,128)S(1)} collective-permute-done((f32[2,256,128]{2,1,0:T(8,128)S(1)}, f32[2,256,128]{2,1,0:T(8,128)S(1)}, u32[]{:S(2)}, u32[]{:S(2)}) %collective-permute-start.3) | collective-permute-done | bytes 262176 | tf_op jit(solution)/shard_map/ppermute | solution.py:44
  32.5 1.8 %collective-permute-done.10.refs_9_.refs_4_ = f32[2,256,128]{2,1,0:T(8,128)S(1)} collective-permute-done((f32[2,256,128]{2,1,0:T(8,128)S(1)}, f32[2,256,128]{2,1,0:T(8,128)S(1)}, u32[]{:S(2)}, u32[]{:S(2)}) %collective-permute-start.10) | collective-permute-done | bytes 262176 | tf_op jit(solution)/shard_map/ppermute | solution.py:40
  34.3 0.7 copy-done.15
  35.0 0.1 copy-done.11
  35.1 0.8 copy-done.6
  35.9 1.8 %shard_map.39 = f32[3,256,128]{2,1,0:T(8,128)} custom-call(f32[2,2,256,128]{3,2,1,0:T(8,128)} %copy-done.5, f32[2,2,256,128]{3,2,1,0:T(8,128)} %copy-done.7, f32[2,2,256,128]{3,2,1,0:T(8,128)} %copy-done.8, f32[2,2,256,128]{3,2,1,0:T(8,128)} %copy-done.6, f32[2,256,128]{2,1,0:T(8,128)} %copy-done.13, f32[2,256,128]{2,1,0:T(8,128)} %copy-done.14, ...), custom_call_target="tpu_custom_call" | custom-call | tf_op jit(solution)/shard_map/pallas_call | solution.py:99
  37.7 0.7 collective-permute-start.12
  38.4 4.9 %collective-permute-start.11 = (f32[3,256,128]{2,1,0:T(8,128)}, f32[3,256,128]{2,1,0:T(8,128)S(1)}, u32[]{:S(2)}, u32[]{:S(2)}) collective-permute-start(f32[3,256,128]{2,1,0:T(8,128)} %shard_map.39), channel_id=1, source_target_pairs={{8,0},{9,1},{10,2},{11,3},{12,4},{14,6},{15,7},{16,8},{17,9},{18,1... | collective-permute-start | bytes 1179656 | tf_op jit(solution)/shard_map/ppermute | solution.py:606
  43.3 1.3 slice.19
  44.6 2.2 %collective-permute-start.14 = (f32[256,1024]{1,0:T(8,128)S(1)}, f32[256,1024]{1,0:T(8,128)S(1)}, u32[]{:S(2)}, u32[]{:S(2)}) collective-permute-start(f32[256,1024]{1,0:T(8,128)S(1)} %slice.19), channel_id=1, source_target_pairs={{8,0},{16,8},{24,16},{32,24},{40,32},{48,40},{56,48},{64,56},{72,6... | collective-permute-start | bytes 3145736 | tf_op jit(solution)/shard_map/ppermute | solution.py:60
  46.9 0.9 collective-permute-start.6
  47.8 4.8 %shard_map.40 = (bf16[18,512,256]{2,1,0:T(8,128)(2,1)}, bf16[17,512,256]{2,1,0:T(8,128)(2,1)}) custom-call(f32[2,2,256,128]{3,2,1,0:T(8,128)} %copy-done.6, f32[2,256,128]{2,1,0:T(8,128)} %copy-done.11, f32[2,256,128]{2,1,0:T(8,128)} %copy-done.16, f32[2,256,128]{2,1,0:T(8,128)} %copy-done.12, ...), custom_call_target="tpu_custom_call", output_to_operand_aliasing={{0}: (5, {}), {1}: (6, {})} | custom-call | flops 3600000000 | bytes 4718592 | tf_op jit(solution)/shard_map/pallas_call | solution.py:164
  52.6 1.1 collective-permute-done.6.refs_0_
  53.7 0.8 collective-permute-done.7.refs_1_
  54.5 0.7 copy-done.18
  55.2 0.1 copy-done.9
  55.3 0.2 copy-done.10
  55.5 3.8 %shard_map.41 = (bf16[18,512,256]{2,1,0:T(8,128)(2,1)}, bf16[17,512,256]{2,1,0:T(8,128)(2,1)}) custom-call(f32[2,256,128]{2,1,0:T(8,128)} %copy-done.17, f32[2,256,128]{2,1,0:T(8,128)} %copy-done.18, f32[3,256,128]{2,1,0:T(8,128)} %copy-done.10, f32[3,256,128]{2,1,0:T(8,128)} %copy-done.9, ...), custom_call_target="tpu_custom_call", output_to_operand_aliasing={{0}: (4, {}), {1}: (5, {})} | custom-call | flops 2100000000 | bytes 2752512 | tf_op jit(solution)/shard_map/pallas_call | solution.py:164
  59.3 9.9 %shard_map.42 = (f32[2048,256]{1,0:T(8,128)}, f32[256,256]{1,0:T(8,128)}, f32[256,1024]{1,0:T(8,128)}) custom-call(bf16[18,512,256]{2,1,0:T(8,128)(2,1)} %get-tuple-element.64.first_hbm, bf16[17,512,256]{2,1,0:T(8,128)(2,1)} %get-tuple-element.65.second_hbm, f32[2048,1024]{1,0:T(8,128)} %data_hbm.3), custom_call_target="tpu_custom_call" | custom-call | flops 4831838208 | bytes 31457280 | tf_op jit(solution)/shard_map/pallas_call | solution.py:374
  69.2 13.2 %collective-permute-start.13 = (f32[256,256]{1,0:T(8,128)}, f32[256,256]{1,0:T(8,128)S(1)}, u32[]{:S(2)}, u32[]{:S(2)}) collective-permute-start(f32[256,256]{1,0:T(8,128)} %get-tuple-element.63.own.own_transition), channel_id=1, source_target_pairs={{0,8},{8,0},{16,24},{24,16},{32,40},{40,32},{48,56},{56,48},{64,72... | collective-permute-start | bytes 786440 | tf_op jit(solution)/shard_map/ppermute | solution.py:48
  82.4 1.4 collective-permute-done.13.received.received_transition
  83.8 0.9 copy-done
  84.7 0.3 shard_map.43.refs_0_
  85.0 0.1 collective-permute-start.17
  85.1 0.1 collective-permute-start.16
  85.2 1.4 collective-permute-start.15
  86.6 1.0 copy-done.19
  87.6 20.4 %shard_map.44 = (f32[2048,1024]{1,0:T(8,128)}, f32[256,512]{1,0:T(8,128)}, f32[256,512]{1,0:T(8,128)}) custom-call(bf16[18,512,256]{2,1,0:T(8,128)(2,1)} %get-tuple-element.64.first_hbm, bf16[17,512,256]{2,1,0:T(8,128)(2,1)} %get-tuple-element.65.second_hbm, f32[2048,1024]{1,0:T(8,128)} %data_hbm.3, f32[256,1024]{1,0:T(8,128)} %copy-done.19, ...), custom_call_target="tpu_custom_call" | custom-call | flops 12884901888 | bytes 31457280 | tf_op jit(solution)/shard_map/pallas_call | solution.py:403
  108.0 1.0 collective-permute-start.18
  109.0 1.7 %collective-permute-done.18.received = f32[256,512]{1,0:T(8,128)S(1)} collective-permute-done((f32[256,512]{1,0:T(8,128)}, f32[256,512]{1,0:T(8,128)S(1)}, u32[]{:S(2)}, u32[]{:S(2)}) %collective-permute-start.18) | collective-permute-done | bytes 524320 | tf_op jit(solution)/shard_map/ppermute | solution.py:48
  110.8 1.0 copy-done.3
  111.8 0.5 shard_map.46
  112.4 1.3 collective-permute-start.19
  113.7 2.7 %collective-permute-start.20 = (f32[256,128]{1,0:T(8,128)S(1)}, f32[256,128]{1,0:T(8,128)S(1)}, u32[]{:S(2)}, u32[]{:S(2)}) collective-permute-start(f32[256,128]{1,0:T(8,128)S(1)} %get-tuple-element.80), channel_id=1, source_target_pairs={{0,32},{8,40},{16,48},{24,56},{32,0},{40,8},{48,16},{56,24},{64,96... | collective-permute-start | bytes 393224 | tf_op jit(solution)/shard_map/ppermute | solution.py:56
  116.4 2.0 %collective-permute-start.21 = (f32[256,128]{1,0:T(8,128)S(1)}, f32[256,128]{1,0:T(8,128)S(1)}, u32[]{:S(2)}, u32[]{:S(2)}) collective-permute-start(f32[256,128]{1,0:T(8,128)S(1)} %get-tuple-element.81), channel_id=1, source_target_pairs={{0,48},{8,56},{16,0},{24,8},{32,16},{40,24},{48,32},{56,40},{64,11... | collective-permute-start | bytes 393224 | tf_op jit(solution)/shard_map/ppermute | solution.py:56
  118.4 0.8 shard_map.45
  119.2 3.5 %collective-permute-done.20.refs_2_ = f32[256,128]{1,0:T(8,128)S(1)} collective-permute-done((f32[256,128]{1,0:T(8,128)S(1)}, f32[256,128]{1,0:T(8,128)S(1)}, u32[]{:S(2)}, u32[]{:S(2)}) %collective-permute-start.20) | collective-permute-done | bytes 131104 | tf_op jit(solution)/shard_map/ppermute | solution.py:56
  122.7 0.9 shard_map.47
  123.6 1.3 collective-permute-start.22
  124.9 6.2 %collective-permute-done.22.entering = f32[256,128]{1,0:T(8,128)S(1)} collective-permute-done((f32[256,128]{1,0:T(8,128)S(1)}, f32[256,128]{1,0:T(8,128)S(1)}, u32[]{:S(2)}, u32[]{:S(2)}) %collective-permute-start.22) | collective-permute-done | bytes 131104 | tf_op jit(solution)/shard_map/ppermute | solution.py:656
  131.1 0.5 shard_map.48
  131.7 0.1 collective-permute-start.23
  131.7 2.8 %collective-permute-start.24 = (f32[256,128]{1,0:T(8,128)S(1)}, f32[256,128]{1,0:T(8,128)S(1)}, u32[]{:S(2)}, u32[]{:S(2)}) collective-permute-start(f32[256,128]{1,0:T(8,128)S(1)} %get-tuple-element.87), channel_id=1, source_target_pairs={{0,32},{8,40},{16,48},{24,56},{32,0},{40,8},{48,16},{56,24},{64,96... | collective-permute-start | bytes 393224 | tf_op jit(solution)/shard_map/ppermute | solution.py:56
  134.5 1.7 %collective-permute-start.25 = (f32[256,128]{1,0:T(8,128)S(1)}, f32[256,128]{1,0:T(8,128)S(1)}, u32[]{:S(2)}, u32[]{:S(2)}) collective-permute-start(f32[256,128]{1,0:T(8,128)S(1)} %get-tuple-element.88), channel_id=1, source_target_pairs={{0,48},{8,56},{16,0},{24,8},{32,16},{40,24},{48,32},{56,40},{64,11... | collective-permute-start | bytes 393224 | tf_op jit(solution)/shard_map/ppermute | solution.py:56
  136.2 0.6 collective-permute-done.23.refs_1_
  136.8 1.6 %collective-permute-done.24.refs_2_ = f32[256,128]{1,0:T(8,128)S(1)} collective-permute-done((f32[256,128]{1,0:T(8,128)S(1)}, f32[256,128]{1,0:T(8,128)S(1)}, u32[]{:S(2)}, u32[]{:S(2)}) %collective-permute-start.24) | collective-permute-done | bytes 131104 | tf_op jit(solution)/shard_map/ppermute | solution.py:56
  138.3 0.9 collective-permute-done.25.refs_3_
  139.3 0.5 shard_map.49
  139.8 3.4 %collective-permute-start.26 = (f32[256,512]{1,0:T(8,128)S(1)}, f32[256,512]{1,0:T(8,128)S(1)}, u32[]{:S(2)}, u32[]{:S(2)}) collective-permute-start(f32[256,512]{1,0:T(8,128)S(1)} %get-tuple-element.90), channel_id=1, source_target_pairs={{0,8},{8,0},{16,24},{24,16},{32,40},{40,32},{48,56},{56,48},{64,72... | collective-permute-start | bytes 1572872 | tf_op jit(solution)/shard_map/ppermute | solution.py:48
  143.2 1.5 %collective-permute-done.26.taken = f32[256,512]{1,0:T(8,128)S(1)} collective-permute-done((f32[256,512]{1,0:T(8,128)S(1)}, f32[256,512]{1,0:T(8,128)S(1)}, u32[]{:S(2)}, u32[]{:S(2)}) %collective-permute-start.26) | collective-permute-done | bytes 524320 | tf_op jit(solution)/shard_map/ppermute | solution.py:48
  144.7 7.1 %shard_map.50 = f32[2048,1024]{1,0:T(8,128)} custom-call(f32[2048,1024]{1,0:T(8,128)} %get-tuple-element.67.rows_hbm, f32[2048,256]{1,0:T(8,128)S(1)} %copy-done.2, f32[256,512]{1,0:T(8,128)S(1)} %get-tuple-element.89.kept, f32[256,512]{1,0:T(8,128)S(1)} %collective-permute-done.26.taken), custom_call_target="tpu_custom_call" | custom-call | tf_op jit(solution)/shard_map/pallas_call | solution.py:550
  (49 shorter events, 0.2 us)
Async XLA Ops:
  1.2 16.6 %copy-start.5 = (f32[2,2,256,128]{3,2,1,0:T(8,128)}, f32[2,2,256,128]{3,2,1,0:T(8,128)S(1)}, u32[]{:S(2)}) copy-start(f32[2,2,256,128]{3,2,1,0:T(8,128)S(1)} %pad_maximum_fusion.refs_0_) | copy-start | bytes 1572868
  1.2 12.9 %collective-permute-start.4 = (f32[2,2,256,128]{3,2,1,0:T(8,128)S(1)}, f32[2,2,256,128]{3,2,1,0:T(8,128)S(1)}, u32[]{:S(2)}, u32[]{:S(2)}) collective-permute-start(f32[2,2,256,128]{3,2,1,0:T(8,128)S(1)} %pad_maximum_fusion.refs_0_), channel_id=1, source_target_pairs={{0,1},{1,0},{2,3},{3,2},{4,5},{5,4},{6,7},{7,6},{8,9},{9,8},{10,11... | collective-permute-start | bytes 1572872 | tf_op jit(solution)/shard_map/ppermute | solution.py:44
  2.2 19.7 %collective-permute-start.5 = (f32[2,2,256,128]{3,2,1,0:T(8,128)S(1)}, f32[2,2,256,128]{3,2,1,0:T(8,128)S(1)}, u32[]{:S(2)}, u32[]{:S(2)}) collective-permute-start(f32[2,2,256,128]{3,2,1,0:T(8,128)S(1)} %pad_maximum_fusion.refs_0_), channel_id=1, source_target_pairs={{0,6},{1,7},{2,0},{3,1},{4,2},{5,3},{6,4},{7,5},{8,14},{9,15},{10,... | collective-permute-start | bytes 1572872 | tf_op jit(solution)/shard_map/ppermute | solution.py:40
  6.0 14.7 %collective-permute-start = (f32[2,256,128]{2,1,0:T(8,128)S(1)}, f32[2,256,128]{2,1,0:T(8,128)S(1)}, u32[]{:S(2)}, u32[]{:S(2)}) collective-permute-start(f32[2,256,128]{2,1,0:T(8,128)S(1)} %get-tuple-element.92), channel_id=1, source_target_pairs={{0,2},{1,3},{2,4},{3,5},{4,6},{5,7},{6,0},{7,1},{8,10},{9,11},{10,... | collective-permute-start | bytes 786440 | tf_op jit(solution)/shard_map/ppermute | solution.py:40
  6.1 15.7 %collective-permute-start.2 = (f32[2,256,128]{2,1,0:T(8,128)S(1)}, f32[2,256,128]{2,1,0:T(8,128)S(1)}, u32[]{:S(2)}, u32[]{:S(2)}) collective-permute-start(f32[2,256,128]{2,1,0:T(8,128)S(1)} %get-tuple-element.91), channel_id=1, source_target_pairs={{0,2},{1,3},{2,4},{3,5},{4,6},{5,7},{6,0},{7,1},{8,10},{9,11},{10,... | collective-permute-start | bytes 786440 | tf_op jit(solution)/shard_map/ppermute | solution.py:40
  14.1 8.4 %copy-start.7 = (f32[2,2,256,128]{3,2,1,0:T(8,128)}, f32[2,2,256,128]{3,2,1,0:T(8,128)S(1)}, u32[]{:S(2)}) copy-start(f32[2,2,256,128]{3,2,1,0:T(8,128)S(1)} %collective-permute-done.4.refs_0_.refs_1_) | copy-start | bytes 1572868
  14.1 20.2 %collective-permute-start.8 = (f32[2,2,256,128]{3,2,1,0:T(8,128)S(1)}, f32[2,2,256,128]{3,2,1,0:T(8,128)S(1)}, u32[]{:S(2)}, u32[]{:S(2)}) collective-permute-start(f32[2,2,256,128]{3,2,1,0:T(8,128)S(1)} %collective-permute-done.4.refs_0_.refs_1_), channel_id=1, source_target_pairs={{0,6},{1,7},{2,0},{3,1},{4,2},{5,3},{6,4},{7,5},{8,14},{9,15},{10,... | collective-permute-start | bytes 1572872 | tf_op jit(solution)/shard_map/ppermute | solution.py:40
  20.8 1.8 %copy-start.13 = (f32[2,256,128]{2,1,0:T(8,128)}, f32[2,256,128]{2,1,0:T(8,128)S(1)}, u32[]{:S(2)}) copy-start(f32[2,256,128]{2,1,0:T(8,128)S(1)} %collective-permute-done.refs_2_.refs_4_) | copy-start | bytes 786436
  20.8 13.5 %collective-permute-start.9 = (f32[2,256,128]{2,1,0:T(8,128)S(1)}, f32[2,256,128]{2,1,0:T(8,128)S(1)}, u32[]{:S(2)}, u32[]{:S(2)}) collective-permute-start(f32[2,256,128]{2,1,0:T(8,128)S(1)} %collective-permute-done.refs_2_.refs_4_), channel_id=1, source_target_pairs={{0,1},{1,0},{2,3},{3,2},{4,5},{5,4},{6,7},{7,6},{8,9},{9,8},{10,11... | collective-permute-start | bytes 786440 | tf_op jit(solution)/shard_map/ppermute | solution.py:44
  21.8 10.7 %collective-permute-start.1 = (f32[2,256,128]{2,1,0:T(8,128)S(1)}, f32[2,256,128]{2,1,0:T(8,128)S(1)}, u32[]{:S(2)}, u32[]{:S(2)}) collective-permute-start(f32[2,256,128]{2,1,0:T(8,128)S(1)} %collective-permute-done.refs_2_.refs_4_), channel_id=1, source_target_pairs={{0,2},{1,3},{2,4},{3,5},{4,6},{5,7},{6,0},{7,1},{8,10},{9,11},{10,... | collective-permute-start | bytes 786440 | tf_op jit(solution)/shard_map/ppermute | solution.py:40
  21.8 0.7 copy-start.14
  21.8 12.5 %collective-permute-start.10 = (f32[2,256,128]{2,1,0:T(8,128)S(1)}, f32[2,256,128]{2,1,0:T(8,128)S(1)}, u32[]{:S(2)}, u32[]{:S(2)}) collective-permute-start(f32[2,256,128]{2,1,0:T(8,128)S(1)} %collective-permute-done.2.refs_3_.refs_5_), channel_id=1, source_target_pairs={{0,2},{1,3},{2,4},{3,5},{4,6},{5,7},{6,0},{7,1},{8,10},{9,11},{10,... | collective-permute-start | bytes 786440 | tf_op jit(solution)/shard_map/ppermute | solution.py:40
  21.9 0.8 copy-start.8
  21.9 10.6 %collective-permute-start.3 = (f32[2,256,128]{2,1,0:T(8,128)S(1)}, f32[2,256,128]{2,1,0:T(8,128)S(1)}, u32[]{:S(2)}, u32[]{:S(2)}) collective-permute-start(f32[2,256,128]{2,1,0:T(8,128)S(1)} %collective-permute-done.2.refs_3_.refs_5_), channel_id=1, source_target_pairs={{0,1},{1,0},{2,3},{3,2},{4,5},{5,4},{6,7},{7,6},{8,9},{9,8},{10,11... | collective-permute-start | bytes 786440 | tf_op jit(solution)/shard_map/ppermute | solution.py:44
  32.5 1.9 %copy-start.16 = (f32[2,256,128]{2,1,0:T(8,128)}, f32[2,256,128]{2,1,0:T(8,128)S(1)}, u32[]{:S(2)}) copy-start(f32[2,256,128]{2,1,0:T(8,128)S(1)} %collective-permute-done.3.refs_7_.refs_2_) | copy-start | bytes 786436
  32.5 1.9 %copy-start.12 = (f32[2,256,128]{2,1,0:T(8,128)}, f32[2,256,128]{2,1,0:T(8,128)S(1)}, u32[]{:S(2)}) copy-start(f32[2,256,128]{2,1,0:T(8,128)S(1)} %collective-permute-done.1.refs_8_.refs_3_) | copy-start | bytes 786436
  34.3 0.7 copy-start.15
  34.3 0.8 copy-start.11
  35.1 0.8 copy-start.6
  37.7 16.8 %collective-permute-start.12 = (f32[3,256,128]{2,1,0:T(8,128)}, f32[3,256,128]{2,1,0:T(8,128)S(1)}, u32[]{:S(2)}, u32[]{:S(2)}) collective-permute-start(f32[3,256,128]{2,1,0:T(8,128)} %shard_map.39), channel_id=1, source_target_pairs={{12,5},{20,13},{28,21},{36,29},{44,37},{52,45},{60,53},{68,61},{76... | collective-permute-start | bytes 1179656 | tf_op jit(solution)/shard_map/ppermute | solution.py:611
  38.4 16.1 %collective-permute-start.11 = (f32[3,256,128]{2,1,0:T(8,128)}, f32[3,256,128]{2,1,0:T(8,128)S(1)}, u32[]{:S(2)}, u32[]{:S(2)}) collective-permute-start(f32[3,256,128]{2,1,0:T(8,128)} %shard_map.39), channel_id=1, source_target_pairs={{8,0},{9,1},{10,2},{11,3},{12,4},{14,6},{15,7},{16,8},{17,9},{18,1... | collective-permute-start | bytes 1179656 | tf_op jit(solution)/shard_map/ppermute | solution.py:606
  44.6 41.9 %collective-permute-start.14 = (f32[256,1024]{1,0:T(8,128)S(1)}, f32[256,1024]{1,0:T(8,128)S(1)}, u32[]{:S(2)}, u32[]{:S(2)}) collective-permute-start(f32[256,1024]{1,0:T(8,128)S(1)} %slice.19), channel_id=1, source_target_pairs={{8,0},{16,8},{24,16},{32,24},{40,32},{48,40},{56,48},{64,56},{72,6... | collective-permute-start | bytes 3145736 | tf_op jit(solution)/shard_map/ppermute | solution.py:60
  46.9 6.8 %collective-permute-start.6 = (f32[2,256,128]{2,1,0:T(8,128)}, f32[2,256,128]{2,1,0:T(8,128)S(1)}, u32[]{:S(2)}, u32[]{:S(2)}) collective-permute-start(f32[2,256,128]{2,1,0:T(8,128)} %copy-done.12), channel_id=1, source_target_pairs={{0,1},{1,0},{2,3},{3,2},{4,5},{5,4},{6,7},{7,6},{8,9},{9,8},{10,11... | collective-permute-start | bytes 786440 | tf_op jit(solution)/shard_map/ppermute | solution.py:44
  47.8 6.6 %collective-permute-start.7 = (f32[2,256,128]{2,1,0:T(8,128)}, f32[2,256,128]{2,1,0:T(8,128)S(1)}, u32[]{:S(2)}, u32[]{:S(2)}) collective-permute-start(f32[2,256,128]{2,1,0:T(8,128)} %copy-done.16), channel_id=1, source_target_pairs={{0,2},{1,3},{2,4},{3,5},{4,6},{5,7},{6,0},{7,1},{8,10},{9,11},{10,... | collective-permute-start | bytes 786440 | tf_op jit(solution)/shard_map/ppermute | solution.py:40
  53.7 0.8 copy-start.17
  54.5 0.7 copy-start.18
  54.5 0.8 copy-start.9
  54.5 1.0 copy-start.10
  69.2 14.6 %collective-permute-start.13 = (f32[256,256]{1,0:T(8,128)}, f32[256,256]{1,0:T(8,128)S(1)}, u32[]{:S(2)}, u32[]{:S(2)}) collective-permute-start(f32[256,256]{1,0:T(8,128)} %get-tuple-element.63.own.own_transition), channel_id=1, source_target_pairs={{0,8},{8,0},{16,24},{24,16},{32,40},{40,32},{48,56},{56,48},{64,72... | collective-permute-start | bytes 786440 | tf_op jit(solution)/shard_map/ppermute | solution.py:48
  83.8 0.9 copy-start
  85.0 23.0 %collective-permute-start.17 = (f32[256,256]{1,0:T(8,128)S(1)}, f32[256,256]{1,0:T(8,128)S(1)}, u32[]{:S(2)}, u32[]{:S(2)}) collective-permute-start(f32[256,256]{1,0:T(8,128)S(1)} %shard_map.43.refs_0_), channel_id=1, source_target_pairs={{0,48},{8,56},{16,0},{24,8},{32,16},{40,24},{48,32},{56,40},{64,11... | collective-permute-start | bytes 786440 | tf_op jit(solution)/shard_map/ppermute | solution.py:56
  85.1 22.9 %collective-permute-start.16 = (f32[256,256]{1,0:T(8,128)S(1)}, f32[256,256]{1,0:T(8,128)S(1)}, u32[]{:S(2)}, u32[]{:S(2)}) collective-permute-start(f32[256,256]{1,0:T(8,128)S(1)} %shard_map.43.refs_0_), channel_id=1, source_target_pairs={{0,32},{8,40},{16,48},{24,56},{32,0},{40,8},{48,16},{56,24},{64,96... | collective-permute-start | bytes 786440 | tf_op jit(solution)/shard_map/ppermute | solution.py:56
  85.2 22.8 %collective-permute-start.15 = (f32[256,256]{1,0:T(8,128)S(1)}, f32[256,256]{1,0:T(8,128)S(1)}, u32[]{:S(2)}, u32[]{:S(2)}) collective-permute-start(f32[256,256]{1,0:T(8,128)S(1)} %shard_map.43.refs_0_), channel_id=1, source_target_pairs={{0,16},{8,24},{16,32},{24,40},{32,48},{40,56},{48,0},{56,8},{64,80... | collective-permute-start | bytes 786440 | tf_op jit(solution)/shard_map/ppermute | solution.py:56
  86.6 1.0 copy-start.19
  87.6 23.2 %copy-start.1 = (f32[256,256]{1,0:T(8,128)S(1)}, f32[256,256]{1,0:T(8,128)}, u32[]{:S(2)}) copy-start(f32[256,256]{1,0:T(8,128)} %get-tuple-element.63.own.own_transition) | copy-start | bytes 786436
  108.0 36.7 %copy-start.2 = (f32[2048,256]{1,0:T(8,128)S(1)}, f32[2048,256]{1,0:T(8,128)}, u32[]{:S(2)}) copy-start(f32[2048,256]{1,0:T(8,128)} %get-tuple-element.68.response_hbm) | copy-start | bytes 6291460
  108.0 2.8 %collective-permute-start.18 = (f32[256,512]{1,0:T(8,128)}, f32[256,512]{1,0:T(8,128)S(1)}, u32[]{:S(2)}, u32[]{:S(2)}) collective-permute-start(f32[256,512]{1,0:T(8,128)} %get-tuple-element.72), channel_id=1, source_target_pairs={{0,8},{8,0},{16,24},{24,16},{32,40},{40,32},{48,56},{56,48},{64,72... | collective-permute-start | bytes 1572872 | tf_op jit(solution)/shard_map/ppermute | solution.py:48
  110.8 1.0 copy-start.3
  111.8 27.4 %copy-start.4 = (f32[256,512]{1,0:T(8,128)S(1)}, f32[256,512]{1,0:T(8,128)}, u32[]{:S(2)}) copy-start(f32[256,512]{1,0:T(8,128)} %get-tuple-element.69.own) | copy-start | bytes 1572868
  112.4 6.8 %collective-permute-start.19 = (f32[256,128]{1,0:T(8,128)S(1)}, f32[256,128]{1,0:T(8,128)S(1)}, u32[]{:S(2)}, u32[]{:S(2)}) collective-permute-start(f32[256,128]{1,0:T(8,128)S(1)} %get-tuple-element.79), channel_id=1, source_target_pairs={{0,16},{8,24},{16,32},{24,40},{32,48},{40,56},{48,0},{56,8},{64,80... | collective-permute-start | bytes 393224 | tf_op jit(solution)/shard_map/ppermute | solution.py:56
  113.7 9.0 %collective-permute-start.20 = (f32[256,128]{1,0:T(8,128)S(1)}, f32[256,128]{1,0:T(8,128)S(1)}, u32[]{:S(2)}, u32[]{:S(2)}) collective-permute-start(f32[256,128]{1,0:T(8,128)S(1)} %get-tuple-element.80), channel_id=1, source_target_pairs={{0,32},{8,40},{16,48},{24,56},{32,0},{40,8},{48,16},{56,24},{64,96... | collective-permute-start | bytes 393224 | tf_op jit(solution)/shard_map/ppermute | solution.py:56
  116.4 6.3 %collective-permute-start.21 = (f32[256,128]{1,0:T(8,128)S(1)}, f32[256,128]{1,0:T(8,128)S(1)}, u32[]{:S(2)}, u32[]{:S(2)}) collective-permute-start(f32[256,128]{1,0:T(8,128)S(1)} %get-tuple-element.81), channel_id=1, source_target_pairs={{0,48},{8,56},{16,0},{24,8},{32,16},{40,24},{48,32},{56,40},{64,11... | collective-permute-start | bytes 393224 | tf_op jit(solution)/shard_map/ppermute | solution.py:56
  123.6 7.5 %collective-permute-start.22 = (f32[256,128]{1,0:T(8,128)S(1)}, f32[256,128]{1,0:T(8,128)S(1)}, u32[]{:S(2)}, u32[]{:S(2)}) collective-permute-start(f32[256,128]{1,0:T(8,128)S(1)} %get-tuple-element.82), channel_id=1, source_target_pairs={{0,64},{8,72},{16,80},{24,88},{32,96},{40,104},{48,112},{56,120},{... | collective-permute-start | bytes 393224 | tf_op jit(solution)/shard_map/ppermute | solution.py:656
  131.7 5.1 %collective-permute-start.23 = (f32[256,128]{1,0:T(8,128)S(1)}, f32[256,128]{1,0:T(8,128)S(1)}, u32[]{:S(2)}, u32[]{:S(2)}) collective-permute-start(f32[256,128]{1,0:T(8,128)S(1)} %get-tuple-element.86), channel_id=1, source_target_pairs={{0,16},{8,24},{16,32},{24,40},{32,48},{40,56},{48,0},{56,8},{64,80... | collective-permute-start | bytes 393224 | tf_op jit(solution)/shard_map/ppermute | solution.py:56
  131.7 6.6 %collective-permute-start.24 = (f32[256,128]{1,0:T(8,128)S(1)}, f32[256,128]{1,0:T(8,128)S(1)}, u32[]{:S(2)}, u32[]{:S(2)}) collective-permute-start(f32[256,128]{1,0:T(8,128)S(1)} %get-tuple-element.87), channel_id=1, source_target_pairs={{0,32},{8,40},{16,48},{24,56},{32,0},{40,8},{48,16},{56,24},{64,96... | collective-permute-start | bytes 393224 | tf_op jit(solution)/shard_map/ppermute | solution.py:56
  134.5 4.7 %collective-permute-start.25 = (f32[256,128]{1,0:T(8,128)S(1)}, f32[256,128]{1,0:T(8,128)S(1)}, u32[]{:S(2)}, u32[]{:S(2)}) collective-permute-start(f32[256,128]{1,0:T(8,128)S(1)} %get-tuple-element.88), channel_id=1, source_target_pairs={{0,48},{8,56},{16,0},{24,8},{32,16},{40,24},{48,32},{56,40},{64,11... | collective-permute-start | bytes 393224 | tf_op jit(solution)/shard_map/ppermute | solution.py:56
  139.8 4.9 %collective-permute-start.26 = (f32[256,512]{1,0:T(8,128)S(1)}, f32[256,512]{1,0:T(8,128)S(1)}, u32[]{:S(2)}, u32[]{:S(2)}) collective-permute-start(f32[256,512]{1,0:T(8,128)S(1)} %get-tuple-element.90), channel_id=1, source_target_pairs={{0,8},{8,0},{16,24},{24,16},{32,40},{40,32},{48,56},{56,48},{64,72... | collective-permute-start | bytes 1572872 | tf_op jit(solution)/shard_map/ppermute | solution.py:48

commit v5 on v4

--- a/solution.py
+++ b/solution.py
@@ -77,10 +77,7 @@
 
         @pl.when(place_of(2 * dz + dx) == 0)
         def _():
-            if len(where) == 1:
-                first, second = pieces[where[0]].at[0], pieces[where[0]].at[1, pl.ds(0, 1)]
-            else:
-                first, second = pieces[where[0]], pieces[where[1]].at[pl.ds(0, 1)]
+            first, second = pieces[where[0]], pieces[where[1]].at[pl.ds(0, 1)]
             copies = [
                 pltpu.make_async_copy(first, out.at[pl.ds(0, 2)], sems.at[0]),
                 pltpu.make_async_copy(second, out.at[pl.ds(2, 1)], sems.at[1]),
@@ -571,30 +568,37 @@
         jnp.int32, (width, width), 1
     )
     own = jnp.concatenate([jnp.where(below, wy_v[:, :, :width], wy_t), wy_v[:, :, width:]], axis=2)
-    tail = from_next_row(eigvecs[: 2 * width])
+    f00, s00 = own[0], own[1]
+    above = eigvecs[: 2 * width]
     depth = 2 * width
     shapes = ((own_blocks + 2, 2 * depth, depth), (own_blocks + 1, 2 * depth, depth))
 
-    f30, s30 = along_z(own[0], 1), along_z(own[1], 1)
-    p01, p10 = across_x(own), along_z(own, -1)
-    buffers = build(None, shapes, [own], placed(0, (0, 0)))
-    f30, *buffers = together(f30, *buffers)
-    f31, f20, p11 = across_x(f30), along_z(f30, 1), along_z(p01, -1)
-    s31, s20 = across_x(s30), along_z(s30, 1)
-    buffers = build(
-        buffers,
-        shapes,
-        [p01, p10, f30, s30],
-        placed(0, (0, 1)) + placed(1, (1, 0)) + placed(2, (3, 0), (0,), False) + placed(3, (3, 0), (1,), False),
-    )
-    f20, s31, *buffers = together(f20, s31, *buffers)
-    f21, s21 = across_x(f20), along_z(s31, 1)
+    def add(buffers, group, pieces, keys):
+        parts = []
+        for source, key in enumerate(keys):
+            parts += placed(source, key, (group,), False)
+        return build(buffers, shapes, pieces, parts)
+
+    f01, f30, f10 = across_x(f00), along_z(f00, 1), along_z(f00, -1)
+    s01, s30, s10 = across_x(s00), along_z(s00, 1), along_z(s00, -1)
+    buffers = build(None, shapes, [f00, s00], placed(0, (0, 0), (0,), False) + placed(1, (0, 0), (1,), False))
+    f01, f30, f10, *buffers = together(f01, f30, f10, *buffers)
+    f31, f20, f11 = across_x(f30), along_z(f30, 1), along_z(f01, -1)
+    buffers = add(buffers, 0, [f01, f30, f10], [(0, 1), (3, 0), (1, 0)])
+    s01, s30, s10, *buffers = together(s01, s30, s10, *buffers)
+    s31, s20, s11 = across_x(s30), along_z(s30, 1), along_z(s01, -1)
+    buffers = add(buffers, 1, [s01, s30, s10], [(0, 1), (3, 0), (1, 0)])
+    f31, f20, f11, *buffers = together(f31, f20, f11, *buffers)
+    f21 = along_z(f11, -1)
+    buffers = add(buffers, 0, [f31, f20, f11], [(3, 1), (2, 0), (1, 1)])
+    s31, s20, s11, *buffers = together(s31, s20, s11, *buffers)
+    s21 = along_z(s31, 1)
     picked = pick_first(
         {
-            (0, 0): [own],
-            (0, 1): [p01],
-            (1, 0): [p10],
-            (1, 1): [p11],
+            (0, 0): [f00, s00],
+            (0, 1): [f01, s01],
+            (1, 0): [f10, s10],
+            (1, 1): [f11, s11],
             (3, 0): [f30, s30],
             (3, 1): [f31, s31],
             (2, 0): [f20, s20],
@@ -612,20 +616,13 @@
             picked, ("row", "vec"), [((i + 1) * vecs + late - 1, i * vecs + late) for i in range(rows - 1)]
         ),
     ]
+    buffers = add(buffers, 1, [s31, s20, s11], [(3, 1), (2, 0), (1, 1)])
+    f21, s21, above, extra, late_extra, *buffers = together(f21, s21, above, *extras, *buffers)
+    tail = from_next_row(above)
     buffers = build(
         buffers,
         shapes,
-        [p11, f31, s31, f20, s20],
-        placed(0, (1, 1))
-        + placed(1, (3, 1), (0,), False)
-        + placed(2, (3, 1), (1,), False)
-        + placed(3, (2, 0), (0,), False)
-        + placed(4, (2, 0), (1,), False),
-    )
-    buffers = build(
-        buffers,
-        shapes,
-        [f21, s21, *extras],
+        [f21, s21, extra, late_extra],
         placed(0, (2, 1), (0,), False)
         + placed(1, (2, 1), (1,), False)
         + [((2, 3, late), [0, 1], 0, lambda vec: own_blocks), ((2, 3, late), [2], 1, lambda vec: own_blocks)],

time: 153 us -> 140 us (0.915)
  waiting for transfers between devices: 34 us -> 21 us
  Pallas kernels: 58.9 us -> 62.6 us
  starting transfers between devices: 50.2 us -> 47.1 us
    ppermute x4, waiting for transfers between devices: 14 us -> 0.01 us  [across_x(): return lax.ppermute(value, 'vec', [(v, v ^ 1) for v in range(2 * Z_SIZE)])]
    ppermute x3, starting transfers between devices: 17.7 us -> 6.79 us  [across_core(): lax.ppermute(value, 'row', [(i, i ^ 1) for i in range(lax.axis_size('row'...]
    ppermute x7 -> x10, starting transfers between devices: 7.75 us -> 14.7 us  [along_z(): return lax.ppermute(value, 'vec', pairs)]
    pallas_call x4 -> x6, Pallas kernels: 16.3 us -> 20.1 us  [build(): pl.pallas_call(functools.partial(build_kernel, parts, has_input), out_sha...]
    unnamed x40 -> x50, local copies, waits for them, and re-layouts: 5.68 us -> 4.66 us
    ppermute x7 -> x10, waiting for transfers between devices: 2.6 us -> 3.59 us  [along_z(): return lax.ppermute(value, 'vec', pairs)]
  transfers between devices with their start and end apart: 27 -> 30, of which waited for: 13 -> 11; matrix products, arithmetic and copies ran while one was open for 1% -> 1% of each run, Pallas kernels for 31% -> 37%
where the time goes in v5:
time: 140 us; the launch traced here: 139 us
  Pallas kernels  62.6 us (45%)
  starting transfers between devices  47.1 us (34%)
  waiting for transfers between devices  21 us (15%)
  local copies, waits for them, and re-layouts  5.98 us (4%)
    pallas_call x1, Pallas kernels, sweep_data(): pl.pallas_call(data_kernel, out_shape=(jax.ShapeDtypeStruct((blocks * wid...  20.3 us
    pallas_call x6, Pallas kernels, build(): pl.pallas_call(functools.partial(build_kernel, parts, has_input), out_sha...  20.1 us
    ppermute x10, starting transfers between devices, along_z(): return lax.ppermute(value, 'vec', pairs)  14.7 us
    ppermute x9, starting transfers between devices, along_y(): lax.ppermute(value, 'row', [(i, target(i)) for i in range(lax.axis_size('...  12.3 us
    pallas_call x1, Pallas kernels, sweep_units(): pl.pallas_call(unit_kernel, out_shape=(jax.ShapeDtypeStruct((blocks * wid...  9.72 us
    pallas_call x1, Pallas kernels, correct(): pl.pallas_call(functools.partial(correct_kernel, tile), out_shape=jax.Sha...  7.05 us
    ppermute x3, starting transfers between devices, across_core(): lax.ppermute(value, 'row', [(i, i ^ 1) for i in range(lax.axis_size('row'...  6.79 us
    ppermute x9, waiting for transfers between devices, along_y(): lax.ppermute(value, 'row', [(i, target(i)) for i in range(lax.axis_size('...  6.78 us
  transfers between devices with their start and end apart: 30, of which 11 were waited for; matrix products, arithmetic and copies ran while one was open for 1% of the time, Pallas kernels for 37%

profile of v5, /device:TPU:5, one launch (start us, length us, event | category | flops | bytes accessed | tf_op | source)
XLA Modules:
  0.0 138.6 jit_solution(17465307846477367687)
XLA Ops:
  0.0 1.2 fusion.3
  1.3 3.8 %collective-permute-start.2 = (f32[2,256,128]{2,1,0:T(8,128)S(1)}, f32[2,256,128]{2,1,0:T(8,128)S(1)}, u32[]{:S(2)}, u32[]{:S(2)}) collective-permute-start(f32[2,256,128]{2,1,0:T(8,128)S(1)} %get-tuple-element.140.refs_0_), channel_id=1, source_target_pairs={{0,6},{1,7},{2,0},{3,1},{4,2},{5,3},{6,4},{7,5},{8,14},{9,15},{10,... | collective-permute-start | bytes 786440 | tf_op jit(solution)/shard_map/ppermute | solution.py:40
  5.1 0.9 collective-permute-start
  6.0 2.7 %collective-permute-start.8 = (f32[2,256,128]{2,1,0:T(8,128)S(1)}, f32[2,256,128]{2,1,0:T(8,128)S(1)}, u32[]{:S(2)}, u32[]{:S(2)}) collective-permute-start(f32[2,256,128]{2,1,0:T(8,128)S(1)} %get-tuple-element.139.refs_1_), channel_id=1, source_target_pairs={{0,6},{1,7},{2,0},{3,1},{4,2},{5,3},{6,4},{7,5},{8,14},{9,15},{10,... | collective-permute-start | bytes 786440 | tf_op jit(solution)/shard_map/ppermute | solution.py:40
  8.7 2.9 %shard_map.37 = (bf16[18,512,256]{2,1,0:T(8,128)(2,1)}, bf16[17,512,256]{2,1,0:T(8,128)(2,1)}) custom-call(f32[2,256,128]{2,1,0:T(8,128)} %copy-done.19, f32[2,256,128]{2,1,0:T(8,128)} %copy-done.18), custom_call_target="tpu_custom_call" | custom-call | flops 1200000000 | bytes 1572864 | tf_op jit(solution)/shard_map/pallas_call | solution.py:161
  11.6 0.6 collective-permute-start.6
  12.2 0.9 collective-permute-done.1.refs_1_.refs_8_
  13.2 1.8 %collective-permute-start.5 = (f32[2,256,128]{2,1,0:T(8,128)S(1)}, f32[2,256,128]{2,1,0:T(8,128)S(1)}, u32[]{:S(2)}, u32[]{:S(2)}) collective-permute-start(f32[2,256,128]{2,1,0:T(8,128)S(1)} %collective-permute-done.refs_0_.refs_2_), channel_id=1, source_target_pairs={{0,6},{1,7},{2,0},{3,1},{4,2},{5,3},{6,4},{7,5},{8,14},{9,15},{10,... | collective-permute-start | bytes 786440 | tf_op jit(solution)/shard_map/ppermute | solution.py:40
  15.0 0.7 collective-permute-done.8.refs_2_.refs_5_
  15.7 0.9 collective-permute-start.3
  16.6 3.4 %shard_map.38 = (bf16[18,512,256]{2,1,0:T(8,128)(2,1)}, bf16[17,512,256]{2,1,0:T(8,128)(2,1)}) custom-call(f32[2,256,128]{2,1,0:T(8,128)} %copy-done.9, f32[2,256,128]{2,1,0:T(8,128)} %copy-done.8, f32[2,256,128]{2,1,0:T(8,128)} %copy-done.5, bf16[18,512,256]{2,1,0:T(8,128)(2,1)} %get-tuple-element.77.refs_3_, ...), custom_call_target="tpu_custom_call", output_to_operand_aliasing={{0}: (3, {}), {1}: (4, {})} | custom-call | flops 1800000000 | bytes 2359296 | tf_op jit(solution)/shard_map/pallas_call | solution.py:161
  20.0 0.5 collective-permute-start.11
  20.5 0.5 collective-permute-start.10
  21.1 3.1 %collective-permute-start.12 = (f32[2,256,128]{2,1,0:T(8,128)S(1)}, f32[2,256,128]{2,1,0:T(8,128)S(1)}, u32[]{:S(2)}, u32[]{:S(2)}) collective-permute-start(f32[2,256,128]{2,1,0:T(8,128)S(1)} %collective-permute-done.6.refs_0_.refs_3_), channel_id=1, source_target_pairs={{0,6},{1,7},{2,0},{3,1},{4,2},{5,3},{6,4},{7,5},{8,14},{9,15},{10,... | collective-permute-start | bytes 786440 | tf_op jit(solution)/shard_map/ppermute | solution.py:40
  24.2 3.4 %shard_map.39 = (bf16[18,512,256]{2,1,0:T(8,128)(2,1)}, bf16[17,512,256]{2,1,0:T(8,128)(2,1)}) custom-call(f32[2,256,128]{2,1,0:T(8,128)} %copy-done.12, f32[2,256,128]{2,1,0:T(8,128)} %copy-done.11, f32[2,256,128]{2,1,0:T(8,128)} %copy-done.10, bf16[18,512,256]{2,1,0:T(8,128)(2,1)} %get-tuple-element.84.refs_3_, ...), custom_call_target="tpu_custom_call", output_to_operand_aliasing={{0}: (3, {}), {1}: (4, {})} | custom-call | flops 1800000000 | bytes 2359296 | tf_op jit(solution)/shard_map/pallas_call | solution.py:161
  27.6 0.7 copy-done.13
  28.3 0.1 copy-done.16
  28.4 3.4 %shard_map.40 = (bf16[18,512,256]{2,1,0:T(8,128)(2,1)}, bf16[17,512,256]{2,1,0:T(8,128)(2,1)}) custom-call(f32[2,256,128]{2,1,0:T(8,128)} %copy-done.16, f32[2,256,128]{2,1,0:T(8,128)} %copy-done.13, f32[2,256,128]{2,1,0:T(8,128)} %copy-done.6, bf16[18,512,256]{2,1,0:T(8,128)(2,1)} %get-tuple-element.91.refs_3_, ...), custom_call_target="tpu_custom_call", output_to_operand_aliasing={{0}: (3, {}), {1}: (4, {})} | custom-call | flops 1800000000 | bytes 2359296 | tf_op jit(solution)/shard_map/pallas_call | solution.py:161
  31.9 0.6 copy-done.17
  32.5 0.1 copy-done.14
  32.6 0.1 copy-done.15
  32.7 1.8 %shard_map.41 = f32[3,256,128]{2,1,0:T(8,128)} custom-call(f32[2,256,128]{2,1,0:T(8,128)} %copy-done.19, f32[2,256,128]{2,1,0:T(8,128)} %copy-done.18, f32[2,256,128]{2,1,0:T(8,128)} %copy-done.9, f32[2,256,128]{2,1,0:T(8,128)} %copy-done.12, f32[2,256,128]{2,1,0:T(8,128)} %copy-done.5, f32[2,256,128]{2,1,0:T(8,128)} %copy-done.10, ...), custom_call_target="tpu_custom_call" | custom-call | tf_op jit(solution)/shard_map/pallas_call | solution.py:96
  34.5 0.7 collective-permute-start.15
  35.2 5.4 %collective-permute-start.14 = (f32[3,256,128]{2,1,0:T(8,128)}, f32[3,256,128]{2,1,0:T(8,128)S(1)}, u32[]{:S(2)}, u32[]{:S(2)}) collective-permute-start(f32[3,256,128]{2,1,0:T(8,128)} %shard_map.41), channel_id=1, source_target_pairs={{8,0},{9,1},{10,2},{11,3},{12,4},{14,6},{15,7},{16,8},{17,9},{18,1... | collective-permute-start | bytes 1179656 | tf_op jit(solution)/shard_map/ppermute | solution.py:610
  40.6 0.1 collective-permute-start.13
  40.7 2.7 %collective-permute-start.9 = (f32[2,256,128]{2,1,0:T(8,128)S(1)}, f32[2,256,128]{2,1,0:T(8,128)S(1)}, u32[]{:S(2)}, u32[]{:S(2)}) collective-permute-start(f32[2,256,128]{2,1,0:T(8,128)S(1)} %copy-done.7), channel_id=1, source_target_pairs={{0,6},{1,7},{2,0},{3,1},{4,2},{5,3},{6,4},{7,5},{8,14},{9,15},{10,... | collective-permute-start | bytes 786440 | tf_op jit(solution)/shard_map/ppermute | solution.py:40
  43.3 1.3 slice.19
  44.7 3.4 %shard_map.42 = (bf16[18,512,256]{2,1,0:T(8,128)(2,1)}, bf16[17,512,256]{2,1,0:T(8,128)(2,1)}) custom-call(f32[2,256,128]{2,1,0:T(8,128)} %copy-done.15, f32[2,256,128]{2,1,0:T(8,128)} %copy-done.14, f32[2,256,128]{2,1,0:T(8,128)} %copy-done.17, bf16[18,512,256]{2,1,0:T(8,128)(2,1)} %get-tuple-element.98.refs_3_, ...), custom_call_target="tpu_custom_call", output_to_operand_aliasing={{0}: (3, {}), {1}: (4, {})} | custom-call | flops 1800000000 | bytes 2359296 | tf_op jit(solution)/shard_map/pallas_call | solution.py:161
  48.0 2.0 %collective-permute-done.13.refs_1_ = f32[2,256,128]{2,1,0:T(8,128)S(1)} collective-permute-done((f32[2,256,128]{2,1,0:T(8,128)}, f32[2,256,128]{2,1,0:T(8,128)S(1)}, u32[]{:S(2)}, u32[]{:S(2)}) %collective-permute-start.13) | collective-permute-done | bytes 262176 | tf_op jit(solution)/shard_map/ppermute | solution.py:40
  50.0 2.9 %collective-permute-start.17 = (f32[256,1024]{1,0:T(8,128)S(1)}, f32[256,1024]{1,0:T(8,128)S(1)}, u32[]{:S(2)}, u32[]{:S(2)}) collective-permute-start(f32[256,1024]{1,0:T(8,128)S(1)} %slice.19), channel_id=1, source_target_pairs={{8,0},{16,8},{24,16},{32,24},{40,32},{48,40},{56,48},{64,56},{72,6... | collective-permute-start | bytes 3145736 | tf_op jit(solution)/shard_map/ppermute | solution.py:60
  53.0 3.8 %shard_map.43 = (bf16[18,512,256]{2,1,0:T(8,128)(2,1)}, bf16[17,512,256]{2,1,0:T(8,128)(2,1)}) custom-call(f32[2,256,128]{2,1,0:T(8,128)} %copy-done.23, f32[2,256,128]{2,1,0:T(8,128)} %copy-done.22, f32[3,256,128]{2,1,0:T(8,128)} %copy-done.21, f32[3,256,128]{2,1,0:T(8,128)} %copy-done.20, ...), custom_call_target="tpu_custom_call", output_to_operand_aliasing={{0}: (4, {}), {1}: (5, {})} | custom-call | flops 2100000000 | bytes 2752512 | tf_op jit(solution)/shard_map/pallas_call | solution.py:161
  56.8 9.7 %shard_map.44 = (f32[2048,256]{1,0:T(8,128)}, f32[256,256]{1,0:T(8,128)}, f32[256,1024]{1,0:T(8,128)}) custom-call(bf16[18,512,256]{2,1,0:T(8,128)(2,1)} %get-tuple-element.111.first_hbm, bf16[17,512,256]{2,1,0:T(8,128)(2,1)} %get-tuple-element.112.second_hbm, f32[2048,1024]{1,0:T(8,128)} %data_hbm.3), custom_call_target="tpu_custom_call" | custom-call | flops 4831838208 | bytes 31457280 | tf_op jit(solution)/shard_map/pallas_call | solution.py:371
  66.5 2.3 %collective-permute-start.16 = (f32[256,256]{1,0:T(8,128)}, f32[256,256]{1,0:T(8,128)S(1)}, u32[]{:S(2)}, u32[]{:S(2)}) collective-permute-start(f32[256,256]{1,0:T(8,128)} %get-tuple-element.110.own.own_transition), channel_id=1, source_target_pairs={{0,8},{8,0},{16,24},{24,16},{32,40},{40,32},{48,56},{56,48},{64,72... | collective-permute-start | bytes 786440 | tf_op jit(solution)/shard_map/ppermute | solution.py:48
  68.8 1.4 collective-permute-done.16.received.received_transition
  70.2 0.9 copy-done
  71.2 0.3 shard_map.45.refs_0_
  71.5 1.0 collective-permute-start.20
  72.5 0.2 collective-permute-start.19
  72.7 0.7 collective-permute-start.18
  73.4 1.0 copy-done.24
  74.4 20.3 %shard_map.46 = (f32[2048,1024]{1,0:T(8,128)}, f32[256,512]{1,0:T(8,128)}, f32[256,512]{1,0:T(8,128)}) custom-call(bf16[18,512,256]{2,1,0:T(8,128)(2,1)} %get-tuple-element.111.first_hbm, bf16[17,512,256]{2,1,0:T(8,128)(2,1)} %get-tuple-element.112.second_hbm, f32[2048,1024]{1,0:T(8,128)} %data_hbm.3, f32[256,1024]{1,0:T(8,128)} %copy-done.24, ...), custom_call_target="tpu_custom_call" | custom-call | flops 12884901888 | bytes 31457280 | tf_op jit(solution)/shard_map/pallas_call | solution.py:400
  94.8 1.1 collective-permute-start.21
  95.9 1.7 %collective-permute-done.21.received = f32[256,512]{1,0:T(8,128)S(1)} collective-permute-done((f32[256,512]{1,0:T(8,128)}, f32[256,512]{1,0:T(8,128)S(1)}, u32[]{:S(2)}, u32[]{:S(2)}) %collective-permute-start.21) | collective-permute-done | bytes 524320 | tf_op jit(solution)/shard_map/ppermute | solution.py:48
  97.6 1.0 copy-done.3
  98.7 0.6 shard_map.48
  99.2 1.8 %collective-permute-start.22 = (f32[256,128]{1,0:T(8,128)S(1)}, f32[256,128]{1,0:T(8,128)S(1)}, u32[]{:S(2)}, u32[]{:S(2)}) collective-permute-start(f32[256,128]{1,0:T(8,128)S(1)} %get-tuple-element.127), channel_id=1, source_target_pairs={{0,16},{8,24},{16,32},{24,40},{32,48},{40,56},{48,0},{56,8},{64,80... | collective-permute-start | bytes 393224 | tf_op jit(solution)/shard_map/ppermute | solution.py:56
  101.0 1.8 %collective-permute-start.23 = (f32[256,128]{1,0:T(8,128)S(1)}, f32[256,128]{1,0:T(8,128)S(1)}, u32[]{:S(2)}, u32[]{:S(2)}) collective-permute-start(f32[256,128]{1,0:T(8,128)S(1)} %get-tuple-element.128), channel_id=1, source_target_pairs={{0,32},{8,40},{16,48},{24,56},{32,0},{40,8},{48,16},{56,24},{64,96... | collective-permute-start | bytes 393224 | tf_op jit(solution)/shard_map/ppermute | solution.py:56
  102.8 2.0 %collective-permute-start.24 = (f32[256,128]{1,0:T(8,128)S(1)}, f32[256,128]{1,0:T(8,128)S(1)}, u32[]{:S(2)}, u32[]{:S(2)}) collective-permute-start(f32[256,128]{1,0:T(8,128)S(1)} %get-tuple-element.129), channel_id=1, source_target_pairs={{0,48},{8,56},{16,0},{24,8},{32,16},{40,24},{48,32},{56,40},{64,11... | collective-permute-start | bytes 393224 | tf_op jit(solution)/shard_map/ppermute | solution.py:56
  104.8 0.8 shard_map.47
  105.6 3.5 %collective-permute-done.23.refs_2_ = f32[256,128]{1,0:T(8,128)S(1)} collective-permute-done((f32[256,128]{1,0:T(8,128)S(1)}, f32[256,128]{1,0:T(8,128)S(1)}, u32[]{:S(2)}, u32[]{:S(2)}) %collective-permute-start.23) | collective-permute-done | bytes 131104 | tf_op jit(solution)/shard_map/ppermute | solution.py:56
  109.0 0.9 shard_map.49
  110.0 1.3 collective-permute-start.25
  111.3 5.9 %collective-permute-done.25.entering = f32[256,128]{1,0:T(8,128)S(1)} collective-permute-done((f32[256,128]{1,0:T(8,128)S(1)}, f32[256,128]{1,0:T(8,128)S(1)}, u32[]{:S(2)}, u32[]{:S(2)}) %collective-permute-start.25) | collective-permute-done | bytes 131104 | tf_op jit(solution)/shard_map/ppermute | solution.py:653
  117.2 0.5 shard_map.50
  117.7 0.1 collective-permute-start.26
  117.8 3.6 %collective-permute-start.27 = (f32[256,128]{1,0:T(8,128)S(1)}, f32[256,128]{1,0:T(8,128)S(1)}, u32[]{:S(2)}, u32[]{:S(2)}) collective-permute-start(f32[256,128]{1,0:T(8,128)S(1)} %get-tuple-element.135), channel_id=1, source_target_pairs={{0,32},{8,40},{16,48},{24,56},{32,0},{40,8},{48,16},{56,24},{64,96... | collective-permute-start | bytes 393224 | tf_op jit(solution)/shard_map/ppermute | solution.py:56
  121.4 1.2 collective-permute-start.28
  122.6 0.2 collective-permute-done.26.refs_1_
  122.8 2.4 %collective-permute-done.27.refs_2_ = f32[256,128]{1,0:T(8,128)S(1)} collective-permute-done((f32[256,128]{1,0:T(8,128)S(1)}, f32[256,128]{1,0:T(8,128)S(1)}, u32[]{:S(2)}, u32[]{:S(2)}) %collective-permute-start.27) | collective-permute-done | bytes 131104 | tf_op jit(solution)/shard_map/ppermute | solution.py:56
  125.2 0.6 collective-permute-done.28.refs_3_
  125.9 0.5 shard_map.51
  126.4 3.4 %collective-permute-start.29 = (f32[256,512]{1,0:T(8,128)S(1)}, f32[256,512]{1,0:T(8,128)S(1)}, u32[]{:S(2)}, u32[]{:S(2)}) collective-permute-start(f32[256,512]{1,0:T(8,128)S(1)} %get-tuple-element.138), channel_id=1, source_target_pairs={{0,8},{8,0},{16,24},{24,16},{32,40},{40,32},{48,56},{56,48},{64,72... | collective-permute-start | bytes 1572872 | tf_op jit(solution)/shard_map/ppermute | solution.py:48
  129.8 1.5 %collective-permute-done.29.taken = f32[256,512]{1,0:T(8,128)S(1)} collective-permute-done((f32[256,512]{1,0:T(8,128)S(1)}, f32[256,512]{1,0:T(8,128)S(1)}, u32[]{:S(2)}, u32[]{:S(2)}) %collective-permute-start.29) | collective-permute-done | bytes 524320 | tf_op jit(solution)/shard_map/ppermute | solution.py:48
  131.3 7.1 %shard_map.52 = f32[2048,1024]{1,0:T(8,128)} custom-call(f32[2048,1024]{1,0:T(8,128)} %get-tuple-element.115.rows_hbm, f32[2048,256]{1,0:T(8,128)S(1)} %copy-done.2, f32[256,512]{1,0:T(8,128)S(1)} %get-tuple-element.137.kept, f32[256,512]{1,0:T(8,128)S(1)} %collective-permute-done.29.taken), custom_call_target="tpu_custom_call" | custom-call | tf_op jit(solution)/shard_map/pallas_call | solution.py:547
  (66 shorter events, 0.2 us)
Async XLA Ops:
  1.2 7.4 %copy-start.18 = (f32[2,256,128]{2,1,0:T(8,128)}, f32[2,256,128]{2,1,0:T(8,128)S(1)}, u32[]{:S(2)}) copy-start(f32[2,256,128]{2,1,0:T(8,128)S(1)} %get-tuple-element.139.refs_1_) | copy-start | bytes 786436
  1.2 7.4 %copy-start.19 = (f32[2,256,128]{2,1,0:T(8,128)}, f32[2,256,128]{2,1,0:T(8,128)S(1)}, u32[]{:S(2)}) copy-start(f32[2,256,128]{2,1,0:T(8,128)S(1)} %get-tuple-element.140.refs_0_) | copy-start | bytes 786436
  1.3 10.3 %collective-permute-start.2 = (f32[2,256,128]{2,1,0:T(8,128)S(1)}, f32[2,256,128]{2,1,0:T(8,128)S(1)}, u32[]{:S(2)}, u32[]{:S(2)}) collective-permute-start(f32[2,256,128]{2,1,0:T(8,128)S(1)} %get-tuple-element.140.refs_0_), channel_id=1, source_target_pairs={{0,6},{1,7},{2,0},{3,1},{4,2},{5,3},{6,4},{7,5},{8,14},{9,15},{10,... | collective-permute-start | bytes 786440 | tf_op jit(solution)/shard_map/ppermute | solution.py:40
  5.1 8.1 %collective-permute-start.1 = (f32[2,256,128]{2,1,0:T(8,128)S(1)}, f32[2,256,128]{2,1,0:T(8,128)S(1)}, u32[]{:S(2)}, u32[]{:S(2)}) collective-permute-start(f32[2,256,128]{2,1,0:T(8,128)S(1)} %get-tuple-element.140.refs_0_), channel_id=1, source_target_pairs={{0,2},{1,3},{2,4},{3,5},{4,6},{5,7},{6,0},{7,1},{8,10},{9,11},{10,... | collective-permute-start | bytes 786440 | tf_op jit(solution)/shard_map/ppermute | solution.py:40
  5.1 8.1 %collective-permute-start = (f32[2,256,128]{2,1,0:T(8,128)S(1)}, f32[2,256,128]{2,1,0:T(8,128)S(1)}, u32[]{:S(2)}, u32[]{:S(2)}) collective-permute-start(f32[2,256,128]{2,1,0:T(8,128)S(1)} %get-tuple-element.140.refs_0_), channel_id=1, source_target_pairs={{0,1},{1,0},{2,3},{3,2},{4,5},{5,4},{6,7},{7,6},{8,9},{9,8},{10,11... | collective-permute-start | bytes 786440 | tf_op jit(solution)/shard_map/ppermute | solution.py:44
  6.0 9.7 %collective-permute-start.8 = (f32[2,256,128]{2,1,0:T(8,128)S(1)}, f32[2,256,128]{2,1,0:T(8,128)S(1)}, u32[]{:S(2)}, u32[]{:S(2)}) collective-permute-start(f32[2,256,128]{2,1,0:T(8,128)S(1)} %get-tuple-element.139.refs_1_), channel_id=1, source_target_pairs={{0,6},{1,7},{2,0},{3,1},{4,2},{5,3},{6,4},{7,5},{8,14},{9,15},{10,... | collective-permute-start | bytes 786440 | tf_op jit(solution)/shard_map/ppermute | solution.py:40
  8.7 11.3 %collective-permute-start.7 = (f32[2,256,128]{2,1,0:T(8,128)S(1)}, f32[2,256,128]{2,1,0:T(8,128)S(1)}, u32[]{:S(2)}, u32[]{:S(2)}) collective-permute-start(f32[2,256,128]{2,1,0:T(8,128)S(1)} %get-tuple-element.139.refs_1_), channel_id=1, source_target_pairs={{0,2},{1,3},{2,4},{3,5},{4,6},{5,7},{6,0},{7,1},{8,10},{9,11},{10,... | collective-permute-start | bytes 786440 | tf_op jit(solution)/shard_map/ppermute | solution.py:40
  11.6 5.0 %copy-start.5 = (f32[2,256,128]{2,1,0:T(8,128)}, f32[2,256,128]{2,1,0:T(8,128)S(1)}, u32[]{:S(2)}) copy-start(f32[2,256,128]{2,1,0:T(8,128)S(1)} %collective-permute-done.2.refs_2_.refs_4_) | copy-start | bytes 786436
  11.6 8.4 %collective-permute-start.6 = (f32[2,256,128]{2,1,0:T(8,128)}, f32[2,256,128]{2,1,0:T(8,128)S(1)}, u32[]{:S(2)}, u32[]{:S(2)}) collective-permute-start(f32[2,256,128]{2,1,0:T(8,128)} %copy-done.18), channel_id=1, source_target_pairs={{0,1},{1,0},{2,3},{3,2},{4,5},{5,4},{6,7},{7,6},{8,9},{9,8},{10,11... | collective-permute-start | bytes 786440 | tf_op jit(solution)/shard_map/ppermute | solution.py:44
  13.1 3.4 %copy-start.8 = (f32[2,256,128]{2,1,0:T(8,128)}, f32[2,256,128]{2,1,0:T(8,128)S(1)}, u32[]{:S(2)}) copy-start(f32[2,256,128]{2,1,0:T(8,128)S(1)} %collective-permute-done.1.refs_1_.refs_8_) | copy-start | bytes 786436
  13.2 3.4 %copy-start.9 = (f32[2,256,128]{2,1,0:T(8,128)}, f32[2,256,128]{2,1,0:T(8,128)S(1)}, u32[]{:S(2)}) copy-start(f32[2,256,128]{2,1,0:T(8,128)S(1)} %collective-permute-done.refs_0_.refs_2_) | copy-start | bytes 786436
  13.2 7.9 %collective-permute-start.5 = (f32[2,256,128]{2,1,0:T(8,128)S(1)}, f32[2,256,128]{2,1,0:T(8,128)S(1)}, u32[]{:S(2)}, u32[]{:S(2)}) collective-permute-start(f32[2,256,128]{2,1,0:T(8,128)S(1)} %collective-permute-done.refs_0_.refs_2_), channel_id=1, source_target_pairs={{0,6},{1,7},{2,0},{3,1},{4,2},{5,3},{6,4},{7,5},{8,14},{9,15},{10,... | collective-permute-start | bytes 786440 | tf_op jit(solution)/shard_map/ppermute | solution.py:40
  15.0 12.6 %collective-permute-start.4 = (f32[2,256,128]{2,1,0:T(8,128)S(1)}, f32[2,256,128]{2,1,0:T(8,128)S(1)}, u32[]{:S(2)}, u32[]{:S(2)}) collective-permute-start(f32[2,256,128]{2,1,0:T(8,128)S(1)} %collective-permute-done.1.refs_1_.refs_8_), channel_id=1, source_target_pairs={{0,2},{1,3},{2,4},{3,5},{4,6},{5,7},{6,0},{7,1},{8,10},{9,11},{10,... | collective-permute-start | bytes 786440 | tf_op jit(solution)/shard_map/ppermute | solution.py:40
  15.7 4.3 %copy-start.10 = (f32[2,256,128]{2,1,0:T(8,128)}, f32[2,256,128]{2,1,0:T(8,128)S(1)}, u32[]{:S(2)}) copy-start(f32[2,256,128]{2,1,0:T(8,128)S(1)} %collective-permute-done.8.refs_2_.refs_5_) | copy-start | bytes 786436
  15.7 11.9 %collective-permute-start.3 = (f32[2,256,128]{2,1,0:T(8,128)S(1)}, f32[2,256,128]{2,1,0:T(8,128)S(1)}, u32[]{:S(2)}, u32[]{:S(2)}) collective-permute-start(f32[2,256,128]{2,1,0:T(8,128)S(1)} %collective-permute-done.1.refs_1_.refs_8_), channel_id=1, source_target_pairs={{0,1},{1,0},{2,3},{3,2},{4,5},{5,4},{6,7},{7,6},{8,9},{9,8},{10,11... | collective-permute-start | bytes 786440 | tf_op jit(solution)/shard_map/ppermute | solution.py:44
  20.0 4.2 %copy-start.11 = (f32[2,256,128]{2,1,0:T(8,128)}, f32[2,256,128]{2,1,0:T(8,128)S(1)}, u32[]{:S(2)}) copy-start(f32[2,256,128]{2,1,0:T(8,128)S(1)} %collective-permute-done.7.refs_1_.refs_9_) | copy-start | bytes 786436
  20.0 4.2 %copy-start.12 = (f32[2,256,128]{2,1,0:T(8,128)}, f32[2,256,128]{2,1,0:T(8,128)S(1)}, u32[]{:S(2)}) copy-start(f32[2,256,128]{2,1,0:T(8,128)S(1)} %collective-permute-done.6.refs_0_.refs_3_) | copy-start | bytes 786436
  20.0 11.8 %collective-permute-start.11 = (f32[2,256,128]{2,1,0:T(8,128)S(1)}, f32[2,256,128]{2,1,0:T(8,128)S(1)}, u32[]{:S(2)}, u32[]{:S(2)}) collective-permute-start(f32[2,256,128]{2,1,0:T(8,128)S(1)} %collective-permute-done.7.refs_1_.refs_9_), channel_id=1, source_target_pairs={{0,2},{1,3},{2,4},{3,5},{4,6},{5,7},{6,0},{7,1},{8,10},{9,11},{10,... | collective-permute-start | bytes 786440 | tf_op jit(solution)/shard_map/ppermute | solution.py:40
  20.5 11.3 %collective-permute-start.10 = (f32[2,256,128]{2,1,0:T(8,128)S(1)}, f32[2,256,128]{2,1,0:T(8,128)S(1)}, u32[]{:S(2)}, u32[]{:S(2)}) collective-permute-start(f32[2,256,128]{2,1,0:T(8,128)S(1)} %collective-permute-done.7.refs_1_.refs_9_), channel_id=1, source_target_pairs={{0,1},{1,0},{2,3},{3,2},{4,5},{5,4},{6,7},{7,6},{8,9},{9,8},{10,11... | collective-permute-start | bytes 786440 | tf_op jit(solution)/shard_map/ppermute | solution.py:44
  21.1 6.5 %copy-start.6 = (f32[2,256,128]{2,1,0:T(8,128)}, f32[2,256,128]{2,1,0:T(8,128)S(1)}, u32[]{:S(2)}) copy-start(f32[2,256,128]{2,1,0:T(8,128)S(1)} %collective-permute-done.5.refs_2_.refs_6_) | copy-start | bytes 786436
  21.1 10.7 %collective-permute-start.12 = (f32[2,256,128]{2,1,0:T(8,128)S(1)}, f32[2,256,128]{2,1,0:T(8,128)S(1)}, u32[]{:S(2)}, u32[]{:S(2)}) collective-permute-start(f32[2,256,128]{2,1,0:T(8,128)S(1)} %collective-permute-done.6.refs_0_.refs_3_), channel_id=1, source_target_pairs={{0,6},{1,7},{2,0},{3,1},{4,2},{5,3},{6,4},{7,5},{8,14},{9,15},{10,... | collective-permute-start | bytes 786440 | tf_op jit(solution)/shard_map/ppermute | solution.py:40
  27.6 0.7 copy-start.13
  27.6 0.8 copy-start.16
  28.4 12.3 %copy-start.7 = (f32[2,256,128]{2,1,0:T(8,128)S(1)}, f32[2,256,128]{2,1,0:T(8,128)}, u32[]{:S(2)}) copy-start(f32[2,256,128]{2,1,0:T(8,128)} %copy-done.6) | copy-start | bytes 786436
  31.8 0.7 copy-start.17
  31.8 0.8 copy-start.14
  31.9 0.8 copy-start.15
  34.5 15.5 %collective-permute-start.15 = (f32[3,256,128]{2,1,0:T(8,128)}, f32[3,256,128]{2,1,0:T(8,128)S(1)}, u32[]{:S(2)}, u32[]{:S(2)}) collective-permute-start(f32[3,256,128]{2,1,0:T(8,128)} %shard_map.41), channel_id=1, source_target_pairs={{12,5},{20,13},{28,21},{36,29},{44,37},{52,45},{60,53},{68,61},{76... | collective-permute-start | bytes 1179656 | tf_op jit(solution)/shard_map/ppermute | solution.py:615
  35.2 14.8 %collective-permute-start.14 = (f32[3,256,128]{2,1,0:T(8,128)}, f32[3,256,128]{2,1,0:T(8,128)S(1)}, u32[]{:S(2)}, u32[]{:S(2)}) collective-permute-start(f32[3,256,128]{2,1,0:T(8,128)} %shard_map.41), channel_id=1, source_target_pairs={{8,0},{9,1},{10,2},{11,3},{12,4},{14,6},{15,7},{16,8},{17,9},{18,1... | collective-permute-start | bytes 1179656 | tf_op jit(solution)/shard_map/ppermute | solution.py:610
  40.6 9.4 %collective-permute-start.13 = (f32[2,256,128]{2,1,0:T(8,128)}, f32[2,256,128]{2,1,0:T(8,128)S(1)}, u32[]{:S(2)}, u32[]{:S(2)}) collective-permute-start(f32[2,256,128]{2,1,0:T(8,128)} %copy-done.15), channel_id=1, source_target_pairs={{0,2},{1,3},{2,4},{3,5},{4,6},{5,7},{6,0},{7,1},{8,10},{9,11},{10,... | collective-permute-start | bytes 786440 | tf_op jit(solution)/shard_map/ppermute | solution.py:40
  40.7 9.3 %collective-permute-start.9 = (f32[2,256,128]{2,1,0:T(8,128)S(1)}, f32[2,256,128]{2,1,0:T(8,128)S(1)}, u32[]{:S(2)}, u32[]{:S(2)}) collective-permute-start(f32[2,256,128]{2,1,0:T(8,128)S(1)} %copy-done.7), channel_id=1, source_target_pairs={{0,6},{1,7},{2,0},{3,1},{4,2},{5,3},{6,4},{7,5},{8,14},{9,15},{10,... | collective-permute-start | bytes 786440 | tf_op jit(solution)/shard_map/ppermute | solution.py:40
  50.0 3.0 %copy-start.22 = (f32[2,256,128]{2,1,0:T(8,128)}, f32[2,256,128]{2,1,0:T(8,128)S(1)}, u32[]{:S(2)}) copy-start(f32[2,256,128]{2,1,0:T(8,128)S(1)} %collective-permute-done.13.refs_1_) | copy-start | bytes 786436
  50.0 3.0 %copy-start.23 = (f32[2,256,128]{2,1,0:T(8,128)}, f32[2,256,128]{2,1,0:T(8,128)S(1)}, u32[]{:S(2)}) copy-start(f32[2,256,128]{2,1,0:T(8,128)S(1)} %collective-permute-done.9.refs_0_) | copy-start | bytes 786436
  50.0 3.0 %copy-start.20 = (f32[3,256,128]{2,1,0:T(8,128)}, f32[3,256,128]{2,1,0:T(8,128)S(1)}, u32[]{:S(2)}) copy-start(f32[3,256,128]{2,1,0:T(8,128)S(1)} %collective-permute-done.15.refs_3_) | copy-start | bytes 1179652
  50.0 3.0 %copy-start.21 = (f32[3,256,128]{2,1,0:T(8,128)}, f32[3,256,128]{2,1,0:T(8,128)S(1)}, u32[]{:S(2)}) copy-start(f32[3,256,128]{2,1,0:T(8,128)S(1)} %collective-permute-done.14.refs_2_) | copy-start | bytes 1179652
  50.0 23.4 %collective-permute-start.17 = (f32[256,1024]{1,0:T(8,128)S(1)}, f32[256,1024]{1,0:T(8,128)S(1)}, u32[]{:S(2)}, u32[]{:S(2)}) collective-permute-start(f32[256,1024]{1,0:T(8,128)S(1)} %slice.19), channel_id=1, source_target_pairs={{8,0},{16,8},{24,16},{32,24},{40,32},{48,40},{56,48},{64,56},{72,6... | collective-permute-start | bytes 3145736 | tf_op jit(solution)/shard_map/ppermute | solution.py:60
  66.5 3.7 %collective-permute-start.16 = (f32[256,256]{1,0:T(8,128)}, f32[256,256]{1,0:T(8,128)S(1)}, u32[]{:S(2)}, u32[]{:S(2)}) collective-permute-start(f32[256,256]{1,0:T(8,128)} %get-tuple-element.110.own.own_transition), channel_id=1, source_target_pairs={{0,8},{8,0},{16,24},{24,16},{32,40},{40,32},{48,56},{56,48},{64,72... | collective-permute-start | bytes 786440 | tf_op jit(solution)/shard_map/ppermute | solution.py:48
  70.2 0.9 copy-start
  71.5 23.3 %collective-permute-start.20 = (f32[256,256]{1,0:T(8,128)S(1)}, f32[256,256]{1,0:T(8,128)S(1)}, u32[]{:S(2)}, u32[]{:S(2)}) collective-permute-start(f32[256,256]{1,0:T(8,128)S(1)} %shard_map.45.refs_0_), channel_id=1, source_target_pairs={{0,48},{8,56},{16,0},{24,8},{32,16},{40,24},{48,32},{56,40},{64,11... | collective-permute-start | bytes 786440 | tf_op jit(solution)/shard_map/ppermute | solution.py:56
  72.5 22.3 %collective-permute-start.19 = (f32[256,256]{1,0:T(8,128)S(1)}, f32[256,256]{1,0:T(8,128)S(1)}, u32[]{:S(2)}, u32[]{:S(2)}) collective-permute-start(f32[256,256]{1,0:T(8,128)S(1)} %shard_map.45.refs_0_), channel_id=1, source_target_pairs={{0,32},{8,40},{16,48},{24,56},{32,0},{40,8},{48,16},{56,24},{64,96... | collective-permute-start | bytes 786440 | tf_op jit(solution)/shard_map/ppermute | solution.py:56
  72.7 22.1 %collective-permute-start.18 = (f32[256,256]{1,0:T(8,128)S(1)}, f32[256,256]{1,0:T(8,128)S(1)}, u32[]{:S(2)}, u32[]{:S(2)}) collective-permute-start(f32[256,256]{1,0:T(8,128)S(1)} %shard_map.45.refs_0_), channel_id=1, source_target_pairs={{0,16},{8,24},{16,32},{24,40},{32,48},{40,56},{48,0},{56,8},{64,80... | collective-permute-start | bytes 786440 | tf_op jit(solution)/shard_map/ppermute | solution.py:56
  73.4 1.0 copy-start.24
  74.4 23.2 %copy-start.1 = (f32[256,256]{1,0:T(8,128)S(1)}, f32[256,256]{1,0:T(8,128)}, u32[]{:S(2)}) copy-start(f32[256,256]{1,0:T(8,128)} %get-tuple-element.110.own.own_transition) | copy-start | bytes 786436
  94.8 36.6 %copy-start.2 = (f32[2048,256]{1,0:T(8,128)S(1)}, f32[2048,256]{1,0:T(8,128)}, u32[]{:S(2)}) copy-start(f32[2048,256]{1,0:T(8,128)} %get-tuple-element.116.response_hbm) | copy-start | bytes 6291460
  94.8 2.8 %collective-permute-start.21 = (f32[256,512]{1,0:T(8,128)}, f32[256,512]{1,0:T(8,128)S(1)}, u32[]{:S(2)}, u32[]{:S(2)}) collective-permute-start(f32[256,512]{1,0:T(8,128)} %get-tuple-element.120), channel_id=1, source_target_pairs={{0,8},{8,0},{16,24},{24,16},{32,40},{40,32},{48,56},{56,48},{64,72... | collective-permute-start | bytes 1572872 | tf_op jit(solution)/shard_map/ppermute | solution.py:48
  97.6 1.0 copy-start.3
  98.7 27.2 %copy-start.4 = (f32[256,512]{1,0:T(8,128)S(1)}, f32[256,512]{1,0:T(8,128)}, u32[]{:S(2)}) copy-start(f32[256,512]{1,0:T(8,128)} %get-tuple-element.117.own) | copy-start | bytes 1572868
  99.2 6.3 %collective-permute-start.22 = (f32[256,128]{1,0:T(8,128)S(1)}, f32[256,128]{1,0:T(8,128)S(1)}, u32[]{:S(2)}, u32[]{:S(2)}) collective-permute-start(f32[256,128]{1,0:T(8,128)S(1)} %get-tuple-element.127), channel_id=1, source_target_pairs={{0,16},{8,24},{16,32},{24,40},{32,48},{40,56},{48,0},{56,8},{64,80... | collective-permute-start | bytes 393224 | tf_op jit(solution)/shard_map/ppermute | solution.py:56
  101.0 8.0 %collective-permute-start.23 = (f32[256,128]{1,0:T(8,128)S(1)}, f32[256,128]{1,0:T(8,128)S(1)}, u32[]{:S(2)}, u32[]{:S(2)}) collective-permute-start(f32[256,128]{1,0:T(8,128)S(1)} %get-tuple-element.128), channel_id=1, source_target_pairs={{0,32},{8,40},{16,48},{24,56},{32,0},{40,8},{48,16},{56,24},{64,96... | collective-permute-start | bytes 393224 | tf_op jit(solution)/shard_map/ppermute | solution.py:56
  102.8 6.3 %collective-permute-start.24 = (f32[256,128]{1,0:T(8,128)S(1)}, f32[256,128]{1,0:T(8,128)S(1)}, u32[]{:S(2)}, u32[]{:S(2)}) collective-permute-start(f32[256,128]{1,0:T(8,128)S(1)} %get-tuple-element.129), channel_id=1, source_target_pairs={{0,48},{8,56},{16,0},{24,8},{32,16},{40,24},{48,32},{56,40},{64,11... | collective-permute-start | bytes 393224 | tf_op jit(solution)/shard_map/ppermute | solution.py:56
  110.0 7.2 %collective-permute-start.25 = (f32[256,128]{1,0:T(8,128)S(1)}, f32[256,128]{1,0:T(8,128)S(1)}, u32[]{:S(2)}, u32[]{:S(2)}) collective-permute-start(f32[256,128]{1,0:T(8,128)S(1)} %get-tuple-element.130), channel_id=1, source_target_pairs={{0,64},{8,72},{16,80},{24,88},{32,96},{40,104},{48,112},{56,120},{... | collective-permute-start | bytes 393224 | tf_op jit(solution)/shard_map/ppermute | solution.py:653
  117.7 5.1 %collective-permute-start.26 = (f32[256,128]{1,0:T(8,128)S(1)}, f32[256,128]{1,0:T(8,128)S(1)}, u32[]{:S(2)}, u32[]{:S(2)}) collective-permute-start(f32[256,128]{1,0:T(8,128)S(1)} %get-tuple-element.134), channel_id=1, source_target_pairs={{0,16},{8,24},{16,32},{24,40},{32,48},{40,56},{48,0},{56,8},{64,80... | collective-permute-start | bytes 393224 | tf_op jit(solution)/shard_map/ppermute | solution.py:56
  117.8 7.4 %collective-permute-start.27 = (f32[256,128]{1,0:T(8,128)S(1)}, f32[256,128]{1,0:T(8,128)S(1)}, u32[]{:S(2)}, u32[]{:S(2)}) collective-permute-start(f32[256,128]{1,0:T(8,128)S(1)} %get-tuple-element.135), channel_id=1, source_target_pairs={{0,32},{8,40},{16,48},{24,56},{32,0},{40,8},{48,16},{56,24},{64,96... | collective-permute-start | bytes 393224 | tf_op jit(solution)/shard_map/ppermute | solution.py:56
  121.4 4.5 %collective-permute-start.28 = (f32[256,128]{1,0:T(8,128)S(1)}, f32[256,128]{1,0:T(8,128)S(1)}, u32[]{:S(2)}, u32[]{:S(2)}) collective-permute-start(f32[256,128]{1,0:T(8,128)S(1)} %get-tuple-element.136), channel_id=1, source_target_pairs={{0,48},{8,56},{16,0},{24,8},{32,16},{40,24},{48,32},{56,40},{64,11... | collective-permute-start | bytes 393224 | tf_op jit(solution)/shard_map/ppermute | solution.py:56
  126.4 5.0 %collective-permute-start.29 = (f32[256,512]{1,0:T(8,128)S(1)}, f32[256,512]{1,0:T(8,128)S(1)}, u32[]{:S(2)}, u32[]{:S(2)}) collective-permute-start(f32[256,512]{1,0:T(8,128)S(1)} %get-tuple-element.138), channel_id=1, source_target_pairs={{0,8},{8,0},{16,24},{24,16},{32,40},{40,32},{48,56},{56,48},{64,72... | collective-permute-start | bytes 1572872 | tf_op jit(solution)/shard_map/ppermute | solution.py:48

commit v6 on v5

--- a/solution.py
+++ b/solution.py
@@ -71,35 +71,42 @@
     return lax.rem(z + dz, Z_SIZE) * 2 + lax.rem(x + dx, 2)
 
 
-def pick_kernel(sources, *refs):
-    pieces, out, sems = refs[:-2], refs[-2], refs[-1]
-    for (dz, dx), where in sources:
+def pick_kernel(keys, cuts, *refs):
+    pieces, outs, sems = refs[: len(keys)], refs[len(keys) : -1], refs[-1]
+    copies = [
+        pltpu.make_async_copy(pieces[keys.index(key)].at[group], out, sems.at[2 + index])
+        for index, ((key, group), out) in enumerate(zip(cuts, outs[1:]))
+    ]
+    for copy in copies:
+        copy.start()
+    for (dz, dx), piece in zip(keys, pieces):
 
         @pl.when(place_of(2 * dz + dx) == 0)
         def _():
-            first, second = pieces[where[0]], pieces[where[1]].at[pl.ds(0, 1)]
-            copies = [
-                pltpu.make_async_copy(first, out.at[pl.ds(0, 2)], sems.at[0]),
-                pltpu.make_async_copy(second, out.at[pl.ds(2, 1)], sems.at[1]),
+            chosen = [
+                pltpu.make_async_copy(piece.at[0], outs[0].at[pl.ds(0, 2)], sems.at[0]),
+                pltpu.make_async_copy(piece.at[1, pl.ds(0, 1)], outs[0].at[pl.ds(2, 1)], sems.at[1]),
             ]
-            for copy in copies:
+            for copy in chosen:
                 copy.start()
-            for copy in copies:
+            for copy in chosen:
                 copy.wait()
 
-
-def pick_first(known):
-    arrays, sources = [], []
-    for key, held in known.items():
-        sources.append((key, tuple(range(len(arrays), len(arrays) + len(held)))))
-        arrays += held
+    for copy in copies:
+        copy.wait()
+
+
+def pick_first(known, cuts):
+    keys = list(known)
+    arrays = [known[key] for key in keys]
+    tail = arrays[0].shape[-2:]
     return pl.pallas_call(
-        functools.partial(pick_kernel, sources),
-        out_shape=jax.ShapeDtypeStruct((3,) + arrays[0].shape[-2:], F32),
+        functools.partial(pick_kernel, keys, cuts),
+        out_shape=tuple(jax.ShapeDtypeStruct((count,) + tail, F32) for count in [3] + [2] * len(cuts)),
         in_specs=[pl.BlockSpec(memory_space=pl.ANY)] * len(arrays),
-        out_specs=pl.BlockSpec(memory_space=pltpu.VMEM),
-        scratch_shapes=[pltpu.SemaphoreType.DMA((2,))],
-        compiler_params=pltpu.CompilerParams(vmem_limit_bytes=VMEM_BYTES),
+        out_specs=tuple(pl.BlockSpec(memory_space=pltpu.VMEM) for _ in range(1 + len(cuts))),
+        scratch_shapes=[pltpu.SemaphoreType.DMA((2 + len(cuts),))],
+        compiler_params=pltpu.CompilerParams(vmem_limit_bytes=16 * 2**20),
     )(*arrays)
 
 
@@ -568,56 +575,37 @@
         jnp.int32, (width, width), 1
     )
     own = jnp.concatenate([jnp.where(below, wy_v[:, :, :width], wy_t), wy_v[:, :, width:]], axis=2)
-    f00, s00 = own[0], own[1]
     above = eigvecs[: 2 * width]
     depth = 2 * width
     shapes = ((own_blocks + 2, 2 * depth, depth), (own_blocks + 1, 2 * depth, depth))
 
-    def add(buffers, group, pieces, keys):
+    def add(buffers, pieces, keys):
         parts = []
         for source, key in enumerate(keys):
-            parts += placed(source, key, (group,), False)
+            parts += placed(source, key)
         return build(buffers, shapes, pieces, parts)
 
-    f01, f30, f10 = across_x(f00), along_z(f00, 1), along_z(f00, -1)
-    s01, s30, s10 = across_x(s00), along_z(s00, 1), along_z(s00, -1)
-    buffers = build(None, shapes, [f00, s00], placed(0, (0, 0), (0,), False) + placed(1, (0, 0), (1,), False))
-    f01, f30, f10, *buffers = together(f01, f30, f10, *buffers)
-    f31, f20, f11 = across_x(f30), along_z(f30, 1), along_z(f01, -1)
-    buffers = add(buffers, 0, [f01, f30, f10], [(0, 1), (3, 0), (1, 0)])
-    s01, s30, s10, *buffers = together(s01, s30, s10, *buffers)
-    s31, s20, s11 = across_x(s30), along_z(s30, 1), along_z(s01, -1)
-    buffers = add(buffers, 1, [s01, s30, s10], [(0, 1), (3, 0), (1, 0)])
-    f31, f20, f11, *buffers = together(f31, f20, f11, *buffers)
-    f21 = along_z(f11, -1)
-    buffers = add(buffers, 0, [f31, f20, f11], [(3, 1), (2, 0), (1, 1)])
-    s31, s20, s11, *buffers = together(s31, s20, s11, *buffers)
-    s21 = along_z(s31, 1)
-    picked = pick_first(
-        {
-            (0, 0): [f00, s00],
-            (0, 1): [f01, s01],
-            (1, 0): [f10, s10],
-            (1, 1): [f11, s11],
-            (3, 0): [f30, s30],
-            (3, 1): [f31, s31],
-            (2, 0): [f20, s20],
-        }
-    )
+    p01, p30, p10 = across_x(own), along_z(own, 1), along_z(own, -1)
+    buffers = add(None, [own], [(0, 0)])
+    p01, p30, p10, *buffers = together(p01, p30, p10, *buffers)
+    p31, p20, p11 = across_x(p30), along_z(p30, 1), along_z(p01, -1)
+    buffers = add(buffers, [p01, p30, p10], [(0, 1), (3, 0), (1, 0)])
+    p31, p20, p11, *buffers = together(p31, p20, p11, *buffers)
+    known = {(0, 0): own, (0, 1): p01, (3, 0): p30, (1, 0): p10, (3, 1): p31, (2, 0): p20, (1, 1): p11}
+    picked, f11, s31 = pick_first(known, [((1, 1), 0), ((3, 1), 1)])
+    f21, s21 = along_z(f11, -1), along_z(s31, 1)
     vecs, rows = lax.axis_size("vec"), lax.axis_size("row")
     late = 5
-    extras = [
-        lax.ppermute(
-            picked,
-            ("row", "vec"),
-            [((i + 1) * vecs + v, i * vecs + v) for i in range(rows - 1) for v in range(vecs) if v != late],
-        ),
-        lax.ppermute(
-            picked, ("row", "vec"), [((i + 1) * vecs + late - 1, i * vecs + late) for i in range(rows - 1)]
-        ),
-    ]
-    buffers = add(buffers, 1, [s31, s20, s11], [(3, 1), (2, 0), (1, 1)])
-    f21, s21, above, extra, late_extra, *buffers = together(f21, s21, above, *extras, *buffers)
+    extra = lax.ppermute(
+        picked,
+        ("row", "vec"),
+        [((i + 1) * vecs + v, i * vecs + v) for i in range(rows - 1) for v in range(vecs) if v != late],
+    )
+    late_extra = lax.ppermute(
+        picked, ("row", "vec"), [((i + 1) * vecs + late - 1, i * vecs + late) for i in range(rows - 1)]
+    )
+    buffers = add(buffers, [p31, p20, p11], [(3, 1), (2, 0), (1, 1)])
+    f21, s21, above, extra, late_extra, *buffers = together(f21, s21, above, extra, late_extra, *buffers)
     tail = from_next_row(above)
     buffers = build(
         buffers,

time: 140 us -> 144 us (1.029)
  waiting for transfers between devices: 21 us -> 35.8 us
  starting transfers between devices: 47.1 us -> 39.3 us
  Pallas kernels: 62.6 us -> 57.6 us
  local copies, waits for them, and re-layouts: 5.98 us -> 7.84 us
    ppermute x10 -> x6, waiting for transfers between devices: 3.59 us -> 18.5 us  [along_z(): return lax.ppermute(value, 'vec', pairs)]
    ppermute x10 -> x6, starting transfers between devices: 14.7 us -> 6.9 us  [along_z(): return lax.ppermute(value, 'vec', pairs)]
    pallas_call x6 -> x4, Pallas kernels: 20.1 us -> 16.3 us  [build(): pl.pallas_call(functools.partial(build_kernel, parts, has_input), out_sha...]
    unnamed x50 -> x42, local copies, waits for them, and re-layouts: 4.66 us -> 6.51 us
    ppermute x4 -> x2, starting transfers between devices: 3.01 us -> 1.83 us  [across_x(): return lax.ppermute(value, 'vec', [(v, v ^ 1) for v in range(2 * Z_SIZE)])]
  transfers between devices with their start and end apart: 30 -> 24, of which waited for: 11 -> 14; matrix products, arithmetic and copies ran while one was open for 1% -> 1% of each run, Pallas kernels for 37% -> 34%
where the time goes in v6:
time: 144 us; the launch traced here: 142 us
  Pallas kernels  57.6 us (40%)
  starting transfers between devices  39.3 us (27%)
  waiting for transfers between devices  35.8 us (25%)
  local copies, waits for them, and re-layouts  7.84 us (5%)
    pallas_call x1, Pallas kernels, sweep_data(): pl.pallas_call(data_kernel, out_shape=(jax.ShapeDtypeStruct((blocks * wid...  20.4 us
    ppermute x6, waiting for transfers between devices, along_z(): return lax.ppermute(value, 'vec', pairs)  18.5 us
    pallas_call x4, Pallas kernels, build(): pl.pallas_call(functools.partial(build_kernel, parts, has_input), out_sha...  16.3 us
    ppermute x9, starting transfers between devices, along_y(): lax.ppermute(value, 'row', [(i, target(i)) for i in range(lax.axis_size('...  12.6 us
    pallas_call x1, Pallas kernels, sweep_units(): pl.pallas_call(unit_kernel, out_shape=(jax.ShapeDtypeStruct((blocks * wid...  9.89 us
    pallas_call x1, Pallas kernels, correct(): pl.pallas_call(functools.partial(correct_kernel, tile), out_shape=jax.Sha...  7.05 us
    ppermute x6, starting transfers between devices, along_z(): return lax.ppermute(value, 'vec', pairs)  6.9 us
    ppermute x9, waiting for transfers between devices, along_y(): lax.ppermute(value, 'row', [(i, target(i)) for i in range(lax.axis_size('...  6.76 us
  transfers between devices with their start and end apart: 24, of which 14 were waited for; matrix products, arithmetic and copies ran while one was open for 1% of the time, Pallas kernels for 34%

profile of v6, /device:TPU:5, one launch (start us, length us, event | category | flops | bytes accessed | tf_op | source)
XLA Modules:
  0.0 142.2 jit_solution(13374324222779883495)
XLA Ops:
  0.0 1.2 slice_select_fusion
  1.2 3.8 %collective-permute-start.2 = (f32[2,2,256,128]{3,2,1,0:T(8,128)S(1)}, f32[2,2,256,128]{3,2,1,0:T(8,128)S(1)}, u32[]{:S(2)}, u32[]{:S(2)}) collective-permute-start(f32[2,2,256,128]{3,2,1,0:T(8,128)S(1)} %pad_maximum_fusion.refs_0_), channel_id=1, source_target_pairs={{0,6},{1,7},{2,0},{3,1},{4,2},{5,3},{6,4},{7,5},{8,14},{9,15},{10,... | collective-permute-start | bytes 1572872 | tf_op jit(solution)/shard_map/ppermute | solution.py:40
  5.1 0.0 collective-permute-start.1
  5.1 0.9 collective-permute-start
  6.0 2.9 %shard_map.37 = (bf16[18,512,256]{2,1,0:T(8,128)(2,1)}, bf16[17,512,256]{2,1,0:T(8,128)(2,1)}) custom-call(f32[2,2,256,128]{3,2,1,0:T(8,128)} %copy-done.3), custom_call_target="tpu_custom_call" | custom-call | flops 1200000000 | bytes 1572864 | tf_op jit(solution)/shard_map/pallas_call | solution.py:168
  8.9 6.8 %collective-permute-done.2.refs_2_.refs_3_ = f32[2,2,256,128]{3,2,1,0:T(8,128)S(1)} collective-permute-done((f32[2,2,256,128]{3,2,1,0:T(8,128)S(1)}, f32[2,2,256,128]{3,2,1,0:T(8,128)S(1)}, u32[]{:S(2)}, u32[]{:S(2)}) %collective-permute-start.2) | collective-permute-done | bytes 524320 | tf_op jit(solution)/shard_map/ppermute | solution.py:40
  15.7 3.1 %collective-permute-done.1.refs_1_.refs_2_ = f32[2,2,256,128]{3,2,1,0:T(8,128)S(1)} collective-permute-done((f32[2,2,256,128]{3,2,1,0:T(8,128)S(1)}, f32[2,2,256,128]{3,2,1,0:T(8,128)S(1)}, u32[]{:S(2)}, u32[]{:S(2)}) %collective-permute-start.1) | collective-permute-done | bytes 524320 | tf_op jit(solution)/shard_map/ppermute | solution.py:40
  18.8 0.0 collective-permute-done.refs_0_.refs_1_
  18.8 1.2 collective-permute-start.5
  19.9 0.4 collective-permute-start.4
  20.3 0.9 collective-permute-start.3
  21.2 4.8 %shard_map.38 = (bf16[18,512,256]{2,1,0:T(8,128)(2,1)}, bf16[17,512,256]{2,1,0:T(8,128)(2,1)}) custom-call(f32[2,2,256,128]{3,2,1,0:T(8,128)} %copy-done.13, f32[2,2,256,128]{3,2,1,0:T(8,128)} %copy-done.10, f32[2,2,256,128]{3,2,1,0:T(8,128)} %copy-done.7, ...), custom_call_target="tpu_custom_call", output_to_operand_aliasing={{0}: (3, {}), {1}: (4, {})} | custom-call | flops 3600000000 | bytes 4718592 | tf_op jit(solution)/shard_map/pallas_call | solution.py:168
  26.1 4.3 %collective-permute-done.5.refs_6_.refs_2_ = f32[2,2,256,128]{3,2,1,0:T(8,128)S(1)} collective-permute-done((f32[2,2,256,128]{3,2,1,0:T(8,128)S(1)}, f32[2,2,256,128]{3,2,1,0:T(8,128)S(1)}, u32[]{:S(2)}, u32[]{:S(2)}) %collective-permute-start.5) | collective-permute-done | bytes 524320 | tf_op jit(solution)/shard_map/ppermute | solution.py:40
  30.4 1.7 %collective-permute-done.4.refs_5_.refs_1_ = f32[2,2,256,128]{3,2,1,0:T(8,128)S(1)} collective-permute-done((f32[2,2,256,128]{3,2,1,0:T(8,128)S(1)}, f32[2,2,256,128]{3,2,1,0:T(8,128)S(1)}, u32[]{:S(2)}, u32[]{:S(2)}) %collective-permute-start.4) | collective-permute-done | bytes 524320 | tf_op jit(solution)/shard_map/ppermute | solution.py:40
  32.1 1.4 copy-done.8
  33.5 1.0 copy-done.11
  34.6 1.0 copy-done.14
  35.6 0.3 shard_map.39
  36.0 0.7 collective-permute-start.9
  36.7 5.3 %collective-permute-start.8 = (f32[3,256,128]{2,1,0:T(8,128)S(1)}, f32[3,256,128]{2,1,0:T(8,128)S(1)}, u32[]{:S(2)}, u32[]{:S(2)}) collective-permute-start(f32[3,256,128]{2,1,0:T(8,128)S(1)} %get-tuple-element.75), channel_id=1, source_target_pairs={{8,0},{9,1},{10,2},{11,3},{12,4},{14,6},{15,7},{16,8},{17,9},{18,1... | collective-permute-start | bytes 1179656 | tf_op jit(solution)/shard_map/ppermute | solution.py:599
  41.9 1.3 slice.11
  43.3 1.3 collective-permute-start.6
  44.6 0.2 collective-permute-start.7
  44.8 4.8 %shard_map.40 = (bf16[18,512,256]{2,1,0:T(8,128)(2,1)}, bf16[17,512,256]{2,1,0:T(8,128)(2,1)}) custom-call(f32[2,2,256,128]{3,2,1,0:T(8,128)} %copy-done.15, f32[2,2,256,128]{3,2,1,0:T(8,128)} %copy-done.12, f32[2,2,256,128]{3,2,1,0:T(8,128)} %copy-done.9, ...), custom_call_target="tpu_custom_call", output_to_operand_aliasing={{0}: (3, {}), {1}: (4, {})} | custom-call | flops 3600000000 | bytes 4718592 | tf_op jit(solution)/shard_map/pallas_call | solution.py:168
  49.6 1.6 %collective-permute-done.6.refs_0_ = f32[2,256,128]{2,1,0:T(8,128)S(1)} collective-permute-done((f32[2,256,128]{2,1,0:T(8,128)S(1)}, f32[2,256,128]{2,1,0:T(8,128)S(1)}, u32[]{:S(2)}, u32[]{:S(2)}) %collective-permute-start.6) | collective-permute-done | bytes 262176 | tf_op jit(solution)/shard_map/ppermute | solution.py:40
  51.3 0.9 collective-permute-done.7.refs_1_
  52.2 0.0 collective-permute-done.9.refs_3_
  52.2 0.0 collective-permute-done.8.refs_2_
  52.2 4.2 %collective-permute-start.11 = (f32[256,1024]{1,0:T(8,128)S(1)}, f32[256,1024]{1,0:T(8,128)S(1)}, u32[]{:S(2)}, u32[]{:S(2)}) collective-permute-start(f32[256,1024]{1,0:T(8,128)S(1)} %slice.11), channel_id=1, source_target_pairs={{8,0},{16,8},{24,16},{32,24},{40,32},{48,40},{56,48},{64,56},{72,6... | collective-permute-start | bytes 3145736 | tf_op jit(solution)/shard_map/ppermute | solution.py:60
  56.5 3.8 %shard_map.41 = (bf16[18,512,256]{2,1,0:T(8,128)(2,1)}, bf16[17,512,256]{2,1,0:T(8,128)(2,1)}) custom-call(f32[2,256,128]{2,1,0:T(8,128)} %copy-done.18, f32[2,256,128]{2,1,0:T(8,128)} %copy-done.19, f32[3,256,128]{2,1,0:T(8,128)} %copy-done.17, f32[3,256,128]{2,1,0:T(8,128)} %copy-done.16, ...), custom_call_target="tpu_custom_call", output_to_operand_aliasing={{0}: (4, {}), {1}: (5, {})} | custom-call | flops 2100000000 | bytes 2752512 | tf_op jit(solution)/shard_map/pallas_call | solution.py:168
  60.3 9.9 %shard_map.42 = (f32[2048,256]{1,0:T(8,128)}, f32[256,256]{1,0:T(8,128)}, f32[256,1024]{1,0:T(8,128)}) custom-call(bf16[18,512,256]{2,1,0:T(8,128)(2,1)} %get-tuple-element.89.first_hbm, bf16[17,512,256]{2,1,0:T(8,128)(2,1)} %get-tuple-element.90.second_hbm, f32[2048,1024]{1,0:T(8,128)} %data_hbm.3), custom_call_target="tpu_custom_call" | custom-call | flops 4831838208 | bytes 31457280 | tf_op jit(solution)/shard_map/pallas_call | solution.py:378
  70.2 2.0 %collective-permute-start.10 = (f32[256,256]{1,0:T(8,128)}, f32[256,256]{1,0:T(8,128)S(1)}, u32[]{:S(2)}, u32[]{:S(2)}) collective-permute-start(f32[256,256]{1,0:T(8,128)} %get-tuple-element.88.own.own_transition), channel_id=1, source_target_pairs={{0,8},{8,0},{16,24},{24,16},{32,40},{40,32},{48,56},{56,48},{64,72... | collective-permute-start | bytes 786440 | tf_op jit(solution)/shard_map/ppermute | solution.py:48
  72.3 1.4 collective-permute-done.10.received.received_transition
  73.6 0.9 copy-done
  74.6 0.3 shard_map.43.refs_0_
  74.9 1.3 collective-permute-start.14
  76.2 0.3 collective-permute-start.13
  76.5 0.7 collective-permute-start.12
  77.2 1.0 copy-done.20
  78.1 20.4 %shard_map.44 = (f32[2048,1024]{1,0:T(8,128)}, f32[256,512]{1,0:T(8,128)}, f32[256,512]{1,0:T(8,128)}) custom-call(bf16[18,512,256]{2,1,0:T(8,128)(2,1)} %get-tuple-element.89.first_hbm, bf16[17,512,256]{2,1,0:T(8,128)(2,1)} %get-tuple-element.90.second_hbm, f32[2048,1024]{1,0:T(8,128)} %data_hbm.3, f32[256,1024]{1,0:T(8,128)} %copy-done.20, ...), custom_call_target="tpu_custom_call" | custom-call | flops 12884901888 | bytes 31457280 | tf_op jit(solution)/shard_map/pallas_call | solution.py:407
  98.6 0.0 collective-permute-done.12.refs_1_
  98.6 1.1 collective-permute-start.15
  99.7 1.7 %collective-permute-done.15.received = f32[256,512]{1,0:T(8,128)S(1)} collective-permute-done((f32[256,512]{1,0:T(8,128)}, f32[256,512]{1,0:T(8,128)S(1)}, u32[]{:S(2)}, u32[]{:S(2)}) %collective-permute-start.15) | collective-permute-done | bytes 524320 | tf_op jit(solution)/shard_map/ppermute | solution.py:48
  101.4 1.0 copy-done.5
  102.5 0.6 shard_map.46
  103.0 1.8 %collective-permute-start.16 = (f32[256,128]{1,0:T(8,128)S(1)}, f32[256,128]{1,0:T(8,128)S(1)}, u32[]{:S(2)}, u32[]{:S(2)}) collective-permute-start(f32[256,128]{1,0:T(8,128)S(1)} %get-tuple-element.105), channel_id=1, source_target_pairs={{0,16},{8,24},{16,32},{24,40},{32,48},{40,56},{48,0},{56,8},{64,80... | collective-permute-start | bytes 393224 | tf_op jit(solution)/shard_map/ppermute | solution.py:56
  104.8 1.5 %collective-permute-start.17 = (f32[256,128]{1,0:T(8,128)S(1)}, f32[256,128]{1,0:T(8,128)S(1)}, u32[]{:S(2)}, u32[]{:S(2)}) collective-permute-start(f32[256,128]{1,0:T(8,128)S(1)} %get-tuple-element.106), channel_id=1, source_target_pairs={{0,32},{8,40},{16,48},{24,56},{32,0},{40,8},{48,16},{56,24},{64,96... | collective-permute-start | bytes 393224 | tf_op jit(solution)/shard_map/ppermute | solution.py:56
  106.3 2.0 %collective-permute-start.18 = (f32[256,128]{1,0:T(8,128)S(1)}, f32[256,128]{1,0:T(8,128)S(1)}, u32[]{:S(2)}, u32[]{:S(2)}) collective-permute-start(f32[256,128]{1,0:T(8,128)S(1)} %get-tuple-element.107), channel_id=1, source_target_pairs={{0,48},{8,56},{16,0},{24,8},{32,16},{40,24},{48,32},{56,40},{64,11... | collective-permute-start | bytes 393224 | tf_op jit(solution)/shard_map/ppermute | solution.py:56
  108.2 0.8 shard_map.45
  109.0 3.3 %collective-permute-done.17.refs_2_ = f32[256,128]{1,0:T(8,128)S(1)} collective-permute-done((f32[256,128]{1,0:T(8,128)S(1)}, f32[256,128]{1,0:T(8,128)S(1)}, u32[]{:S(2)}, u32[]{:S(2)}) %collective-permute-start.17) | collective-permute-done | bytes 131104 | tf_op jit(solution)/shard_map/ppermute | solution.py:56
  112.3 0.9 shard_map.47
  113.2 1.3 collective-permute-start.19
  114.5 5.9 %collective-permute-done.19.entering = f32[256,128]{1,0:T(8,128)S(1)} collective-permute-done((f32[256,128]{1,0:T(8,128)S(1)}, f32[256,128]{1,0:T(8,128)S(1)}, u32[]{:S(2)}, u32[]{:S(2)}) %collective-permute-start.19) | collective-permute-done | bytes 131104 | tf_op jit(solution)/shard_map/ppermute | solution.py:641
  120.4 0.5 shard_map.48
  121.0 0.8 collective-permute-start.20
  121.8 3.3 %collective-permute-start.21 = (f32[256,128]{1,0:T(8,128)S(1)}, f32[256,128]{1,0:T(8,128)S(1)}, u32[]{:S(2)}, u32[]{:S(2)}) collective-permute-start(f32[256,128]{1,0:T(8,128)S(1)} %get-tuple-element.113), channel_id=1, source_target_pairs={{0,32},{8,40},{16,48},{24,56},{32,0},{40,8},{48,16},{56,24},{64,96... | collective-permute-start | bytes 393224 | tf_op jit(solution)/shard_map/ppermute | solution.py:56
  125.0 1.0 collective-permute-start.22
  126.1 0.1 collective-permute-done.20.refs_1_
  126.2 2.7 %collective-permute-done.21.refs_2_ = f32[256,128]{1,0:T(8,128)S(1)} collective-permute-done((f32[256,128]{1,0:T(8,128)S(1)}, f32[256,128]{1,0:T(8,128)S(1)}, u32[]{:S(2)}, u32[]{:S(2)}) %collective-permute-start.21) | collective-permute-done | bytes 131104 | tf_op jit(solution)/shard_map/ppermute | solution.py:56
  128.9 0.7 collective-permute-done.22.refs_3_
  129.5 0.5 shard_map.49
  130.1 3.4 %collective-permute-start.23 = (f32[256,512]{1,0:T(8,128)S(1)}, f32[256,512]{1,0:T(8,128)S(1)}, u32[]{:S(2)}, u32[]{:S(2)}) collective-permute-start(f32[256,512]{1,0:T(8,128)S(1)} %get-tuple-element.116), channel_id=1, source_target_pairs={{0,8},{8,0},{16,24},{24,16},{32,40},{40,32},{48,56},{56,48},{64,72... | collective-permute-start | bytes 1572872 | tf_op jit(solution)/shard_map/ppermute | solution.py:48
  133.5 1.5 %collective-permute-done.23.taken = f32[256,512]{1,0:T(8,128)S(1)} collective-permute-done((f32[256,512]{1,0:T(8,128)S(1)}, f32[256,512]{1,0:T(8,128)S(1)}, u32[]{:S(2)}, u32[]{:S(2)}) %collective-permute-start.23) | collective-permute-done | bytes 524320 | tf_op jit(solution)/shard_map/ppermute | solution.py:48
  135.0 7.1 %shard_map.50 = f32[2048,1024]{1,0:T(8,128)} custom-call(f32[2048,1024]{1,0:T(8,128)} %get-tuple-element.93.rows_hbm, f32[2048,256]{1,0:T(8,128)S(1)} %copy-done.2, f32[256,512]{1,0:T(8,128)S(1)} %get-tuple-element.115.kept, f32[256,512]{1,0:T(8,128)S(1)} %collective-permute-done.23.taken), custom_call_target="tpu_custom_call" | custom-call | tf_op jit(solution)/shard_map/pallas_call | solution.py:554
  (44 shorter events, 0.1 us)
Async XLA Ops:
  1.2 4.8 %copy-start.3 = (f32[2,2,256,128]{3,2,1,0:T(8,128)}, f32[2,2,256,128]{3,2,1,0:T(8,128)S(1)}, u32[]{:S(2)}) copy-start(f32[2,2,256,128]{3,2,1,0:T(8,128)S(1)} %pad_maximum_fusion.refs_0_) | copy-start | bytes 1572868
  1.2 14.4 %collective-permute-start.2 = (f32[2,2,256,128]{3,2,1,0:T(8,128)S(1)}, f32[2,2,256,128]{3,2,1,0:T(8,128)S(1)}, u32[]{:S(2)}, u32[]{:S(2)}) collective-permute-start(f32[2,2,256,128]{3,2,1,0:T(8,128)S(1)} %pad_maximum_fusion.refs_0_), channel_id=1, source_target_pairs={{0,6},{1,7},{2,0},{3,1},{4,2},{5,3},{6,4},{7,5},{8,14},{9,15},{10,... | collective-permute-start | bytes 1572872 | tf_op jit(solution)/shard_map/ppermute | solution.py:40
  5.1 13.7 %collective-permute-start.1 = (f32[2,2,256,128]{3,2,1,0:T(8,128)S(1)}, f32[2,2,256,128]{3,2,1,0:T(8,128)S(1)}, u32[]{:S(2)}, u32[]{:S(2)}) collective-permute-start(f32[2,2,256,128]{3,2,1,0:T(8,128)S(1)} %pad_maximum_fusion.refs_0_), channel_id=1, source_target_pairs={{0,2},{1,3},{2,4},{3,5},{4,6},{5,7},{6,0},{7,1},{8,10},{9,11},{10,... | collective-permute-start | bytes 1572872 | tf_op jit(solution)/shard_map/ppermute | solution.py:40
  5.1 13.7 %collective-permute-start = (f32[2,2,256,128]{3,2,1,0:T(8,128)S(1)}, f32[2,2,256,128]{3,2,1,0:T(8,128)S(1)}, u32[]{:S(2)}, u32[]{:S(2)}) collective-permute-start(f32[2,2,256,128]{3,2,1,0:T(8,128)S(1)} %pad_maximum_fusion.refs_0_), channel_id=1, source_target_pairs={{0,1},{1,0},{2,3},{3,2},{4,5},{5,4},{6,7},{7,6},{8,9},{9,8},{10,11... | collective-permute-start | bytes 1572872 | tf_op jit(solution)/shard_map/ppermute | solution.py:44
  15.7 5.6 %copy-start.7 = (f32[2,2,256,128]{3,2,1,0:T(8,128)}, f32[2,2,256,128]{3,2,1,0:T(8,128)S(1)}, u32[]{:S(2)}) copy-start(f32[2,2,256,128]{3,2,1,0:T(8,128)S(1)} %collective-permute-done.2.refs_2_.refs_3_) | copy-start | bytes 1572868
  18.8 2.5 %copy-start.10 = (f32[2,2,256,128]{3,2,1,0:T(8,128)}, f32[2,2,256,128]{3,2,1,0:T(8,128)S(1)}, u32[]{:S(2)}) copy-start(f32[2,2,256,128]{3,2,1,0:T(8,128)S(1)} %collective-permute-done.1.refs_1_.refs_2_) | copy-start | bytes 1572868
  18.8 2.5 %copy-start.13 = (f32[2,2,256,128]{3,2,1,0:T(8,128)}, f32[2,2,256,128]{3,2,1,0:T(8,128)S(1)}, u32[]{:S(2)}) copy-start(f32[2,2,256,128]{3,2,1,0:T(8,128)S(1)} %collective-permute-done.refs_0_.refs_1_) | copy-start | bytes 1572868
  18.8 13.4 %copy-start.4 = (f32[2,2,256,128]{3,2,1,0:T(8,128)S(1)}, f32[2,2,256,128]{3,2,1,0:T(8,128)}, u32[]{:S(2)}) copy-start(f32[2,2,256,128]{3,2,1,0:T(8,128)} %copy-done.3) | copy-start | bytes 1572868
  18.8 11.6 %collective-permute-start.5 = (f32[2,2,256,128]{3,2,1,0:T(8,128)S(1)}, f32[2,2,256,128]{3,2,1,0:T(8,128)S(1)}, u32[]{:S(2)}, u32[]{:S(2)}) collective-permute-start(f32[2,2,256,128]{3,2,1,0:T(8,128)S(1)} %collective-permute-done.refs_0_.refs_1_), channel_id=1, source_target_pairs={{0,6},{1,7},{2,0},{3,1},{4,2},{5,3},{6,4},{7,5},{8,14},{9,15},{10,... | collective-permute-start | bytes 1572872 | tf_op jit(solution)/shard_map/ppermute | solution.py:40
  19.9 12.2 %collective-permute-start.4 = (f32[2,2,256,128]{3,2,1,0:T(8,128)S(1)}, f32[2,2,256,128]{3,2,1,0:T(8,128)S(1)}, u32[]{:S(2)}, u32[]{:S(2)}) collective-permute-start(f32[2,2,256,128]{3,2,1,0:T(8,128)S(1)} %collective-permute-done.1.refs_1_.refs_2_), channel_id=1, source_target_pairs={{0,2},{1,3},{2,4},{3,5},{4,6},{5,7},{6,0},{7,1},{8,10},{9,11},{10,... | collective-permute-start | bytes 1572872 | tf_op jit(solution)/shard_map/ppermute | solution.py:40
  20.3 11.8 %collective-permute-start.3 = (f32[2,2,256,128]{3,2,1,0:T(8,128)S(1)}, f32[2,2,256,128]{3,2,1,0:T(8,128)S(1)}, u32[]{:S(2)}, u32[]{:S(2)}) collective-permute-start(f32[2,2,256,128]{3,2,1,0:T(8,128)S(1)} %collective-permute-done.1.refs_1_.refs_2_), channel_id=1, source_target_pairs={{0,1},{1,0},{2,3},{3,2},{4,5},{5,4},{6,7},{7,6},{8,9},{9,8},{10,11... | collective-permute-start | bytes 1572872 | tf_op jit(solution)/shard_map/ppermute | solution.py:44
  30.4 14.4 %copy-start.9 = (f32[2,2,256,128]{3,2,1,0:T(8,128)}, f32[2,2,256,128]{3,2,1,0:T(8,128)S(1)}, u32[]{:S(2)}) copy-start(f32[2,2,256,128]{3,2,1,0:T(8,128)S(1)} %collective-permute-done.5.refs_6_.refs_2_) | copy-start | bytes 1572868
  32.1 12.7 %copy-start.12 = (f32[2,2,256,128]{3,2,1,0:T(8,128)}, f32[2,2,256,128]{3,2,1,0:T(8,128)S(1)}, u32[]{:S(2)}) copy-start(f32[2,2,256,128]{3,2,1,0:T(8,128)S(1)} %collective-permute-done.4.refs_5_.refs_1_) | copy-start | bytes 1572868
  32.1 12.7 %copy-start.15 = (f32[2,2,256,128]{3,2,1,0:T(8,128)}, f32[2,2,256,128]{3,2,1,0:T(8,128)S(1)}, u32[]{:S(2)}) copy-start(f32[2,2,256,128]{3,2,1,0:T(8,128)S(1)} %collective-permute-done.3.refs_4_.refs_0_) | copy-start | bytes 1572868
  32.1 1.4 copy-start.8
  33.5 1.0 copy-start.11
  34.6 1.0 copy-start.14
  36.0 16.3 %collective-permute-start.9 = (f32[3,256,128]{2,1,0:T(8,128)S(1)}, f32[3,256,128]{2,1,0:T(8,128)S(1)}, u32[]{:S(2)}, u32[]{:S(2)}) collective-permute-start(f32[3,256,128]{2,1,0:T(8,128)S(1)} %get-tuple-element.75), channel_id=1, source_target_pairs={{12,5},{20,13},{28,21},{36,29},{44,37},{52,45},{60,53},{68,61},{76... | collective-permute-start | bytes 1179656 | tf_op jit(solution)/shard_map/ppermute | solution.py:604
  36.7 15.6 %collective-permute-start.8 = (f32[3,256,128]{2,1,0:T(8,128)S(1)}, f32[3,256,128]{2,1,0:T(8,128)S(1)}, u32[]{:S(2)}, u32[]{:S(2)}) collective-permute-start(f32[3,256,128]{2,1,0:T(8,128)S(1)} %get-tuple-element.75), channel_id=1, source_target_pairs={{8,0},{9,1},{10,2},{11,3},{12,4},{14,6},{15,7},{16,8},{17,9},{18,1... | collective-permute-start | bytes 1179656 | tf_op jit(solution)/shard_map/ppermute | solution.py:599
  43.3 8.0 %collective-permute-start.6 = (f32[2,256,128]{2,1,0:T(8,128)S(1)}, f32[2,256,128]{2,1,0:T(8,128)S(1)}, u32[]{:S(2)}, u32[]{:S(2)}) collective-permute-start(f32[2,256,128]{2,1,0:T(8,128)S(1)} %get-tuple-element.73), channel_id=1, source_target_pairs={{0,6},{1,7},{2,0},{3,1},{4,2},{5,3},{6,4},{7,5},{8,14},{9,15},{10,... | collective-permute-start | bytes 786440 | tf_op jit(solution)/shard_map/ppermute | solution.py:40
  44.6 7.6 %collective-permute-start.7 = (f32[2,256,128]{2,1,0:T(8,128)S(1)}, f32[2,256,128]{2,1,0:T(8,128)S(1)}, u32[]{:S(2)}, u32[]{:S(2)}) collective-permute-start(f32[2,256,128]{2,1,0:T(8,128)S(1)} %get-tuple-element.74), channel_id=1, source_target_pairs={{0,2},{1,3},{2,4},{3,5},{4,6},{5,7},{6,0},{7,1},{8,10},{9,11},{10,... | collective-permute-start | bytes 786440 | tf_op jit(solution)/shard_map/ppermute | solution.py:40
  51.3 5.2 %copy-start.18 = (f32[2,256,128]{2,1,0:T(8,128)}, f32[2,256,128]{2,1,0:T(8,128)S(1)}, u32[]{:S(2)}) copy-start(f32[2,256,128]{2,1,0:T(8,128)S(1)} %collective-permute-done.6.refs_0_) | copy-start | bytes 786436
  52.2 4.3 %copy-start.19 = (f32[2,256,128]{2,1,0:T(8,128)}, f32[2,256,128]{2,1,0:T(8,128)S(1)}, u32[]{:S(2)}) copy-start(f32[2,256,128]{2,1,0:T(8,128)S(1)} %collective-permute-done.7.refs_1_) | copy-start | bytes 786436
  52.2 4.3 %copy-start.16 = (f32[3,256,128]{2,1,0:T(8,128)}, f32[3,256,128]{2,1,0:T(8,128)S(1)}, u32[]{:S(2)}) copy-start(f32[3,256,128]{2,1,0:T(8,128)S(1)} %collective-permute-done.9.refs_3_) | copy-start | bytes 1179652
  52.2 4.3 %copy-start.17 = (f32[3,256,128]{2,1,0:T(8,128)}, f32[3,256,128]{2,1,0:T(8,128)S(1)}, u32[]{:S(2)}) copy-start(f32[3,256,128]{2,1,0:T(8,128)S(1)} %collective-permute-done.8.refs_2_) | copy-start | bytes 1179652
  52.2 24.9 %collective-permute-start.11 = (f32[256,1024]{1,0:T(8,128)S(1)}, f32[256,1024]{1,0:T(8,128)S(1)}, u32[]{:S(2)}, u32[]{:S(2)}) collective-permute-start(f32[256,1024]{1,0:T(8,128)S(1)} %slice.11), channel_id=1, source_target_pairs={{8,0},{16,8},{24,16},{32,24},{40,32},{48,40},{56,48},{64,56},{72,6... | collective-permute-start | bytes 3145736 | tf_op jit(solution)/shard_map/ppermute | solution.py:60
  70.2 3.4 %collective-permute-start.10 = (f32[256,256]{1,0:T(8,128)}, f32[256,256]{1,0:T(8,128)S(1)}, u32[]{:S(2)}, u32[]{:S(2)}) collective-permute-start(f32[256,256]{1,0:T(8,128)} %get-tuple-element.88.own.own_transition), channel_id=1, source_target_pairs={{0,8},{8,0},{16,24},{24,16},{32,40},{40,32},{48,56},{56,48},{64,72... | collective-permute-start | bytes 786440 | tf_op jit(solution)/shard_map/ppermute | solution.py:48
  73.6 0.9 copy-start
  74.9 23.7 %collective-permute-start.14 = (f32[256,256]{1,0:T(8,128)S(1)}, f32[256,256]{1,0:T(8,128)S(1)}, u32[]{:S(2)}, u32[]{:S(2)}) collective-permute-start(f32[256,256]{1,0:T(8,128)S(1)} %shard_map.43.refs_0_), channel_id=1, source_target_pairs={{0,48},{8,56},{16,0},{24,8},{32,16},{40,24},{48,32},{56,40},{64,11... | collective-permute-start | bytes 786440 | tf_op jit(solution)/shard_map/ppermute | solution.py:56
  76.2 22.4 %collective-permute-start.13 = (f32[256,256]{1,0:T(8,128)S(1)}, f32[256,256]{1,0:T(8,128)S(1)}, u32[]{:S(2)}, u32[]{:S(2)}) collective-permute-start(f32[256,256]{1,0:T(8,128)S(1)} %shard_map.43.refs_0_), channel_id=1, source_target_pairs={{0,32},{8,40},{16,48},{24,56},{32,0},{40,8},{48,16},{56,24},{64,96... | collective-permute-start | bytes 786440 | tf_op jit(solution)/shard_map/ppermute | solution.py:56
  76.5 22.1 %collective-permute-start.12 = (f32[256,256]{1,0:T(8,128)S(1)}, f32[256,256]{1,0:T(8,128)S(1)}, u32[]{:S(2)}, u32[]{:S(2)}) collective-permute-start(f32[256,256]{1,0:T(8,128)S(1)} %shard_map.43.refs_0_), channel_id=1, source_target_pairs={{0,16},{8,24},{16,32},{24,40},{32,48},{40,56},{48,0},{56,8},{64,80... | collective-permute-start | bytes 786440 | tf_op jit(solution)/shard_map/ppermute | solution.py:56
  77.2 1.0 copy-start.20
  78.1 23.3 %copy-start.1 = (f32[256,256]{1,0:T(8,128)S(1)}, f32[256,256]{1,0:T(8,128)}, u32[]{:S(2)}) copy-start(f32[256,256]{1,0:T(8,128)} %get-tuple-element.88.own.own_transition) | copy-start | bytes 786436
  98.6 36.4 %copy-start.2 = (f32[2048,256]{1,0:T(8,128)S(1)}, f32[2048,256]{1,0:T(8,128)}, u32[]{:S(2)}) copy-start(f32[2048,256]{1,0:T(8,128)} %get-tuple-element.94.response_hbm) | copy-start | bytes 6291460
  98.6 2.8 %collective-permute-start.15 = (f32[256,512]{1,0:T(8,128)}, f32[256,512]{1,0:T(8,128)S(1)}, u32[]{:S(2)}, u32[]{:S(2)}) collective-permute-start(f32[256,512]{1,0:T(8,128)} %get-tuple-element.98), channel_id=1, source_target_pairs={{0,8},{8,0},{16,24},{24,16},{32,40},{40,32},{48,56},{56,48},{64,72... | collective-permute-start | bytes 1572872 | tf_op jit(solution)/shard_map/ppermute | solution.py:48
  101.4 1.0 copy-start.5
  102.5 27.1 %copy-start.6 = (f32[256,512]{1,0:T(8,128)S(1)}, f32[256,512]{1,0:T(8,128)}, u32[]{:S(2)}) copy-start(f32[256,512]{1,0:T(8,128)} %get-tuple-element.95.own) | copy-start | bytes 1572868
  103.0 6.0 %collective-permute-start.16 = (f32[256,128]{1,0:T(8,128)S(1)}, f32[256,128]{1,0:T(8,128)S(1)}, u32[]{:S(2)}, u32[]{:S(2)}) collective-permute-start(f32[256,128]{1,0:T(8,128)S(1)} %get-tuple-element.105), channel_id=1, source_target_pairs={{0,16},{8,24},{16,32},{24,40},{32,48},{40,56},{48,0},{56,8},{64,80... | collective-permute-start | bytes 393224 | tf_op jit(solution)/shard_map/ppermute | solution.py:56
  104.8 7.5 %collective-permute-start.17 = (f32[256,128]{1,0:T(8,128)S(1)}, f32[256,128]{1,0:T(8,128)S(1)}, u32[]{:S(2)}, u32[]{:S(2)}) collective-permute-start(f32[256,128]{1,0:T(8,128)S(1)} %get-tuple-element.106), channel_id=1, source_target_pairs={{0,32},{8,40},{16,48},{24,56},{32,0},{40,8},{48,16},{56,24},{64,96... | collective-permute-start | bytes 393224 | tf_op jit(solution)/shard_map/ppermute | solution.py:56
  106.3 6.0 %collective-permute-start.18 = (f32[256,128]{1,0:T(8,128)S(1)}, f32[256,128]{1,0:T(8,128)S(1)}, u32[]{:S(2)}, u32[]{:S(2)}) collective-permute-start(f32[256,128]{1,0:T(8,128)S(1)} %get-tuple-element.107), channel_id=1, source_target_pairs={{0,48},{8,56},{16,0},{24,8},{32,16},{40,24},{48,32},{56,40},{64,11... | collective-permute-start | bytes 393224 | tf_op jit(solution)/shard_map/ppermute | solution.py:56
  113.2 7.2 %collective-permute-start.19 = (f32[256,128]{1,0:T(8,128)S(1)}, f32[256,128]{1,0:T(8,128)S(1)}, u32[]{:S(2)}, u32[]{:S(2)}) collective-permute-start(f32[256,128]{1,0:T(8,128)S(1)} %get-tuple-element.108), channel_id=1, source_target_pairs={{0,64},{8,72},{16,80},{24,88},{32,96},{40,104},{48,112},{56,120},{... | collective-permute-start | bytes 393224 | tf_op jit(solution)/shard_map/ppermute | solution.py:641
  121.0 5.2 %collective-permute-start.20 = (f32[256,128]{1,0:T(8,128)S(1)}, f32[256,128]{1,0:T(8,128)S(1)}, u32[]{:S(2)}, u32[]{:S(2)}) collective-permute-start(f32[256,128]{1,0:T(8,128)S(1)} %get-tuple-element.112), channel_id=1, source_target_pairs={{0,16},{8,24},{16,32},{24,40},{32,48},{40,56},{48,0},{56,8},{64,80... | collective-permute-start | bytes 393224 | tf_op jit(solution)/shard_map/ppermute | solution.py:56
  121.8 7.1 %collective-permute-start.21 = (f32[256,128]{1,0:T(8,128)S(1)}, f32[256,128]{1,0:T(8,128)S(1)}, u32[]{:S(2)}, u32[]{:S(2)}) collective-permute-start(f32[256,128]{1,0:T(8,128)S(1)} %get-tuple-element.113), channel_id=1, source_target_pairs={{0,32},{8,40},{16,48},{24,56},{32,0},{40,8},{48,16},{56,24},{64,96... | collective-permute-start | bytes 393224 | tf_op jit(solution)/shard_map/ppermute | solution.py:56
  125.0 4.5 %collective-permute-start.22 = (f32[256,128]{1,0:T(8,128)S(1)}, f32[256,128]{1,0:T(8,128)S(1)}, u32[]{:S(2)}, u32[]{:S(2)}) collective-permute-start(f32[256,128]{1,0:T(8,128)S(1)} %get-tuple-element.114), channel_id=1, source_target_pairs={{0,48},{8,56},{16,0},{24,8},{32,16},{40,24},{48,32},{56,40},{64,11... | collective-permute-start | bytes 393224 | tf_op jit(solution)/shard_map/ppermute | solution.py:56
  130.1 4.9 %collective-permute-start.23 = (f32[256,512]{1,0:T(8,128)S(1)}, f32[256,512]{1,0:T(8,128)S(1)}, u32[]{:S(2)}, u32[]{:S(2)}) collective-permute-start(f32[256,512]{1,0:T(8,128)S(1)} %get-tuple-element.116), channel_id=1, source_target_pairs={{0,8},{8,0},{16,24},{24,16},{32,40},{40,32},{48,56},{56,48},{64,72... | collective-permute-start | bytes 1572872 | tf_op jit(solution)/shard_map/ppermute | solution.py:48

commit v7 on v5

--- a/solution.py
+++ b/solution.py
@@ -71,36 +71,43 @@
     return lax.rem(z + dz, Z_SIZE) * 2 + lax.rem(x + dx, 2)
 
 
-def pick_kernel(sources, *refs):
-    pieces, out, sems = refs[:-2], refs[-2], refs[-1]
-    for (dz, dx), where in sources:
+def pick_kernel(sources, rows, *refs):
+    pieces, out, above, sems = refs[:-3], refs[-3], refs[-2], refs[-1]
+    head = pltpu.make_async_copy(rows.at[pl.ds(0, above.shape[0])], above, sems.at[2])
+    head.start()
+    for (dz, dx), (first, second) in sources:
 
         @pl.when(place_of(2 * dz + dx) == 0)
         def _():
-            first, second = pieces[where[0]], pieces[where[1]].at[pl.ds(0, 1)]
             copies = [
-                pltpu.make_async_copy(first, out.at[pl.ds(0, 2)], sems.at[0]),
-                pltpu.make_async_copy(second, out.at[pl.ds(2, 1)], sems.at[1]),
+                pltpu.make_async_copy(pieces[first], out.at[pl.ds(0, 2)], sems.at[0]),
+                pltpu.make_async_copy(pieces[second].at[pl.ds(0, 1)], out.at[pl.ds(2, 1)], sems.at[1]),
             ]
             for copy in copies:
                 copy.start()
             for copy in copies:
                 copy.wait()
 
-
-def pick_first(known):
+    head.wait()
+
+
+def pick_first(rows, known):
     arrays, sources = [], []
     for key, held in known.items():
-        sources.append((key, tuple(range(len(arrays), len(arrays) + len(held)))))
+        sources.append((key, (len(arrays), len(arrays) + 1)))
         arrays += held
+    depth, width = arrays[0].shape[-2:]
     return pl.pallas_call(
         functools.partial(pick_kernel, sources),
-        out_shape=jax.ShapeDtypeStruct((3,) + arrays[0].shape[-2:], F32),
-        in_specs=[pl.BlockSpec(memory_space=pl.ANY)] * len(arrays),
-        out_specs=pl.BlockSpec(memory_space=pltpu.VMEM),
-        scratch_shapes=[pltpu.SemaphoreType.DMA((2,))],
+        out_shape=(
+            jax.ShapeDtypeStruct((3, depth, width), F32),
+            jax.ShapeDtypeStruct((depth, rows.shape[1]), F32),
+        ),
+        in_specs=[pl.BlockSpec(memory_space=pl.ANY)] * (1 + len(arrays)),
+        out_specs=(pl.BlockSpec(memory_space=pltpu.VMEM),) * 2,
+        scratch_shapes=[pltpu.SemaphoreType.DMA((3,))],
         compiler_params=pltpu.CompilerParams(vmem_limit_bytes=VMEM_BYTES),
-    )(*arrays)
+    )(rows, *arrays)
 
 
 def build_reflection(packed):
@@ -311,8 +318,9 @@
 
     @pl.when(jnp.logical_not(is_first))
     def _():
-        for m in range(granules):
-            start_all(first_copies(m) + second_copies(m))
+        for m in range(1, granules):
+            start_all(first_copies(m) + second_copies(m - 1))
+        start_all(second_copies(granules - 1))
         rows = lax.broadcasted_iota(jnp.int32, (width, width), 0)
         cols = lax.broadcasted_iota(jnp.int32, (width, width), 1)
         eye = jnp.where(rows == cols, 1.0, 0.0)
@@ -321,7 +329,7 @@
         second_state[...] = jnp.concatenate([zeros, eye], axis=1)
         between[...] = jnp.zeros_like(between)
         initial[...] = jnp.zeros_like(initial)
-        wait_all(first_copies(0) + second_copies(0))
+        wait_all(second_copies(0))
         run_sweep(
             first, second, None, first_state, second_state, between, result, out, first_copies, second_copies, sems
         )
@@ -337,11 +345,13 @@
     first_copies, second_copies = sweep_copies(
         first_hbm, second_hbm, data_hbm, tail_hbm, first, second, data, sems
     )
-    for m in range(first.shape[0] // 2):
-        start_all(first_copies(m) + second_copies(m))
+    granules = first.shape[0] // 2
+    for m in range(1, granules):
+        start_all(first_copies(m) + second_copies(m - 1))
+    start_all(second_copies(granules - 1))
     first_state[...] = initial[:width]
     second_state[...] = initial[width:]
-    wait_all(first_copies(0) + second_copies(0))
+    wait_all(second_copies(0))
     run_sweep(first, second, data, first_state, second_state, between, result, out, first_copies, second_copies, sems)
     half = own_state.shape[1]
     core = lax.rem(lax.axis_index("row"), 2)
@@ -388,7 +398,7 @@
             pltpu.VMEM((blocks * width, depth), F32),
             pltpu.SemaphoreType.DMA((4, blocks)),
         ],
-        compiler_params=PARAMS,
+        compiler_params=pltpu.CompilerParams(vmem_limit_bytes=50 * 2**20),
         cost_estimate=estimate(blocks, depth, 3 * depth),
     )(first, second, data)
 
@@ -416,7 +426,7 @@
             pltpu.VMEM((blocks * width, cols), F32),
             pltpu.SemaphoreType.DMA((4, blocks)),
         ],
-        compiler_params=PARAMS,
+        compiler_params=pltpu.CompilerParams(vmem_limit_bytes=50 * 2**20),
         cost_estimate=estimate(blocks, depth, 2 * cols),
     )(first, second, data, tail, initial)
 
@@ -569,31 +579,27 @@
     )
     own = jnp.concatenate([jnp.where(below, wy_v[:, :, :width], wy_t), wy_v[:, :, width:]], axis=2)
     f00, s00 = own[0], own[1]
-    above = eigvecs[: 2 * width]
     depth = 2 * width
     shapes = ((own_blocks + 2, 2 * depth, depth), (own_blocks + 1, 2 * depth, depth))
 
-    def add(buffers, group, pieces, keys):
+    def add(buffers, first_pieces, second_pieces, keys):
         parts = []
-        for source, key in enumerate(keys):
-            parts += placed(source, key, (group,), False)
-        return build(buffers, shapes, pieces, parts)
+        for group, pieces in enumerate((first_pieces, second_pieces)):
+            for source, key in enumerate(keys):
+                parts += placed(group * len(keys) + source, key, (group,), False)
+        return build(buffers, shapes, first_pieces + second_pieces, parts)
 
     f01, f30, f10 = across_x(f00), along_z(f00, 1), along_z(f00, -1)
     s01, s30, s10 = across_x(s00), along_z(s00, 1), along_z(s00, -1)
-    buffers = build(None, shapes, [f00, s00], placed(0, (0, 0), (0,), False) + placed(1, (0, 0), (1,), False))
+    buffers = add(None, [f00], [s00], [(0, 0)])
     f01, f30, f10, *buffers = together(f01, f30, f10, *buffers)
     f31, f20, f11 = across_x(f30), along_z(f30, 1), along_z(f01, -1)
-    buffers = add(buffers, 0, [f01, f30, f10], [(0, 1), (3, 0), (1, 0)])
-    s01, s30, s10, *buffers = together(s01, s30, s10, *buffers)
     s31, s20, s11 = across_x(s30), along_z(s30, 1), along_z(s01, -1)
-    buffers = add(buffers, 1, [s01, s30, s10], [(0, 1), (3, 0), (1, 0)])
-    f31, f20, f11, *buffers = together(f31, f20, f11, *buffers)
-    f21 = along_z(f11, -1)
-    buffers = add(buffers, 0, [f31, f20, f11], [(3, 1), (2, 0), (1, 1)])
-    s31, s20, s11, *buffers = together(s31, s20, s11, *buffers)
-    s21 = along_z(s31, 1)
-    picked = pick_first(
+    buffers = add(buffers, [f01, f30, f10], [s01, s30, s10], [(0, 1), (3, 0), (1, 0)])
+    f31, f20, f11, s31, s20, s11, *buffers = together(f31, f20, f11, s31, s20, s11, *buffers)
+    f21, s21 = along_z(f11, -1), along_z(s31, 1)
+    picked, above = pick_first(
+        eigvecs,
         {
             (0, 0): [f00, s00],
             (0, 1): [f01, s01],
@@ -616,7 +622,7 @@
             picked, ("row", "vec"), [((i + 1) * vecs + late - 1, i * vecs + late) for i in range(rows - 1)]
         ),
     ]
-    buffers = add(buffers, 1, [s31, s20, s11], [(3, 1), (2, 0), (1, 1)])
+    buffers = add(buffers, [f31, f20, f11], [s31, s20, s11], [(3, 1), (2, 0), (1, 1)])
     f21, s21, above, extra, late_extra, *buffers = together(f21, s21, above, *extras, *buffers)
     tail = from_next_row(above)
     buffers = build(

time: 140 us -> 135 us (0.964)
  local copies, waits for them, and re-layouts: 5.98 us -> 1 us
  Pallas kernels: 62.6 us -> 57.9 us
  waiting for transfers between devices: 21 us -> 25.3 us
  starting transfers between devices: 47.1 us -> 48.6 us
    pallas_call x6 -> x4, Pallas kernels: 20.1 us -> 16.3 us  [build(): pl.pallas_call(functools.partial(build_kernel, parts, has_input), out_sha...]
    unnamed x50 -> x38, local copies, waits for them, and re-layouts: 4.66 us -> 1 us
    ppermute x10, waiting for transfers between devices: 3.59 us -> 7.23 us  [along_z(): return lax.ppermute(value, 'vec', pairs)]
    pallas_call x1, Pallas kernels: 20.3 us -> 17.6 us  [sweep_data(): pl.pallas_call(data_kernel, out_shape=(jax.ShapeDtypeStruct((blocks * wid...]
  transfers between devices with their start and end apart: 30 -> 30, of which waited for: 11 -> 14; matrix products, arithmetic and copies ran while one was open for 1% -> 0% of each run, Pallas kernels for 37% -> 34%
where the time goes in v7:
time: 135 us
  Pallas kernels  57.9 us (43%)
  starting transfers between devices  48.6 us (36%)
  waiting for transfers between devices  25.3 us (19%)
    pallas_call x1, Pallas kernels, sweep_data(): pl.pallas_call(data_kernel, out_shape=(jax.ShapeDtypeStruct((blocks * wid...  17.6 us
    pallas_call x4, Pallas kernels, build(): pl.pallas_call(functools.partial(build_kernel, parts, has_input), out_sha...  16.3 us
    ppermute x10, starting transfers between devices, along_z(): return lax.ppermute(value, 'vec', pairs)  16 us
    ppermute x9, starting transfers between devices, along_y(): lax.ppermute(value, 'row', [(i, target(i)) for i in range(lax.axis_size('...  12.4 us
    pallas_call x1, Pallas kernels, sweep_units(): pl.pallas_call(unit_kernel, out_shape=(jax.ShapeDtypeStruct((blocks * wid...  10.8 us
    ppermute x10, waiting for transfers between devices, along_z(): return lax.ppermute(value, 'vec', pairs)  7.23 us
    pallas_call x1, Pallas kernels, correct(): pl.pallas_call(functools.partial(correct_kernel, tile), out_shape=jax.Sha...  7.05 us
    ppermute x9, waiting for transfers between devices, along_y(): lax.ppermute(value, 'row', [(i, target(i)) for i in range(lax.axis_size('...  6.8 us
  transfers between devices with their start and end apart: 30, of which 14 were waited for; matrix products, arithmetic and copies ran while one was open for 0% of the time, Pallas kernels for 34%

profile of v7, /device:TPU:5, one launch (start us, length us, event | category | flops | bytes accessed | tf_op | source)
XLA Modules:
  0.0 134.6 jit_solution(5568120870976190256)
XLA Ops:
  0.0 1.2 fusion.3
  1.3 1.0 collective-permute-start.9
  2.3 3.8 %collective-permute-start.2 = (f32[2,256,128]{2,1,0:T(8,128)S(1)}, f32[2,256,128]{2,1,0:T(8,128)S(1)}, u32[]{:S(2)}, u32[]{:S(2)}) collective-permute-start(f32[2,256,128]{2,1,0:T(8,128)S(1)} %get-tuple-element.122.refs_0_), channel_id=1, source_target_pairs={{0,6},{1,7},{2,0},{3,1},{4,2},{5,3},{6,4},{7,5},{8,14},{9,15},{10,... | collective-permute-start | bytes 786440 | tf_op jit(solution)/shard_map/ppermute | solution.py:40
  6.0 0.5 collective-permute-start
  6.6 2.7 %collective-permute-start.11 = (f32[2,256,128]{2,1,0:T(8,128)S(1)}, f32[2,256,128]{2,1,0:T(8,128)S(1)}, u32[]{:S(2)}, u32[]{:S(2)}) collective-permute-start(f32[2,256,128]{2,1,0:T(8,128)S(1)} %get-tuple-element.121.refs_1_), channel_id=1, source_target_pairs={{0,6},{1,7},{2,0},{3,1},{4,2},{5,3},{6,4},{7,5},{8,14},{9,15},{10,... | collective-permute-start | bytes 786440 | tf_op jit(solution)/shard_map/ppermute | solution.py:40
  9.2 0.0 collective-permute-done.9.refs_3_
  9.2 0.9 collective-permute-start.6
  10.1 0.5 collective-permute-done.2.refs_2_.refs_4_
  10.7 3.4 %collective-permute-start.10 = (f32[2,256,128]{2,1,0:T(8,128)S(1)}, f32[2,256,128]{2,1,0:T(8,128)S(1)}, u32[]{:S(2)}, u32[]{:S(2)}) collective-permute-start(f32[2,256,128]{2,1,0:T(8,128)S(1)} %collective-permute-done.9.refs_3_), channel_id=1, source_target_pairs={{0,6},{1,7},{2,0},{3,1},{4,2},{5,3},{6,4},{7,5},{8,14},{9,15},{10,... | collective-permute-start | bytes 786440 | tf_op jit(solution)/shard_map/ppermute | solution.py:40
  14.1 2.9 %shard_map.37 = (bf16[18,512,256]{2,1,0:T(8,128)(2,1)}, bf16[17,512,256]{2,1,0:T(8,128)(2,1)}) custom-call(f32[2,256,128]{2,1,0:T(8,128)} %copy-done.1, f32[2,256,128]{2,1,0:T(8,128)} %copy-done), custom_call_target="tpu_custom_call" | custom-call | flops 1200000000 | bytes 1572864 | tf_op jit(solution)/shard_map/pallas_call | solution.py:168
  17.0 0.1 collective-permute-start.4
  17.1 0.6 collective-permute-start.3
  17.7 0.0 collective-permute-done.11.refs_5_
  17.7 2.6 %collective-permute-start.5 = (f32[2,256,128]{2,1,0:T(8,128)S(1)}, f32[2,256,128]{2,1,0:T(8,128)S(1)}, u32[]{:S(2)}, u32[]{:S(2)}) collective-permute-start(f32[2,256,128]{2,1,0:T(8,128)S(1)} %collective-permute-done.refs_0_.refs_2_), channel_id=1, source_target_pairs={{0,6},{1,7},{2,0},{3,1},{4,2},{5,3},{6,4},{7,5},{8,14},{9,15},{10,... | collective-permute-start | bytes 786440 | tf_op jit(solution)/shard_map/ppermute | solution.py:40
  20.3 0.0 collective-permute-done.6.refs_4_.refs_9_
  20.3 1.6 %collective-permute-done.10.refs_7_.refs_5_ = f32[2,256,128]{2,1,0:T(8,128)S(1)} collective-permute-done((f32[2,256,128]{2,1,0:T(8,128)S(1)}, f32[2,256,128]{2,1,0:T(8,128)S(1)}, u32[]{:S(2)}, u32[]{:S(2)}) %collective-permute-start.10) | collective-permute-done | bytes 262176 | tf_op jit(solution)/shard_map/ppermute | solution.py:40
  21.9 0.5 collective-permute-start.7
  22.5 4.8 %shard_map.38 = (bf16[18,512,256]{2,1,0:T(8,128)(2,1)}, bf16[17,512,256]{2,1,0:T(8,128)(2,1)}) custom-call(f32[2,256,128]{2,1,0:T(8,128)} %copy-done.8, f32[2,256,128]{2,1,0:T(8,128)} %copy-done.7, f32[2,256,128]{2,1,0:T(8,128)} %copy-done.5, f32[2,256,128]{2,1,0:T(8,128)} %copy-done.4, ...), custom_call_target="tpu_custom_call", output_to_operand_aliasing={{0}: (6, {}), {1}: (7, {})} | custom-call | flops 3600000000 | bytes 4718592 | tf_op jit(solution)/shard_map/pallas_call | solution.py:168
  27.3 1.7 %collective-permute-done.8.refs_13_.refs_4_ = f32[2,256,128]{2,1,0:T(8,128)S(1)} collective-permute-done((f32[2,256,128]{2,1,0:T(8,128)S(1)}, f32[2,256,128]{2,1,0:T(8,128)S(1)}, u32[]{:S(2)}, u32[]{:S(2)}) %collective-permute-start.8) | collective-permute-done | bytes 262176 | tf_op jit(solution)/shard_map/ppermute | solution.py:40
  29.1 1.1 collective-permute-done.7.refs_11_.refs_3_
  30.2 0.0 collective-permute-done.5.refs_6_.refs_2_
  30.2 0.7 copy-done.15
  30.9 0.1 copy-done.13
  31.0 0.1 copy-done.11
  31.1 0.1 copy-done.12
  31.2 2.5 %shard_map.39 = (f32[3,256,128]{2,1,0:T(8,128)}, f32[256,1024]{1,0:T(8,128)}) custom-call(f32[2048,1024]{1,0:T(8,128)} %data_hbm.3, f32[2,256,128]{2,1,0:T(8,128)} %copy-done.1, f32[2,256,128]{2,1,0:T(8,128)} %copy-done, f32[2,256,128]{2,1,0:T(8,128)} %copy-done.8, f32[2,256,128]{2,1,0:T(8,128)} %copy-done.4, f32[2,256,128]{2,1,0:T(8,128)} %copy-done.5, ...), custom_call_target="tpu_custom_call" | custom-call | tf_op jit(solution)/shard_map/pallas_call | solution.py:100
  33.7 0.8 collective-permute-start.15
  34.5 4.9 %collective-permute-start.14 = (f32[3,256,128]{2,1,0:T(8,128)}, f32[3,256,128]{2,1,0:T(8,128)S(1)}, u32[]{:S(2)}, u32[]{:S(2)}) collective-permute-start(f32[3,256,128]{2,1,0:T(8,128)} %get-tuple-element.79), channel_id=1, source_target_pairs={{8,0},{9,1},{10,2},{11,3},{12,4},{14,6},{15,7},{16,8},{17,9},{18,1... | collective-permute-start | bytes 1179656 | tf_op jit(solution)/shard_map/ppermute | solution.py:616
  39.4 2.6 %collective-permute-start.12 = (f32[2,256,128]{2,1,0:T(8,128)}, f32[2,256,128]{2,1,0:T(8,128)S(1)}, u32[]{:S(2)}, u32[]{:S(2)}) collective-permute-start(f32[2,256,128]{2,1,0:T(8,128)} %copy-done.13), channel_id=1, source_target_pairs={{0,6},{1,7},{2,0},{3,1},{4,2},{5,3},{6,4},{7,5},{8,14},{9,15},{10,... | collective-permute-start | bytes 786440 | tf_op jit(solution)/shard_map/ppermute | solution.py:40
  41.9 4.8 %shard_map.40 = (bf16[18,512,256]{2,1,0:T(8,128)(2,1)}, bf16[17,512,256]{2,1,0:T(8,128)(2,1)}) custom-call(f32[2,256,128]{2,1,0:T(8,128)} %copy-done.12, f32[2,256,128]{2,1,0:T(8,128)} %copy-done.11, f32[2,256,128]{2,1,0:T(8,128)} %copy-done.13, f32[2,256,128]{2,1,0:T(8,128)} %copy-done.15, ...), custom_call_target="tpu_custom_call", output_to_operand_aliasing={{0}: (6, {}), {1}: (7, {})} | custom-call | flops 3600000000 | bytes 4718592 | tf_op jit(solution)/shard_map/pallas_call | solution.py:168
  46.8 0.4 collective-permute-done.12.refs_0_
  47.2 3.0 %collective-permute-done.13.refs_1_ = f32[2,256,128]{2,1,0:T(8,128)S(1)} collective-permute-done((f32[2,256,128]{2,1,0:T(8,128)}, f32[2,256,128]{2,1,0:T(8,128)S(1)}, u32[]{:S(2)}, u32[]{:S(2)}) %collective-permute-start.13) | collective-permute-done | bytes 262176 | tf_op jit(solution)/shard_map/ppermute | solution.py:40
  50.2 3.8 %collective-permute-start.17 = (f32[256,1024]{1,0:T(8,128)S(1)}, f32[256,1024]{1,0:T(8,128)S(1)}, u32[]{:S(2)}, u32[]{:S(2)}) collective-permute-start(f32[256,1024]{1,0:T(8,128)S(1)} %copy-done.18), channel_id=1, source_target_pairs={{8,0},{16,8},{24,16},{32,24},{40,32},{48,40},{56,48},{64,56},{72,6... | collective-permute-start | bytes 3145736 | tf_op jit(solution)/shard_map/ppermute | solution.py:60
  54.1 3.8 %shard_map.41 = (bf16[18,512,256]{2,1,0:T(8,128)(2,1)}, bf16[17,512,256]{2,1,0:T(8,128)(2,1)}) custom-call(f32[2,256,128]{2,1,0:T(8,128)} %copy-done.16, f32[2,256,128]{2,1,0:T(8,128)} %copy-done.17, f32[3,256,128]{2,1,0:T(8,128)} %copy-done.3, f32[3,256,128]{2,1,0:T(8,128)} %copy-done.2, ...), custom_call_target="tpu_custom_call", output_to_operand_aliasing={{0}: (4, {}), {1}: (5, {})} | custom-call | flops 2100000000 | bytes 2752512 | tf_op jit(solution)/shard_map/pallas_call | solution.py:168
  57.9 10.8 %shard_map.42 = (f32[2048,256]{1,0:T(8,128)S(1)}, f32[256,256]{1,0:T(8,128)S(1)}, f32[256,1024]{1,0:T(8,128)S(1)}) custom-call(bf16[18,512,256]{2,1,0:T(8,128)(2,1)} %get-tuple-element.93.first_hbm, bf16[17,512,256]{2,1,0:T(8,128)(2,1)} %get-tuple-element.94.second_hbm, f32[2048,1024]{1,0:T(8,128)} %data_hbm.3), custom_call_target="tpu_custom_call" | custom-call | flops 4831838208 | bytes 31457280 | tf_op jit(solution)/shard_map/pallas_call | solution.py:381
  68.7 2.3 %collective-permute-start.16 = (f32[256,256]{1,0:T(8,128)S(1)}, f32[256,256]{1,0:T(8,128)S(1)}, u32[]{:S(2)}, u32[]{:S(2)}) collective-permute-start(f32[256,256]{1,0:T(8,128)S(1)} %get-tuple-element.92.own.own_transition), channel_id=1, source_target_pairs={{0,8},{8,0},{16,24},{24,16},{32,40},{40,32},{48,56},{56,48},{64,72... | collective-permute-start | bytes 786440 | tf_op jit(solution)/shard_map/ppermute | solution.py:48
  71.0 1.2 collective-permute-done.16.received.received_transition
  72.2 0.3 shard_map.43.refs_0_
  72.5 1.0 collective-permute-start.20
  73.5 0.3 collective-permute-start.19
  73.8 0.7 collective-permute-start.18
  74.5 17.6 %shard_map.44 = (f32[2048,1024]{1,0:T(8,128)}, f32[256,512]{1,0:T(8,128)S(1)}, f32[256,512]{1,0:T(8,128)S(1)}) custom-call(bf16[18,512,256]{2,1,0:T(8,128)(2,1)} %get-tuple-element.93.first_hbm, bf16[17,512,256]{2,1,0:T(8,128)(2,1)} %get-tuple-element.94.second_hbm, f32[2048,1024]{1,0:T(8,128)} %data_hbm.3, ...), custom_call_target="tpu_custom_call" | custom-call | flops 12884901888 | bytes 31457280 | tf_op jit(solution)/shard_map/pallas_call | solution.py:410
  92.1 1.1 collective-permute-start.21
  93.2 1.5 %collective-permute-done.21.received = f32[256,512]{1,0:T(8,128)S(1)} collective-permute-done((f32[256,512]{1,0:T(8,128)S(1)}, f32[256,512]{1,0:T(8,128)S(1)}, u32[]{:S(2)}, u32[]{:S(2)}) %collective-permute-start.21) | collective-permute-done | bytes 524320 | tf_op jit(solution)/shard_map/ppermute | solution.py:48
  94.8 0.5 shard_map.46
  95.3 1.8 %collective-permute-start.22 = (f32[256,128]{1,0:T(8,128)S(1)}, f32[256,128]{1,0:T(8,128)S(1)}, u32[]{:S(2)}, u32[]{:S(2)}) collective-permute-start(f32[256,128]{1,0:T(8,128)S(1)} %get-tuple-element.109), channel_id=1, source_target_pairs={{0,16},{8,24},{16,32},{24,40},{32,48},{40,56},{48,0},{56,8},{64,80... | collective-permute-start | bytes 393224 | tf_op jit(solution)/shard_map/ppermute | solution.py:56
  97.1 1.8 %collective-permute-start.23 = (f32[256,128]{1,0:T(8,128)S(1)}, f32[256,128]{1,0:T(8,128)S(1)}, u32[]{:S(2)}, u32[]{:S(2)}) collective-permute-start(f32[256,128]{1,0:T(8,128)S(1)} %get-tuple-element.110), channel_id=1, source_target_pairs={{0,32},{8,40},{16,48},{24,56},{32,0},{40,8},{48,16},{56,24},{64,96... | collective-permute-start | bytes 393224 | tf_op jit(solution)/shard_map/ppermute | solution.py:56
  98.8 2.0 %collective-permute-start.24 = (f32[256,128]{1,0:T(8,128)S(1)}, f32[256,128]{1,0:T(8,128)S(1)}, u32[]{:S(2)}, u32[]{:S(2)}) collective-permute-start(f32[256,128]{1,0:T(8,128)S(1)} %get-tuple-element.111), channel_id=1, source_target_pairs={{0,48},{8,56},{16,0},{24,8},{32,16},{40,24},{48,32},{56,40},{64,11... | collective-permute-start | bytes 393224 | tf_op jit(solution)/shard_map/ppermute | solution.py:56
  100.8 0.8 shard_map.45
  101.6 3.4 %collective-permute-done.23.refs_2_ = f32[256,128]{1,0:T(8,128)S(1)} collective-permute-done((f32[256,128]{1,0:T(8,128)S(1)}, f32[256,128]{1,0:T(8,128)S(1)}, u32[]{:S(2)}, u32[]{:S(2)}) %collective-permute-start.23) | collective-permute-done | bytes 131104 | tf_op jit(solution)/shard_map/ppermute | solution.py:56
  105.1 0.9 shard_map.47
  106.0 1.3 collective-permute-start.25
  107.3 5.9 %collective-permute-done.25.entering = f32[256,128]{1,0:T(8,128)S(1)} collective-permute-done((f32[256,128]{1,0:T(8,128)S(1)}, f32[256,128]{1,0:T(8,128)S(1)}, u32[]{:S(2)}, u32[]{:S(2)}) %collective-permute-start.25) | collective-permute-done | bytes 131104 | tf_op jit(solution)/shard_map/ppermute | solution.py:659
  113.2 0.5 shard_map.48
  113.7 0.1 collective-permute-start.26
  113.8 3.6 %collective-permute-start.27 = (f32[256,128]{1,0:T(8,128)S(1)}, f32[256,128]{1,0:T(8,128)S(1)}, u32[]{:S(2)}, u32[]{:S(2)}) collective-permute-start(f32[256,128]{1,0:T(8,128)S(1)} %get-tuple-element.117), channel_id=1, source_target_pairs={{0,32},{8,40},{16,48},{24,56},{32,0},{40,8},{48,16},{56,24},{64,96... | collective-permute-start | bytes 393224 | tf_op jit(solution)/shard_map/ppermute | solution.py:56
  117.4 1.2 collective-permute-start.28
  118.6 0.2 collective-permute-done.26.refs_1_
  118.8 2.5 %collective-permute-done.27.refs_2_ = f32[256,128]{1,0:T(8,128)S(1)} collective-permute-done((f32[256,128]{1,0:T(8,128)S(1)}, f32[256,128]{1,0:T(8,128)S(1)}, u32[]{:S(2)}, u32[]{:S(2)}) %collective-permute-start.27) | collective-permute-done | bytes 131104 | tf_op jit(solution)/shard_map/ppermute | solution.py:56
  121.3 0.7 collective-permute-done.28.refs_3_
  122.0 0.5 shard_map.49
  122.5 3.4 %collective-permute-start.29 = (f32[256,512]{1,0:T(8,128)S(1)}, f32[256,512]{1,0:T(8,128)S(1)}, u32[]{:S(2)}, u32[]{:S(2)}) collective-permute-start(f32[256,512]{1,0:T(8,128)S(1)} %get-tuple-element.120), channel_id=1, source_target_pairs={{0,8},{8,0},{16,24},{24,16},{32,40},{40,32},{48,56},{56,48},{64,72... | collective-permute-start | bytes 1572872 | tf_op jit(solution)/shard_map/ppermute | solution.py:48
  125.9 1.5 %collective-permute-done.29.taken = f32[256,512]{1,0:T(8,128)S(1)} collective-permute-done((f32[256,512]{1,0:T(8,128)S(1)}, f32[256,512]{1,0:T(8,128)S(1)}, u32[]{:S(2)}, u32[]{:S(2)}) %collective-permute-start.29) | collective-permute-done | bytes 524320 | tf_op jit(solution)/shard_map/ppermute | solution.py:48
  127.4 7.1 %shard_map.50 = f32[2048,1024]{1,0:T(8,128)} custom-call(f32[2048,1024]{1,0:T(8,128)} %get-tuple-element.97.rows_hbm, f32[2048,256]{1,0:T(8,128)S(1)} %get-tuple-element.98.response_hbm, f32[256,512]{1,0:T(8,128)S(1)} %get-tuple-element.119.kept, f32[256,512]{1,0:T(8,128)S(1)} %collective-permute-done.29.taken), custom_call_target="tpu_custom_call" | custom-call | tf_op jit(solution)/shard_map/pallas_call | solution.py:557
  (51 shorter events, 0.2 us)
Async XLA Ops:
  1.2 12.8 %copy-start = (f32[2,256,128]{2,1,0:T(8,128)}, f32[2,256,128]{2,1,0:T(8,128)S(1)}, u32[]{:S(2)}) copy-start(f32[2,256,128]{2,1,0:T(8,128)S(1)} %get-tuple-element.121.refs_1_) | copy-start | bytes 786436
  1.2 12.8 %copy-start.1 = (f32[2,256,128]{2,1,0:T(8,128)}, f32[2,256,128]{2,1,0:T(8,128)S(1)}, u32[]{:S(2)}) copy-start(f32[2,256,128]{2,1,0:T(8,128)S(1)} %get-tuple-element.122.refs_0_) | copy-start | bytes 786436
  1.3 8.0 %collective-permute-start.9 = (f32[2,256,128]{2,1,0:T(8,128)S(1)}, f32[2,256,128]{2,1,0:T(8,128)S(1)}, u32[]{:S(2)}, u32[]{:S(2)}) collective-permute-start(f32[2,256,128]{2,1,0:T(8,128)S(1)} %get-tuple-element.121.refs_1_), channel_id=1, source_target_pairs={{0,1},{1,0},{2,3},{3,2},{4,5},{5,4},{6,7},{7,6},{8,9},{9,8},{10,11... | collective-permute-start | bytes 786440 | tf_op jit(solution)/shard_map/ppermute | solution.py:44
  2.3 8.4 %collective-permute-start.2 = (f32[2,256,128]{2,1,0:T(8,128)S(1)}, f32[2,256,128]{2,1,0:T(8,128)S(1)}, u32[]{:S(2)}, u32[]{:S(2)}) collective-permute-start(f32[2,256,128]{2,1,0:T(8,128)S(1)} %get-tuple-element.122.refs_0_), channel_id=1, source_target_pairs={{0,6},{1,7},{2,0},{3,1},{4,2},{5,3},{6,4},{7,5},{8,14},{9,15},{10,... | collective-permute-start | bytes 786440 | tf_op jit(solution)/shard_map/ppermute | solution.py:40
  6.0 11.0 %collective-permute-start.1 = (f32[2,256,128]{2,1,0:T(8,128)S(1)}, f32[2,256,128]{2,1,0:T(8,128)S(1)}, u32[]{:S(2)}, u32[]{:S(2)}) collective-permute-start(f32[2,256,128]{2,1,0:T(8,128)S(1)} %get-tuple-element.122.refs_0_), channel_id=1, source_target_pairs={{0,2},{1,3},{2,4},{3,5},{4,6},{5,7},{6,0},{7,1},{8,10},{9,11},{10,... | collective-permute-start | bytes 786440 | tf_op jit(solution)/shard_map/ppermute | solution.py:40
  6.0 11.0 %collective-permute-start = (f32[2,256,128]{2,1,0:T(8,128)S(1)}, f32[2,256,128]{2,1,0:T(8,128)S(1)}, u32[]{:S(2)}, u32[]{:S(2)}) collective-permute-start(f32[2,256,128]{2,1,0:T(8,128)S(1)} %get-tuple-element.122.refs_0_), channel_id=1, source_target_pairs={{0,1},{1,0},{2,3},{3,2},{4,5},{5,4},{6,7},{7,6},{8,9},{9,8},{10,11... | collective-permute-start | bytes 786440 | tf_op jit(solution)/shard_map/ppermute | solution.py:44
  6.6 11.2 %collective-permute-start.11 = (f32[2,256,128]{2,1,0:T(8,128)S(1)}, f32[2,256,128]{2,1,0:T(8,128)S(1)}, u32[]{:S(2)}, u32[]{:S(2)}) collective-permute-start(f32[2,256,128]{2,1,0:T(8,128)S(1)} %get-tuple-element.121.refs_1_), channel_id=1, source_target_pairs={{0,6},{1,7},{2,0},{3,1},{4,2},{5,3},{6,4},{7,5},{8,14},{9,15},{10,... | collective-permute-start | bytes 786440 | tf_op jit(solution)/shard_map/ppermute | solution.py:40
  9.2 13.2 %copy-start.4 = (f32[2,256,128]{2,1,0:T(8,128)}, f32[2,256,128]{2,1,0:T(8,128)S(1)}, u32[]{:S(2)}) copy-start(f32[2,256,128]{2,1,0:T(8,128)S(1)} %collective-permute-done.9.refs_3_) | copy-start | bytes 786436
  9.2 11.1 %collective-permute-start.6 = (f32[2,256,128]{2,1,0:T(8,128)S(1)}, f32[2,256,128]{2,1,0:T(8,128)S(1)}, u32[]{:S(2)}, u32[]{:S(2)}) collective-permute-start(f32[2,256,128]{2,1,0:T(8,128)S(1)} %get-tuple-element.121.refs_1_), channel_id=1, source_target_pairs={{0,2},{1,3},{2,4},{3,5},{4,6},{5,7},{6,0},{7,1},{8,10},{9,11},{10,... | collective-permute-start | bytes 786440 | tf_op jit(solution)/shard_map/ppermute | solution.py:40
  10.7 11.8 %copy-start.5 = (f32[2,256,128]{2,1,0:T(8,128)}, f32[2,256,128]{2,1,0:T(8,128)S(1)}, u32[]{:S(2)}) copy-start(f32[2,256,128]{2,1,0:T(8,128)S(1)} %collective-permute-done.2.refs_2_.refs_4_) | copy-start | bytes 786436
  10.7 11.2 %collective-permute-start.10 = (f32[2,256,128]{2,1,0:T(8,128)S(1)}, f32[2,256,128]{2,1,0:T(8,128)S(1)}, u32[]{:S(2)}, u32[]{:S(2)}) collective-permute-start(f32[2,256,128]{2,1,0:T(8,128)S(1)} %collective-permute-done.9.refs_3_), channel_id=1, source_target_pairs={{0,6},{1,7},{2,0},{3,1},{4,2},{5,3},{6,4},{7,5},{8,14},{9,15},{10,... | collective-permute-start | bytes 786440 | tf_op jit(solution)/shard_map/ppermute | solution.py:40
  17.0 5.5 %copy-start.7 = (f32[2,256,128]{2,1,0:T(8,128)}, f32[2,256,128]{2,1,0:T(8,128)S(1)}, u32[]{:S(2)}) copy-start(f32[2,256,128]{2,1,0:T(8,128)S(1)} %collective-permute-done.1.refs_1_.refs_8_) | copy-start | bytes 786436
  17.0 5.5 %copy-start.8 = (f32[2,256,128]{2,1,0:T(8,128)}, f32[2,256,128]{2,1,0:T(8,128)S(1)}, u32[]{:S(2)}) copy-start(f32[2,256,128]{2,1,0:T(8,128)S(1)} %collective-permute-done.refs_0_.refs_2_) | copy-start | bytes 786436
  17.0 13.2 %collective-permute-start.4 = (f32[2,256,128]{2,1,0:T(8,128)S(1)}, f32[2,256,128]{2,1,0:T(8,128)S(1)}, u32[]{:S(2)}, u32[]{:S(2)}) collective-permute-start(f32[2,256,128]{2,1,0:T(8,128)S(1)} %collective-permute-done.1.refs_1_.refs_8_), channel_id=1, source_target_pairs={{0,2},{1,3},{2,4},{3,5},{4,6},{5,7},{6,0},{7,1},{8,10},{9,11},{10,... | collective-permute-start | bytes 786440 | tf_op jit(solution)/shard_map/ppermute | solution.py:40
  17.1 13.1 %collective-permute-start.3 = (f32[2,256,128]{2,1,0:T(8,128)S(1)}, f32[2,256,128]{2,1,0:T(8,128)S(1)}, u32[]{:S(2)}, u32[]{:S(2)}) collective-permute-start(f32[2,256,128]{2,1,0:T(8,128)S(1)} %collective-permute-done.1.refs_1_.refs_8_), channel_id=1, source_target_pairs={{0,1},{1,0},{2,3},{3,2},{4,5},{5,4},{6,7},{7,6},{8,9},{9,8},{10,11... | collective-permute-start | bytes 786440 | tf_op jit(solution)/shard_map/ppermute | solution.py:44
  17.7 4.7 %copy-start.9 = (f32[2,256,128]{2,1,0:T(8,128)}, f32[2,256,128]{2,1,0:T(8,128)S(1)}, u32[]{:S(2)}) copy-start(f32[2,256,128]{2,1,0:T(8,128)S(1)} %collective-permute-done.11.refs_5_) | copy-start | bytes 786436
  17.7 12.5 %collective-permute-start.5 = (f32[2,256,128]{2,1,0:T(8,128)S(1)}, f32[2,256,128]{2,1,0:T(8,128)S(1)}, u32[]{:S(2)}, u32[]{:S(2)}) collective-permute-start(f32[2,256,128]{2,1,0:T(8,128)S(1)} %collective-permute-done.refs_0_.refs_2_), channel_id=1, source_target_pairs={{0,6},{1,7},{2,0},{3,1},{4,2},{5,3},{6,4},{7,5},{8,14},{9,15},{10,... | collective-permute-start | bytes 786440 | tf_op jit(solution)/shard_map/ppermute | solution.py:40
  20.3 2.2 %copy-start.10 = (f32[2,256,128]{2,1,0:T(8,128)}, f32[2,256,128]{2,1,0:T(8,128)S(1)}, u32[]{:S(2)}) copy-start(f32[2,256,128]{2,1,0:T(8,128)S(1)} %collective-permute-done.6.refs_4_.refs_9_) | copy-start | bytes 786436
  20.3 8.7 %collective-permute-start.8 = (f32[2,256,128]{2,1,0:T(8,128)S(1)}, f32[2,256,128]{2,1,0:T(8,128)S(1)}, u32[]{:S(2)}, u32[]{:S(2)}) collective-permute-start(f32[2,256,128]{2,1,0:T(8,128)S(1)} %collective-permute-done.6.refs_4_.refs_9_), channel_id=1, source_target_pairs={{0,2},{1,3},{2,4},{3,5},{4,6},{5,7},{6,0},{7,1},{8,10},{9,11},{10,... | collective-permute-start | bytes 786440 | tf_op jit(solution)/shard_map/ppermute | solution.py:40
  21.9 5.4 %copy-start.6 = (f32[2,256,128]{2,1,0:T(8,128)}, f32[2,256,128]{2,1,0:T(8,128)S(1)}, u32[]{:S(2)}) copy-start(f32[2,256,128]{2,1,0:T(8,128)S(1)} %collective-permute-done.10.refs_7_.refs_5_) | copy-start | bytes 786436
  21.9 8.3 %collective-permute-start.7 = (f32[2,256,128]{2,1,0:T(8,128)S(1)}, f32[2,256,128]{2,1,0:T(8,128)S(1)}, u32[]{:S(2)}, u32[]{:S(2)}) collective-permute-start(f32[2,256,128]{2,1,0:T(8,128)S(1)} %collective-permute-done.6.refs_4_.refs_9_), channel_id=1, source_target_pairs={{0,1},{1,0},{2,3},{3,2},{4,5},{5,4},{6,7},{7,6},{8,9},{9,8},{10,11... | collective-permute-start | bytes 786440 | tf_op jit(solution)/shard_map/ppermute | solution.py:44
  29.0 1.2 copy-start.14
  30.2 0.7 copy-start.15
  30.2 0.8 copy-start.13
  30.2 0.9 copy-start.11
  30.2 1.0 copy-start.12
  33.7 16.5 %copy-start.18 = (f32[256,1024]{1,0:T(8,128)S(1)}, f32[256,1024]{1,0:T(8,128)}, u32[]{:S(2)}) copy-start(f32[256,1024]{1,0:T(8,128)} %get-tuple-element.95) | copy-start | bytes 3145732
  33.7 16.5 %collective-permute-start.15 = (f32[3,256,128]{2,1,0:T(8,128)}, f32[3,256,128]{2,1,0:T(8,128)S(1)}, u32[]{:S(2)}, u32[]{:S(2)}) collective-permute-start(f32[3,256,128]{2,1,0:T(8,128)} %get-tuple-element.79), channel_id=1, source_target_pairs={{12,5},{20,13},{28,21},{36,29},{44,37},{52,45},{60,53},{68,61},{76... | collective-permute-start | bytes 1179656 | tf_op jit(solution)/shard_map/ppermute | solution.py:621
  34.5 15.7 %collective-permute-start.14 = (f32[3,256,128]{2,1,0:T(8,128)}, f32[3,256,128]{2,1,0:T(8,128)S(1)}, u32[]{:S(2)}, u32[]{:S(2)}) collective-permute-start(f32[3,256,128]{2,1,0:T(8,128)} %get-tuple-element.79), channel_id=1, source_target_pairs={{8,0},{9,1},{10,2},{11,3},{12,4},{14,6},{15,7},{16,8},{17,9},{18,1... | collective-permute-start | bytes 1179656 | tf_op jit(solution)/shard_map/ppermute | solution.py:616
  39.4 7.8 %collective-permute-start.12 = (f32[2,256,128]{2,1,0:T(8,128)}, f32[2,256,128]{2,1,0:T(8,128)S(1)}, u32[]{:S(2)}, u32[]{:S(2)}) collective-permute-start(f32[2,256,128]{2,1,0:T(8,128)} %copy-done.13), channel_id=1, source_target_pairs={{0,6},{1,7},{2,0},{3,1},{4,2},{5,3},{6,4},{7,5},{8,14},{9,15},{10,... | collective-permute-start | bytes 786440 | tf_op jit(solution)/shard_map/ppermute | solution.py:40
  41.9 8.2 %collective-permute-start.13 = (f32[2,256,128]{2,1,0:T(8,128)}, f32[2,256,128]{2,1,0:T(8,128)S(1)}, u32[]{:S(2)}, u32[]{:S(2)}) collective-permute-start(f32[2,256,128]{2,1,0:T(8,128)} %copy-done.15), channel_id=1, source_target_pairs={{0,2},{1,3},{2,4},{3,5},{4,6},{5,7},{6,0},{7,1},{8,10},{9,11},{10,... | collective-permute-start | bytes 786440 | tf_op jit(solution)/shard_map/ppermute | solution.py:40
  47.2 6.8 %copy-start.16 = (f32[2,256,128]{2,1,0:T(8,128)}, f32[2,256,128]{2,1,0:T(8,128)S(1)}, u32[]{:S(2)}) copy-start(f32[2,256,128]{2,1,0:T(8,128)S(1)} %collective-permute-done.12.refs_0_) | copy-start | bytes 786436
  50.2 3.9 %copy-start.17 = (f32[2,256,128]{2,1,0:T(8,128)}, f32[2,256,128]{2,1,0:T(8,128)S(1)}, u32[]{:S(2)}) copy-start(f32[2,256,128]{2,1,0:T(8,128)S(1)} %collective-permute-done.13.refs_1_) | copy-start | bytes 786436
  50.2 3.9 %copy-start.2 = (f32[3,256,128]{2,1,0:T(8,128)}, f32[3,256,128]{2,1,0:T(8,128)S(1)}, u32[]{:S(2)}) copy-start(f32[3,256,128]{2,1,0:T(8,128)S(1)} %collective-permute-done.15.refs_3_) | copy-start | bytes 1179652
  50.2 3.9 %copy-start.3 = (f32[3,256,128]{2,1,0:T(8,128)}, f32[3,256,128]{2,1,0:T(8,128)S(1)}, u32[]{:S(2)}) copy-start(f32[3,256,128]{2,1,0:T(8,128)S(1)} %collective-permute-done.14.refs_2_) | copy-start | bytes 1179652
  50.2 24.3 %collective-permute-start.17 = (f32[256,1024]{1,0:T(8,128)S(1)}, f32[256,1024]{1,0:T(8,128)S(1)}, u32[]{:S(2)}, u32[]{:S(2)}) collective-permute-start(f32[256,1024]{1,0:T(8,128)S(1)} %copy-done.18), channel_id=1, source_target_pairs={{8,0},{16,8},{24,16},{32,24},{40,32},{48,40},{56,48},{64,56},{72,6... | collective-permute-start | bytes 3145736 | tf_op jit(solution)/shard_map/ppermute | solution.py:60
  68.7 3.5 %collective-permute-start.16 = (f32[256,256]{1,0:T(8,128)S(1)}, f32[256,256]{1,0:T(8,128)S(1)}, u32[]{:S(2)}, u32[]{:S(2)}) collective-permute-start(f32[256,256]{1,0:T(8,128)S(1)} %get-tuple-element.92.own.own_transition), channel_id=1, source_target_pairs={{0,8},{8,0},{16,24},{24,16},{32,40},{40,32},{48,56},{56,48},{64,72... | collective-permute-start | bytes 786440 | tf_op jit(solution)/shard_map/ppermute | solution.py:48
  72.5 19.6 %collective-permute-start.20 = (f32[256,256]{1,0:T(8,128)S(1)}, f32[256,256]{1,0:T(8,128)S(1)}, u32[]{:S(2)}, u32[]{:S(2)}) collective-permute-start(f32[256,256]{1,0:T(8,128)S(1)} %shard_map.43.refs_0_), channel_id=1, source_target_pairs={{0,48},{8,56},{16,0},{24,8},{32,16},{40,24},{48,32},{56,40},{64,11... | collective-permute-start | bytes 786440 | tf_op jit(solution)/shard_map/ppermute | solution.py:56
  73.5 18.6 %collective-permute-start.19 = (f32[256,256]{1,0:T(8,128)S(1)}, f32[256,256]{1,0:T(8,128)S(1)}, u32[]{:S(2)}, u32[]{:S(2)}) collective-permute-start(f32[256,256]{1,0:T(8,128)S(1)} %shard_map.43.refs_0_), channel_id=1, source_target_pairs={{0,32},{8,40},{16,48},{24,56},{32,0},{40,8},{48,16},{56,24},{64,96... | collective-permute-start | bytes 786440 | tf_op jit(solution)/shard_map/ppermute | solution.py:56
  73.8 18.4 %collective-permute-start.18 = (f32[256,256]{1,0:T(8,128)S(1)}, f32[256,256]{1,0:T(8,128)S(1)}, u32[]{:S(2)}, u32[]{:S(2)}) collective-permute-start(f32[256,256]{1,0:T(8,128)S(1)} %shard_map.43.refs_0_), channel_id=1, source_target_pairs={{0,16},{8,24},{16,32},{24,40},{32,48},{40,56},{48,0},{56,8},{64,80... | collective-permute-start | bytes 786440 | tf_op jit(solution)/shard_map/ppermute | solution.py:56
  92.1 2.6 %collective-permute-start.21 = (f32[256,512]{1,0:T(8,128)S(1)}, f32[256,512]{1,0:T(8,128)S(1)}, u32[]{:S(2)}, u32[]{:S(2)}) collective-permute-start(f32[256,512]{1,0:T(8,128)S(1)} %get-tuple-element.102), channel_id=1, source_target_pairs={{0,8},{8,0},{16,24},{24,16},{32,40},{40,32},{48,56},{56,48},{64,72... | collective-permute-start | bytes 1572872 | tf_op jit(solution)/shard_map/ppermute | solution.py:48
  95.3 6.3 %collective-permute-start.22 = (f32[256,128]{1,0:T(8,128)S(1)}, f32[256,128]{1,0:T(8,128)S(1)}, u32[]{:S(2)}, u32[]{:S(2)}) collective-permute-start(f32[256,128]{1,0:T(8,128)S(1)} %get-tuple-element.109), channel_id=1, source_target_pairs={{0,16},{8,24},{16,32},{24,40},{32,48},{40,56},{48,0},{56,8},{64,80... | collective-permute-start | bytes 393224 | tf_op jit(solution)/shard_map/ppermute | solution.py:56
  97.1 8.0 %collective-permute-start.23 = (f32[256,128]{1,0:T(8,128)S(1)}, f32[256,128]{1,0:T(8,128)S(1)}, u32[]{:S(2)}, u32[]{:S(2)}) collective-permute-start(f32[256,128]{1,0:T(8,128)S(1)} %get-tuple-element.110), channel_id=1, source_target_pairs={{0,32},{8,40},{16,48},{24,56},{32,0},{40,8},{48,16},{56,24},{64,96... | collective-permute-start | bytes 393224 | tf_op jit(solution)/shard_map/ppermute | solution.py:56
  98.8 6.2 %collective-permute-start.24 = (f32[256,128]{1,0:T(8,128)S(1)}, f32[256,128]{1,0:T(8,128)S(1)}, u32[]{:S(2)}, u32[]{:S(2)}) collective-permute-start(f32[256,128]{1,0:T(8,128)S(1)} %get-tuple-element.111), channel_id=1, source_target_pairs={{0,48},{8,56},{16,0},{24,8},{32,16},{40,24},{48,32},{56,40},{64,11... | collective-permute-start | bytes 393224 | tf_op jit(solution)/shard_map/ppermute | solution.py:56
  106.0 7.2 %collective-permute-start.25 = (f32[256,128]{1,0:T(8,128)S(1)}, f32[256,128]{1,0:T(8,128)S(1)}, u32[]{:S(2)}, u32[]{:S(2)}) collective-permute-start(f32[256,128]{1,0:T(8,128)S(1)} %get-tuple-element.112), channel_id=1, source_target_pairs={{0,64},{8,72},{16,80},{24,88},{32,96},{40,104},{48,112},{56,120},{... | collective-permute-start | bytes 393224 | tf_op jit(solution)/shard_map/ppermute | solution.py:659
  113.7 5.1 %collective-permute-start.26 = (f32[256,128]{1,0:T(8,128)S(1)}, f32[256,128]{1,0:T(8,128)S(1)}, u32[]{:S(2)}, u32[]{:S(2)}) collective-permute-start(f32[256,128]{1,0:T(8,128)S(1)} %get-tuple-element.116), channel_id=1, source_target_pairs={{0,16},{8,24},{16,32},{24,40},{32,48},{40,56},{48,0},{56,8},{64,80... | collective-permute-start | bytes 393224 | tf_op jit(solution)/shard_map/ppermute | solution.py:56
  113.8 7.5 %collective-permute-start.27 = (f32[256,128]{1,0:T(8,128)S(1)}, f32[256,128]{1,0:T(8,128)S(1)}, u32[]{:S(2)}, u32[]{:S(2)}) collective-permute-start(f32[256,128]{1,0:T(8,128)S(1)} %get-tuple-element.117), channel_id=1, source_target_pairs={{0,32},{8,40},{16,48},{24,56},{32,0},{40,8},{48,16},{56,24},{64,96... | collective-permute-start | bytes 393224 | tf_op jit(solution)/shard_map/ppermute | solution.py:56
  117.4 4.5 %collective-permute-start.28 = (f32[256,128]{1,0:T(8,128)S(1)}, f32[256,128]{1,0:T(8,128)S(1)}, u32[]{:S(2)}, u32[]{:S(2)}) collective-permute-start(f32[256,128]{1,0:T(8,128)S(1)} %get-tuple-element.118), channel_id=1, source_target_pairs={{0,48},{8,56},{16,0},{24,8},{32,16},{40,24},{48,32},{56,40},{64,11... | collective-permute-start | bytes 393224 | tf_op jit(solution)/shard_map/ppermute | solution.py:56
  122.5 4.9 %collective-permute-start.29 = (f32[256,512]{1,0:T(8,128)S(1)}, f32[256,512]{1,0:T(8,128)S(1)}, u32[]{:S(2)}, u32[]{:S(2)}) collective-permute-start(f32[256,512]{1,0:T(8,128)S(1)} %get-tuple-element.120), channel_id=1, source_target_pairs={{0,8},{8,0},{16,24},{24,16},{32,40},{40,32},{48,56},{56,48},{64,72... | collective-permute-start | bytes 1572872 | tf_op jit(solution)/shard_map/ppermute | solution.py:48

commit v8 on v7

--- a/solution.py
+++ b/solution.py
@@ -426,7 +426,7 @@
             pltpu.VMEM((blocks * width, cols), F32),
             pltpu.SemaphoreType.DMA((4, blocks)),
         ],
-        compiler_params=pltpu.CompilerParams(vmem_limit_bytes=50 * 2**20),
+        compiler_params=pltpu.CompilerParams(vmem_limit_bytes=46 * 2**20),
         cost_estimate=estimate(blocks, depth, 2 * cols),
     )(first, second, data, tail, initial)
 
@@ -596,8 +596,9 @@
     f31, f20, f11 = across_x(f30), along_z(f30, 1), along_z(f01, -1)
     s31, s20, s11 = across_x(s30), along_z(s30, 1), along_z(s01, -1)
     buffers = add(buffers, [f01, f30, f10], [s01, s30, s10], [(0, 1), (3, 0), (1, 0)])
-    f31, f20, f11, s31, s20, s11, *buffers = together(f31, f20, f11, s31, s20, s11, *buffers)
-    f21, s21 = along_z(f11, -1), along_z(s31, 1)
+    f21 = along_z(f11, -1)
+    f31, f20, f11, f21, s31, s20, s11, *buffers = together(f31, f20, f11, f21, s31, s20, s11, *buffers)
+    s21 = along_z(s31, 1)
     picked, above = pick_first(
         eigvecs,
         {
@@ -623,7 +624,7 @@
         ),
     ]
     buffers = add(buffers, [f31, f20, f11], [s31, s20, s11], [(3, 1), (2, 0), (1, 1)])
-    f21, s21, above, extra, late_extra, *buffers = together(f21, s21, above, *extras, *buffers)
+    f21, s21, extra, late_extra, *buffers = together(f21, s21, *extras, *buffers)
     tail = from_next_row(above)
     buffers = build(
         buffers,

time: 135 us -> 139 us (1.030)
  waiting for transfers between devices: 25.3 us -> 32.4 us
  starting transfers between devices: 48.6 us -> 44.5 us
    ppermute x4, waiting for transfers between devices: 1.13 us -> 4.41 us  [across_x(): return lax.ppermute(value, 'vec', [(v, v ^ 1) for v in range(2 * Z_SIZE)])]
    ppermute x3, starting transfers between devices: 6.76 us -> 4.62 us  [across_core(): lax.ppermute(value, 'row', [(i, i ^ 1) for i in range(lax.axis_size('row'...]
    ppermute x10, starting transfers between devices: 16 us -> 13.9 us  [along_z(): return lax.ppermute(value, 'vec', pairs)]
    ppermute x10, waiting for transfers between devices: 7.23 us -> 9.29 us  [along_z(): return lax.ppermute(value, 'vec', pairs)]
    ppermute x1, starting transfers between devices: 3.82 us -> 1.92 us  [from_next_row(): lax.ppermute(value, 'row', [(i + 1, i) for i in range(lax.axis_size('row'...]
    ppermute x9, waiting for transfers between devices: 6.8 us -> 8.54 us  [along_y(): lax.ppermute(value, 'row', [(i, target(i)) for i in range(lax.axis_size('...]
  transfers between devices with their start and end apart: 30 -> 30, of which waited for: 14 -> 14; matrix products, arithmetic and copies ran while one was open for 0% -> 0% of each run, Pallas kernels for 34% -> 33%
where the time goes in v8:
time: 139 us; the launch traced here: 138 us
  Pallas kernels  57.9 us (42%)
  starting transfers between devices  44.5 us (32%)
  waiting for transfers between devices  32.4 us (23%)
  local copies, waits for them, and re-layouts  1.9 us (1%)
    pallas_call x1, Pallas kernels, sweep_data(): pl.pallas_call(data_kernel, out_shape=(jax.ShapeDtypeStruct((blocks * wid...  17.5 us
    pallas_call x4, Pallas kernels, build(): pl.pallas_call(functools.partial(build_kernel, parts, has_input), out_sha...  16.3 us
    ppermute x10, starting transfers between devices, along_z(): return lax.ppermute(value, 'vec', pairs)  13.9 us
    ppermute x9, starting transfers between devices, along_y(): lax.ppermute(value, 'row', [(i, target(i)) for i in range(lax.axis_size('...  13.6 us
    pallas_call x1, Pallas kernels, sweep_units(): pl.pallas_call(unit_kernel, out_shape=(jax.ShapeDtypeStruct((blocks * wid...  11 us
    ppermute x10, waiting for transfers between devices, along_z(): return lax.ppermute(value, 'vec', pairs)  9.29 us
    ppermute x9, waiting for transfers between devices, along_y(): lax.ppermute(value, 'row', [(i, target(i)) for i in range(lax.axis_size('...  8.54 us
    pallas_call x1, Pallas kernels, correct(): pl.pallas_call(functools.partial(correct_kernel, tile), out_shape=jax.Sha...  7.05 us
  transfers between devices with their start and end apart: 30, of which 14 were waited for; matrix products, arithmetic and copies ran while one was open for 0% of the time, Pallas kernels for 33%

profile of v8, /device:TPU:5, one launch (start us, length us, event | category | flops | bytes accessed | tf_op | source)
XLA Modules:
  0.0 138.5 jit_solution(17570682809749198691)
XLA Ops:
  0.0 1.2 fusion.3
  1.3 3.8 %collective-permute-start.2 = (f32[2,256,128]{2,1,0:T(8,128)S(1)}, f32[2,256,128]{2,1,0:T(8,128)S(1)}, u32[]{:S(2)}, u32[]{:S(2)}) collective-permute-start(f32[2,256,128]{2,1,0:T(8,128)S(1)} %get-tuple-element.122.refs_0_), channel_id=1, source_target_pairs={{0,6},{1,7},{2,0},{3,1},{4,2},{5,3},{6,4},{7,5},{8,14},{9,15},{10,... | collective-permute-start | bytes 786440 | tf_op jit(solution)/shard_map/ppermute | solution.py:40
  5.1 0.9 collective-permute-start
  6.0 0.5 collective-permute-start.10
  6.6 2.7 %collective-permute-start.12 = (f32[2,256,128]{2,1,0:T(8,128)S(1)}, f32[2,256,128]{2,1,0:T(8,128)S(1)}, u32[]{:S(2)}, u32[]{:S(2)}) collective-permute-start(f32[2,256,128]{2,1,0:T(8,128)S(1)} %get-tuple-element.121.refs_1_), channel_id=1, source_target_pairs={{0,6},{1,7},{2,0},{3,1},{4,2},{5,3},{6,4},{7,5},{8,14},{9,15},{10,... | collective-permute-start | bytes 786440 | tf_op jit(solution)/shard_map/ppermute | solution.py:40
  9.2 2.9 %shard_map.37 = (bf16[18,512,256]{2,1,0:T(8,128)(2,1)}, bf16[17,512,256]{2,1,0:T(8,128)(2,1)}) custom-call(f32[2,256,128]{2,1,0:T(8,128)} %copy-done.2, f32[2,256,128]{2,1,0:T(8,128)} %copy-done.1), custom_call_target="tpu_custom_call" | custom-call | flops 1200000000 | bytes 1572864 | tf_op jit(solution)/shard_map/pallas_call | solution.py:168
  12.1 0.1 collective-permute-start.7
  12.2 0.9 collective-permute-done.1.refs_1_.refs_8_
  13.2 4.4 %collective-permute-done.10.refs_3_ = f32[2,256,128]{2,1,0:T(8,128)S(1)} collective-permute-done((f32[2,256,128]{2,1,0:T(8,128)S(1)}, f32[2,256,128]{2,1,0:T(8,128)S(1)}, u32[]{:S(2)}, u32[]{:S(2)}) %collective-permute-start.10) | collective-permute-done | bytes 262176 | tf_op jit(solution)/shard_map/ppermute | solution.py:44
  17.6 2.4 %collective-permute-start.11 = (f32[2,256,128]{2,1,0:T(8,128)S(1)}, f32[2,256,128]{2,1,0:T(8,128)S(1)}, u32[]{:S(2)}, u32[]{:S(2)}) collective-permute-start(f32[2,256,128]{2,1,0:T(8,128)S(1)} %collective-permute-done.10.refs_3_), channel_id=1, source_target_pairs={{0,6},{1,7},{2,0},{3,1},{4,2},{5,3},{6,4},{7,5},{8,14},{9,15},{10,... | collective-permute-start | bytes 786440 | tf_op jit(solution)/shard_map/ppermute | solution.py:40
  20.0 1.4 %collective-permute-start.4 = (f32[2,256,128]{2,1,0:T(8,128)S(1)}, f32[2,256,128]{2,1,0:T(8,128)S(1)}, u32[]{:S(2)}, u32[]{:S(2)}) collective-permute-start(f32[2,256,128]{2,1,0:T(8,128)S(1)} %collective-permute-done.1.refs_1_.refs_8_), channel_id=1, source_target_pairs={{0,2},{1,3},{2,4},{3,5},{4,6},{5,7},{6,0},{7,1},{8,10},{9,11},{10,... | collective-permute-start | bytes 786440 | tf_op jit(solution)/shard_map/ppermute | solution.py:40
  21.4 0.9 collective-permute-start.3
  22.3 0.1 collective-permute-start.9
  22.4 1.1 collective-permute-done.11.refs_7_.refs_5_
  23.5 0.9 collective-permute-start.8
  24.4 4.7 %collective-permute-done.5.refs_6_.refs_2_ = f32[2,256,128]{2,1,0:T(8,128)S(1)} collective-permute-done((f32[2,256,128]{2,1,0:T(8,128)S(1)}, f32[2,256,128]{2,1,0:T(8,128)S(1)}, u32[]{:S(2)}, u32[]{:S(2)}) %collective-permute-start.5) | collective-permute-done | bytes 262176 | tf_op jit(solution)/shard_map/ppermute | solution.py:40
  29.1 3.3 %collective-permute-start.6 = (f32[2,256,128]{2,1,0:T(8,128)S(1)}, f32[2,256,128]{2,1,0:T(8,128)S(1)}, u32[]{:S(2)}, u32[]{:S(2)}) collective-permute-start(f32[2,256,128]{2,1,0:T(8,128)S(1)} %collective-permute-done.5.refs_6_.refs_2_), channel_id=1, source_target_pairs={{0,6},{1,7},{2,0},{3,1},{4,2},{5,3},{6,4},{7,5},{8,14},{9,15},{10,... | collective-permute-start | bytes 786440 | tf_op jit(solution)/shard_map/ppermute | solution.py:40
  32.4 4.8 %shard_map.38 = (bf16[18,512,256]{2,1,0:T(8,128)(2,1)}, bf16[17,512,256]{2,1,0:T(8,128)(2,1)}) custom-call(f32[2,256,128]{2,1,0:T(8,128)} %copy-done.7, f32[2,256,128]{2,1,0:T(8,128)} %copy-done.6, f32[2,256,128]{2,1,0:T(8,128)} %copy-done.5, f32[2,256,128]{2,1,0:T(8,128)} %copy-done.8, ...), custom_call_target="tpu_custom_call", output_to_operand_aliasing={{0}: (6, {}), {1}: (7, {})} | custom-call | flops 3600000000 | bytes 4718592 | tf_op jit(solution)/shard_map/pallas_call | solution.py:168
  37.4 0.6 copy-done.16
  38.0 0.1 copy-done.17
  38.1 0.1 copy-done.12
  38.2 0.1 copy-done.14
  38.3 2.5 %shard_map.39 = (f32[3,256,128]{2,1,0:T(8,128)}, f32[256,1024]{1,0:T(8,128)}) custom-call(f32[2048,1024]{1,0:T(8,128)} %data_hbm.3, f32[2,256,128]{2,1,0:T(8,128)} %copy-done.2, f32[2,256,128]{2,1,0:T(8,128)} %copy-done.1, f32[2,256,128]{2,1,0:T(8,128)} %copy-done.7, f32[2,256,128]{2,1,0:T(8,128)} %copy-done.8, f32[2,256,128]{2,1,0:T(8,128)} %copy-done.5, ...), custom_call_target="tpu_custom_call" | custom-call | tf_op jit(solution)/shard_map/pallas_call | solution.py:100
  40.7 0.7 collective-permute-start.15
  41.4 5.3 %collective-permute-start.14 = (f32[3,256,128]{2,1,0:T(8,128)}, f32[3,256,128]{2,1,0:T(8,128)S(1)}, u32[]{:S(2)}, u32[]{:S(2)}) collective-permute-start(f32[3,256,128]{2,1,0:T(8,128)} %get-tuple-element.79), channel_id=1, source_target_pairs={{8,0},{9,1},{10,2},{11,3},{12,4},{14,6},{15,7},{16,8},{17,9},{18,1... | collective-permute-start | bytes 1179656 | tf_op jit(solution)/shard_map/ppermute | solution.py:617
  46.7 0.1 collective-permute-start.13
  46.8 1.9 %collective-permute-start.17 = (f32[256,1024]{1,0:T(8,128)}, f32[256,1024]{1,0:T(8,128)S(1)}, u32[]{:S(2)}, u32[]{:S(2)}) collective-permute-start(f32[256,1024]{1,0:T(8,128)} %get-tuple-element.95), channel_id=1, source_target_pairs={{8,0},{16,8},{24,16},{32,24},{40,32},{48,40},{56,48},{64,56},{72,6... | collective-permute-start | bytes 3145736 | tf_op jit(solution)/shard_map/ppermute | solution.py:60
  48.7 4.8 %shard_map.40 = (bf16[18,512,256]{2,1,0:T(8,128)(2,1)}, bf16[17,512,256]{2,1,0:T(8,128)(2,1)}) custom-call(f32[2,256,128]{2,1,0:T(8,128)} %copy-done.14, f32[2,256,128]{2,1,0:T(8,128)} %copy-done.12, f32[2,256,128]{2,1,0:T(8,128)} %copy-done.11, f32[2,256,128]{2,1,0:T(8,128)} %copy-done.17, ...), custom_call_target="tpu_custom_call", output_to_operand_aliasing={{0}: (6, {}), {1}: (7, {})} | custom-call | flops 3600000000 | bytes 4718592 | tf_op jit(solution)/shard_map/pallas_call | solution.py:168
  53.6 2.6 %collective-permute-done.13.refs_1_ = f32[2,256,128]{2,1,0:T(8,128)S(1)} collective-permute-done((f32[2,256,128]{2,1,0:T(8,128)}, f32[2,256,128]{2,1,0:T(8,128)S(1)}, u32[]{:S(2)}, u32[]{:S(2)}) %collective-permute-start.13) | collective-permute-done | bytes 262176 | tf_op jit(solution)/shard_map/ppermute | solution.py:40
  56.2 0.7 copy-done.18
  56.8 0.1 copy-done.3
  57.0 0.1 copy-done.4
  57.1 3.8 %shard_map.41 = (bf16[18,512,256]{2,1,0:T(8,128)(2,1)}, bf16[17,512,256]{2,1,0:T(8,128)(2,1)}) custom-call(f32[2,256,128]{2,1,0:T(8,128)} %copy-done.15, f32[2,256,128]{2,1,0:T(8,128)} %copy-done.18, f32[3,256,128]{2,1,0:T(8,128)} %copy-done.4, f32[3,256,128]{2,1,0:T(8,128)} %copy-done.3, ...), custom_call_target="tpu_custom_call", output_to_operand_aliasing={{0}: (4, {}), {1}: (5, {})} | custom-call | flops 2100000000 | bytes 2752512 | tf_op jit(solution)/shard_map/pallas_call | solution.py:168
  60.9 11.0 %shard_map.42 = (f32[2048,256]{1,0:T(8,128)S(1)}, f32[256,256]{1,0:T(8,128)S(1)}, f32[256,1024]{1,0:T(8,128)S(1)}) custom-call(bf16[18,512,256]{2,1,0:T(8,128)(2,1)} %get-tuple-element.93.first_hbm, bf16[17,512,256]{2,1,0:T(8,128)(2,1)} %get-tuple-element.94.second_hbm, f32[2048,1024]{1,0:T(8,128)} %data_hbm.3), custom_call_target="tpu_custom_call" | custom-call | flops 4831838208 | bytes 31457280 | tf_op jit(solution)/shard_map/pallas_call | solution.py:381
  71.9 0.9 collective-permute-start.16
  72.8 1.2 collective-permute-done.16.received.received_transition
  73.9 0.3 shard_map.43.refs_0_
  74.2 2.8 %collective-permute-start.20 = (f32[256,256]{1,0:T(8,128)S(1)}, f32[256,256]{1,0:T(8,128)S(1)}, u32[]{:S(2)}, u32[]{:S(2)}) collective-permute-start(f32[256,256]{1,0:T(8,128)S(1)} %shard_map.43.refs_0_), channel_id=1, source_target_pairs={{0,48},{8,56},{16,0},{24,8},{32,16},{40,24},{48,32},{56,40},{64,11... | collective-permute-start | bytes 786440 | tf_op jit(solution)/shard_map/ppermute | solution.py:56
  77.1 0.3 collective-permute-start.19
  77.4 0.7 collective-permute-start.18
  78.1 17.5 %shard_map.44 = (f32[2048,1024]{1,0:T(8,128)}, f32[256,512]{1,0:T(8,128)S(1)}, f32[256,512]{1,0:T(8,128)S(1)}) custom-call(bf16[18,512,256]{2,1,0:T(8,128)(2,1)} %get-tuple-element.93.first_hbm, bf16[17,512,256]{2,1,0:T(8,128)(2,1)S(1)} %copy-done, f32[2048,1024]{1,0:T(8,128)} %data_hbm.3, f32[256,1024]{1,0:T(8,128)S(1)} %collective-permute-done.17.tail_hbm, ...), custom_call_target="tpu_custom_call" | custom-call | flops 12884901888 | bytes 31457280 | tf_op jit(solution)/shard_map/pallas_call | solution.py:410
  95.7 1.3 collective-permute-start.21
  97.0 1.5 %collective-permute-done.21.received = f32[256,512]{1,0:T(8,128)S(1)} collective-permute-done((f32[256,512]{1,0:T(8,128)S(1)}, f32[256,512]{1,0:T(8,128)S(1)}, u32[]{:S(2)}, u32[]{:S(2)}) %collective-permute-start.21) | collective-permute-done | bytes 524320 | tf_op jit(solution)/shard_map/ppermute | solution.py:48
  98.5 0.5 shard_map.46
  99.0 1.7 %collective-permute-start.22 = (f32[256,128]{1,0:T(8,128)S(1)}, f32[256,128]{1,0:T(8,128)S(1)}, u32[]{:S(2)}, u32[]{:S(2)}) collective-permute-start(f32[256,128]{1,0:T(8,128)S(1)} %get-tuple-element.109), channel_id=1, source_target_pairs={{0,16},{8,24},{16,32},{24,40},{32,48},{40,56},{48,0},{56,8},{64,80... | collective-permute-start | bytes 393224 | tf_op jit(solution)/shard_map/ppermute | solution.py:56
  100.7 1.5 %collective-permute-start.23 = (f32[256,128]{1,0:T(8,128)S(1)}, f32[256,128]{1,0:T(8,128)S(1)}, u32[]{:S(2)}, u32[]{:S(2)}) collective-permute-start(f32[256,128]{1,0:T(8,128)S(1)} %get-tuple-element.110), channel_id=1, source_target_pairs={{0,32},{8,40},{16,48},{24,56},{32,0},{40,8},{48,16},{56,24},{64,96... | collective-permute-start | bytes 393224 | tf_op jit(solution)/shard_map/ppermute | solution.py:56
  102.3 0.9 collective-permute-start.24
  103.2 0.8 shard_map.45
  104.0 1.0 collective-permute-done.22.refs_1_
  105.0 3.3 %collective-permute-done.23.refs_2_ = f32[256,128]{1,0:T(8,128)S(1)} collective-permute-done((f32[256,128]{1,0:T(8,128)S(1)}, f32[256,128]{1,0:T(8,128)S(1)}, u32[]{:S(2)}, u32[]{:S(2)}) %collective-permute-start.23) | collective-permute-done | bytes 131104 | tf_op jit(solution)/shard_map/ppermute | solution.py:56
  108.3 0.9 shard_map.47
  109.2 1.3 collective-permute-start.25
  110.5 5.9 %collective-permute-done.25.entering = f32[256,128]{1,0:T(8,128)S(1)} collective-permute-done((f32[256,128]{1,0:T(8,128)S(1)}, f32[256,128]{1,0:T(8,128)S(1)}, u32[]{:S(2)}, u32[]{:S(2)}) %collective-permute-start.25) | collective-permute-done | bytes 131104 | tf_op jit(solution)/shard_map/ppermute | solution.py:660
  116.5 0.5 shard_map.48
  117.0 3.0 %collective-permute-start.26 = (f32[256,128]{1,0:T(8,128)S(1)}, f32[256,128]{1,0:T(8,128)S(1)}, u32[]{:S(2)}, u32[]{:S(2)}) collective-permute-start(f32[256,128]{1,0:T(8,128)S(1)} %get-tuple-element.116), channel_id=1, source_target_pairs={{0,16},{8,24},{16,32},{24,40},{32,48},{40,56},{48,0},{56,8},{64,80... | collective-permute-start | bytes 393224 | tf_op jit(solution)/shard_map/ppermute | solution.py:56
  120.0 1.7 %collective-permute-start.27 = (f32[256,128]{1,0:T(8,128)S(1)}, f32[256,128]{1,0:T(8,128)S(1)}, u32[]{:S(2)}, u32[]{:S(2)}) collective-permute-start(f32[256,128]{1,0:T(8,128)S(1)} %get-tuple-element.117), channel_id=1, source_target_pairs={{0,32},{8,40},{16,48},{24,56},{32,0},{40,8},{48,16},{56,24},{64,96... | collective-permute-start | bytes 393224 | tf_op jit(solution)/shard_map/ppermute | solution.py:56
  121.8 0.8 collective-permute-start.28
  122.5 0.4 collective-permute-done.26.refs_1_
  122.9 3.3 %collective-permute-done.27.refs_2_ = f32[256,128]{1,0:T(8,128)S(1)} collective-permute-done((f32[256,128]{1,0:T(8,128)S(1)}, f32[256,128]{1,0:T(8,128)S(1)}, u32[]{:S(2)}, u32[]{:S(2)}) %collective-permute-start.27) | collective-permute-done | bytes 131104 | tf_op jit(solution)/shard_map/ppermute | solution.py:56
  126.2 0.5 collective-permute-done.28.refs_3_
  126.7 0.5 shard_map.49
  127.3 2.4 %collective-permute-start.29 = (f32[256,512]{1,0:T(8,128)S(1)}, f32[256,512]{1,0:T(8,128)S(1)}, u32[]{:S(2)}, u32[]{:S(2)}) collective-permute-start(f32[256,512]{1,0:T(8,128)S(1)} %get-tuple-element.120), channel_id=1, source_target_pairs={{0,8},{8,0},{16,24},{24,16},{32,40},{40,32},{48,56},{56,48},{64,72... | collective-permute-start | bytes 1572872 | tf_op jit(solution)/shard_map/ppermute | solution.py:48
  129.7 1.5 %collective-permute-done.29.taken = f32[256,512]{1,0:T(8,128)S(1)} collective-permute-done((f32[256,512]{1,0:T(8,128)S(1)}, f32[256,512]{1,0:T(8,128)S(1)}, u32[]{:S(2)}, u32[]{:S(2)}) %collective-permute-start.29) | collective-permute-done | bytes 524320 | tf_op jit(solution)/shard_map/ppermute | solution.py:48
  131.2 7.1 %shard_map.50 = f32[2048,1024]{1,0:T(8,128)} custom-call(f32[2048,1024]{1,0:T(8,128)} %get-tuple-element.97.rows_hbm, f32[2048,256]{1,0:T(8,128)S(1)} %get-tuple-element.98.response_hbm, f32[256,512]{1,0:T(8,128)S(1)} %get-tuple-element.119.kept, f32[256,512]{1,0:T(8,128)S(1)} %collective-permute-done.29.taken), custom_call_target="tpu_custom_call" | custom-call | tf_op jit(solution)/shard_map/pallas_call | solution.py:557
  (51 shorter events, 0.2 us)
Async XLA Ops:
  1.2 8.0 %copy-start.1 = (f32[2,256,128]{2,1,0:T(8,128)}, f32[2,256,128]{2,1,0:T(8,128)S(1)}, u32[]{:S(2)}) copy-start(f32[2,256,128]{2,1,0:T(8,128)S(1)} %get-tuple-element.121.refs_1_) | copy-start | bytes 786436
  1.2 8.0 %copy-start.2 = (f32[2,256,128]{2,1,0:T(8,128)}, f32[2,256,128]{2,1,0:T(8,128)S(1)}, u32[]{:S(2)}) copy-start(f32[2,256,128]{2,1,0:T(8,128)S(1)} %get-tuple-element.122.refs_0_) | copy-start | bytes 786436
  1.3 10.9 %collective-permute-start.2 = (f32[2,256,128]{2,1,0:T(8,128)S(1)}, f32[2,256,128]{2,1,0:T(8,128)S(1)}, u32[]{:S(2)}, u32[]{:S(2)}) collective-permute-start(f32[2,256,128]{2,1,0:T(8,128)S(1)} %get-tuple-element.122.refs_0_), channel_id=1, source_target_pairs={{0,6},{1,7},{2,0},{3,1},{4,2},{5,3},{6,4},{7,5},{8,14},{9,15},{10,... | collective-permute-start | bytes 786440 | tf_op jit(solution)/shard_map/ppermute | solution.py:40
  5.1 8.1 %collective-permute-start.1 = (f32[2,256,128]{2,1,0:T(8,128)S(1)}, f32[2,256,128]{2,1,0:T(8,128)S(1)}, u32[]{:S(2)}, u32[]{:S(2)}) collective-permute-start(f32[2,256,128]{2,1,0:T(8,128)S(1)} %get-tuple-element.122.refs_0_), channel_id=1, source_target_pairs={{0,2},{1,3},{2,4},{3,5},{4,6},{5,7},{6,0},{7,1},{8,10},{9,11},{10,... | collective-permute-start | bytes 786440 | tf_op jit(solution)/shard_map/ppermute | solution.py:40
  5.1 8.1 %collective-permute-start = (f32[2,256,128]{2,1,0:T(8,128)S(1)}, f32[2,256,128]{2,1,0:T(8,128)S(1)}, u32[]{:S(2)}, u32[]{:S(2)}) collective-permute-start(f32[2,256,128]{2,1,0:T(8,128)S(1)} %get-tuple-element.122.refs_0_), channel_id=1, source_target_pairs={{0,1},{1,0},{2,3},{3,2},{4,5},{5,4},{6,7},{7,6},{8,9},{9,8},{10,11... | collective-permute-start | bytes 786440 | tf_op jit(solution)/shard_map/ppermute | solution.py:44
  6.0 11.6 %collective-permute-start.10 = (f32[2,256,128]{2,1,0:T(8,128)S(1)}, f32[2,256,128]{2,1,0:T(8,128)S(1)}, u32[]{:S(2)}, u32[]{:S(2)}) collective-permute-start(f32[2,256,128]{2,1,0:T(8,128)S(1)} %get-tuple-element.121.refs_1_), channel_id=1, source_target_pairs={{0,1},{1,0},{2,3},{3,2},{4,5},{5,4},{6,7},{7,6},{8,9},{9,8},{10,11... | collective-permute-start | bytes 786440 | tf_op jit(solution)/shard_map/ppermute | solution.py:44
  6.6 14.9 %collective-permute-start.12 = (f32[2,256,128]{2,1,0:T(8,128)S(1)}, f32[2,256,128]{2,1,0:T(8,128)S(1)}, u32[]{:S(2)}, u32[]{:S(2)}) collective-permute-start(f32[2,256,128]{2,1,0:T(8,128)S(1)} %get-tuple-element.121.refs_1_), channel_id=1, source_target_pairs={{0,6},{1,7},{2,0},{3,1},{4,2},{5,3},{6,4},{7,5},{8,14},{9,15},{10,... | collective-permute-start | bytes 786440 | tf_op jit(solution)/shard_map/ppermute | solution.py:40
  12.1 20.3 %copy-start.5 = (f32[2,256,128]{2,1,0:T(8,128)}, f32[2,256,128]{2,1,0:T(8,128)S(1)}, u32[]{:S(2)}) copy-start(f32[2,256,128]{2,1,0:T(8,128)S(1)} %collective-permute-done.2.refs_2_.refs_4_) | copy-start | bytes 786436
  12.1 10.2 %collective-permute-start.7 = (f32[2,256,128]{2,1,0:T(8,128)}, f32[2,256,128]{2,1,0:T(8,128)S(1)}, u32[]{:S(2)}, u32[]{:S(2)}) collective-permute-start(f32[2,256,128]{2,1,0:T(8,128)} %copy-done.1), channel_id=1, source_target_pairs={{0,2},{1,3},{2,4},{3,5},{4,6},{5,7},{6,0},{7,1},{8,10},{9,11},{10,... | collective-permute-start | bytes 786440 | tf_op jit(solution)/shard_map/ppermute | solution.py:40
  13.1 19.3 %copy-start.6 = (f32[2,256,128]{2,1,0:T(8,128)}, f32[2,256,128]{2,1,0:T(8,128)S(1)}, u32[]{:S(2)}) copy-start(f32[2,256,128]{2,1,0:T(8,128)S(1)} %collective-permute-done.1.refs_1_.refs_8_) | copy-start | bytes 786436
  13.2 19.3 %copy-start.7 = (f32[2,256,128]{2,1,0:T(8,128)}, f32[2,256,128]{2,1,0:T(8,128)S(1)}, u32[]{:S(2)}) copy-start(f32[2,256,128]{2,1,0:T(8,128)S(1)} %collective-permute-done.refs_0_.refs_2_) | copy-start | bytes 786436
  17.6 14.9 %copy-start.8 = (f32[2,256,128]{2,1,0:T(8,128)}, f32[2,256,128]{2,1,0:T(8,128)S(1)}, u32[]{:S(2)}) copy-start(f32[2,256,128]{2,1,0:T(8,128)S(1)} %collective-permute-done.10.refs_3_) | copy-start | bytes 786436
  17.6 5.9 %collective-permute-start.11 = (f32[2,256,128]{2,1,0:T(8,128)S(1)}, f32[2,256,128]{2,1,0:T(8,128)S(1)}, u32[]{:S(2)}, u32[]{:S(2)}) collective-permute-start(f32[2,256,128]{2,1,0:T(8,128)S(1)} %collective-permute-done.10.refs_3_), channel_id=1, source_target_pairs={{0,6},{1,7},{2,0},{3,1},{4,2},{5,3},{6,4},{7,5},{8,14},{9,15},{10,... | collective-permute-start | bytes 786440 | tf_op jit(solution)/shard_map/ppermute | solution.py:40
  19.9 9.2 %collective-permute-start.5 = (f32[2,256,128]{2,1,0:T(8,128)S(1)}, f32[2,256,128]{2,1,0:T(8,128)S(1)}, u32[]{:S(2)}, u32[]{:S(2)}) collective-permute-start(f32[2,256,128]{2,1,0:T(8,128)S(1)} %collective-permute-done.refs_0_.refs_2_), channel_id=1, source_target_pairs={{0,6},{1,7},{2,0},{3,1},{4,2},{5,3},{6,4},{7,5},{8,14},{9,15},{10,... | collective-permute-start | bytes 786440 | tf_op jit(solution)/shard_map/ppermute | solution.py:40
  20.0 17.3 %collective-permute-start.4 = (f32[2,256,128]{2,1,0:T(8,128)S(1)}, f32[2,256,128]{2,1,0:T(8,128)S(1)}, u32[]{:S(2)}, u32[]{:S(2)}) collective-permute-start(f32[2,256,128]{2,1,0:T(8,128)S(1)} %collective-permute-done.1.refs_1_.refs_8_), channel_id=1, source_target_pairs={{0,2},{1,3},{2,4},{3,5},{4,6},{5,7},{6,0},{7,1},{8,10},{9,11},{10,... | collective-permute-start | bytes 786440 | tf_op jit(solution)/shard_map/ppermute | solution.py:40
  21.4 11.0 %copy-start.9 = (f32[2,256,128]{2,1,0:T(8,128)}, f32[2,256,128]{2,1,0:T(8,128)S(1)}, u32[]{:S(2)}) copy-start(f32[2,256,128]{2,1,0:T(8,128)S(1)} %collective-permute-done.12.refs_5_) | copy-start | bytes 786436
  21.4 15.9 %collective-permute-start.3 = (f32[2,256,128]{2,1,0:T(8,128)S(1)}, f32[2,256,128]{2,1,0:T(8,128)S(1)}, u32[]{:S(2)}, u32[]{:S(2)}) collective-permute-start(f32[2,256,128]{2,1,0:T(8,128)S(1)} %collective-permute-done.1.refs_1_.refs_8_), channel_id=1, source_target_pairs={{0,1},{1,0},{2,3},{3,2},{4,5},{5,4},{6,7},{7,6},{8,9},{9,8},{10,11... | collective-permute-start | bytes 786440 | tf_op jit(solution)/shard_map/ppermute | solution.py:44
  22.3 10.1 %copy-start.13 = (f32[2,256,128]{2,1,0:T(8,128)}, f32[2,256,128]{2,1,0:T(8,128)S(1)}, u32[]{:S(2)}) copy-start(f32[2,256,128]{2,1,0:T(8,128)S(1)} %collective-permute-done.7.refs_4_.refs_9_) | copy-start | bytes 786436
  22.3 14.9 %collective-permute-start.9 = (f32[2,256,128]{2,1,0:T(8,128)S(1)}, f32[2,256,128]{2,1,0:T(8,128)S(1)}, u32[]{:S(2)}, u32[]{:S(2)}) collective-permute-start(f32[2,256,128]{2,1,0:T(8,128)S(1)} %collective-permute-done.7.refs_4_.refs_9_), channel_id=1, source_target_pairs={{0,2},{1,3},{2,4},{3,5},{4,6},{5,7},{6,0},{7,1},{8,10},{9,11},{10,... | collective-permute-start | bytes 786440 | tf_op jit(solution)/shard_map/ppermute | solution.py:40
  23.5 13.8 %copy-start.10 = (f32[2,256,128]{2,1,0:T(8,128)}, f32[2,256,128]{2,1,0:T(8,128)S(1)}, u32[]{:S(2)}) copy-start(f32[2,256,128]{2,1,0:T(8,128)S(1)} %collective-permute-done.11.refs_7_.refs_5_) | copy-start | bytes 786436
  23.5 13.8 %collective-permute-start.8 = (f32[2,256,128]{2,1,0:T(8,128)S(1)}, f32[2,256,128]{2,1,0:T(8,128)S(1)}, u32[]{:S(2)}, u32[]{:S(2)}) collective-permute-start(f32[2,256,128]{2,1,0:T(8,128)S(1)} %collective-permute-done.7.refs_4_.refs_9_), channel_id=1, source_target_pairs={{0,1},{1,0},{2,3},{3,2},{4,5},{5,4},{6,7},{7,6},{8,9},{9,8},{10,11... | collective-permute-start | bytes 786440 | tf_op jit(solution)/shard_map/ppermute | solution.py:44
  29.1 8.1 %copy-start.11 = (f32[2,256,128]{2,1,0:T(8,128)}, f32[2,256,128]{2,1,0:T(8,128)S(1)}, u32[]{:S(2)}) copy-start(f32[2,256,128]{2,1,0:T(8,128)S(1)} %collective-permute-done.5.refs_6_.refs_2_) | copy-start | bytes 786436
  29.1 8.2 %collective-permute-start.6 = (f32[2,256,128]{2,1,0:T(8,128)S(1)}, f32[2,256,128]{2,1,0:T(8,128)S(1)}, u32[]{:S(2)}, u32[]{:S(2)}) collective-permute-start(f32[2,256,128]{2,1,0:T(8,128)S(1)} %collective-permute-done.5.refs_6_.refs_2_), channel_id=1, source_target_pairs={{0,6},{1,7},{2,0},{3,1},{4,2},{5,3},{6,4},{7,5},{8,14},{9,15},{10,... | collective-permute-start | bytes 786440 | tf_op jit(solution)/shard_map/ppermute | solution.py:40
  37.3 0.7 copy-start.16
  37.3 0.8 copy-start.17
  37.3 0.9 copy-start.12
  37.3 0.9 copy-start.14
  37.4 3.4 %copy-start.15 = (f32[2,256,128]{2,1,0:T(8,128)}, f32[2,256,128]{2,1,0:T(8,128)S(1)}, u32[]{:S(2)}) copy-start(f32[2,256,128]{2,1,0:T(8,128)S(1)} %collective-permute-done.6.refs_0_) | copy-start | bytes 786436
  40.7 15.4 %collective-permute-start.15 = (f32[3,256,128]{2,1,0:T(8,128)}, f32[3,256,128]{2,1,0:T(8,128)S(1)}, u32[]{:S(2)}, u32[]{:S(2)}) collective-permute-start(f32[3,256,128]{2,1,0:T(8,128)} %get-tuple-element.79), channel_id=1, source_target_pairs={{12,5},{20,13},{28,21},{36,29},{44,37},{52,45},{60,53},{68,61},{76... | collective-permute-start | bytes 1179656 | tf_op jit(solution)/shard_map/ppermute | solution.py:622
  41.4 14.7 %collective-permute-start.14 = (f32[3,256,128]{2,1,0:T(8,128)}, f32[3,256,128]{2,1,0:T(8,128)S(1)}, u32[]{:S(2)}, u32[]{:S(2)}) collective-permute-start(f32[3,256,128]{2,1,0:T(8,128)} %get-tuple-element.79), channel_id=1, source_target_pairs={{8,0},{9,1},{10,2},{11,3},{12,4},{14,6},{15,7},{16,8},{17,9},{18,1... | collective-permute-start | bytes 1179656 | tf_op jit(solution)/shard_map/ppermute | solution.py:617
  46.7 9.4 %collective-permute-start.13 = (f32[2,256,128]{2,1,0:T(8,128)}, f32[2,256,128]{2,1,0:T(8,128)S(1)}, u32[]{:S(2)}, u32[]{:S(2)}) collective-permute-start(f32[2,256,128]{2,1,0:T(8,128)} %copy-done.17), channel_id=1, source_target_pairs={{0,2},{1,3},{2,4},{3,5},{4,6},{5,7},{6,0},{7,1},{8,10},{9,11},{10,... | collective-permute-start | bytes 786440 | tf_op jit(solution)/shard_map/ppermute | solution.py:40
  46.8 31.3 %collective-permute-start.17 = (f32[256,1024]{1,0:T(8,128)}, f32[256,1024]{1,0:T(8,128)S(1)}, u32[]{:S(2)}, u32[]{:S(2)}) collective-permute-start(f32[256,1024]{1,0:T(8,128)} %get-tuple-element.95), channel_id=1, source_target_pairs={{8,0},{16,8},{24,16},{32,24},{40,32},{48,40},{56,48},{64,56},{72,6... | collective-permute-start | bytes 3145736 | tf_op jit(solution)/shard_map/ppermute | solution.py:60
  56.1 0.7 copy-start.18
  56.1 0.8 copy-start.3
  56.1 1.0 copy-start.4
  60.9 17.2 %copy-start = (bf16[17,512,256]{2,1,0:T(8,128)(2,1)S(1)}, bf16[17,512,256]{2,1,0:T(8,128)(2,1)}, u32[]{:S(2)}) copy-start(bf16[17,512,256]{2,1,0:T(8,128)(2,1)} %get-tuple-element.94.second_hbm) | copy-start | bytes 13369348
  71.9 2.0 %collective-permute-start.16 = (f32[256,256]{1,0:T(8,128)S(1)}, f32[256,256]{1,0:T(8,128)S(1)}, u32[]{:S(2)}, u32[]{:S(2)}) collective-permute-start(f32[256,256]{1,0:T(8,128)S(1)} %get-tuple-element.92.own.own_transition), channel_id=1, source_target_pairs={{0,8},{8,0},{16,24},{24,16},{32,40},{40,32},{48,56},{56,48},{64,72... | collective-permute-start | bytes 786440 | tf_op jit(solution)/shard_map/ppermute | solution.py:48
  74.2 21.4 %collective-permute-start.20 = (f32[256,256]{1,0:T(8,128)S(1)}, f32[256,256]{1,0:T(8,128)S(1)}, u32[]{:S(2)}, u32[]{:S(2)}) collective-permute-start(f32[256,256]{1,0:T(8,128)S(1)} %shard_map.43.refs_0_), channel_id=1, source_target_pairs={{0,48},{8,56},{16,0},{24,8},{32,16},{40,24},{48,32},{56,40},{64,11... | collective-permute-start | bytes 786440 | tf_op jit(solution)/shard_map/ppermute | solution.py:56
  77.1 18.6 %collective-permute-start.19 = (f32[256,256]{1,0:T(8,128)S(1)}, f32[256,256]{1,0:T(8,128)S(1)}, u32[]{:S(2)}, u32[]{:S(2)}) collective-permute-start(f32[256,256]{1,0:T(8,128)S(1)} %shard_map.43.refs_0_), channel_id=1, source_target_pairs={{0,32},{8,40},{16,48},{24,56},{32,0},{40,8},{48,16},{56,24},{64,96... | collective-permute-start | bytes 786440 | tf_op jit(solution)/shard_map/ppermute | solution.py:56
  77.4 18.2 %collective-permute-start.18 = (f32[256,256]{1,0:T(8,128)S(1)}, f32[256,256]{1,0:T(8,128)S(1)}, u32[]{:S(2)}, u32[]{:S(2)}) collective-permute-start(f32[256,256]{1,0:T(8,128)S(1)} %shard_map.43.refs_0_), channel_id=1, source_target_pairs={{0,16},{8,24},{16,32},{24,40},{32,48},{40,56},{48,0},{56,8},{64,80... | collective-permute-start | bytes 786440 | tf_op jit(solution)/shard_map/ppermute | solution.py:56
  95.7 2.8 %collective-permute-start.21 = (f32[256,512]{1,0:T(8,128)S(1)}, f32[256,512]{1,0:T(8,128)S(1)}, u32[]{:S(2)}, u32[]{:S(2)}) collective-permute-start(f32[256,512]{1,0:T(8,128)S(1)} %get-tuple-element.102), channel_id=1, source_target_pairs={{0,8},{8,0},{16,24},{24,16},{32,40},{40,32},{48,56},{56,48},{64,72... | collective-permute-start | bytes 1572872 | tf_op jit(solution)/shard_map/ppermute | solution.py:48
  99.0 6.0 %collective-permute-start.22 = (f32[256,128]{1,0:T(8,128)S(1)}, f32[256,128]{1,0:T(8,128)S(1)}, u32[]{:S(2)}, u32[]{:S(2)}) collective-permute-start(f32[256,128]{1,0:T(8,128)S(1)} %get-tuple-element.109), channel_id=1, source_target_pairs={{0,16},{8,24},{16,32},{24,40},{32,48},{40,56},{48,0},{56,8},{64,80... | collective-permute-start | bytes 393224 | tf_op jit(solution)/shard_map/ppermute | solution.py:56
  100.7 7.6 %collective-permute-start.23 = (f32[256,128]{1,0:T(8,128)S(1)}, f32[256,128]{1,0:T(8,128)S(1)}, u32[]{:S(2)}, u32[]{:S(2)}) collective-permute-start(f32[256,128]{1,0:T(8,128)S(1)} %get-tuple-element.110), channel_id=1, source_target_pairs={{0,32},{8,40},{16,48},{24,56},{32,0},{40,8},{48,16},{56,24},{64,96... | collective-permute-start | bytes 393224 | tf_op jit(solution)/shard_map/ppermute | solution.py:56
  102.3 6.1 %collective-permute-start.24 = (f32[256,128]{1,0:T(8,128)S(1)}, f32[256,128]{1,0:T(8,128)S(1)}, u32[]{:S(2)}, u32[]{:S(2)}) collective-permute-start(f32[256,128]{1,0:T(8,128)S(1)} %get-tuple-element.111), channel_id=1, source_target_pairs={{0,48},{8,56},{16,0},{24,8},{32,16},{40,24},{48,32},{56,40},{64,11... | collective-permute-start | bytes 393224 | tf_op jit(solution)/shard_map/ppermute | solution.py:56
  109.2 7.2 %collective-permute-start.25 = (f32[256,128]{1,0:T(8,128)S(1)}, f32[256,128]{1,0:T(8,128)S(1)}, u32[]{:S(2)}, u32[]{:S(2)}) collective-permute-start(f32[256,128]{1,0:T(8,128)S(1)} %get-tuple-element.112), channel_id=1, source_target_pairs={{0,64},{8,72},{16,80},{24,88},{32,96},{40,104},{48,112},{56,120},{... | collective-permute-start | bytes 393224 | tf_op jit(solution)/shard_map/ppermute | solution.py:660
  117.0 6.0 %collective-permute-start.26 = (f32[256,128]{1,0:T(8,128)S(1)}, f32[256,128]{1,0:T(8,128)S(1)}, u32[]{:S(2)}, u32[]{:S(2)}) collective-permute-start(f32[256,128]{1,0:T(8,128)S(1)} %get-tuple-element.116), channel_id=1, source_target_pairs={{0,16},{8,24},{16,32},{24,40},{32,48},{40,56},{48,0},{56,8},{64,80... | collective-permute-start | bytes 393224 | tf_op jit(solution)/shard_map/ppermute | solution.py:56
  120.0 6.2 %collective-permute-start.27 = (f32[256,128]{1,0:T(8,128)S(1)}, f32[256,128]{1,0:T(8,128)S(1)}, u32[]{:S(2)}, u32[]{:S(2)}) collective-permute-start(f32[256,128]{1,0:T(8,128)S(1)} %get-tuple-element.117), channel_id=1, source_target_pairs={{0,32},{8,40},{16,48},{24,56},{32,0},{40,8},{48,16},{56,24},{64,96... | collective-permute-start | bytes 393224 | tf_op jit(solution)/shard_map/ppermute | solution.py:56
  121.8 5.0 %collective-permute-start.28 = (f32[256,128]{1,0:T(8,128)S(1)}, f32[256,128]{1,0:T(8,128)S(1)}, u32[]{:S(2)}, u32[]{:S(2)}) collective-permute-start(f32[256,128]{1,0:T(8,128)S(1)} %get-tuple-element.118), channel_id=1, source_target_pairs={{0,48},{8,56},{16,0},{24,8},{32,16},{40,24},{48,32},{56,40},{64,11... | collective-permute-start | bytes 393224 | tf_op jit(solution)/shard_map/ppermute | solution.py:56
  127.3 4.0 %collective-permute-start.29 = (f32[256,512]{1,0:T(8,128)S(1)}, f32[256,512]{1,0:T(8,128)S(1)}, u32[]{:S(2)}, u32[]{:S(2)}) collective-permute-start(f32[256,512]{1,0:T(8,128)S(1)} %get-tuple-element.120), channel_id=1, source_target_pairs={{0,8},{8,0},{16,24},{24,16},{32,40},{40,32},{48,56},{56,48},{64,72... | collective-permute-start | bytes 1572872 | tf_op jit(solution)/shard_map/ppermute | solution.py:48

commit v9 on v7

--- a/solution.py
+++ b/solution.py
@@ -426,7 +426,7 @@
             pltpu.VMEM((blocks * width, cols), F32),
             pltpu.SemaphoreType.DMA((4, blocks)),
         ],
-        compiler_params=pltpu.CompilerParams(vmem_limit_bytes=50 * 2**20),
+        compiler_params=pltpu.CompilerParams(vmem_limit_bytes=46 * 2**20),
         cost_estimate=estimate(blocks, depth, 2 * cols),
     )(first, second, data, tail, initial)
 
@@ -623,7 +623,7 @@
         ),
     ]
     buffers = add(buffers, [f31, f20, f11], [s31, s20, s11], [(3, 1), (2, 0), (1, 1)])
-    f21, s21, above, extra, late_extra, *buffers = together(f21, s21, above, *extras, *buffers)
+    f21, s21, extra, late_extra, *buffers = together(f21, s21, *extras, *buffers)
     tail = from_next_row(above)
     buffers = build(
         buffers,

time: 135 us -> 134 us (level)
    ppermute x10, waiting for transfers between devices: 7.23 us -> 4.34 us  [along_z(): return lax.ppermute(value, 'vec', pairs)]
    ppermute x9, waiting for transfers between devices: 6.8 us -> 8.53 us  [along_y(): lax.ppermute(value, 'row', [(i, target(i)) for i in range(lax.axis_size('...]
where the time goes in v9:
time: 134 us; the launch traced here: 133 us
  Pallas kernels  57.9 us (43%)
  starting transfers between devices  47.8 us (36%)
  waiting for transfers between devices  24.1 us (18%)
  local copies, waits for them, and re-layouts  1.95 us (1%)
    pallas_call x1, Pallas kernels, sweep_data(): pl.pallas_call(data_kernel, out_shape=(jax.ShapeDtypeStruct((blocks * wid...  17.5 us
    pallas_call x4, Pallas kernels, build(): pl.pallas_call(functools.partial(build_kernel, parts, has_input), out_sha...  16.3 us
    ppermute x10, starting transfers between devices, along_z(): return lax.ppermute(value, 'vec', pairs)  16 us
    ppermute x9, starting transfers between devices, along_y(): lax.ppermute(value, 'row', [(i, target(i)) for i in range(lax.axis_size('...  13.5 us
    pallas_call x1, Pallas kernels, sweep_units(): pl.pallas_call(unit_kernel, out_shape=(jax.ShapeDtypeStruct((blocks * wid...  11 us
    ppermute x9, waiting for transfers between devices, along_y(): lax.ppermute(value, 'row', [(i, target(i)) for i in range(lax.axis_size('...  8.53 us
    pallas_call x1, Pallas kernels, correct(): pl.pallas_call(functools.partial(correct_kernel, tile), out_shape=jax.Sha...  7.05 us
    ppermute x1, waiting for transfers between devices, local(): lax.ppermute(total, 'row', [(i, i + rows // 2) for i in range(rows // 2)])  5.92 us
  transfers between devices with their start and end apart: 30, of which 14 were waited for; matrix products, arithmetic and copies ran while one was open for 0% of the time, Pallas kernels for 34%

profile of v9, /device:TPU:5, one launch (start us, length us, event | category | flops | bytes accessed | tf_op | source)
XLA Modules:
  0.0 133.5 jit_solution(9903340098454254391)
XLA Ops:
  0.0 1.2 fusion.3
  1.3 1.0 collective-permute-start.9
  2.3 3.8 %collective-permute-start.2 = (f32[2,256,128]{2,1,0:T(8,128)S(1)}, f32[2,256,128]{2,1,0:T(8,128)S(1)}, u32[]{:S(2)}, u32[]{:S(2)}) collective-permute-start(f32[2,256,128]{2,1,0:T(8,128)S(1)} %get-tuple-element.120.refs_0_), channel_id=1, source_target_pairs={{0,6},{1,7},{2,0},{3,1},{4,2},{5,3},{6,4},{7,5},{8,14},{9,15},{10,... | collective-permute-start | bytes 786440 | tf_op jit(solution)/shard_map/ppermute | solution.py:40
  6.0 0.5 collective-permute-start
  6.6 2.7 %collective-permute-start.11 = (f32[2,256,128]{2,1,0:T(8,128)S(1)}, f32[2,256,128]{2,1,0:T(8,128)S(1)}, u32[]{:S(2)}, u32[]{:S(2)}) collective-permute-start(f32[2,256,128]{2,1,0:T(8,128)S(1)} %get-tuple-element.119.refs_1_), channel_id=1, source_target_pairs={{0,6},{1,7},{2,0},{3,1},{4,2},{5,3},{6,4},{7,5},{8,14},{9,15},{10,... | collective-permute-start | bytes 786440 | tf_op jit(solution)/shard_map/ppermute | solution.py:40
  9.2 0.9 collective-permute-start.6
  10.1 0.5 collective-permute-done.2.refs_2_.refs_4_
  10.7 3.4 %collective-permute-start.10 = (f32[2,256,128]{2,1,0:T(8,128)S(1)}, f32[2,256,128]{2,1,0:T(8,128)S(1)}, u32[]{:S(2)}, u32[]{:S(2)}) collective-permute-start(f32[2,256,128]{2,1,0:T(8,128)S(1)} %collective-permute-done.9.refs_3_), channel_id=1, source_target_pairs={{0,6},{1,7},{2,0},{3,1},{4,2},{5,3},{6,4},{7,5},{8,14},{9,15},{10,... | collective-permute-start | bytes 786440 | tf_op jit(solution)/shard_map/ppermute | solution.py:40
  14.1 2.9 %shard_map.37 = (bf16[18,512,256]{2,1,0:T(8,128)(2,1)}, bf16[17,512,256]{2,1,0:T(8,128)(2,1)}) custom-call(f32[2,256,128]{2,1,0:T(8,128)} %copy-done.2, f32[2,256,128]{2,1,0:T(8,128)} %copy-done.1), custom_call_target="tpu_custom_call" | custom-call | flops 1200000000 | bytes 1572864 | tf_op jit(solution)/shard_map/pallas_call | solution.py:168
  17.0 0.1 collective-permute-start.4
  17.1 0.6 collective-permute-start.3
  17.8 2.6 %collective-permute-start.5 = (f32[2,256,128]{2,1,0:T(8,128)S(1)}, f32[2,256,128]{2,1,0:T(8,128)S(1)}, u32[]{:S(2)}, u32[]{:S(2)}) collective-permute-start(f32[2,256,128]{2,1,0:T(8,128)S(1)} %collective-permute-done.refs_0_.refs_2_), channel_id=1, source_target_pairs={{0,6},{1,7},{2,0},{3,1},{4,2},{5,3},{6,4},{7,5},{8,14},{9,15},{10,... | collective-permute-start | bytes 786440 | tf_op jit(solution)/shard_map/ppermute | solution.py:40
  20.3 1.6 %collective-permute-done.10.refs_7_.refs_5_ = f32[2,256,128]{2,1,0:T(8,128)S(1)} collective-permute-done((f32[2,256,128]{2,1,0:T(8,128)S(1)}, f32[2,256,128]{2,1,0:T(8,128)S(1)}, u32[]{:S(2)}, u32[]{:S(2)}) %collective-permute-start.10) | collective-permute-done | bytes 262176 | tf_op jit(solution)/shard_map/ppermute | solution.py:40
  21.9 0.5 collective-permute-start.7
  22.5 4.8 %shard_map.38 = (bf16[18,512,256]{2,1,0:T(8,128)(2,1)}, bf16[17,512,256]{2,1,0:T(8,128)(2,1)}) custom-call(f32[2,256,128]{2,1,0:T(8,128)} %copy-done.9, f32[2,256,128]{2,1,0:T(8,128)} %copy-done.8, f32[2,256,128]{2,1,0:T(8,128)} %copy-done.7, f32[2,256,128]{2,1,0:T(8,128)} %copy-done.5, ...), custom_call_target="tpu_custom_call", output_to_operand_aliasing={{0}: (6, {}), {1}: (7, {})} | custom-call | flops 3600000000 | bytes 4718592 | tf_op jit(solution)/shard_map/pallas_call | solution.py:168
  27.3 1.8 %collective-permute-done.8.refs_13_.refs_4_ = f32[2,256,128]{2,1,0:T(8,128)S(1)} collective-permute-done((f32[2,256,128]{2,1,0:T(8,128)S(1)}, f32[2,256,128]{2,1,0:T(8,128)S(1)}, u32[]{:S(2)}, u32[]{:S(2)}) %collective-permute-start.8) | collective-permute-done | bytes 262176 | tf_op jit(solution)/shard_map/ppermute | solution.py:40
  29.1 1.1 collective-permute-done.7.refs_11_.refs_3_
  30.2 0.6 copy-done.16
  30.9 0.1 copy-done.14
  31.0 0.1 copy-done.11
  31.1 0.1 copy-done.12
  31.2 2.5 %shard_map.39 = (f32[3,256,128]{2,1,0:T(8,128)}, f32[256,1024]{1,0:T(8,128)}) custom-call(f32[2048,1024]{1,0:T(8,128)} %data_hbm.3, f32[2,256,128]{2,1,0:T(8,128)} %copy-done.2, f32[2,256,128]{2,1,0:T(8,128)} %copy-done.1, f32[2,256,128]{2,1,0:T(8,128)} %copy-done.9, f32[2,256,128]{2,1,0:T(8,128)} %copy-done.5, f32[2,256,128]{2,1,0:T(8,128)} %copy-done.7, ...), custom_call_target="tpu_custom_call" | custom-call | tf_op jit(solution)/shard_map/pallas_call | solution.py:100
  33.7 0.7 collective-permute-start.15
  34.4 4.9 %collective-permute-start.14 = (f32[3,256,128]{2,1,0:T(8,128)}, f32[3,256,128]{2,1,0:T(8,128)S(1)}, u32[]{:S(2)}, u32[]{:S(2)}) collective-permute-start(f32[3,256,128]{2,1,0:T(8,128)} %get-tuple-element.77), channel_id=1, source_target_pairs={{8,0},{9,1},{10,2},{11,3},{12,4},{14,6},{15,7},{16,8},{17,9},{18,1... | collective-permute-start | bytes 1179656 | tf_op jit(solution)/shard_map/ppermute | solution.py:616
  39.3 2.5 %collective-permute-start.12 = (f32[2,256,128]{2,1,0:T(8,128)}, f32[2,256,128]{2,1,0:T(8,128)S(1)}, u32[]{:S(2)}, u32[]{:S(2)}) collective-permute-start(f32[2,256,128]{2,1,0:T(8,128)} %copy-done.14), channel_id=1, source_target_pairs={{0,6},{1,7},{2,0},{3,1},{4,2},{5,3},{6,4},{7,5},{8,14},{9,15},{10,... | collective-permute-start | bytes 786440 | tf_op jit(solution)/shard_map/ppermute | solution.py:40
  41.8 2.9 %collective-permute-start.17 = (f32[256,1024]{1,0:T(8,128)}, f32[256,1024]{1,0:T(8,128)S(1)}, u32[]{:S(2)}, u32[]{:S(2)}) collective-permute-start(f32[256,1024]{1,0:T(8,128)} %get-tuple-element.93), channel_id=1, source_target_pairs={{8,0},{16,8},{24,16},{32,24},{40,32},{48,40},{56,48},{64,56},{72,6... | collective-permute-start | bytes 3145736 | tf_op jit(solution)/shard_map/ppermute | solution.py:60
  44.7 4.8 %shard_map.40 = (bf16[18,512,256]{2,1,0:T(8,128)(2,1)}, bf16[17,512,256]{2,1,0:T(8,128)(2,1)}) custom-call(f32[2,256,128]{2,1,0:T(8,128)} %copy-done.12, f32[2,256,128]{2,1,0:T(8,128)} %copy-done.11, f32[2,256,128]{2,1,0:T(8,128)} %copy-done.14, f32[2,256,128]{2,1,0:T(8,128)} %copy-done.16, ...), custom_call_target="tpu_custom_call", output_to_operand_aliasing={{0}: (6, {}), {1}: (7, {})} | custom-call | flops 3600000000 | bytes 4718592 | tf_op jit(solution)/shard_map/pallas_call | solution.py:168
  49.6 0.5 collective-permute-done.13.refs_1_
  50.1 0.2 copy-done.17
  50.3 0.5 copy-done.18
  50.7 0.1 copy-done.3
  50.9 0.2 copy-done.4
  51.0 3.8 %shard_map.41 = (bf16[18,512,256]{2,1,0:T(8,128)(2,1)}, bf16[17,512,256]{2,1,0:T(8,128)(2,1)}) custom-call(f32[2,256,128]{2,1,0:T(8,128)} %copy-done.17, f32[2,256,128]{2,1,0:T(8,128)} %copy-done.18, f32[3,256,128]{2,1,0:T(8,128)} %copy-done.4, f32[3,256,128]{2,1,0:T(8,128)} %copy-done.3, ...), custom_call_target="tpu_custom_call", output_to_operand_aliasing={{0}: (4, {}), {1}: (5, {})} | custom-call | flops 2100000000 | bytes 2752512 | tf_op jit(solution)/shard_map/pallas_call | solution.py:168
  54.8 11.0 %shard_map.42 = (f32[2048,256]{1,0:T(8,128)S(1)}, f32[256,256]{1,0:T(8,128)S(1)}, f32[256,1024]{1,0:T(8,128)S(1)}) custom-call(bf16[18,512,256]{2,1,0:T(8,128)(2,1)} %get-tuple-element.91.first_hbm, bf16[17,512,256]{2,1,0:T(8,128)(2,1)} %get-tuple-element.92.second_hbm, f32[2048,1024]{1,0:T(8,128)} %data_hbm.3), custom_call_target="tpu_custom_call" | custom-call | flops 4831838208 | bytes 31457280 | tf_op jit(solution)/shard_map/pallas_call | solution.py:381
  65.8 2.0 %collective-permute-start.16 = (f32[256,256]{1,0:T(8,128)S(1)}, f32[256,256]{1,0:T(8,128)S(1)}, u32[]{:S(2)}, u32[]{:S(2)}) collective-permute-start(f32[256,256]{1,0:T(8,128)S(1)} %get-tuple-element.90.own.own_transition), channel_id=1, source_target_pairs={{0,8},{8,0},{16,24},{24,16},{32,40},{40,32},{48,56},{56,48},{64,72... | collective-permute-start | bytes 786440 | tf_op jit(solution)/shard_map/ppermute | solution.py:48
  67.8 1.2 collective-permute-done.16.received.received_transition
  69.0 0.3 shard_map.43.refs_0_
  69.3 2.8 %collective-permute-start.20 = (f32[256,256]{1,0:T(8,128)S(1)}, f32[256,256]{1,0:T(8,128)S(1)}, u32[]{:S(2)}, u32[]{:S(2)}) collective-permute-start(f32[256,256]{1,0:T(8,128)S(1)} %shard_map.43.refs_0_), channel_id=1, source_target_pairs={{0,48},{8,56},{16,0},{24,8},{32,16},{40,24},{48,32},{56,40},{64,11... | collective-permute-start | bytes 786440 | tf_op jit(solution)/shard_map/ppermute | solution.py:56
  72.1 0.3 collective-permute-start.19
  72.4 0.7 collective-permute-start.18
  73.1 17.5 %shard_map.44 = (f32[2048,1024]{1,0:T(8,128)}, f32[256,512]{1,0:T(8,128)S(1)}, f32[256,512]{1,0:T(8,128)S(1)}) custom-call(bf16[18,512,256]{2,1,0:T(8,128)(2,1)} %get-tuple-element.91.first_hbm, bf16[17,512,256]{2,1,0:T(8,128)(2,1)S(1)} %copy-done, f32[2048,1024]{1,0:T(8,128)} %data_hbm.3, f32[256,1024]{1,0:T(8,128)S(1)} %collective-permute-done.17.tail_hbm, ...), custom_call_target="tpu_custom_call" | custom-call | flops 12884901888 | bytes 31457280 | tf_op jit(solution)/shard_map/pallas_call | solution.py:410
  90.7 1.3 collective-permute-start.21
  92.0 1.5 %collective-permute-done.21.received = f32[256,512]{1,0:T(8,128)S(1)} collective-permute-done((f32[256,512]{1,0:T(8,128)S(1)}, f32[256,512]{1,0:T(8,128)S(1)}, u32[]{:S(2)}, u32[]{:S(2)}) %collective-permute-start.21) | collective-permute-done | bytes 524320 | tf_op jit(solution)/shard_map/ppermute | solution.py:48
  93.5 0.5 shard_map.46
  94.1 1.7 %collective-permute-start.22 = (f32[256,128]{1,0:T(8,128)S(1)}, f32[256,128]{1,0:T(8,128)S(1)}, u32[]{:S(2)}, u32[]{:S(2)}) collective-permute-start(f32[256,128]{1,0:T(8,128)S(1)} %get-tuple-element.107), channel_id=1, source_target_pairs={{0,16},{8,24},{16,32},{24,40},{32,48},{40,56},{48,0},{56,8},{64,80... | collective-permute-start | bytes 393224 | tf_op jit(solution)/shard_map/ppermute | solution.py:56
  95.8 1.5 %collective-permute-start.23 = (f32[256,128]{1,0:T(8,128)S(1)}, f32[256,128]{1,0:T(8,128)S(1)}, u32[]{:S(2)}, u32[]{:S(2)}) collective-permute-start(f32[256,128]{1,0:T(8,128)S(1)} %get-tuple-element.108), channel_id=1, source_target_pairs={{0,32},{8,40},{16,48},{24,56},{32,0},{40,8},{48,16},{56,24},{64,96... | collective-permute-start | bytes 393224 | tf_op jit(solution)/shard_map/ppermute | solution.py:56
  97.3 0.9 collective-permute-start.24
  98.3 0.8 shard_map.45
  99.0 1.0 collective-permute-done.22.refs_1_
  100.1 3.3 %collective-permute-done.23.refs_2_ = f32[256,128]{1,0:T(8,128)S(1)} collective-permute-done((f32[256,128]{1,0:T(8,128)S(1)}, f32[256,128]{1,0:T(8,128)S(1)}, u32[]{:S(2)}, u32[]{:S(2)}) %collective-permute-start.23) | collective-permute-done | bytes 131104 | tf_op jit(solution)/shard_map/ppermute | solution.py:56
  103.4 0.9 shard_map.47
  104.3 1.3 collective-permute-start.25
  105.6 5.9 %collective-permute-done.25.entering = f32[256,128]{1,0:T(8,128)S(1)} collective-permute-done((f32[256,128]{1,0:T(8,128)S(1)}, f32[256,128]{1,0:T(8,128)S(1)}, u32[]{:S(2)}, u32[]{:S(2)}) %collective-permute-start.25) | collective-permute-done | bytes 131104 | tf_op jit(solution)/shard_map/ppermute | solution.py:659
  111.5 0.5 shard_map.48
  112.0 3.0 %collective-permute-start.26 = (f32[256,128]{1,0:T(8,128)S(1)}, f32[256,128]{1,0:T(8,128)S(1)}, u32[]{:S(2)}, u32[]{:S(2)}) collective-permute-start(f32[256,128]{1,0:T(8,128)S(1)} %get-tuple-element.114), channel_id=1, source_target_pairs={{0,16},{8,24},{16,32},{24,40},{32,48},{40,56},{48,0},{56,8},{64,80... | collective-permute-start | bytes 393224 | tf_op jit(solution)/shard_map/ppermute | solution.py:56
  115.1 1.7 %collective-permute-start.27 = (f32[256,128]{1,0:T(8,128)S(1)}, f32[256,128]{1,0:T(8,128)S(1)}, u32[]{:S(2)}, u32[]{:S(2)}) collective-permute-start(f32[256,128]{1,0:T(8,128)S(1)} %get-tuple-element.115), channel_id=1, source_target_pairs={{0,32},{8,40},{16,48},{24,56},{32,0},{40,8},{48,16},{56,24},{64,96... | collective-permute-start | bytes 393224 | tf_op jit(solution)/shard_map/ppermute | solution.py:56
  116.8 0.8 collective-permute-start.28
  117.6 0.4 collective-permute-done.26.refs_1_
  118.0 3.3 %collective-permute-done.27.refs_2_ = f32[256,128]{1,0:T(8,128)S(1)} collective-permute-done((f32[256,128]{1,0:T(8,128)S(1)}, f32[256,128]{1,0:T(8,128)S(1)}, u32[]{:S(2)}, u32[]{:S(2)}) %collective-permute-start.27) | collective-permute-done | bytes 131104 | tf_op jit(solution)/shard_map/ppermute | solution.py:56
  121.3 0.5 collective-permute-done.28.refs_3_
  121.8 0.5 shard_map.49
  122.3 2.4 %collective-permute-start.29 = (f32[256,512]{1,0:T(8,128)S(1)}, f32[256,512]{1,0:T(8,128)S(1)}, u32[]{:S(2)}, u32[]{:S(2)}) collective-permute-start(f32[256,512]{1,0:T(8,128)S(1)} %get-tuple-element.118), channel_id=1, source_target_pairs={{0,8},{8,0},{16,24},{24,16},{32,40},{40,32},{48,56},{56,48},{64,72... | collective-permute-start | bytes 1572872 | tf_op jit(solution)/shard_map/ppermute | solution.py:48
  124.7 1.5 %collective-permute-done.29.taken = f32[256,512]{1,0:T(8,128)S(1)} collective-permute-done((f32[256,512]{1,0:T(8,128)S(1)}, f32[256,512]{1,0:T(8,128)S(1)}, u32[]{:S(2)}, u32[]{:S(2)}) %collective-permute-start.29) | collective-permute-done | bytes 524320 | tf_op jit(solution)/shard_map/ppermute | solution.py:48
  126.3 7.1 %shard_map.50 = f32[2048,1024]{1,0:T(8,128)} custom-call(f32[2048,1024]{1,0:T(8,128)} %get-tuple-element.95.rows_hbm, f32[2048,256]{1,0:T(8,128)S(1)} %get-tuple-element.96.response_hbm, f32[256,512]{1,0:T(8,128)S(1)} %get-tuple-element.117.kept, f32[256,512]{1,0:T(8,128)S(1)} %collective-permute-done.29.taken), custom_call_target="tpu_custom_call" | custom-call | tf_op jit(solution)/shard_map/pallas_call | solution.py:557
  (51 shorter events, 0.2 us)
Async XLA Ops:
  1.2 12.8 %copy-start.1 = (f32[2,256,128]{2,1,0:T(8,128)}, f32[2,256,128]{2,1,0:T(8,128)S(1)}, u32[]{:S(2)}) copy-start(f32[2,256,128]{2,1,0:T(8,128)S(1)} %get-tuple-element.119.refs_1_) | copy-start | bytes 786436
  1.2 12.8 %copy-start.2 = (f32[2,256,128]{2,1,0:T(8,128)}, f32[2,256,128]{2,1,0:T(8,128)S(1)}, u32[]{:S(2)}) copy-start(f32[2,256,128]{2,1,0:T(8,128)S(1)} %get-tuple-element.120.refs_0_) | copy-start | bytes 786436
  1.3 8.0 %collective-permute-start.9 = (f32[2,256,128]{2,1,0:T(8,128)S(1)}, f32[2,256,128]{2,1,0:T(8,128)S(1)}, u32[]{:S(2)}, u32[]{:S(2)}) collective-permute-start(f32[2,256,128]{2,1,0:T(8,128)S(1)} %get-tuple-element.119.refs_1_), channel_id=1, source_target_pairs={{0,1},{1,0},{2,3},{3,2},{4,5},{5,4},{6,7},{7,6},{8,9},{9,8},{10,11... | collective-permute-start | bytes 786440 | tf_op jit(solution)/shard_map/ppermute | solution.py:44
  2.3 8.4 %collective-permute-start.2 = (f32[2,256,128]{2,1,0:T(8,128)S(1)}, f32[2,256,128]{2,1,0:T(8,128)S(1)}, u32[]{:S(2)}, u32[]{:S(2)}) collective-permute-start(f32[2,256,128]{2,1,0:T(8,128)S(1)} %get-tuple-element.120.refs_0_), channel_id=1, source_target_pairs={{0,6},{1,7},{2,0},{3,1},{4,2},{5,3},{6,4},{7,5},{8,14},{9,15},{10,... | collective-permute-start | bytes 786440 | tf_op jit(solution)/shard_map/ppermute | solution.py:40
  6.0 11.0 %collective-permute-start.1 = (f32[2,256,128]{2,1,0:T(8,128)S(1)}, f32[2,256,128]{2,1,0:T(8,128)S(1)}, u32[]{:S(2)}, u32[]{:S(2)}) collective-permute-start(f32[2,256,128]{2,1,0:T(8,128)S(1)} %get-tuple-element.120.refs_0_), channel_id=1, source_target_pairs={{0,2},{1,3},{2,4},{3,5},{4,6},{5,7},{6,0},{7,1},{8,10},{9,11},{10,... | collective-permute-start | bytes 786440 | tf_op jit(solution)/shard_map/ppermute | solution.py:40
  6.0 11.0 %collective-permute-start = (f32[2,256,128]{2,1,0:T(8,128)S(1)}, f32[2,256,128]{2,1,0:T(8,128)S(1)}, u32[]{:S(2)}, u32[]{:S(2)}) collective-permute-start(f32[2,256,128]{2,1,0:T(8,128)S(1)} %get-tuple-element.120.refs_0_), channel_id=1, source_target_pairs={{0,1},{1,0},{2,3},{3,2},{4,5},{5,4},{6,7},{7,6},{8,9},{9,8},{10,11... | collective-permute-start | bytes 786440 | tf_op jit(solution)/shard_map/ppermute | solution.py:44
  6.6 11.2 %collective-permute-start.11 = (f32[2,256,128]{2,1,0:T(8,128)S(1)}, f32[2,256,128]{2,1,0:T(8,128)S(1)}, u32[]{:S(2)}, u32[]{:S(2)}) collective-permute-start(f32[2,256,128]{2,1,0:T(8,128)S(1)} %get-tuple-element.119.refs_1_), channel_id=1, source_target_pairs={{0,6},{1,7},{2,0},{3,1},{4,2},{5,3},{6,4},{7,5},{8,14},{9,15},{10,... | collective-permute-start | bytes 786440 | tf_op jit(solution)/shard_map/ppermute | solution.py:40
  9.2 13.2 %copy-start.5 = (f32[2,256,128]{2,1,0:T(8,128)}, f32[2,256,128]{2,1,0:T(8,128)S(1)}, u32[]{:S(2)}) copy-start(f32[2,256,128]{2,1,0:T(8,128)S(1)} %collective-permute-done.9.refs_3_) | copy-start | bytes 786436
  9.2 11.1 %collective-permute-start.6 = (f32[2,256,128]{2,1,0:T(8,128)S(1)}, f32[2,256,128]{2,1,0:T(8,128)S(1)}, u32[]{:S(2)}, u32[]{:S(2)}) collective-permute-start(f32[2,256,128]{2,1,0:T(8,128)S(1)} %get-tuple-element.119.refs_1_), channel_id=1, source_target_pairs={{0,2},{1,3},{2,4},{3,5},{4,6},{5,7},{6,0},{7,1},{8,10},{9,11},{10,... | collective-permute-start | bytes 786440 | tf_op jit(solution)/shard_map/ppermute | solution.py:40
  10.7 11.8 %copy-start.7 = (f32[2,256,128]{2,1,0:T(8,128)}, f32[2,256,128]{2,1,0:T(8,128)S(1)}, u32[]{:S(2)}) copy-start(f32[2,256,128]{2,1,0:T(8,128)S(1)} %collective-permute-done.2.refs_2_.refs_4_) | copy-start | bytes 786436
  10.7 11.2 %collective-permute-start.10 = (f32[2,256,128]{2,1,0:T(8,128)S(1)}, f32[2,256,128]{2,1,0:T(8,128)S(1)}, u32[]{:S(2)}, u32[]{:S(2)}) collective-permute-start(f32[2,256,128]{2,1,0:T(8,128)S(1)} %collective-permute-done.9.refs_3_), channel_id=1, source_target_pairs={{0,6},{1,7},{2,0},{3,1},{4,2},{5,3},{6,4},{7,5},{8,14},{9,15},{10,... | collective-permute-start | bytes 786440 | tf_op jit(solution)/shard_map/ppermute | solution.py:40
  17.0 5.5 %copy-start.8 = (f32[2,256,128]{2,1,0:T(8,128)}, f32[2,256,128]{2,1,0:T(8,128)S(1)}, u32[]{:S(2)}) copy-start(f32[2,256,128]{2,1,0:T(8,128)S(1)} %collective-permute-done.1.refs_1_.refs_8_) | copy-start | bytes 786436
  17.0 5.5 %copy-start.9 = (f32[2,256,128]{2,1,0:T(8,128)}, f32[2,256,128]{2,1,0:T(8,128)S(1)}, u32[]{:S(2)}) copy-start(f32[2,256,128]{2,1,0:T(8,128)S(1)} %collective-permute-done.refs_0_.refs_2_) | copy-start | bytes 786436
  17.0 13.2 %collective-permute-start.4 = (f32[2,256,128]{2,1,0:T(8,128)S(1)}, f32[2,256,128]{2,1,0:T(8,128)S(1)}, u32[]{:S(2)}, u32[]{:S(2)}) collective-permute-start(f32[2,256,128]{2,1,0:T(8,128)S(1)} %collective-permute-done.1.refs_1_.refs_8_), channel_id=1, source_target_pairs={{0,2},{1,3},{2,4},{3,5},{4,6},{5,7},{6,0},{7,1},{8,10},{9,11},{10,... | collective-permute-start | bytes 786440 | tf_op jit(solution)/shard_map/ppermute | solution.py:40
  17.1 13.1 %collective-permute-start.3 = (f32[2,256,128]{2,1,0:T(8,128)S(1)}, f32[2,256,128]{2,1,0:T(8,128)S(1)}, u32[]{:S(2)}, u32[]{:S(2)}) collective-permute-start(f32[2,256,128]{2,1,0:T(8,128)S(1)} %collective-permute-done.1.refs_1_.refs_8_), channel_id=1, source_target_pairs={{0,1},{1,0},{2,3},{3,2},{4,5},{5,4},{6,7},{7,6},{8,9},{9,8},{10,11... | collective-permute-start | bytes 786440 | tf_op jit(solution)/shard_map/ppermute | solution.py:44
  17.8 4.7 %copy-start.10 = (f32[2,256,128]{2,1,0:T(8,128)}, f32[2,256,128]{2,1,0:T(8,128)S(1)}, u32[]{:S(2)}) copy-start(f32[2,256,128]{2,1,0:T(8,128)S(1)} %collective-permute-done.11.refs_5_) | copy-start | bytes 786436
  17.8 12.4 %collective-permute-start.5 = (f32[2,256,128]{2,1,0:T(8,128)S(1)}, f32[2,256,128]{2,1,0:T(8,128)S(1)}, u32[]{:S(2)}, u32[]{:S(2)}) collective-permute-start(f32[2,256,128]{2,1,0:T(8,128)S(1)} %collective-permute-done.refs_0_.refs_2_), channel_id=1, source_target_pairs={{0,6},{1,7},{2,0},{3,1},{4,2},{5,3},{6,4},{7,5},{8,14},{9,15},{10,... | collective-permute-start | bytes 786440 | tf_op jit(solution)/shard_map/ppermute | solution.py:40
  20.3 2.1 %copy-start.13 = (f32[2,256,128]{2,1,0:T(8,128)}, f32[2,256,128]{2,1,0:T(8,128)S(1)}, u32[]{:S(2)}) copy-start(f32[2,256,128]{2,1,0:T(8,128)S(1)} %collective-permute-done.6.refs_4_.refs_9_) | copy-start | bytes 786436
  20.3 8.7 %collective-permute-start.8 = (f32[2,256,128]{2,1,0:T(8,128)S(1)}, f32[2,256,128]{2,1,0:T(8,128)S(1)}, u32[]{:S(2)}, u32[]{:S(2)}) collective-permute-start(f32[2,256,128]{2,1,0:T(8,128)S(1)} %collective-permute-done.6.refs_4_.refs_9_), channel_id=1, source_target_pairs={{0,2},{1,3},{2,4},{3,5},{4,6},{5,7},{6,0},{7,1},{8,10},{9,11},{10,... | collective-permute-start | bytes 786440 | tf_op jit(solution)/shard_map/ppermute | solution.py:40
  21.9 5.4 %copy-start.6 = (f32[2,256,128]{2,1,0:T(8,128)}, f32[2,256,128]{2,1,0:T(8,128)S(1)}, u32[]{:S(2)}) copy-start(f32[2,256,128]{2,1,0:T(8,128)S(1)} %collective-permute-done.10.refs_7_.refs_5_) | copy-start | bytes 786436
  21.9 8.3 %collective-permute-start.7 = (f32[2,256,128]{2,1,0:T(8,128)S(1)}, f32[2,256,128]{2,1,0:T(8,128)S(1)}, u32[]{:S(2)}, u32[]{:S(2)}) collective-permute-start(f32[2,256,128]{2,1,0:T(8,128)S(1)} %collective-permute-done.6.refs_4_.refs_9_), channel_id=1, source_target_pairs={{0,1},{1,0},{2,3},{3,2},{4,5},{5,4},{6,7},{7,6},{8,9},{9,8},{10,11... | collective-permute-start | bytes 786440 | tf_op jit(solution)/shard_map/ppermute | solution.py:44
  29.1 1.1 copy-start.15
  30.2 0.7 copy-start.16
  30.2 0.8 copy-start.14
  30.2 0.9 copy-start.11
  30.2 0.9 copy-start.12
  33.7 16.4 %collective-permute-start.15 = (f32[3,256,128]{2,1,0:T(8,128)}, f32[3,256,128]{2,1,0:T(8,128)S(1)}, u32[]{:S(2)}, u32[]{:S(2)}) collective-permute-start(f32[3,256,128]{2,1,0:T(8,128)} %get-tuple-element.77), channel_id=1, source_target_pairs={{12,5},{20,13},{28,21},{36,29},{44,37},{52,45},{60,53},{68,61},{76... | collective-permute-start | bytes 1179656 | tf_op jit(solution)/shard_map/ppermute | solution.py:621
  34.4 15.7 %collective-permute-start.14 = (f32[3,256,128]{2,1,0:T(8,128)}, f32[3,256,128]{2,1,0:T(8,128)S(1)}, u32[]{:S(2)}, u32[]{:S(2)}) collective-permute-start(f32[3,256,128]{2,1,0:T(8,128)} %get-tuple-element.77), channel_id=1, source_target_pairs={{8,0},{9,1},{10,2},{11,3},{12,4},{14,6},{15,7},{16,8},{17,9},{18,1... | collective-permute-start | bytes 1179656 | tf_op jit(solution)/shard_map/ppermute | solution.py:616
  39.3 10.3 %collective-permute-start.12 = (f32[2,256,128]{2,1,0:T(8,128)}, f32[2,256,128]{2,1,0:T(8,128)S(1)}, u32[]{:S(2)}, u32[]{:S(2)}) collective-permute-start(f32[2,256,128]{2,1,0:T(8,128)} %copy-done.14), channel_id=1, source_target_pairs={{0,6},{1,7},{2,0},{3,1},{4,2},{5,3},{6,4},{7,5},{8,14},{9,15},{10,... | collective-permute-start | bytes 786440 | tf_op jit(solution)/shard_map/ppermute | solution.py:40
  41.8 8.2 %collective-permute-start.13 = (f32[2,256,128]{2,1,0:T(8,128)}, f32[2,256,128]{2,1,0:T(8,128)S(1)}, u32[]{:S(2)}, u32[]{:S(2)}) collective-permute-start(f32[2,256,128]{2,1,0:T(8,128)} %copy-done.16), channel_id=1, source_target_pairs={{0,2},{1,3},{2,4},{3,5},{4,6},{5,7},{6,0},{7,1},{8,10},{9,11},{10,... | collective-permute-start | bytes 786440 | tf_op jit(solution)/shard_map/ppermute | solution.py:40
  41.8 31.3 %collective-permute-start.17 = (f32[256,1024]{1,0:T(8,128)}, f32[256,1024]{1,0:T(8,128)S(1)}, u32[]{:S(2)}, u32[]{:S(2)}) collective-permute-start(f32[256,1024]{1,0:T(8,128)} %get-tuple-element.93), channel_id=1, source_target_pairs={{8,0},{16,8},{24,16},{32,24},{40,32},{48,40},{56,48},{64,56},{72,6... | collective-permute-start | bytes 3145736 | tf_op jit(solution)/shard_map/ppermute | solution.py:60
  49.5 0.7 copy-start.17
  50.0 0.7 copy-start.18
  50.0 0.8 copy-start.3
  50.0 1.0 copy-start.4
  54.8 18.3 %copy-start = (bf16[17,512,256]{2,1,0:T(8,128)(2,1)S(1)}, bf16[17,512,256]{2,1,0:T(8,128)(2,1)}, u32[]{:S(2)}) copy-start(bf16[17,512,256]{2,1,0:T(8,128)(2,1)} %get-tuple-element.92.second_hbm) | copy-start | bytes 13369348
  65.8 3.2 %collective-permute-start.16 = (f32[256,256]{1,0:T(8,128)S(1)}, f32[256,256]{1,0:T(8,128)S(1)}, u32[]{:S(2)}, u32[]{:S(2)}) collective-permute-start(f32[256,256]{1,0:T(8,128)S(1)} %get-tuple-element.90.own.own_transition), channel_id=1, source_target_pairs={{0,8},{8,0},{16,24},{24,16},{32,40},{40,32},{48,56},{56,48},{64,72... | collective-permute-start | bytes 786440 | tf_op jit(solution)/shard_map/ppermute | solution.py:48
  69.3 21.3 %collective-permute-start.20 = (f32[256,256]{1,0:T(8,128)S(1)}, f32[256,256]{1,0:T(8,128)S(1)}, u32[]{:S(2)}, u32[]{:S(2)}) collective-permute-start(f32[256,256]{1,0:T(8,128)S(1)} %shard_map.43.refs_0_), channel_id=1, source_target_pairs={{0,48},{8,56},{16,0},{24,8},{32,16},{40,24},{48,32},{56,40},{64,11... | collective-permute-start | bytes 786440 | tf_op jit(solution)/shard_map/ppermute | solution.py:56
  72.1 18.6 %collective-permute-start.19 = (f32[256,256]{1,0:T(8,128)S(1)}, f32[256,256]{1,0:T(8,128)S(1)}, u32[]{:S(2)}, u32[]{:S(2)}) collective-permute-start(f32[256,256]{1,0:T(8,128)S(1)} %shard_map.43.refs_0_), channel_id=1, source_target_pairs={{0,32},{8,40},{16,48},{24,56},{32,0},{40,8},{48,16},{56,24},{64,96... | collective-permute-start | bytes 786440 | tf_op jit(solution)/shard_map/ppermute | solution.py:56
  72.4 18.2 %collective-permute-start.18 = (f32[256,256]{1,0:T(8,128)S(1)}, f32[256,256]{1,0:T(8,128)S(1)}, u32[]{:S(2)}, u32[]{:S(2)}) collective-permute-start(f32[256,256]{1,0:T(8,128)S(1)} %shard_map.43.refs_0_), channel_id=1, source_target_pairs={{0,16},{8,24},{16,32},{24,40},{32,48},{40,56},{48,0},{56,8},{64,80... | collective-permute-start | bytes 786440 | tf_op jit(solution)/shard_map/ppermute | solution.py:56
  90.7 2.8 %collective-permute-start.21 = (f32[256,512]{1,0:T(8,128)S(1)}, f32[256,512]{1,0:T(8,128)S(1)}, u32[]{:S(2)}, u32[]{:S(2)}) collective-permute-start(f32[256,512]{1,0:T(8,128)S(1)} %get-tuple-element.100), channel_id=1, source_target_pairs={{0,8},{8,0},{16,24},{24,16},{32,40},{40,32},{48,56},{56,48},{64,72... | collective-permute-start | bytes 1572872 | tf_op jit(solution)/shard_map/ppermute | solution.py:48
  94.1 6.0 %collective-permute-start.22 = (f32[256,128]{1,0:T(8,128)S(1)}, f32[256,128]{1,0:T(8,128)S(1)}, u32[]{:S(2)}, u32[]{:S(2)}) collective-permute-start(f32[256,128]{1,0:T(8,128)S(1)} %get-tuple-element.107), channel_id=1, source_target_pairs={{0,16},{8,24},{16,32},{24,40},{32,48},{40,56},{48,0},{56,8},{64,80... | collective-permute-start | bytes 393224 | tf_op jit(solution)/shard_map/ppermute | solution.py:56
  95.8 7.6 %collective-permute-start.23 = (f32[256,128]{1,0:T(8,128)S(1)}, f32[256,128]{1,0:T(8,128)S(1)}, u32[]{:S(2)}, u32[]{:S(2)}) collective-permute-start(f32[256,128]{1,0:T(8,128)S(1)} %get-tuple-element.108), channel_id=1, source_target_pairs={{0,32},{8,40},{16,48},{24,56},{32,0},{40,8},{48,16},{56,24},{64,96... | collective-permute-start | bytes 393224 | tf_op jit(solution)/shard_map/ppermute | solution.py:56
  97.3 6.1 %collective-permute-start.24 = (f32[256,128]{1,0:T(8,128)S(1)}, f32[256,128]{1,0:T(8,128)S(1)}, u32[]{:S(2)}, u32[]{:S(2)}) collective-permute-start(f32[256,128]{1,0:T(8,128)S(1)} %get-tuple-element.109), channel_id=1, source_target_pairs={{0,48},{8,56},{16,0},{24,8},{32,16},{40,24},{48,32},{56,40},{64,11... | collective-permute-start | bytes 393224 | tf_op jit(solution)/shard_map/ppermute | solution.py:56
  104.3 7.2 %collective-permute-start.25 = (f32[256,128]{1,0:T(8,128)S(1)}, f32[256,128]{1,0:T(8,128)S(1)}, u32[]{:S(2)}, u32[]{:S(2)}) collective-permute-start(f32[256,128]{1,0:T(8,128)S(1)} %get-tuple-element.110), channel_id=1, source_target_pairs={{0,64},{8,72},{16,80},{24,88},{32,96},{40,104},{48,112},{56,120},{... | collective-permute-start | bytes 393224 | tf_op jit(solution)/shard_map/ppermute | solution.py:659
  112.0 5.9 %collective-permute-start.26 = (f32[256,128]{1,0:T(8,128)S(1)}, f32[256,128]{1,0:T(8,128)S(1)}, u32[]{:S(2)}, u32[]{:S(2)}) collective-permute-start(f32[256,128]{1,0:T(8,128)S(1)} %get-tuple-element.114), channel_id=1, source_target_pairs={{0,16},{8,24},{16,32},{24,40},{32,48},{40,56},{48,0},{56,8},{64,80... | collective-permute-start | bytes 393224 | tf_op jit(solution)/shard_map/ppermute | solution.py:56
  115.1 6.2 %collective-permute-start.27 = (f32[256,128]{1,0:T(8,128)S(1)}, f32[256,128]{1,0:T(8,128)S(1)}, u32[]{:S(2)}, u32[]{:S(2)}) collective-permute-start(f32[256,128]{1,0:T(8,128)S(1)} %get-tuple-element.115), channel_id=1, source_target_pairs={{0,32},{8,40},{16,48},{24,56},{32,0},{40,8},{48,16},{56,24},{64,96... | collective-permute-start | bytes 393224 | tf_op jit(solution)/shard_map/ppermute | solution.py:56
  116.8 5.0 %collective-permute-start.28 = (f32[256,128]{1,0:T(8,128)S(1)}, f32[256,128]{1,0:T(8,128)S(1)}, u32[]{:S(2)}, u32[]{:S(2)}) collective-permute-start(f32[256,128]{1,0:T(8,128)S(1)} %get-tuple-element.116), channel_id=1, source_target_pairs={{0,48},{8,56},{16,0},{24,8},{32,16},{40,24},{48,32},{56,40},{64,11... | collective-permute-start | bytes 393224 | tf_op jit(solution)/shard_map/ppermute | solution.py:56
  122.3 4.0 %collective-permute-start.29 = (f32[256,512]{1,0:T(8,128)S(1)}, f32[256,512]{1,0:T(8,128)S(1)}, u32[]{:S(2)}, u32[]{:S(2)}) collective-permute-start(f32[256,512]{1,0:T(8,128)S(1)} %get-tuple-element.118), channel_id=1, source_target_pairs={{0,8},{8,0},{16,24},{24,16},{32,40},{40,32},{48,56},{56,48},{64,72... | collective-permute-start | bytes 1572872 | tf_op jit(solution)/shard_map/ppermute | solution.py:48
